TPU v7x, 128 devices: a whole 4x4x4 slice. The times are simulated.
128 devices in a mesh: row: 8 (over z, core), col: 16 (over y, x).
Axes of the slice: x: 4, y: 4, z: 4, core: 2. Of those that a mesh axis runs over, the one named last changes fastest.
Arguments:
- front_entries: float32 [16384, 16384], P('row', 'col'), may hold values from -6 to 6
- children: float32 [20480, 10240], P('row', 'col'), may hold values from -6 to 6
- child_maps: int32 [2, 80], replicated, may hold values from 0 to 127, as said below
- pivots: int32 [1024], replicated, may hold values from 0 to 16383, as said below
- diag_inverses: float32 [2, 512, 512], replicated, may hold values from -0.005859375 to 0.005859375
Outputs:
- factored: float32 [16384, 16384], P('row', 'col')
Inputs may be any that keep to these rules, and one draw needn't show every extreme that they name: For each child the front blocks are distinct, and child_maps[h, i] equals i modulo 16: a child block lies in the same block-column of the device grid as its front block. `pivots`: distinct front rows.
All inputs are finite; a program needn't handle non-finite values.
Results may differ from a plain program's by a relative error of at most 0.0001.
Values sent between devices are 32-bit elements; how exact they have to be, the bound alone decides.
No kernel may reach another device: no remote copies, remote signals or barrier semaphores. Data moves between devices by JAX's collectives and lax.ppermute only.
A program may use at most 128 MiB of HBM per device.

v0:
```python
import jax
import jax.numpy as jnp
from jax import lax
from jax.sharding import PartitionSpec as P

BLK = 128
PANEL = 512


def from_partner(block, axis, bit):
    count = lax.axis_size(axis)
    route = []
    for low in range(count):
        high = low | 1 << bit
        if high != low and high < count:
            route += [(low, high), (high, low)]
    return lax.ppermute(block, axis, route)


def lookup(table, wanted):
    hits = jnp.arange(table.shape[0], dtype=jnp.int32)[None, :] == wanted[:, None]
    return jnp.sum(jnp.where(hits, table[None, :], 0), axis=1)


def local(front_entries, children, child_maps, pivots, diag_inverses):
    rows_dev, cols_dev = front_entries.shape
    nrow = lax.axis_size("row")
    ncol = lax.axis_size("col")
    here_row = lax.axis_index("row")
    here_col = lax.axis_index("col")
    half_rows = nrow // 2
    side = here_row // half_rows
    blocks_r = rows_dev // BLK
    blocks_c = cols_dev // BLK
    child_rows, child_cols = children.shape
    kept_blocks = child_rows // BLK // 2
    child_cblocks = child_cols // BLK
    pieces = children.reshape(kept_blocks, 2, BLK, child_cols)
    kept = lax.dynamic_index_in_dim(pieces, side, 1, keepdims=False)
    sent = lax.dynamic_index_in_dim(pieces, 1 - side, 1, keepdims=False)
    received = from_partner(sent, "row", half_rows.bit_length() - 1)
    block_ids = jnp.arange(kept_blocks, dtype=jnp.int32) * nrow + here_row
    column_ids = jnp.arange(child_cblocks, dtype=jnp.int32) * ncol + here_col
    local_rows = jnp.arange(blocks_r, dtype=jnp.int32)
    local_cols = jnp.arange(blocks_c, dtype=jnp.int32)

    def place(piece, which):
        mapping = lax.dynamic_index_in_dim(child_maps, which, 0, keepdims=False)
        target_r = lookup(mapping, block_ids) // nrow
        target_c = lookup(mapping, column_ids) // ncol
        select_r = (target_r[:, None] == local_rows[None, :]).astype(jnp.float32)
        select_c = (target_c[:, None] == local_cols[None, :]).astype(jnp.float32)
        grid = piece.reshape(kept_blocks, BLK, child_cblocks, BLK)
        return jnp.einsum(
            "mb,minj,nd->bidj", select_r, grid, select_c, precision=lax.Precision.HIGHEST
        )

    front = front_entries.reshape(blocks_r, BLK, blocks_c, BLK)
    front = front + place(kept, side) + place(received, 1 - side)
    front = front.reshape(rows_dev, cols_dev)
    row_span = jnp.arange(rows_dev, dtype=jnp.int32)
    col_span = jnp.arange(cols_dev, dtype=jnp.int32)
    row_nat = (row_span // BLK * nrow + here_row) * BLK + row_span % BLK
    col_nat = (col_span // BLK * ncol + here_col) * BLK + col_span % BLK
    panel_blocks = PANEL // BLK
    for step in range(2):
        used = pivots[: (step + 1) * PANEL]
        chosen = pivots[step * PANEL : (step + 1) * PANEL]
        owner = chosen // BLK % nrow
        local_index = chosen // BLK // nrow * BLK + chosen % BLK
        picked = jnp.take(front, local_index, axis=0, mode="clip")
        keep_mask = (owner == here_row)[:, None] & (col_nat >= (step + 1) * PANEL)[None, :]
        upper = lax.psum(jnp.where(keep_mask, picked, jnp.float32(0.0)), "row")
        inverse = diag_inverses[step]
        slot = here_col - step * panel_blocks
        owns = (slot >= 0) & (slot < panel_blocks)
        slot_safe = jnp.clip(slot, 0, panel_blocks - 1)
        inverse_rows = lax.dynamic_slice_in_dim(inverse, slot_safe * BLK, BLK, 0)
        term = jnp.dot(
            front[:, :BLK],
            inverse_rows,
            precision=lax.Precision.HIGHEST,
            preferred_element_type=jnp.float32,
        )
        lower = lax.psum(jnp.where(owns, term, jnp.float32(0.0)), "col")
        active = jnp.all(row_nat[:, None] != used[None, :], axis=1)
        update = jnp.dot(
            lower, upper, precision=lax.Precision.HIGHEST, preferred_element_type=jnp.float32
        )
        front = front - jnp.where(active[:, None], update, jnp.float32(0.0))
        mine = lax.dynamic_slice_in_dim(lower, slot_safe * BLK, BLK, 1)
        fresh = jnp.where(owns & active[:, None], mine, front[:, :BLK])
        front = jnp.concatenate([fresh, front[:, BLK:]], axis=1)
    return front


def solution(mesh):
    return jax.shard_map(
        local,
        mesh=mesh,
        in_specs=(P("row", "col"), P("row", "col"), P(), P(), P()),
        out_specs=P("row", "col"),
        check_vma=False,
    )
```

profile of v0, /device:TPU:1, one launch (start us, length us, event | category | flops | bytes accessed | tf_op | source)
XLA Modules:
  0.0 551.1 jit_solution(16375475215832235578)
XLA Ops:
  6.5 0.0 all-reduce.7.cloned.1.call-start
  6.5 6.4 %constant_dynamic-slice_fusion.2 = (f32[10,1,128,640]{3,2,1,0:T(8,128)}, f32[10,128,640]{2,1,0:T(8,128)}) fusion(f32[10,2,128,640]{3,2,1,0:T(8,128)} %bitcast.72, s32[]{:T(128)S(6)} %select_n.187, s32[]{:T(128)S(6)} %select_n.192), kind=kLoop, calls=%fused_computation.117 | loop fusion | bytes 13107208 | tf_op jit(solution)/shard_map/jit(dynamic_index_in_dim)/dynamic_slice | solution.py:39
  12.9 4.4 collective-permute-start
  17.3 3.5 copy.31
  20.9 5.6 %copy.32 = f32[10,128,5,128]{3,0,2,1:T(8,128)} copy(f32[10,128,5,128]{1,3,2,0:T(8,128)S(1)} %bitcast.69) | data formatting | bytes 6553600 | tf_op jit(solution)/shard_map/reshape | solution.py:53
  26.4 9.1 %copy.47 = f32[256,8,8,128]{3,2,1,0:T(8,128)} copy(f32[256,8,8,128]{3,1,2,0:T(8,128)} %bitcast.71) | data formatting | bytes 16777216
  35.6 0.2 select_reduce_fusion.3
  35.8 0.2 select_reduce_fusion.1
  36.0 5.2 fusion.27
  41.2 47.0 %collective-permute-done = f32[10,128,640]{2,1,0:T(8,128)} collective-permute-done((f32[10,128,640]{2,1,0:T(8,128)}, f32[10,128,640]{2,1,0:T(8,128)}, u32[]{:S(2)}, u32[]{:S(2)}) %collective-permute-start) | collective-permute-done | bytes 3276832 | tf_op jit(solution)/shard_map/ppermute | solution.py:17
  88.3 3.5 copy.35
  91.8 5.8 %copy.36 = f32[10,128,5,128]{3,0,2,1:T(8,128)} copy(f32[10,128,5,128]{1,3,2,0:T(8,128)S(1)} %bitcast.70) | data formatting | bytes 6553600 | tf_op jit(solution)/shard_map/reshape | solution.py:53
  97.6 5.3 fusion.30
  102.9 0.0 slice-start
  102.9 0.0 slice-start.1
  102.9 5.7 %fusion = f32[128,128,16,8]{1,3,2,0:T(8,128)S(1)} fusion(f32[128,5,128,16]{2,3,1,0:T(8,128)S(1)} %fusion.30, s32[5]{0:T(128)S(1)} %get-tuple-element.21), kind=kOutput, calls=%fused_computation.7 | convolution fusion | flops 125829160 | bytes 13631508 | tf_op jit(solution)/shard_map/mb,minj,nd->bidj/dot_general | solution.py:54
  108.6 11.1 %bitcast_add_fusion = f32[16,128,8,128]{3,2,0,1:T(8,128)} fusion(f32[128,128,16,8]{1,3,2,0:T(8,128)S(1)} %fusion, f32[128,5,128,16]{2,3,1,0:T(8,128)S(1)} %bitcast.67, s32[5]{0:T(128)S(1)} %get-tuple-element.22, f32[16,128,8,128]{3,2,1,0:T(8,128)} %bitcast.68), kind=kOutput, calls=%fused_computation.5 | convolution fusion | flops 130023464 | bytes 30408724 | tf_op jit(solution)/shard_map/mb,minj,nd->bidj/dot_general | solution.py:54
  119.7 4.2 copy.38
  124.0 6.1 %copy.59 = f32[256,8,8,128]{3,1,2,0:T(8,128)} copy(f32[256,8,8,128]{3,2,1,0:T(8,128)S(1)} %bitcast.62) | data formatting | bytes 16777216
  130.1 6.2 %gather_fusion = f32[512,1024]{1,0:T(8,128)S(1)} fusion(f32[2048,1024]{1,0:T(8,128)} %bitcast.64, s32[1024]{0:T(1024)S(1)} %pad_clamp_fusion.1), kind=kCustom, calls=%fused_computation | custom fusion | bytes 4196352 | tf_op jit(solution)/shard_map/jit(_take)/gather | solution.py:71
  136.3 1.6 and_select_fusion.1
  137.9 0.0 all-reduce.7.cloned.1.call-update
  137.9 0.0 all-reduce.5.cloned.1.call-start
  138.0 2.7 fusion.61
  140.7 6.2 %convolution_select_fusion.1 = f32[2048,512]{1,0:T(8,128)} fusion(pred[]{:T(512)S(6)} %and.213, f32[2048,1024]{1,0:T(8,128)} %bitcast.65, f32[1,512,512]{2,1,0:T(8,128)S(1)} %get-tuple-element.14, s32[]{:T(128)S(6)} %select_n.197), kind=kOutput, calls=%fused_computation.17 | convolution fusion | flops 1611661312 | bytes 5505029 | tf_op jit(solution)/shard_map/dot_general | solution.py:79
  146.9 0.0 all-reduce.5.cloned.1.call-update
  146.9 0.0 all-reduce.11.cloned.1.call-start
  147.0 0.8 compare_reduce_fusion.1
  147.8 56.7 %all-reduce.7.cloned.1.call-done = f32[512,1024]{1,0:T(8,128)} async-done(((f32[512,1024]{1,0:T(8,128)}), f32[512,1024]{1,0:T(8,128)}) %all-reduce.7.cloned.1.call-update) | async-done | bytes 2097168 | tf_op jit(solution)/shard_map/psum | solution.py:73
  204.4 107.8 %all-reduce.5.cloned.1.call-done = f32[2048,512]{1,0:T(8,128)} async-done(((f32[2048,512]{1,0:T(8,128)}), f32[2048,512]{1,0:T(8,128)}) %all-reduce.5.cloned.1.call-update) | async-done | bytes 4194320 | tf_op jit(solution)/shard_map/psum | solution.py:85
  312.3 19.7 %select_subtract_fusion.1 = f32[2048,1024]{1,0:T(8,128)S(1)} fusion(pred[2048]{0:T(1024)(128)(4,1)S(1)} %compare_reduce_fusion.1, f32[2048,512]{1,0:T(8,128)} %all-reduce.5.cloned.1.call-done, f32[512,1024]{1,0:T(8,128)} %all-reduce.7.cloned.1.call-done, f32[256,8,8,128]{3,2,1,0:T(8,128)} %bitcast.63), kind=kOutput, calls=%fused_computation.12 | convolution fusion | flops 12889096192 | bytes 23070720 | tf_op jit(solution)/shard_map/dot_general | solution.py:87
  331.9 0.9 slice.43
  332.8 2.4 slice_select_fusion.1
  335.2 0.5 copy-done.1
  335.7 4.6 pad_maximum_fusion
  340.3 6.2 %gather_fusion.1 = f32[512,1024]{1,0:T(8,128)S(1)} fusion(f32[2048,1024]{1,0:T(8,128)} %pad_maximum_fusion, s32[1024]{0:T(1024)S(1)} %pad_clamp_fusion), kind=kCustom, calls=%fused_computation.1 | custom fusion | bytes 4196352 | tf_op jit(solution)/shard_map/jit(_take)/gather | solution.py:71
  346.5 1.6 and_select_fusion
  348.1 0.0 all-reduce.11.cloned.1.call-update
  348.2 0.0 all-reduce.9.cloned.1.call-start
  348.2 6.1 %convolution_select_fusion = f32[2048,512]{1,0:T(8,128)} fusion(f32[2048,128]{1,0:T(8,128)S(1)} %slice_select_fusion.1, pred[]{:T(512)S(6)} %and.208, f32[1,512,512]{2,1,0:T(8,128)} %get-tuple-element.13, s32[]{:T(128)S(6)} %select_n.208), kind=kOutput, calls=%fused_computation.16 | convolution fusion | flops 1611661312 | bytes 5505029 | tf_op jit(solution)/shard_map/dot_general | solution.py:79
  354.3 0.0 all-reduce.9.cloned.1.call-update
  354.3 0.9 compare_reduce_fusion
  355.2 57.1 %all-reduce.11.cloned.1.call-done = f32[512,1024]{1,0:T(8,128)} async-done(((f32[512,1024]{1,0:T(8,128)}), f32[512,1024]{1,0:T(8,128)}) %all-reduce.11.cloned.1.call-update) | async-done | bytes 2097168 | tf_op jit(solution)/shard_map/psum | solution.py:73
  412.3 107.7 %all-reduce.9.cloned.1.call-done = f32[2048,512]{1,0:T(8,128)} async-done(((f32[2048,512]{1,0:T(8,128)}), f32[2048,512]{1,0:T(8,128)}) %all-reduce.9.cloned.1.call-update) | async-done | bytes 4194320 | tf_op jit(solution)/shard_map/psum | solution.py:85
  520.0 17.3 %select_subtract_fusion = f32[2048,1024]{1,0:T(8,128)S(1)} fusion(pred[2048]{0:T(1024)(128)(4,1)S(1)} %compare_reduce_fusion, f32[2048,512]{1,0:T(8,128)} %all-reduce.9.cloned.1.call-done, f32[512,1024]{1,0:T(8,128)} %all-reduce.11.cloned.1.call-done, f32[2048,896]{1,0:T(8,128)} %copy-done.1, f32[2048,128]{1,0:T(8,128)S(1)} %slice_select_fusion.1), kind=kOutput, calls=%fused_computation.11 | convolution fusion | flops 12891193344 | bytes 23070720 | tf_op jit(solution)/shard_map/dot_general | solution.py:87
  537.3 0.9 slice.45
  538.2 1.6 slice_select_fusion
  539.7 4.6 pad_maximum_fusion.1
  (26 shorter events, 0.2 us)
Async XLA Ops:
  6.5 197.9 %all-reduce.7.cloned.1.call-start = ((), (), s32[]{:S(2)}) async-start(), calls=%async_computation.1 | async-start | bytes 4194304 | tf_op jit(solution)/shard_map/psum | solution.py:73
  12.9 75.4 %collective-permute-start = (f32[10,128,640]{2,1,0:T(8,128)}, f32[10,128,640]{2,1,0:T(8,128)}, u32[]{:S(2)}, u32[]{:S(2)}) collective-permute-start(f32[10,128,640]{2,1,0:T(8,128)} %get-tuple-element.12), channel_id=1, source_target_pairs={{0,64},{64,0},{16,80},{80,16},{32,96},{96,32},{48,112},{112,48},{1... | collective-permute-start | bytes 9830408 | tf_op jit(solution)/shard_map/ppermute | solution.py:17
  26.4 9.1 %copy-start.4 = (s32[2,80]{1,0:T(2,128)S(1)}, s32[2,80]{1,0:T(2,128)}, u32[]{:S(2)}) copy-start(s32[2,80]{1,0:T(2,128)} %param.7) | copy-start | bytes 1924
  26.4 9.1 %copy-start.3 = (s32[1024]{0:T(1024)S(1)}, s32[1024]{0:T(1024)}, u32[]{:S(2)}) copy-start(s32[1024]{0:T(1024)} %param.8) | copy-start | bytes 12292
  26.4 9.6 %copy-start.2 = (f32[10,128,5,128]{3,0,2,1:T(8,128)S(1)}, f32[10,128,5,128]{3,0,2,1:T(8,128)}, u32[]{:S(2)}) copy-start(f32[10,128,5,128]{3,0,2,1:T(8,128)} %copy.32) | copy-start | bytes 9830404
  102.9 5.7 %slice-start = ((s8[5242880]{0:T(1024)(128)(4,1)}), s8[4194304]{0:T(1024)(128)(4,1)S(1)}, s32[]{:S(2)}) async-start(s8[5242880]{0:T(1024)(128)(4,1)} %bitcast.66), calls=%async_computation.4 | async-start | bytes 8388608
  102.9 5.7 %slice-start.1 = ((s8[5242880]{0:T(1024)(128)(4,1)}), s8[1048576]{0:T(1024)(128)(4,1)S(1)}, s32[]{:S(2)}) async-start(s8[5242880]{0:T(1024)(128)(4,1)} %bitcast.66), calls=%async_computation.5 | async-start | bytes 2097152
  124.0 6.2 %copy-start = (f32[16,128,8,128]{3,2,1,0:T(8,128)}, f32[16,128,8,128]{3,2,1,0:T(8,128)S(1)}, u32[]{:S(2)}) copy-start(f32[16,128,8,128]{3,2,1,0:T(8,128)S(1)} %copy.38) | copy-start | bytes 25165828
  137.9 174.3 %all-reduce.5.cloned.1.call-start = ((), (), s32[]{:S(2)}) async-start(), calls=%async_computation | async-start | bytes 8388608 | tf_op jit(solution)/shard_map/psum | solution.py:85
  146.9 265.4 %all-reduce.11.cloned.1.call-start = ((), (), s32[]{:S(2)}) async-start(), calls=%async_computation.3 | async-start | bytes 4194304 | tf_op jit(solution)/shard_map/psum | solution.py:73
  332.8 3.0 copy-start.1
  348.2 171.9 %all-reduce.9.cloned.1.call-start = ((), (), s32[]{:S(2)}) async-start(), calls=%async_computation.2 | async-start | bytes 8388608 | tf_op jit(solution)/shard_map/psum | solution.py:85
Sparse Core Ops, SparseCore 0:
  138.1 66.3 all-reduce.6
  207.8 104.4 all-reduce.4
  348.3 63.9 all-reduce.10
  415.5 104.4 all-reduce.8
where the time goes:
time: 557 us; the launch traced here: 551 us
  waiting for transfers between devices  376 us (68%)
  matrix products  76.5 us (14%)
  local copies, waits for them, and re-layouts  61.5 us (11%)
  other arithmetic  18.5 us (3%)
  between operations  13.6 us (2%)
    psum x2, waiting for transfers between devices, local(): lower = lax.psum(jnp.where(owns, term, jnp.float32(0.0)), 'col')  216 us
    psum x2, waiting for transfers between devices, local(): upper = lax.psum(jnp.where(keep_mask, picked, jnp.float32(0.0)), 'row')  114 us
    ppermute x1, waiting for transfers between devices, from_partner(): return lax.ppermute(block, axis, route)  47 us
    dot_general x2, matrix products, local(): jnp.dot(lower, upper, precision=lax.Precision.HIGHEST, preferred_element_...  36.9 us
    dot_general x4, matrix products, place(): jnp.einsum('mb,minj,nd->bidj', select_r, grid, select_c, precision=lax.Pr...  27.3 us
    unnamed x16, local copies, waits for them, and re-layouts  15.7 us
    gather x2, local copies, waits for them, and re-layouts, local(): picked = jnp.take(front, local_index, axis=0, mode='clip')  12.4 us
    dot_general x2, matrix products, local(): jnp.dot(front[:, :BLK], inverse_rows, precision=lax.Precision.HIGHEST, pr...  12.3 us
  transfers between devices with their start and end apart: 5, of which 5 were waited for; matrix products, arithmetic and copies ran while one was open for 7% of the time, Pallas kernels for 0%

commit v1 on v0

v1 whole, which is shorter than its diff:
```python
import functools

import jax
import jax.numpy as jnp
from jax import lax
from jax.experimental import pallas as pl
from jax.experimental.pallas import tpu as pltpu
from jax.sharding import PartitionSpec as P

BLK = 128
PANEL = 512
MIB = 1 << 20
F32 = jnp.float32
BF16 = jnp.bfloat16
SMEM = pl.BlockSpec(memory_space=pltpu.SMEM)
VMEM = pl.BlockSpec(memory_space=pltpu.VMEM)
ANY = pl.BlockSpec(memory_space=pl.ANY)
KEPT_AT = 0
GOT_AT = 16
KEPT_COL = 32
GOT_COL = 40
ROW, COL, SIDE = 48, 49, 50


def split(x):
    high = x.astype(BF16)
    return high, (x - high.astype(F32)).astype(BF16)


def dot3(a, b):
    dot = functools.partial(jnp.dot, preferred_element_type=F32)
    return dot(a[0], b[0]) + (dot(a[0], b[1]) + dot(a[1], b[0]))


def params(mib):
    return pltpu.CompilerParams(vmem_limit_bytes=mib * MIB)


def cost(flops, moved):
    return pl.CostEstimate(flops=flops, bytes_accessed=moved, transcendentals=0)


def first_block(maps, child, here_col):
    place, found = jnp.int32(0), jnp.int32(0)
    for d in range(5):
        hit = (maps[child, d * 16 + here_col] // 16 == 0).astype(jnp.int32)
        place, found = place + d * hit, found + hit
    return place, found


def prepare_kernel(maps, front, pieces, first, rest, panel, table, kept, sem):
    here_row, here_col = lax.axis_index("row"), lax.axis_index("col")
    side = here_row // 4
    other = 1 - side
    place, found = first_block(maps, side, here_col)
    got_place, _ = first_block(maps, other, here_col)

    def columns(d):
        return pl.ds(pl.multiple_of(d * BLK, BLK), BLK)

    copies = [
        pltpu.make_async_copy(pieces.at[:, other, :, columns(place)], first, sem.at[0]),
        pltpu.make_async_copy(pieces.at[:, side, :, columns(place)], kept, sem.at[1]),
        pltpu.make_async_copy(front.at[:, pl.ds(0, BLK)], panel, sem.at[2]),
    ]
    for j in range(4):
        d = j + (j >= place).astype(jnp.int32)
        copies.append(
            pltpu.make_async_copy(pieces.at[:, other, :, columns(d)], rest.at[j], sem.at[3 + j])
        )
    for copy in copies:
        copy.start()
    for kk in range(16):
        table[KEPT_AT + kk] = -1
        table[GOT_AT + kk] = -1
    for m in range(10):
        table[KEPT_AT + maps[side, m * 8 + here_row] // 8] = m
        table[GOT_AT + maps[other, m * 8 + here_row] // 8] = m
    for d in range(5):
        table[KEPT_COL + d] = maps[side, d * 16 + here_col] // 16
    table[GOT_COL] = maps[other, got_place * 16 + here_col] // 16
    for j in range(4):
        d = j + (j >= got_place).astype(jnp.int32)
        table[GOT_COL + 1 + j] = maps[other, d * 16 + here_col] // 16
    table[ROW] = here_row
    table[COL] = here_col
    table[SIDE] = side
    copies[1].wait()
    copies[2].wait()

    @pl.when(found > 0)
    def _():
        for m in range(10):
            at = pl.multiple_of(maps[side, m * 8 + here_row] // 8 * BLK, BLK)
            panel[pl.ds(at, BLK), :] += kept[m]

    copies[0].wait()
    for copy in copies[3:]:
        copy.wait()


def prepare(maps, front, pieces):
    return pl.pallas_call(
        prepare_kernel,
        out_shape=[
            jax.ShapeDtypeStruct((10, BLK, BLK), F32),
            jax.ShapeDtypeStruct((4, 10, BLK, BLK), F32),
            jax.ShapeDtypeStruct((2048, BLK), F32),
            jax.ShapeDtypeStruct((64,), jnp.int32),
        ],
        in_specs=[SMEM, ANY, ANY],
        out_specs=[ANY, ANY, VMEM, SMEM],
        scratch_shapes=[pltpu.VMEM((10, BLK, BLK), F32), pltpu.SemaphoreType.DMA((7,))],
        compiler_params=params(8),
        cost_estimate=cost(0, 9 * MIB),
        name="prepare",
    )(maps, front, pieces)


def pivot_kernel(
    maps, pivots, front, children, own, away, corner, marks, spread, inverse, sem, child_sem
):
    here_row, here_col = lax.axis_index("row"), lax.axis_index("col")
    side, quarter = here_row // 4, here_row % 4
    core = here_row % 2
    own[...] = jnp.zeros_like(own)
    away[...] = jnp.zeros_like(away)
    marks[...] = jnp.zeros_like(marks)
    spread[...] = jnp.zeros_like(spread)

    def clear(b, carry):
        inverse[b] = -1
        return carry

    lax.fori_loop(0, 128, clear, 0, unroll=16)
    for k in range(20):
        inverse[maps[side, 4 * k + quarter]] = k

    started = jnp.int32(0), jnp.int32(0)
    for half in range(2):

        def visit(p, counts, half=half):
            pivot = pivots[half * PANEL + p]
            block, offset = pivot >> 7, pivot & 127
            child_block = inverse[block]
            mine = (block & 7) == here_row
            shared = ((block & 3) == quarter) & (child_block >= 0)

            @pl.when(mine)
            def _():
                at = (block >> 3) * BLK + offset
                marks[pl.ds(at, 1), :] = jnp.full((1, BLK), half + 1, F32)

                @pl.when(core == half)
                def _():
                    pltpu.make_async_copy(
                        front.at[pl.ds(at, 1), :], own.at[pl.ds(p, 1), :], sem
                    ).start()

                @pl.when(core != half)
                def _():
                    pltpu.make_async_copy(
                        front.at[pl.ds(at, 1), :], away.at[pl.ds(p, 1), :], sem
                    ).start()

            @pl.when(shared)
            def _():
                pltpu.make_async_copy(
                    children.at[pl.ds(child_block * BLK + offset, 1), :],
                    spread.at[half ^ core, pl.ds(p, 1), :],
                    child_sem,
                ).start()

            return counts[0] + mine.astype(jnp.int32), counts[1] + shared.astype(jnp.int32)

        started = lax.fori_loop(0, PANEL, visit, started, unroll=4)

    def wait_front(_, carry):
        pltpu.make_async_copy(front.at[pl.ds(0, 1), :], own.at[pl.ds(0, 1), :], sem).wait()
        return carry

    def wait_child(_, carry):
        pltpu.make_async_copy(
            children.at[pl.ds(0, 1), :], spread.at[0, pl.ds(0, 1), :], child_sem
        ).wait()
        return carry

    lax.fori_loop(0, started[0], wait_front, 0)
    lax.fori_loop(0, started[1], wait_child, 0)
    for d in range(5):
        to = pl.ds(pl.multiple_of(maps[side, d * 16 + here_col] // 16 * BLK, BLK), BLK)
        own[:, to] += spread[0, :, d * BLK : (d + 1) * BLK]
        away[:, to] += spread[1, :, d * BLK : (d + 1) * BLK]
    wanted = jnp.where(here_col < 4, 1, 0)
    corner[...] = jnp.where(wanted == core, own[:, :BLK], away[:, :BLK])


def pivot_terms(maps, pivots, front, children):
    return pl.pallas_call(
        pivot_kernel,
        out_shape=[
            jax.ShapeDtypeStruct((PANEL, 1024), F32),
            jax.ShapeDtypeStruct((PANEL, 1024), F32),
            jax.ShapeDtypeStruct((PANEL, BLK), F32),
            jax.ShapeDtypeStruct((2048, BLK), F32),
        ],
        in_specs=[SMEM, SMEM, ANY, ANY],
        out_specs=[VMEM, VMEM, VMEM, VMEM],
        scratch_shapes=[
            pltpu.VMEM((2, PANEL, 640), F32),
            pltpu.SMEM((128,), jnp.int32),
            pltpu.SemaphoreType.DMA(()),
            pltpu.SemaphoreType.DMA(()),
        ],
        compiler_params=params(20),
        cost_estimate=cost(0, 24 * MIB),
        name="pivot_terms",
    )(maps, pivots, front, children)


def panel_kernel(table, panel, got, corner, top, bottom):
    top[:1024, :] = panel[:1024, :]
    bottom[:1024, :] = panel[1024:, :]

    @pl.when(table[GOT_COL] == 0)
    def _():
        for kk in range(16):
            m = table[GOT_AT + kk]
            half = top if kk < 8 else bottom
            at = kk % 8 * BLK

            @pl.when(m >= 0)
            def _(half=half, at=at, m=m):
                half[at : at + BLK, :] += got[m]

    top[1024:, :] = corner[:256, :]
    bottom[1024:, :] = corner[256:, :]


def whole_panel(table, panel, got, corner):
    shape = jax.ShapeDtypeStruct((1280, BLK), F32)
    return pl.pallas_call(
        panel_kernel,
        out_shape=[shape, shape],
        in_specs=[SMEM, VMEM, VMEM, VMEM],
        out_specs=[VMEM, VMEM],
        compiler_params=params(12),
        cost_estimate=cost(0, 3 * MIB),
        name="whole_panel",
    )(table, panel, got, corner)


def lower_kernel(
    table, tiles, corners, inverses, marks, high, low, picked, cross, inv_h, inv_l, next_h, next_l
):
    def beside(ref, blocks):
        return jnp.concatenate([ref[b] for b in blocks], axis=1)

    @pl.when(pl.program_id(0) == 0)
    def _():
        for p in range(2):
            inv_h[p], inv_l[p] = split(inverses[p])
        next_h[:256], next_l[:256] = split(beside(corners, range(4, 8)))
        next_h[256:], next_l[256:] = split(beside(corners, range(8, 12)))
        inverse = inv_h[0], inv_l[0]
        cross[:256] = dot3(split(beside(corners, range(0, 4))), inverse)
        cross[256:] = dot3(split(beside(corners, range(12, 16))), inverse)

    col = table[COL]
    slot = col % 4
    for half in range(2):
        mark = jnp.concatenate([marks[half]] * 4, axis=1)
        first = beside(tiles, range(0, 4) if half == 0 else range(12, 16))
        second = beside(tiles, range(4, 8) if half == 0 else range(8, 12))
        lower = dot3(split(first), (inv_h[0], inv_l[0]))
        lower = jnp.where(mark != 1, lower, 0.0)
        terms = split(lower)
        high[half, :, :PANEL], low[half, :, :PANEL] = terms
        second = second - dot3(terms, (next_h[...], next_l[...]))
        later = dot3(split(second), (inv_h[1], inv_l[1]))
        later = jnp.where(mark == 0, later, 0.0)
        high[half, :, PANEL:], low[half, :, PANEL:] = split(later)
        chosen = jnp.where(col < 4, lower, later)
        out = chosen[:, :BLK]
        for s in range(1, 4):
            out = jnp.where(slot == s, chosen[:, s * BLK : (s + 1) * BLK], out)
        picked[half] = out


def lowers(table, gathered, inverses, marks):
    return pl.pallas_call(
        lower_kernel,
        out_shape=[
            jax.ShapeDtypeStruct((2, 1024, 1024), BF16),
            jax.ShapeDtypeStruct((2, 1024, 1024), BF16),
            jax.ShapeDtypeStruct((2, 1024, BLK), F32),
            jax.ShapeDtypeStruct((PANEL, PANEL), F32),
        ],
        grid_spec=pltpu.PrefetchScalarGridSpec(
            num_scalar_prefetch=1,
            grid=(4,),
            in_specs=[
                pl.BlockSpec((16, 256, BLK), lambda t, s: (0, t, 0)),
                pl.BlockSpec((16, 256, BLK), lambda t, s: (0, 4, 0)),
                pl.BlockSpec((2, PANEL, PANEL), lambda t, s: (0, 0, 0)),
                pl.BlockSpec((2, 256, BLK), lambda t, s: (0, t, 0)),
            ],
            out_specs=[
                pl.BlockSpec((2, 256, 1024), lambda t, s: (0, t, 0)),
                pl.BlockSpec((2, 256, 1024), lambda t, s: (0, t, 0)),
                pl.BlockSpec((2, 256, BLK), lambda t, s: (0, t, 0)),
                pl.BlockSpec((PANEL, PANEL), lambda t, s: (0, 0)),
            ],
            scratch_shapes=[
                pltpu.VMEM((2, PANEL, PANEL), BF16),
                pltpu.VMEM((2, PANEL, PANEL), BF16),
                pltpu.VMEM((PANEL, PANEL), BF16),
                pltpu.VMEM((PANEL, PANEL), BF16),
            ],
        ),
        compiler_params=params(44),
        cost_estimate=cost(3 * 6 * 2048 * PANEL * PANEL, 24 * MIB),
        name="lowers",
    )(table, gathered, gathered, inverses, marks.reshape(2, 1024, BLK))


def update_kernel(
    table, front, kept_a, kept_b, got0_a, got0_b, got_a, got_b, high, low, picked, marks,
    own, swapped, cross, out, upper_h, upper_l,
):
    step = pl.program_id(0)
    here_row, col = table[ROW], table[COL]

    @pl.when(step == 0)
    def _():
        core = here_row % 2
        lane = lax.broadcasted_iota(jnp.int32, (PANEL, 1024), 1)
        inside = lane < BLK
        first = jnp.where(core == 0, own[...], swapped[...])
        first = jnp.where(inside & (col < 4), 0.0, first)
        terms = split(first)
        upper_h[:PANEL], upper_l[:PANEL] = terms
        second = jnp.where(core == 0, swapped[...], own[...])
        second = second - dot3(split(cross[...]), terms)
        second = jnp.where(inside & (col < 8), 0.0, second)
        upper_h[PANEL:], upper_l[PANEL:] = split(second)

    change = dot3((high[...], low[...]), (upper_h[...], upper_l[...]))
    out[...] = front[...] - change
    for part in range(2):
        rows = slice(part * BLK, (part + 1) * BLK)
        kept = kept_a if part == 0 else kept_b
        got0 = got0_a if part == 0 else got0_b
        got = got_a if part == 0 else got_b

        @pl.when(table[KEPT_AT + 2 * step + part] >= 0)
        def _(rows=rows, kept=kept):
            for d in range(5):
                to = pl.ds(pl.multiple_of(table[KEPT_COL + d] * BLK, BLK), BLK)
                out[rows, to] += kept[0, 0, :, d * BLK : (d + 1) * BLK]

        @pl.when(table[GOT_AT + 2 * step + part] >= 0)
        def _(rows=rows, got0=got0, got=got):
            for j in range(5):
                to = pl.ds(pl.multiple_of(table[GOT_COL + j] * BLK, BLK), BLK)
                out[rows, to] += got0[0] if j == 0 else got[j - 1, 0]

    @pl.when(col < 8)
    def _():
        active = jnp.where(col < 4, (marks[...] != 1).astype(F32), (marks[...] == 0).astype(F32))
        out[:, :BLK] = jnp.where(active > 0, picked[...], out[:, :BLK])


def update(table, front, pieces, got0, got, high, low, picked, marks, own, swapped, cross):
    def kept_at(part):
        return lambda t, s: (jnp.maximum(s[KEPT_AT + 2 * t + part], 0), s[SIDE], 0, 0)

    def got0_at(part):
        return lambda t, s: (jnp.maximum(s[GOT_AT + 2 * t + part], 0), 0, 0)

    def got_at(part):
        return lambda t, s: (0, jnp.maximum(s[GOT_AT + 2 * t + part], 0), 0, 0)

    tile = pl.BlockSpec((256, 1024), lambda t, s: (t, 0))
    narrow = pl.BlockSpec((256, BLK), lambda t, s: (t, 0))
    whole = pl.BlockSpec((PANEL, 1024), lambda t, s: (0, 0))
    return pl.pallas_call(
        update_kernel,
        out_shape=jax.ShapeDtypeStruct((2048, 1024), F32),
        grid_spec=pltpu.PrefetchScalarGridSpec(
            num_scalar_prefetch=1,
            grid=(8,),
            in_specs=[
                tile,
                pl.BlockSpec((1, 1, BLK, 640), kept_at(0)),
                pl.BlockSpec((1, 1, BLK, 640), kept_at(1)),
                pl.BlockSpec((1, BLK, BLK), got0_at(0)),
                pl.BlockSpec((1, BLK, BLK), got0_at(1)),
                pl.BlockSpec((4, 1, BLK, BLK), got_at(0)),
                pl.BlockSpec((4, 1, BLK, BLK), got_at(1)),
                tile,
                tile,
                narrow,
                narrow,
                whole,
                whole,
                pl.BlockSpec((PANEL, PANEL), lambda t, s: (0, 0)),
            ],
            out_specs=tile,
            scratch_shapes=[pltpu.VMEM((1024, 1024), BF16), pltpu.VMEM((1024, 1024), BF16)],
        ),
        compiler_params=params(48),
        cost_estimate=cost(6 * 2048 * 1024 * 1024, 40 * MIB),
        name="update",
    )(
        table, front, pieces, pieces, got0, got0, got, got,
        high.reshape(2048, 1024), low.reshape(2048, 1024), picked.reshape(2048, BLK), marks,
        own, swapped, cross,
    )


def swap(block, axis, partner, count):
    return lax.ppermute(block, axis, [(i, partner(i)) for i in range(count)])


def next_core(i):
    return i ^ 1


def even_chip(i):
    return i ^ 2


def odd_chip(i):
    return (3 - i // 2) * 2 + i % 2


def row_sum(own, away, here_row):
    chip = here_row // 2
    even_bit = (chip ^ (chip >> 1)) & 1
    odd_bit = chip >> 1
    total = own + swap(away, "row", next_core, 8)
    parts = []
    for which in range(2):
        steps = [(even_chip, even_bit), (odd_chip, odd_bit)]
        if which:
            steps.reverse()
        part = total[which * 256 : (which + 1) * 256]
        for partner, bit in steps:
            size = part.shape[0] // 2
            leave = jnp.where(bit == 0, part[size:], part[:size])
            stay = jnp.where(bit == 0, part[:size], part[size:])
            part = stay + swap(leave, "row", partner, 8)
        for partner, bit in steps[::-1]:
            came = swap(part, "row", partner, 8)
            part = jnp.concatenate(
                [jnp.where(bit == 0, part, came), jnp.where(bit == 0, came, part)], axis=0
            )
        parts.append(part)
    half = jnp.concatenate(parts, axis=0)
    return half, swap(half, "row", next_core, 8)


def local(front, children, child_maps, pivots, diag_inverses):
    here_row, here_col = lax.axis_index("row"), lax.axis_index("col")
    pieces = children.reshape(10, 2, BLK, 640)
    first, rest, panel, table = prepare(child_maps, front, pieces)
    across = functools.partial(swap, axis="row", partner=lambda i: i ^ 4, count=8)
    got0 = across(first)
    own, away, corner, marks = pivot_terms(child_maps, pivots, front, children)
    corner = lax.psum(corner, "row")
    rest, got0 = lax.optimization_barrier((rest, got0))
    got = across(rest)
    top, bottom = whole_panel(table, panel, got0, corner)
    folded = lax.ppermute(bottom, "col", [(c, (3 - c // 4) * 4 + c % 4) for c in range(8)])
    gathered = lax.all_gather(jnp.where(here_col < 8, top, folded), "col")
    half, swapped = row_sum(own, away, here_row)
    high, low, picked, cross = lowers(table, gathered, diag_inverses, marks)
    return update(
        table, front, pieces, got0, got, high, low, picked, marks, half, swapped, cross
    )


def solution(mesh):
    return jax.shard_map(
        local,
        mesh=mesh,
        in_specs=(P("row", "col"), P("row", "col"), P(), P(), P()),
        out_specs=P("row", "col"),
        check_vma=False,
    )
```

time: 557 us -> 299 us (0.54)
  waiting for transfers between devices: 376 us -> 106 us
  starting transfers between devices: 4.55 us -> 85.2 us
  matrix products: 76.5 us -> 0 us
  Pallas kernels: 0 us -> 71.9 us
  local copies, waits for them, and re-layouts: 61.5 us -> 17 us
  other arithmetic: 18.5 us -> 4.14 us
    psum x4 -> x1, waiting for transfers between devices: 329 us -> 59.8 us  [local(): corner = lax.psum(corner, 'row')]
    ppermute x1 -> x13, starting transfers between devices: 4.43 us -> 85.1 us  [the longest x12 79.9 us: swap(): return lax.ppermute(block, axis, [(i, partner(i)) for i in range(count)])]
    dot_general x8 -> x0, matrix products: 76.5 us -> none  [the longest x2 36.9 us: local(): jnp.dot(lower, upper, precision=lax.Precision.HIGHEST, preferred_element_...]
    pallas_call x0 -> x5, Pallas kernels: none -> 71.9 us  [the longest x1 25.6 us: pivot_terms(): pl.pallas_call(pivot_kernel, out_shape=[jax.ShapeDtypeStruct((PANEL, 1024...]
    gather x2 -> x0, local copies, waits for them, and re-layouts: 12.4 us -> none  [local(): picked = jnp.take(front, local_index, axis=0, mode='clip')]
    reshape x2 -> x0, local copies, waits for them, and re-layouts: 11.3 us -> none  [place(): grid = piece.reshape(kept_blocks, BLK, child_cblocks, BLK)]
    dynamic_slice x2 -> x0, local copies, waits for them, and re-layouts: 9.89 us -> none  [local(): kept = lax.dynamic_index_in_dim(pieces, side, 1, keepdims=False)]
    concatenate x2 -> x3, other arithmetic: 9.18 us -> 0.22 us  [the longest x1 0.14 us: row_sum(): half = jnp.concatenate(parts, axis=0)]
  transfers between devices with their start and end apart: 5 -> 15, of which waited for: 5 -> 9; matrix products, arithmetic and copies ran while one was open for 7% -> 1% of each run, Pallas kernels for 0% -> 15%
where the time goes in v1:
time: 299 us; the launch traced here: 298 us
  waiting for transfers between devices  106 us (35%)
  starting transfers between devices  85.2 us (28%)
  Pallas kernels  71.9 us (24%)
  local copies, waits for them, and re-layouts  17 us (6%)
  between operations  13.6 us (5%)
  other arithmetic  4.14 us (1%)
    ppermute x12, starting transfers between devices, swap(): return lax.ppermute(block, axis, [(i, partner(i)) for i in range(count)])  79.9 us
    psum x1, waiting for transfers between devices, local(): corner = lax.psum(corner, 'row')  59.8 us
    ppermute x12, waiting for transfers between devices, swap(): return lax.ppermute(block, axis, [(i, partner(i)) for i in range(count)])  35.5 us
    pallas_call x1, Pallas kernels, pivot_terms(): pl.pallas_call(pivot_kernel, out_shape=[jax.ShapeDtypeStruct((PANEL, 1024...  25.6 us
    pallas_call x1, Pallas kernels, update(): pl.pallas_call(update_kernel, out_shape=jax.ShapeDtypeStruct((2048, 1024)...  23.3 us
    pallas_call x1, Pallas kernels, lowers(): pl.pallas_call(lower_kernel, out_shape=[jax.ShapeDtypeStruct((2, 1024, 10...  18.4 us
    unnamed x32, local copies, waits for them, and re-layouts  17 us
    ppermute x1, waiting for transfers between devices, local(): lax.ppermute(bottom, 'col', [(c, (3 - c // 4) * 4 + c % 4) for c in range...  10.7 us
  transfers between devices with their start and end apart: 15, of which 9 were waited for; matrix products, arithmetic and copies ran while one was open for 1% of the time, Pallas kernels for 15%

profile of v1, /device:TPU:1, one launch (start us, length us, event | category | flops | bytes accessed | tf_op | source)
XLA Modules:
  0.0 297.9 jit_solution(16196938621142749263)
XLA Ops:
  6.5 2.9 copy-done
  9.4 3.4 %copy-done.2 = f32[2048,1024]{1,0:T(8,128)S(1)} copy-done((f32[2048,1024]{1,0:T(8,128)S(1)}, f32[2048,1024]{1,0:T(8,128)}, u32[]{:S(2)}) %copy-start.2) | copy-done | bytes 8388632
  12.8 0.7 copy-done.12
  13.5 3.0 %prepare.1 = (f32[10,128,128]{2,1,0:T(8,128)S(1)}, f32[4,10,128,128]{3,2,1,0:T(8,128)}, f32[2048,128]{1,0:T(8,128)S(1)}, s32[64]{0:T(128)S(1)}) custom-call(s32[2,80]{1,0:T(2,128)S(1)} %copy-done.12, f32[2048,1024]{1,0:T(8,128)S(1)} %copy-done.2, f32[10,2,128,640]{3,2,1,0:T(8,128)S(1)} %bitcast.8), custom_call_target="tpu_custom_call" | custom-call | bytes 9437184 | tf_op jit(solution)/shard_map/prepare/pallas_call | solution.py:103
  16.5 4.5 %collective-permute-start = (f32[10,128,128]{2,1,0:T(8,128)S(1)}, f32[10,128,128]{2,1,0:T(8,128)S(1)}, u32[]{:S(2)}, u32[]{:S(2)}) collective-permute-start(f32[10,128,128]{2,1,0:T(8,128)S(1)} %get-tuple-element.23), channel_id=1, source_target_pairs={{0,64},{16,80},{32,96},{48,112},{64,0},{80,16},{96,32},{112,48},{1... | collective-permute-start | bytes 1966088 | tf_op jit(solution)/shard_map/ppermute | solution.py:423
  21.0 0.7 copy-done.11
  21.7 25.6 %pivot_terms.1 = (f32[512,1024]{1,0:T(8,128)S(1)}, f32[512,1024]{1,0:T(8,128)S(1)}, f32[512,128]{1,0:T(8,128)}, f32[2048,128]{1,0:T(8,128)S(1)}) custom-call(s32[2,80]{1,0:T(2,128)S(1)} %copy-done.13, s32[1024]{0:T(1024)S(1)} %copy-done.11, f32[2048,1024]{1,0:T(8,128)S(1)} %copy-done.3, f32[2560,640]{1,0:T(8,128)S(1)} %copy-done.1), custom_call_target="tpu_custom_call" | custom-call | bytes 25165824 | tf_op jit(solution)/shard_map/pivot_terms/pallas_call | solution.py:199
  47.3 1.0 copy-done.7
  48.3 1.4 copy-done.15
  49.6 0.0 all-reduce.2.cloned.1.call-update
  49.7 0.0 all-gather.3.cloned.1.call-start
  49.7 59.8 %all-reduce.2.cloned.1.call-done.corner = f32[512,128]{1,0:T(8,128)} async-done(((f32[512,128]{1,0:T(8,128)}), f32[512,128]{1,0:T(8,128)}) %all-reduce.2.cloned.1.call-update) | async-done | bytes 262160 | tf_op jit(solution)/shard_map/psum | solution.py:471
  109.6 1.2 copy-done.6
  110.8 0.9 copy-done.10
  111.7 1.6 whole_panel.1
  113.4 5.2 %collective-permute-start.2 = (f32[1280,128]{1,0:T(8,128)}, f32[1280,128]{1,0:T(8,128)}, u32[]{:S(2)}, u32[]{:S(2)}) collective-permute-start(f32[1280,128]{1,0:T(8,128)} %get-tuple-element.29), channel_id=1, source_target_pairs={{0,12},{1,13},{2,14},{3,15},{4,8},{5,9},{6,10},{7,11},{16,28},{17,... | collective-permute-start | bytes 1966088 | tf_op jit(solution)/shard_map/ppermute | solution.py:475
  118.6 10.7 %collective-permute-done.2 = f32[1280,128]{1,0:T(8,128)} collective-permute-done((f32[1280,128]{1,0:T(8,128)}, f32[1280,128]{1,0:T(8,128)}, u32[]{:S(2)}, u32[]{:S(2)}) %collective-permute-start.2) | collective-permute-done | bytes 655392 | tf_op jit(solution)/shard_map/ppermute | solution.py:475
  129.3 0.9 broadcast_select_fusion
  130.2 0.0 all-gather.3.cloned.1.call-update
  130.3 3.7 %collective-permute-start.3 = (f32[512,1024]{1,0:T(8,128)}, f32[512,1024]{1,0:T(8,128)}, u32[]{:S(2)}, u32[]{:S(2)}) collective-permute-start(f32[512,1024]{1,0:T(8,128)} %copy-done.15), channel_id=1, source_target_pairs={{0,16},{16,0},{32,48},{48,32},{64,80},{80,64},{96,112},{112,96},{1... | collective-permute-start | bytes 6291464 | tf_op jit(solution)/shard_map/ppermute | solution.py:423
  134.0 4.1 %collective-permute-done.3 = f32[512,1024]{1,0:T(8,128)} collective-permute-done((f32[512,1024]{1,0:T(8,128)}, f32[512,1024]{1,0:T(8,128)}, u32[]{:S(2)}, u32[]{:S(2)}) %collective-permute-start.3) | collective-permute-done | bytes 2097184 | tf_op jit(solution)/shard_map/ppermute | solution.py:423
  138.1 2.1 add.18
  140.2 0.2 slice_select_fusion.1
  140.4 0.1 collective-permute-start.4
  140.5 3.1 %collective-permute-start.8 = (f32[128,1024]{1,0:T(8,128)S(1)}, f32[128,1024]{1,0:T(8,128)S(1)}, u32[]{:S(2)}, u32[]{:S(2)}) collective-permute-start(f32[128,1024]{1,0:T(8,128)S(1)} %get-tuple-element.40), channel_id=1, source_target_pairs={{0,96},{16,112},{32,64},{48,80},{64,32},{80,48},{96,0},{112,16},{1... | collective-permute-start | bytes 1572872 | tf_op jit(solution)/shard_map/ppermute | solution.py:423
  143.5 10.2 %collective-permute-done.4 = f32[128,1024]{1,0:T(8,128)S(1)} collective-permute-done((f32[128,1024]{1,0:T(8,128)S(1)}, f32[128,1024]{1,0:T(8,128)S(1)}, u32[]{:S(2)}, u32[]{:S(2)}) %collective-permute-start.4) | collective-permute-done | bytes 524320 | tf_op jit(solution)/shard_map/ppermute | solution.py:423
  153.7 1.8 collective-permute-done.8
  155.5 0.3 select_add_fusion.1
  155.9 2.5 collective-permute-start.5
  158.4 0.1 collective-permute-start.9
  158.5 5.6 %collective-permute-done.5 = f32[64,1024]{1,0:T(8,128)S(1)} collective-permute-done((f32[64,1024]{1,0:T(8,128)S(1)}, f32[64,1024]{1,0:T(8,128)S(1)}, u32[]{:S(2)}, u32[]{:S(2)}) %collective-permute-start.5) | collective-permute-done | bytes 262176 | tf_op jit(solution)/shard_map/ppermute | solution.py:423
  164.1 2.3 collective-permute-start.6
  166.5 0.1 collective-permute-start.10
  166.6 4.9 %collective-permute-done.6 = f32[64,1024]{1,0:T(8,128)S(1)} collective-permute-done((f32[64,1024]{1,0:T(8,128)S(1)}, f32[64,1024]{1,0:T(8,128)S(1)}, u32[]{:S(2)}, u32[]{:S(2)}) %collective-permute-start.6) | collective-permute-done | bytes 262176 | tf_op jit(solution)/shard_map/ppermute | solution.py:423
  171.5 0.1 collective-permute-start.7
  171.6 0.5 collective-permute-done.10
  172.2 1.6 collective-permute-start.11
  173.8 1.3 collective-permute-start.1
  175.1 8.5 %collective-permute-done.7 = f32[128,1024]{1,0:T(8,128)S(1)} collective-permute-done((f32[128,1024]{1,0:T(8,128)S(1)}, f32[128,1024]{1,0:T(8,128)S(1)}, u32[]{:S(2)}, u32[]{:S(2)}) %collective-permute-start.7) | collective-permute-done | bytes 524320 | tf_op jit(solution)/shard_map/ppermute | solution.py:423
  183.6 0.1 broadcast_select_fusion.4
  183.7 0.1 broadcast_select_fusion.2
  183.8 0.1 pad_maximum_fusion.own
  184.0 60.5 %collective-permute-start.12 = (f32[512,1024]{1,0:T(8,128)S(1)}, f32[512,1024]{1,0:T(8,128)}, u32[]{:S(2)}, u32[]{:S(2)}) collective-permute-start(f32[512,1024]{1,0:T(8,128)S(1)} %pad_maximum_fusion.own), channel_id=1, source_target_pairs={{0,16},{16,0},{32,48},{48,32},{64,80},{80,64},{96,112},{112,96},{1... | collective-permute-start | bytes 6291464 | tf_op jit(solution)/shard_map/ppermute | solution.py:423
  244.5 1.2 copy-done.8
  245.8 1.6 copy-done.14
  247.4 18.4 %lowers.1 = (bf16[2,1024,1024]{2,1,0:T(8,128)(2,1)S(1)}, bf16[2,1024,1024]{2,1,0:T(8,128)(2,1)}, f32[2,1024,128]{2,1,0:T(8,128)S(1)}, f32[512,512]{1,0:T(8,128)S(1)}) custom-call(s32[64]{0:T(128)S(1)} %get-tuple-element.21.table, f32[16,1280,128]{2,1,0:T(8,128)} %bitcast.13, f32[16,1280,128]{2,1,0:T(8,128)} %bitcast.14, f32[2,512,512]{2,1,0:T(8,128)S(1)} %copy-done.14, ...), custom_call_target="tpu_custom_call" | custom-call | flops 9663676416 | bytes 25165824 | tf_op jit(solution)/shard_map/lowers/pallas_call | solution.py:291
  265.8 2.0 copy-done.4
  267.8 23.3 %update.1 = f32[2048,1024]{1,0:T(8,128)} custom-call(s32[64]{0:T(128)S(1)} %get-tuple-element.21.table, f32[2048,1024]{1,0:T(8,128)} %front.5, f32[10,2,128,640]{3,2,1,0:T(8,128)} %bitcast.6, f32[10,2,128,640]{3,2,1,0:T(8,128)} %bitcast.7, f32[10,128,128]{2,1,0:T(8,128)S(1)} %collective-permute-done.got.got0_a.got0_b, ...), custom_call_target="tpu_custom_call" | custom-call | flops 12884901888 | bytes 41943040 | tf_op jit(solution)/shard_map/update/pallas_call | solution.py:387
  (36 shorter events, 0.4 us)
Async XLA Ops:
  6.5 103.0 %all-reduce.2.cloned.1.call-start = ((), (), s32[]{:S(2)}) async-start(), calls=%async_computation | async-start | bytes 524288 | tf_op jit(solution)/shard_map/psum | solution.py:471
  6.5 2.9 copy-start
  9.4 3.4 %copy-start.2 = (f32[2048,1024]{1,0:T(8,128)S(1)}, f32[2048,1024]{1,0:T(8,128)}, u32[]{:S(2)}) copy-start(f32[2048,1024]{1,0:T(8,128)} %front.5) | copy-start | bytes 25165828
  12.8 0.7 copy-start.12
  13.5 7.5 %copy-start.1 = (f32[2560,640]{1,0:T(8,128)S(1)}, f32[2560,640]{1,0:T(8,128)}, u32[]{:S(2)}) copy-start(f32[2560,640]{1,0:T(8,128)} %children.1) | copy-start | bytes 19660804
  13.5 7.5 %copy-start.3 = (f32[2048,1024]{1,0:T(8,128)S(1)}, f32[2048,1024]{1,0:T(8,128)}, u32[]{:S(2)}) copy-start(f32[2048,1024]{1,0:T(8,128)} %front.5) | copy-start | bytes 25165828
  13.5 7.5 %copy-start.13 = (s32[2,80]{1,0:T(2,128)S(1)}, s32[2,80]{1,0:T(2,128)}, u32[]{:S(2)}) copy-start(s32[2,80]{1,0:T(2,128)} %maps.3) | copy-start | bytes 1924
  16.5 30.8 %copy-start.5 = (f32[2048,128]{1,0:T(8,128)}, f32[2048,128]{1,0:T(8,128)S(1)}, u32[]{:S(2)}) copy-start(f32[2048,128]{1,0:T(8,128)S(1)} %get-tuple-element.26.panel) | copy-start | bytes 3145732
  16.5 33.2 %collective-permute-start = (f32[10,128,128]{2,1,0:T(8,128)S(1)}, f32[10,128,128]{2,1,0:T(8,128)S(1)}, u32[]{:S(2)}, u32[]{:S(2)}) collective-permute-start(f32[10,128,128]{2,1,0:T(8,128)S(1)} %get-tuple-element.23), channel_id=1, source_target_pairs={{0,64},{16,80},{32,96},{48,112},{64,0},{80,16},{96,32},{112,48},{1... | collective-permute-start | bytes 1966088 | tf_op jit(solution)/shard_map/ppermute | solution.py:423
  21.0 0.7 copy-start.11
  47.3 1.0 copy-start.7
  48.3 1.4 copy-start.15
  49.7 194.9 %all-gather.3.cloned.1.call-start = ((), (), s32[]{:S(2)}) async-start(), calls=%async_computation.1 | async-start | bytes 11141120 | tf_op jit(solution)/shard_map/all_gather | solution.py:476
  109.6 1.2 copy-start.6
  110.8 0.9 copy-start.10
  113.4 15.9 %collective-permute-start.2 = (f32[1280,128]{1,0:T(8,128)}, f32[1280,128]{1,0:T(8,128)}, u32[]{:S(2)}, u32[]{:S(2)}) collective-permute-start(f32[1280,128]{1,0:T(8,128)} %get-tuple-element.29), channel_id=1, source_target_pairs={{0,12},{1,13},{2,14},{3,15},{4,8},{5,9},{6,10},{7,11},{16,28},{17,... | collective-permute-start | bytes 1966088 | tf_op jit(solution)/shard_map/ppermute | solution.py:475
  130.3 7.9 %collective-permute-start.3 = (f32[512,1024]{1,0:T(8,128)}, f32[512,1024]{1,0:T(8,128)}, u32[]{:S(2)}, u32[]{:S(2)}) collective-permute-start(f32[512,1024]{1,0:T(8,128)} %copy-done.15), channel_id=1, source_target_pairs={{0,16},{16,0},{32,48},{48,32},{64,80},{80,64},{96,112},{112,96},{1... | collective-permute-start | bytes 6291464 | tf_op jit(solution)/shard_map/ppermute | solution.py:423
  140.4 13.3 %collective-permute-start.4 = (f32[128,1024]{1,0:T(8,128)S(1)}, f32[128,1024]{1,0:T(8,128)S(1)}, u32[]{:S(2)}, u32[]{:S(2)}) collective-permute-start(f32[128,1024]{1,0:T(8,128)S(1)} %get-tuple-element.39), channel_id=1, source_target_pairs={{0,32},{16,48},{32,0},{48,16},{64,96},{80,112},{96,64},{112,80},{1... | collective-permute-start | bytes 1572872 | tf_op jit(solution)/shard_map/ppermute | solution.py:423
  140.5 15.1 %collective-permute-start.8 = (f32[128,1024]{1,0:T(8,128)S(1)}, f32[128,1024]{1,0:T(8,128)S(1)}, u32[]{:S(2)}, u32[]{:S(2)}) collective-permute-start(f32[128,1024]{1,0:T(8,128)S(1)} %get-tuple-element.40), channel_id=1, source_target_pairs={{0,96},{16,112},{32,64},{48,80},{64,32},{80,48},{96,0},{112,16},{1... | collective-permute-start | bytes 1572872 | tf_op jit(solution)/shard_map/ppermute | solution.py:423
  155.9 8.2 %collective-permute-start.5 = (f32[64,1024]{1,0:T(8,128)S(1)}, f32[64,1024]{1,0:T(8,128)S(1)}, u32[]{:S(2)}, u32[]{:S(2)}) collective-permute-start(f32[64,1024]{1,0:T(8,128)S(1)} %slice_select_fusion.3), channel_id=1, source_target_pairs={{0,96},{16,112},{32,64},{48,80},{64,32},{80,48},{96,0},{112,16},{1... | collective-permute-start | bytes 786440 | tf_op jit(solution)/shard_map/ppermute | solution.py:423
  158.4 8.0 %collective-permute-start.9 = (f32[64,1024]{1,0:T(8,128)S(1)}, f32[64,1024]{1,0:T(8,128)S(1)}, u32[]{:S(2)}, u32[]{:S(2)}) collective-permute-start(f32[64,1024]{1,0:T(8,128)S(1)} %slice_select_fusion.2), channel_id=1, source_target_pairs={{0,32},{16,48},{32,0},{48,16},{64,96},{80,112},{96,64},{112,80},{1... | collective-permute-start | bytes 786440 | tf_op jit(solution)/shard_map/ppermute | solution.py:423
  164.1 7.3 %collective-permute-start.6 = (f32[64,1024]{1,0:T(8,128)S(1)}, f32[64,1024]{1,0:T(8,128)S(1)}, u32[]{:S(2)}, u32[]{:S(2)}) collective-permute-start(f32[64,1024]{1,0:T(8,128)S(1)} %select_add_fusion.3), channel_id=1, source_target_pairs={{0,96},{16,112},{32,64},{48,80},{64,32},{80,48},{96,0},{112,16},{1... | collective-permute-start | bytes 786440 | tf_op jit(solution)/shard_map/ppermute | solution.py:423
  166.5 5.6 %collective-permute-start.10 = (f32[64,1024]{1,0:T(8,128)S(1)}, f32[64,1024]{1,0:T(8,128)S(1)}, u32[]{:S(2)}, u32[]{:S(2)}) collective-permute-start(f32[64,1024]{1,0:T(8,128)S(1)} %select_add_fusion.2), channel_id=1, source_target_pairs={{0,32},{16,48},{32,0},{48,16},{64,96},{80,112},{96,64},{112,80},{1... | collective-permute-start | bytes 786440 | tf_op jit(solution)/shard_map/ppermute | solution.py:423
  171.5 12.0 %collective-permute-start.7 = (f32[128,1024]{1,0:T(8,128)S(1)}, f32[128,1024]{1,0:T(8,128)S(1)}, u32[]{:S(2)}, u32[]{:S(2)}) collective-permute-start(f32[128,1024]{1,0:T(8,128)S(1)} %pad_maximum_fusion.1), channel_id=1, source_target_pairs={{0,32},{16,48},{32,0},{48,16},{64,96},{80,112},{96,64},{112,80},{1... | collective-permute-start | bytes 1572872 | tf_op jit(solution)/shard_map/ppermute | solution.py:423
  172.2 11.5 %collective-permute-start.11 = (f32[128,1024]{1,0:T(8,128)S(1)}, f32[128,1024]{1,0:T(8,128)S(1)}, u32[]{:S(2)}, u32[]{:S(2)}) collective-permute-start(f32[128,1024]{1,0:T(8,128)S(1)} %pad_maximum_fusion.2), channel_id=1, source_target_pairs={{0,96},{16,112},{32,64},{48,80},{64,32},{80,48},{96,0},{112,16},{1... | collective-permute-start | bytes 1572872 | tf_op jit(solution)/shard_map/ppermute | solution.py:423
  173.8 93.9 %collective-permute-start.1 = (f32[4,10,128,128]{3,2,1,0:T(8,128)}, f32[4,10,128,128]{3,2,1,0:T(8,128)}, u32[]{:S(2)}, u32[]{:S(2)}) collective-permute-start(f32[4,10,128,128]{3,2,1,0:T(8,128)} %get-tuple-element.25), channel_id=1, source_target_pairs={{0,64},{16,80},{32,96},{48,112},{64,0},{80,16},{96,32},{112,48},{1... | collective-permute-start | bytes 7864328 | tf_op jit(solution)/shard_map/ppermute | solution.py:423
  184.0 83.8 %collective-permute-start.12 = (f32[512,1024]{1,0:T(8,128)S(1)}, f32[512,1024]{1,0:T(8,128)}, u32[]{:S(2)}, u32[]{:S(2)}) collective-permute-start(f32[512,1024]{1,0:T(8,128)S(1)} %pad_maximum_fusion.own), channel_id=1, source_target_pairs={{0,16},{16,0},{32,48},{48,32},{64,80},{80,64},{96,112},{112,96},{1... | collective-permute-start | bytes 6291464 | tf_op jit(solution)/shard_map/ppermute | solution.py:423
  244.5 1.2 copy-start.8
  245.8 1.6 copy-start.14
  247.4 20.4 %copy-start.9 = (f32[2048,128]{1,0:T(8,128)S(1)}, f32[2048,128]{1,0:T(8,128)}, u32[]{:S(2)}) copy-start(f32[2048,128]{1,0:T(8,128)} %copy-done.7) | copy-start | bytes 3145732
  265.8 2.0 copy-start.4
Sparse Core Ops, SparseCore 0:
  49.8 59.7 all-reduce.1
  130.4 86.3 all-gather.2

commit v2 on v0

v2 whole, which is shorter than its diff:
```python
import functools

import jax
import jax.numpy as jnp
from jax import lax
from jax.experimental import pallas as pl
from jax.experimental.pallas import tpu as pltpu
from jax.sharding import PartitionSpec as P

BLK = 128
PANEL = 512
MIB = 1 << 20
F32 = jnp.float32
BF16 = jnp.bfloat16
SMEM = pl.BlockSpec(memory_space=pltpu.SMEM)
VMEM = pl.BlockSpec(memory_space=pltpu.VMEM)
HBM = pl.BlockSpec(memory_space=pltpu.HBM)
KEPT_AT = 0
GOT_AT = 16
KEPT_COL = 32
GOT_COL = 40
ROW, COL, SIDE = 48, 49, 50
GOT_ROW = 52


def split(x):
    high = x.astype(BF16)
    return high, (x - high.astype(F32)).astype(BF16)


def dot3(a, b):
    rows = a[0].shape[0]
    both = jnp.dot(jnp.concatenate(a, axis=0), b[0], preferred_element_type=F32)
    return both[:rows] + (both[rows:] + jnp.dot(a[0], b[1], preferred_element_type=F32))


def params(mib):
    return pltpu.CompilerParams(vmem_limit_bytes=mib * MIB)


def in_hbm(x):
    return pltpu.with_memory_space_constraint(x, pltpu.HBM)


def cost(flops, moved):
    return pl.CostEstimate(flops=flops, bytes_accessed=moved, transcendentals=0)


def first_block(maps, child, here_col):
    place, found = jnp.int32(0), jnp.int32(0)
    for d in range(5):
        hit = (maps[child, d * 16 + here_col] // 16 == 0).astype(jnp.int32)
        place, found = place + d * hit, found + hit
    return place, found


def prepare_kernel(
    maps, pivots, front, pieces, first, rest_a, rest_b, rest_c, rest_d, panel, own, away, table,
    sending, kept, total, sem,
):
    here_row, here_col = lax.axis_index("row"), lax.axis_index("col")
    side, core = here_row // 4, here_row % 2
    other = 1 - side
    place, found = first_block(maps, side, here_col)
    got_place, _ = first_block(maps, other, here_col)

    def columns(d):
        return pl.ds(pl.multiple_of(d * BLK, BLK), BLK)

    reads = [
        pltpu.make_async_copy(pieces.at[:, other], sending, sem.at[0]),
        pltpu.make_async_copy(pieces.at[:, side, :, columns(place)], kept, sem.at[1]),
        pltpu.make_async_copy(front.at[:, pl.ds(0, BLK)], panel, sem.at[2]),
    ]
    writes = []
    for j, target in enumerate((rest_a, rest_b, rest_c, rest_d)):
        d = j + (j >= place).astype(jnp.int32)
        writes.append(pltpu.make_async_copy(sending.at[:, :, columns(d)], target, sem.at[3 + j]))
    for copy in reads:
        copy.start()
    for kk in range(16):
        table[KEPT_AT + kk] = -1
        table[GOT_AT + kk] = -1
    for m in range(10):
        table[KEPT_AT + maps[side, m * 8 + here_row] // 8] = m
        target = maps[other, m * 8 + here_row] // 8
        table[GOT_AT + target] = m
        table[GOT_ROW + m] = target
    for d in range(5):
        table[KEPT_COL + d] = maps[side, d * 16 + here_col] // 16
    table[GOT_COL] = maps[other, got_place * 16 + here_col] // 16
    for j in range(4):
        d = j + (j >= got_place).astype(jnp.int32)
        table[GOT_COL + 1 + j] = maps[other, d * 16 + here_col] // 16
    table[ROW] = here_row
    table[COL] = here_col
    table[SIDE] = side
    turned = pivots[...].T
    wanted = jnp.concatenate(
        [jnp.where(here_col < 4, turned[:, 4 + k : 5 + k], turned[:, k : k + 1]) for k in range(4)],
        axis=0,
    )
    block, offset = wanted >> 7, wanted & 127
    mine = jnp.where((block & 7) == here_row, (block >> 3) * BLK + offset, -1)
    sent = jnp.full_like(mine, -1)
    for m in range(10):
        hit = (block == maps[side, m * 8 + (here_row ^ 4)]) & (found > 0)
        sent = jnp.where(hit, m * BLK + offset, sent)
    reads[0].wait()
    for copy in writes:
        copy.start()
    first[...] = sending[:, :, columns(place)]
    reads[1].wait()
    reads[2].wait()

    @pl.when(found > 0)
    def _():
        for m in range(10):
            at = pl.multiple_of(maps[side, m * 8 + here_row] // 8 * BLK, BLK)
            panel[pl.ds(at, BLK), :] += kept[m]

    def rows_of(index, values, base):
        lane = lax.broadcasted_iota(jnp.int32, (PANEL, values.shape[0]), 1) + base
        chosen = jnp.where(lane == index, 1.0, 0.0).astype(BF16)
        both = jnp.concatenate(split(values), axis=1)
        return jnp.dot(chosen, both, preferred_element_type=F32)

    terms = jnp.zeros((PANEL, 2 * BLK), F32)
    for k in range(8):
        terms += rows_of(mine, panel[k * 256 : (k + 1) * 256, :], k * 256)
    for k in range(5):
        values = first[2 * k : 2 * k + 2].reshape(256, BLK)
        terms += rows_of(sent, values, k * 256)
    total[...] = terms[:, :BLK] + terms[:, BLK:]
    own[...] = total[pl.ds(pl.multiple_of(core * 256, 256), 256), :]
    away[...] = total[pl.ds(pl.multiple_of((1 - core) * 256, 256), 256), :]
    for copy in writes:
        copy.wait()


def prepare(maps, pivots, front, pieces):
    column = jax.ShapeDtypeStruct((10, BLK, BLK), F32)
    return pl.pallas_call(
        prepare_kernel,
        out_shape=[
            column,
            column,
            column,
            column,
            column,
            jax.ShapeDtypeStruct((2048, BLK), F32),
            jax.ShapeDtypeStruct((256, BLK), F32),
            jax.ShapeDtypeStruct((256, BLK), F32),
            jax.ShapeDtypeStruct((64,), jnp.int32),
        ],
        in_specs=[SMEM, VMEM, HBM, HBM],
        out_specs=[VMEM, HBM, HBM, HBM, HBM, VMEM, VMEM, VMEM, SMEM],
        scratch_shapes=[
            pltpu.VMEM((10, BLK, 640), F32),
            pltpu.VMEM((10, BLK, BLK), F32),
            pltpu.VMEM((PANEL, BLK), F32),
            pltpu.SemaphoreType.DMA((7,)),
        ],
        compiler_params=params(24),
        cost_estimate=cost(0, 9 * MIB),
        name="prepare",
    )(maps, pivots.reshape(8, BLK), in_hbm(front), in_hbm(pieces))


def pivot_kernel(mine_half, maps, pivots, front, children, *refs):
    rows, marks, spread, inverse, front_list, child_list, sem, child_sem = refs[-8:]
    rows[...] = jnp.zeros_like(rows)
    marks[...] = refs[0][...] if mine_half else jnp.zeros_like(marks)
    here_row, here_col = lax.axis_index("row"), lax.axis_index("col")
    side, quarter, core = here_row // 4, here_row % 4, here_row % 2
    half = core if mine_half else 1 - core
    spread[...] = jnp.zeros_like(spread)

    def clear(b, carry):
        inverse[b] = -1
        return carry

    lax.fori_loop(0, 128, clear, 0, unroll=16)
    for k in range(20):
        inverse[maps[side, 4 * k + quarter]] = k

    def visit(p, counts):
        pivot = pivots[half * PANEL + p]
        block, offset = pivot >> 7, pivot & 127
        child_block = inverse[block]
        mine = (block & 7) == here_row
        shared = ((block & 3) == quarter) & (child_block >= 0)
        front_list[counts[0]] = (((block >> 3) * BLK + offset) << 9) | p
        child_list[counts[1]] = ((child_block * BLK + offset) << 9) | p
        return counts[0] + mine.astype(jnp.int32), counts[1] + shared.astype(jnp.int32)

    counts = lax.fori_loop(0, PANEL, visit, (jnp.int32(0), jnp.int32(0)), unroll=8)
    mark = jnp.full((1, BLK), half + 1, jnp.int32).astype(F32)

    def take_front(n, carry):
        at, p = front_list[n] >> 9, front_list[n] & 511
        pltpu.make_async_copy(front.at[pl.ds(at, 1), :], rows.at[pl.ds(p, 1), :], sem).start()
        marks[pl.ds(at, 1), :] = mark
        return carry

    def take_child(n, carry):
        at, p = child_list[n] >> 9, child_list[n] & 511
        pltpu.make_async_copy(
            children.at[pl.ds(at, 1), :], spread.at[pl.ds(p, 1), :], child_sem
        ).start()
        return carry

    def wait(source, target, semaphore, count):
        def some(size):
            def body(_, carry):
                pltpu.make_async_copy(
                    source.at[pl.ds(0, size), :], target.at[pl.ds(0, size), :], semaphore
                ).wait()
                return carry

            return body

        lax.fori_loop(0, count // 16, some(16), 0)
        lax.fori_loop(0, count % 16, some(1), 0)

    lax.fori_loop(0, counts[0], take_front, 0)
    lax.fori_loop(0, counts[1], take_child, 0)
    wait(front, rows, sem, counts[0])
    wait(children, spread, child_sem, counts[1])
    for d in range(5):
        to = pl.ds(pl.multiple_of(maps[side, d * 16 + here_col] // 16 * BLK, BLK), BLK)
        rows[:, to] += spread[:, d * BLK : (d + 1) * BLK]


def pivot_terms(maps, pivots, front, children, *before):
    mine_half = len(before) > 0
    return pl.pallas_call(
        functools.partial(pivot_kernel, mine_half),
        out_shape=[
            jax.ShapeDtypeStruct((PANEL, 1024), F32),
            jax.ShapeDtypeStruct((2048, BLK), F32),
        ],
        in_specs=[SMEM, SMEM, HBM, HBM] + [VMEM] * len(before),
        out_specs=[VMEM, VMEM],
        scratch_shapes=[
            pltpu.VMEM((PANEL, 640), F32),
            pltpu.SMEM((128,), jnp.int32),
            pltpu.SMEM((PANEL + 1,), jnp.int32),
            pltpu.SMEM((PANEL + 1,), jnp.int32),
            pltpu.SemaphoreType.DMA(()),
            pltpu.SemaphoreType.DMA(()),
        ],
        compiler_params=params(12),
        cost_estimate=cost(0, 24 * MIB),
        name="pivot_terms_mine" if mine_half else "pivot_terms_other",
    )(maps, pivots, in_hbm(front), in_hbm(children), *before)


def panel_kernel(table, panel, got, top, bottom):
    top[...] = panel[:1024, :]
    bottom[...] = panel[1024:, :]

    @pl.when(table[GOT_COL] == 0)
    def _():
        for kk in range(16):
            m = table[GOT_AT + kk]
            half = top if kk < 8 else bottom
            at = kk % 8 * BLK

            @pl.when(m >= 0)
            def _(half=half, at=at, m=m):
                half[at : at + BLK, :] += got[m]


def whole_panel(table, panel, got):
    shape = jax.ShapeDtypeStruct((1024, BLK), F32)
    return pl.pallas_call(
        panel_kernel,
        out_shape=[shape, shape],
        in_specs=[SMEM, VMEM, VMEM],
        out_specs=[VMEM, VMEM],
        compiler_params=params(12),
        cost_estimate=cost(0, 3 * MIB),
        name="whole_panel",
    )(table, panel, got)


def flips(delta):
    return (delta & 1) ^ (delta >> 1), delta >> 1


def corner_kernel(table, own, swapped, inverses, factor_h, factor_l, cross):
    here_row, here_col = table[ROW], table[COL]
    core, x, y = here_row % 2, here_col % 4, here_col // 4
    mine = (y ^ (y >> 1)) & 1

    def corner(panel, half):
        blocks = []
        for xx in range(4):
            one, three = flips(xx ^ x)
            pair = mine ^ panel
            slot = jnp.where(half == 0, pair | (one << 1) | (three << 2), one | (three << 1) | (pair << 2))
            blocks.append(jnp.where(core == half, own[slot], swapped[slot]))
        return jnp.concatenate(blocks, axis=1)

    for p in range(2):
        factor_h[p], factor_l[p] = split(inverses[p])
    for half in range(2):
        rows = slice(half * 256, (half + 1) * 256)
        factor_h[2, rows, :], factor_l[2, rows, :] = split(corner(1, half))
        cross[rows, :] = dot3(split(corner(0, half)), (factor_h[0], factor_l[0]))


def corners(table, own, swapped, inverses):
    return pl.pallas_call(
        corner_kernel,
        out_shape=[
            jax.ShapeDtypeStruct((3, PANEL, PANEL), BF16),
            jax.ShapeDtypeStruct((3, PANEL, PANEL), BF16),
            jax.ShapeDtypeStruct((PANEL, PANEL), F32),
        ],
        in_specs=[SMEM, VMEM, VMEM, VMEM],
        out_specs=[VMEM] * 3,
        compiler_params=params(20),
        cost_estimate=cost(6 * PANEL**3, 8 * MIB),
        name="corners",
    )(table, own, swapped, inverses)


def upper_kernel(table, own, swapped, cross, high, low):
    here_row, col = table[ROW], table[COL]
    core = here_row % 2
    inside = lax.broadcasted_iota(jnp.int32, (PANEL, 1024), 1) < BLK
    first = jnp.where(core == 0, own[...], swapped[...])
    first = jnp.where(inside & (col < 4), 0.0, first)
    terms = split(first)
    high[:PANEL], low[:PANEL] = terms
    second = jnp.where(core == 0, swapped[...], own[...])
    second = second - dot3(split(cross[...]), terms)
    second = jnp.where(inside & (col < 8), 0.0, second)
    high[PANEL:], low[PANEL:] = split(second)


def uppers(table, own, swapped, cross):
    shape = jax.ShapeDtypeStruct((1024, 1024), BF16)
    return pl.pallas_call(
        upper_kernel,
        out_shape=[shape, shape],
        in_specs=[SMEM, VMEM, VMEM, VMEM],
        out_specs=[VMEM, VMEM],
        compiler_params=params(28),
        cost_estimate=cost(6 * PANEL * PANEL * 1024, 9 * MIB),
        name="uppers",
    )(table, own, swapped, cross)


def block_at(base, part, t, s):
    return jnp.maximum(s[base + part // 2 * 8 + 2 * t + part % 2], 0)


TILE = pl.BlockSpec((2, 256, 1024), lambda t, s: (0, t, 0))


def extend_kernel(columns, table, front, *refs):
    out, refs = refs[-1], refs[:-1]
    kept, *got = (refs[4 * k : 4 * k + 4] for k in range(1 + columns))
    step = pl.program_id(0)
    out[...] = front[...]
    for part in range(4):
        half, rest = part // 2, part % 2
        span = slice(rest * BLK, (rest + 1) * BLK)
        kk = half * 8 + 2 * step + rest

        @pl.when(table[KEPT_AT + kk] >= 0)
        def _(half=half, span=span, part=part):
            for d in range(5):
                to = pl.ds(pl.multiple_of(table[KEPT_COL + d] * BLK, BLK), BLK)
                out[half, span, to] += kept[part][0, 0, :, d * BLK : (d + 1) * BLK]

        @pl.when(table[GOT_AT + kk] >= 0)
        def _(half=half, span=span, part=part):
            for j in range(columns):
                to = pl.ds(pl.multiple_of(table[GOT_COL + j] * BLK, BLK), BLK)
                out[half, span, to] += got[j][part][0]


def extend(table, front, pieces, got):
    def kept_at(part):
        return lambda t, s: (block_at(KEPT_AT, part, t, s), s[SIDE], 0, 0)

    def got_at(part):
        return lambda t, s: (block_at(GOT_AT, part, t, s), 0, 0)

    kept_specs = [pl.BlockSpec((1, 1, BLK, 640), kept_at(part)) for part in range(4)]
    got_specs = [pl.BlockSpec((1, BLK, BLK), got_at(part)) for part in range(4)]
    return pl.pallas_call(
        functools.partial(extend_kernel, len(got)),
        out_shape=pltpu.HBM((2, 1024, 1024), F32),
        grid_spec=pltpu.PrefetchScalarGridSpec(
            num_scalar_prefetch=1,
            grid=(4,),
            in_specs=[TILE, *kept_specs, *got_specs * len(got)],
            out_specs=TILE,
        ),
        compiler_params=params(20),
        cost_estimate=cost(0, 22 * MIB),
        name="extend",
    )(table, in_hbm(front.reshape(2, 1024, 1024)), *[in_hbm(pieces)] * 4, *[g for g in got for _ in range(4)])


ORDERS = ((1, 3, 4, 12), (3, 1, 12, 4)), ((4, 12, 1, 3), (12, 4, 3, 1))


def update_kernel(table, front, *refs):
    blocks = refs[:4], refs[4:8]
    factor_h, factor_l, upper_h, upper_l, marks, out, panels, lower_h, lower_l = refs[8:]
    step = pl.program_id(0)
    col, core = table[COL], table[ROW] % 2

    def assemble(which):
        held, came, held_far, came_far = blocks[which]
        for c in range(16):
            one_x, three_x = flips((c ^ col) & 3)
            one_y, three_y = flips((c ^ col) >> 2)
            bits = {1: one_x, 3: three_x, 4: one_y, 12: three_y}
            even, odd = (ORDERS[q][which] for q in range(2))
            flip = [jnp.where(core == 0, bits[e], bits[o]) for e, o in zip(even, odd)]
            slot = flip[0] | (flip[1] << 1)
            later, far = flip[2] == 1, flip[3] == 1
            near_block = jnp.where(later, came[slot], held[slot])
            far_block = jnp.where(later, came_far[slot], held_far[slot])
            block = jnp.where(far, far_block, near_block)
            y, x = c // 4, c % 4
            rows = slice(0, 256) if y < 2 else slice(256, PANEL)
            panels[min(y, 3 - y), rows, x * BLK : (x + 1) * BLK] = block

    for which in range(2):
        pl.when(step // 2 == which)(functools.partial(assemble, which))

    mark = jnp.concatenate([marks[...].reshape(PANEL, BLK)] * 4, axis=1)
    lower = dot3(split(panels[0]), (factor_h[0], factor_l[0]))
    lower = jnp.where(mark != 1, lower, 0.0)
    terms = split(lower)
    lower_h[:, :PANEL], lower_l[:, :PANEL] = terms
    second = panels[1] - dot3(terms, (factor_h[2], factor_l[2]))
    later = dot3(split(second), (factor_h[1], factor_l[1]))
    later = jnp.where(mark == 0, later, 0.0)
    lower_h[:, PANEL:], lower_l[:, PANEL:] = split(later)
    change = dot3((lower_h[...], lower_l[...]), (upper_h[...], upper_l[...]))
    out[...] = front[...] - change.reshape(2, 256, 1024)

    @pl.when(col < 8)
    def _():
        chosen = jnp.where(col < 4, lower, later)
        fresh = chosen[:, :BLK]
        for s in range(1, 4):
            fresh = jnp.where(col % 4 == s, chosen[:, s * BLK : (s + 1) * BLK], fresh)
        active = jnp.where(col < 4, (marks[...] != 1).astype(F32), (marks[...] == 0).astype(F32))
        out[:, :, :BLK] = jnp.where(active > 0, fresh.reshape(2, 256, BLK), out[:, :, :BLK])


def update(table, front, blocks, factors, upper, marks):
    def whole(x):
        return pl.BlockSpec(x.shape, lambda t, s: (0,) * x.ndim, pipeline_mode=pl.Buffered(1))

    first = pl.BlockSpec((4, 256, BLK), lambda t, s: (0, jnp.minimum(t, 1), 0))
    second = pl.BlockSpec((4, 256, BLK), lambda t, s: (0, jnp.maximum(t - 2, 0), 0))
    constants = *factors, *upper
    return pl.pallas_call(
        update_kernel,
        out_shape=pltpu.HBM((2, 1024, 1024), F32),
        grid_spec=pltpu.PrefetchScalarGridSpec(
            num_scalar_prefetch=1,
            grid=(4,),
            in_specs=[
                TILE,
                *[first] * 4,
                *[second] * 4,
                *[whole(x) for x in constants],
                pl.BlockSpec((2, 256, BLK), lambda t, s: (0, t, 0)),
            ],
            out_specs=TILE,
            scratch_shapes=[
                pltpu.VMEM((2, PANEL, PANEL), F32),
                pltpu.VMEM((PANEL, 1024), BF16),
                pltpu.VMEM((PANEL, 1024), BF16),
            ],
        ),
        compiler_params=params(34),
        cost_estimate=cost(6 * 2048 * 1024 * 1024 + 3 * 6 * 2048 * PANEL * PANEL, 36 * MIB),
        name="update",
    )(table, in_hbm(front), *blocks[0], *blocks[1], *constants, marks.reshape(2, 1024, BLK))


def finish_kernel(table, front, got_b, got_c, got_d, out, held, read_sem, write_sem):
    del front
    got = got_b, got_c, got_d
    copies = []
    for j in range(3):
        for m in range(10):
            rows = pl.ds(pl.multiple_of(table[GOT_ROW + m] * BLK, BLK), BLK)
            columns = pl.ds(pl.multiple_of(table[GOT_COL + 2 + j] * BLK, BLK), BLK)
            there, here = out.at[rows, columns], held.at[j, m]
            copies.append(
                (
                    pltpu.make_async_copy(there, here, read_sem.at[j, m]),
                    pltpu.make_async_copy(here, there, write_sem.at[j, m]),
                )
            )
    for read, _ in copies:
        read.start()
    for n, (read, write) in enumerate(copies):
        read.wait()
        held[n // 10, n % 10] += got[n // 10][n % 10]
        write.start()
    for _, write in copies:
        write.wait()


def finish(table, front, *got):
    return pl.pallas_call(
        finish_kernel,
        out_shape=jax.ShapeDtypeStruct((2048, 1024), F32),
        in_specs=[SMEM, HBM, VMEM, VMEM, VMEM],
        out_specs=HBM,
        scratch_shapes=[
            pltpu.VMEM((3, 10, BLK, BLK), F32),
            pltpu.SemaphoreType.DMA((3, 10)),
            pltpu.SemaphoreType.DMA((3, 10)),
        ],
        input_output_aliases={1: 0},
        compiler_params=params(8),
        cost_estimate=cost(0, 6 * MIB),
        name="finish",
    )(table, front, *got)


def swap(block, axis, partner):
    count = lax.axis_size(axis)
    return lax.ppermute(block, axis, [(i, partner(i)) for i in range(count)])


def fold(block, here_col):
    came = lax.ppermute(block[1], "col", [(c, c ^ 12) for c in range(8)])
    return jnp.where(here_col < 8, block[0], came)


def local(front, children, child_maps, pivots, diag_inverses):
    here_row, here_col = lax.axis_index("row"), lax.axis_index("col")
    chip = here_row // 2
    together = lax.optimization_barrier
    pieces = children.reshape(10, 2, BLK, 640)

    def by_row(block, mask):
        return swap(block, "row", lambda i: i ^ mask)

    def by_col(block, mask):
        return swap(block, "col", lambda i: i ^ mask)

    bits = (chip ^ (chip >> 1)) & 1, chip >> 1
    rings = [[(r, r ^ ((2, 6), (6, 2))[r % 2][k]) for r in range(8)] for k in range(2)]
    bits = [jnp.where(here_row % 2 == 0, bits[k], bits[1 - k]) for k in range(2)]

    def halve(terms, step):
        size = terms[0].shape[0] // 2

        def half(bit):
            return sum(lax.dynamic_slice_in_dim(term, bit * size, size, 0) for term in terms)

        came = lax.ppermute(half(1 - bits[step]), "row", rings[step])
        return half(bits[step]) + came

    def double(part, step):
        came = lax.ppermute(part, "row", rings[step])
        low, high = jnp.where(bits[step] == 0, part, came), jnp.where(bits[step] == 0, came, part)
        return jnp.concatenate([low, high], axis=0)

    def gather_step(block, which, step):
        route = [
            (r * 16 + c, r * 16 + (c ^ ORDERS[r % 2][which][step]))
            for r in range(8)
            for c in range(16)
        ]
        return lax.ppermute(block, ("row", "col"), route)

    first, rest_a, rest_b, rest_c, rest_d, panel, corner, away, table = prepare(
        child_maps, pivots, front, pieces
    )
    got0 = by_row(first, 4)
    corner = corner + by_row(away, 1)
    corner = corner + (by_row(corner, 2) + (by_row(corner, 6) + by_row(corner, 4)))
    away_rows, marks = pivot_terms(child_maps, pivots, front, children)
    got0, away_rows, rest_a, marks, corner = together((got0, away_rows, rest_a, marks, corner))

    top, bottom = whole_panel(table, panel, got0)
    mine = fold((top, bottom), here_col)
    corner = fold((corner, corner), here_col)[None]
    got_a = by_row(rest_a, 4)
    own_rows, marks = pivot_terms(child_maps, pivots, front, children, marks)
    total = own_rows, by_row(away_rows, 1)
    mine, corner, total, got_a, rest_b = together((mine, corner, total, got_a, rest_b))

    def corner_step(block, step):
        masks = ((4, 1, 3), (1, 3, 4))
        route = [
            (r * 16 + c, r * 16 + (c ^ masks[r % 2][step])) for r in range(8) for c in range(16)
        ]
        return jnp.concatenate([block, lax.ppermute(block, ("row", "col"), route)], axis=0)

    held = [mine[None, :PANEL], mine[None, PANEL:]]
    for k in range(2):
        came = [gather_step(held[w], w, k) for w in range(2)]
        held = [jnp.concatenate([h, c], axis=0) for h, c in zip(held, came)]
        corner = corner_step(corner, k)
        total = halve(total if k == 0 else (total,), k)
        held, corner, total = together((held, corner, total))
    came = [gather_step(held[w], w, 2) for w in range(2)]
    corner = corner_step(corner, 2)
    total = double(total, 1)
    came, corner, total = together((came, corner, total))
    held_far = [gather_step(held[w], w, 3) for w in range(2)]
    factors = corners(table, corner, by_row(corner, 1), diag_inverses)
    total = double(total, 0)
    came, held_far, total, rest_b = together((came, held_far, total, rest_b))
    came_far = [gather_step(came[w], w, 3) for w in range(2)]
    got_b = by_row(rest_b, 4)
    upper = uppers(table, total, by_row(total, 1), factors[2])
    front = extend(table, front, pieces, (got0, got_a))
    came_far, got_b, rest_c, rest_d = together((came_far, got_b, rest_c, rest_d))
    got_c = by_row(rest_c, 4)
    got_d = by_row(rest_d, 4)
    blocks = [(held[w], came[w], held_far[w], came_far[w]) for w in range(2)]
    front = update(table, front, blocks, factors[:2], upper, marks)
    return finish(table, front.reshape(2048, 1024), got_b, got_c, got_d)


def solution(mesh):
    return jax.shard_map(
        local,
        mesh=mesh,
        in_specs=(P("row", "col"), P("row", "col"), P(), P(), P()),
        out_specs=P("row", "col"),
        check_vma=False,
    )
```

time: 557 us -> 198 us (0.36)
  waiting for transfers between devices: 376 us -> 48.6 us
  matrix products: 76.5 us -> 0 us
  Pallas kernels: 0 us -> 73.3 us
  local copies, waits for them, and re-layouts: 61.5 us -> 6.3 us
  starting transfers between devices: 4.55 us -> 45.5 us
  between operations: 13.6 us -> 0.47 us
    psum x4 -> x0, waiting for transfers between devices: 329 us -> none  [the longest x2 216 us: local(): lower = lax.psum(jnp.where(owns, term, jnp.float32(0.0)), 'col')]
    dot_general x8 -> x0, matrix products: 76.5 us -> none  [the longest x2 36.9 us: local(): jnp.dot(lower, upper, precision=lax.Precision.HIGHEST, preferred_element_...]
    pallas_call x0 -> x9, Pallas kernels: none -> 73.3 us  [the longest x1 30.7 us: update(): pl.pallas_call(update_kernel, out_shape=pltpu.HBM((2, 1024, 1024), F32),...]
    ppermute x1 -> x31, starting transfers between devices: 4.43 us -> 45.5 us  [the longest x12 18.2 us: swap(): return lax.ppermute(block, axis, [(i, partner(i)) for i in range(count)])]
    gather x2 -> x0, local copies, waits for them, and re-layouts: 12.4 us -> none  [local(): picked = jnp.take(front, local_index, axis=0, mode='clip')]
    unnamed x16 -> x40, local copies, waits for them, and re-layouts: 15.7 us -> 4.4 us
    reshape x2 -> x0, local copies, waits for them, and re-layouts: 11.3 us -> none  [place(): grid = piece.reshape(kept_blocks, BLK, child_cblocks, BLK)]
    dynamic_slice x2 -> x1, local copies, waits for them, and re-layouts: 9.89 us -> 1.08 us  [half(): lax.dynamic_slice_in_dim(term, bit * size, size, 0)]
  transfers between devices with their start and end apart: 5 -> 31, of which waited for: 5 -> 13; matrix products, arithmetic and copies ran while one was open for 7% -> 9% of each run, Pallas kernels for 0% -> 33%
where the time goes in v2:
time: 198 us; the launch traced here: 197 us
  Pallas kernels  73.3 us (37%)
  waiting for transfers between devices  48.6 us (25%)
  starting transfers between devices  45.5 us (23%)
  other arithmetic  22.7 us (11%)
  local copies, waits for them, and re-layouts  6.3 us (3%)
    pallas_call x1, Pallas kernels, update(): pl.pallas_call(update_kernel, out_shape=pltpu.HBM((2, 1024, 1024), F32),...  30.7 us
    pallas_call x2, Pallas kernels, pivot_terms(): pl.pallas_call(functools.partial(pivot_kernel, mine_half), out_shape=[jax...  18.5 us
    ppermute x12, starting transfers between devices, swap(): return lax.ppermute(block, axis, [(i, partner(i)) for i in range(count)])  18.2 us
    ppermute x2, waiting for transfers between devices, double(): came = lax.ppermute(part, 'row', rings[step])  15.5 us
    ppermute x3, waiting for transfers between devices, corner_step(): lax.ppermute(block, ('row', 'col'), route)  13.2 us
    ppermute x12, waiting for transfers between devices, swap(): return lax.ppermute(block, axis, [(i, partner(i)) for i in range(count)])  13.1 us
    ppermute x10, starting transfers between devices, gather_step(): return lax.ppermute(block, ('row', 'col'), route)  10.8 us
    pallas_call x1, Pallas kernels, extend(): pl.pallas_call(functools.partial(extend_kernel, len(got)), out_shape=pltp...  9.54 us
  transfers between devices with their start and end apart: 31, of which 13 were waited for; matrix products, arithmetic and copies ran while one was open for 9% of the time, Pallas kernels for 33%

profile of v2, /device:TPU:1, one launch (start us, length us, event | category | flops | bytes accessed | tf_op | source)
XLA Modules:
  0.0 196.9 jit_solution(1946883215083589605)
XLA Ops:
  1.4 5.0 %prepare.1 = (f32[10,128,128]{2,1,0:T(8,128)S(1)}, f32[10,128,128]{2,1,0:T(8,128)}, f32[10,128,128]{2,1,0:T(8,128)S(1)}, f32[10,128,128]{2,1,0:T(8,128)S(1)}, f3...) custom-call(s32[2,80]{1,0:T(2,128)S(1)} %copy-done.7, ...), custom_call_target="tpu_custom_call" | custom-call | bytes 9437184 | tf_op jit(solution)/shard_map/prepare/pallas_call | solution.py:143
  6.4 4.5 %collective-permute-start = (f32[10,128,128]{2,1,0:T(8,128)S(1)}, f32[10,128,128]{2,1,0:T(8,128)S(1)}, u32[]{:S(2)}, u32[]{:S(2)}) collective-permute-start(f32[10,128,128]{2,1,0:T(8,128)S(1)} %get-tuple-element.60), channel_id=1, source_target_pairs={{0,64},{16,80},{32,96},{48,112},{64,0},{80,16},{96,32},{112,48},{1... | collective-permute-start | bytes 1966088 | tf_op jit(solution)/shard_map/ppermute | solution.py:540
  12.9 3.1 %collective-permute-start.3 = (f32[256,128]{1,0:T(8,128)S(1)}, f32[256,128]{1,0:T(8,128)S(1)}, u32[]{:S(2)}, u32[]{:S(2)}) collective-permute-start(f32[256,128]{1,0:T(8,128)S(1)} %add.44), channel_id=1, source_target_pairs={{0,96},{16,112},{32,64},{48,80},{64,32},{80,48},{96,0},{112,16},{1... | collective-permute-start | bytes 393224 | tf_op jit(solution)/shard_map/ppermute | solution.py:540
  16.0 10.0 %pivot_terms_other.1 = (f32[512,1024]{1,0:T(8,128)}, f32[2048,128]{1,0:T(8,128)S(1)}) custom-call(s32[2,80]{1,0:T(2,128)S(1)} %copy-done.7, s32[1024]{0:T(1024)S(1)} %copy-done.5, f32[2048,1024]{1,0:T(8,128)} %front.5, f32[2560,640]{1,0:T(8,128)} %children.3), custom_call_target="tpu_custom_call" | custom-call | bytes 25165824 | tf_op jit(solution)/shard_map/pivot_terms_other/pallas_call | solution.py:237
  28.2 3.5 %collective-permute-done.3 = f32[256,128]{1,0:T(8,128)S(1)} collective-permute-done((f32[256,128]{1,0:T(8,128)S(1)}, f32[256,128]{1,0:T(8,128)S(1)}, u32[]{:S(2)}, u32[]{:S(2)}) %collective-permute-start.3) | collective-permute-done | bytes 131104 | tf_op jit(solution)/shard_map/ppermute | solution.py:540
  31.8 1.3 collective-permute-start.7
  33.1 1.6 whole_panel.1
  35.5 5.4 %collective-permute-start.5 = (f32[1024,128]{1,0:T(8,128)}, f32[1024,128]{1,0:T(8,128)}, u32[]{:S(2)}, u32[]{:S(2)}) collective-permute-start(f32[1024,128]{1,0:T(8,128)} %get-tuple-element.69), channel_id=1, source_target_pairs={{0,12},{1,13},{2,14},{3,15},{4,8},{5,9},{6,10},{7,11},{16,28},{17,... | collective-permute-start | bytes 1572872 | tf_op jit(solution)/shard_map/ppermute | solution.py:544
  40.9 2.2 %collective-permute-start.8 = (f32[10,128,128]{2,1,0:T(8,128)}, f32[10,128,128]{2,1,0:T(8,128)S(1)}, u32[]{:S(2)}, u32[]{:S(2)}) collective-permute-start(f32[10,128,128]{2,1,0:T(8,128)} %get-tuple-element.74), channel_id=1, source_target_pairs={{0,64},{16,80},{32,96},{48,112},{64,0},{80,16},{96,32},{112,48},{1... | collective-permute-start | bytes 1966088 | tf_op jit(solution)/shard_map/ppermute | solution.py:540
  43.1 1.9 collective-permute-start.6
  45.1 1.2 copy-done.2
  46.3 8.5 %pivot_terms_mine.1 = (f32[512,1024]{1,0:T(8,128)S(1)}, f32[2048,128]{1,0:T(8,128)S(1)}) custom-call(s32[2,80]{1,0:T(2,128)S(1)} %copy-done.8, s32[1024]{0:T(1024)S(1)} %copy-done.6, f32[2048,1024]{1,0:T(8,128)} %front.5, f32[2560,640]{1,0:T(8,128)} %children.3, f32[2048,128]{1,0:T(8,128)S(1)} %copy-done.2), custom_call_target="tpu_custom_call" | custom-call | bytes 25165824 | tf_op jit(solution)/shard_map/pivot_terms_mine/pallas_call | solution.py:237
  55.7 3.0 %collective-permute-done.8.refs_8_.refs_9_.refs_10_.refs_11_ = f32[10,128,128]{2,1,0:T(8,128)S(1)} collective-permute-done((f32[10,128,128]{2,1,0:T(8,128)}, f32[10,128,128]{2,1,0:T(8,128)S(1)}, u32[]{:S(2)}, u32[]{:S(2)}) %collective-permute-start.8) | collective-permute-done | bytes 655392 | tf_op jit(solution)/shard_map/ppermute | solution.py:540
  58.7 2.4 %dynamic-slice_add_fusion = f32[256,1024]{1,0:T(8,128)} fusion(f32[512,1024]{1,0:T(8,128)} %collective-permute-done.7, s32[]{:T(128)S(6)} %select_n.81, f32[512,1024]{1,0:T(8,128)S(1)} %get-tuple-element.79), kind=kLoop, calls=%fused_computation.5 | loop fusion | flops 262144 | bytes 3145732 | tf_op jit(solution)/shard_map/add | solution.py:568
  61.0 2.4 %collective-permute-start.12 = (f32[256,1024]{1,0:T(8,128)}, f32[256,1024]{1,0:T(8,128)}, u32[]{:S(2)}, u32[]{:S(2)}) collective-permute-start(f32[256,1024]{1,0:T(8,128)} %dynamic-slice_add_fusion), channel_id=1, source_target_pairs={{0,32},{16,112},{32,0},{48,80},{64,96},{80,48},{96,64},{112,16},{1... | collective-permute-start | bytes 3145736 | tf_op jit(solution)/shard_map/ppermute | solution.py:570
  64.2 2.0 %collective-permute-start.10 = (f32[1,512,128]{2,1,0:T(8,128)}, f32[1,512,128]{2,1,0:T(8,128)}, u32[]{:S(2)}, u32[]{:S(2)}) collective-permute-start(f32[1,512,128]{2,1,0:T(8,128)} %get-tuple-element.117), channel_id=1, source_target_pairs={{0,3},{1,2},{2,1},{3,0},{4,7},{5,6},{6,5},{7,4},{8,11},{9,10},{10,... | collective-permute-start | bytes 786440 | tf_op jit(solution)/shard_map/ppermute | solution.py:584
  66.2 1.2 collective-permute-start.11
  67.4 3.6 %collective-permute-done.11 = f32[1,256,128]{2,1,0:T(8,128)S(1)} collective-permute-done((f32[1,256,128]{2,1,0:T(8,128)}, f32[1,256,128]{2,1,0:T(8,128)S(1)}, u32[]{:S(2)}, u32[]{:S(2)}) %collective-permute-start.11) | collective-permute-done | bytes 131104 | tf_op jit(solution)/shard_map/ppermute | solution.py:608
  71.1 1.6 pad_maximum_fusion.8
  72.7 1.9 pad_maximum_fusion.6
  74.6 1.9 pad_maximum_fusion.5
  76.5 2.8 %add_add_fusion = f32[256,1024]{1,0:T(8,128)} fusion(f32[256,1024]{1,0:T(8,128)} %collective-permute-done.12, f32[512,1024]{1,0:T(8,128)} %collective-permute-done.7, s32[]{:T(128)S(6)} %select_n.80, f32[512,1024]{1,0:T(8,128)S(1)} %get-tuple-element.79), kind=kLoop, calls=%fused_computation.6 | loop fusion | flops 524288 | bytes 4194308 | tf_op jit(solution)/shard_map/add | solution.py:571
  79.2 1.8 collective-permute-start.13
  81.0 2.5 %collective-permute-start.15 = (f32[2,256,128]{2,1,0:T(8,128)}, f32[2,256,128]{2,1,0:T(8,128)S(1)}, u32[]{:S(2)}, u32[]{:S(2)}) collective-permute-start(f32[2,256,128]{2,1,0:T(8,128)} %pad_maximum_fusion.8), channel_id=1, source_target_pairs={{0,1},{1,0},{2,3},{3,2},{4,5},{5,4},{6,7},{7,6},{8,9},{9,8},{10,11... | collective-permute-start | bytes 786440 | tf_op jit(solution)/shard_map/ppermute | solution.py:608
  84.7 5.5 %collective-permute-done.15 = f32[2,256,128]{2,1,0:T(8,128)S(1)} collective-permute-done((f32[2,256,128]{2,1,0:T(8,128)}, f32[2,256,128]{2,1,0:T(8,128)S(1)}, u32[]{:S(2)}, u32[]{:S(2)}) %collective-permute-start.15) | collective-permute-done | bytes 262176 | tf_op jit(solution)/shard_map/ppermute | solution.py:608
  91.2 1.5 pad_maximum_fusion.1.refs_0_
  92.7 2.2 %pad_maximum_fusion.2.refs_4_ = f32[4,512,128]{2,1,0:T(8,128)} fusion(f32[2,512,128]{2,1,0:T(8,128)} %collective-permute-done.14, f32[2,512,128]{2,1,0:T(8,128)} %pad_maximum_fusion.6), kind=kLoop, calls=%fused_computation.2 | loop fusion | flops 262144 | bytes 2097152 | tf_op jit(solution)/shard_map/concatenate | solution.py:613
  96.9 2.6 %collective-permute-start.18 = (f32[4,512,128]{2,1,0:T(8,128)}, f32[4,512,128]{2,1,0:T(8,128)}, u32[]{:S(2)}, u32[]{:S(2)}) collective-permute-start(f32[4,512,128]{2,1,0:T(8,128)} %pad_maximum_fusion.2.refs_4_), channel_id=1, source_target_pairs={{0,12},{1,13},{2,14},{3,15},{4,8},{5,9},{6,10},{7,11},{8,4},{9,5},... | collective-permute-start | bytes 3145736 | tf_op jit(solution)/shard_map/ppermute | solution.py:584
  99.5 5.1 %collective-permute-done.20 = f32[128,1024]{1,0:T(8,128)} collective-permute-done((f32[128,1024]{1,0:T(8,128)S(1)}, f32[128,1024]{1,0:T(8,128)}, u32[]{:S(2)}, u32[]{:S(2)}) %collective-permute-start.20) | collective-permute-done | bytes 524320 | tf_op jit(solution)/shard_map/ppermute | solution.py:574
  104.6 1.2 broadcast_select_fusion.3
  106.8 4.1 %collective-permute-done.19 = f32[4,256,128]{2,1,0:T(8,128)} collective-permute-done((f32[4,256,128]{2,1,0:T(8,128)S(1)}, f32[4,256,128]{2,1,0:T(8,128)}, u32[]{:S(2)}, u32[]{:S(2)}) %collective-permute-start.19) | collective-permute-done | bytes 524320 | tf_op jit(solution)/shard_map/ppermute | solution.py:608
  111.0 1.2 pad_maximum_fusion.3.own
  112.2 5.0 %collective-permute-done.18.refs_5_ = f32[4,512,128]{2,1,0:T(8,128)} collective-permute-done((f32[4,512,128]{2,1,0:T(8,128)}, f32[4,512,128]{2,1,0:T(8,128)}, u32[]{:S(2)}, u32[]{:S(2)}) %collective-permute-start.18) | collective-permute-done | bytes 1048608 | tf_op jit(solution)/shard_map/ppermute | solution.py:584
  117.2 2.9 %collective-permute-start.23 = (f32[256,1024]{1,0:T(8,128)}, f32[256,1024]{1,0:T(8,128)}, u32[]{:S(2)}, u32[]{:S(2)}) collective-permute-start(f32[256,1024]{1,0:T(8,128)} %pad_maximum_fusion.4), channel_id=1, source_target_pairs={{0,32},{16,112},{32,0},{48,80},{64,96},{80,48},{96,64},{112,16},{1... | collective-permute-start | bytes 3145736 | tf_op jit(solution)/shard_map/ppermute | solution.py:574
  120.0 2.4 %collective-permute-start.21 = (f32[4,512,128]{2,1,0:T(8,128)S(1)}, f32[4,512,128]{2,1,0:T(8,128)}, u32[]{:S(2)}, u32[]{:S(2)}) collective-permute-start(f32[4,512,128]{2,1,0:T(8,128)S(1)} %pad_maximum_fusion.1.refs_0_), channel_id=1, source_target_pairs={{0,12},{1,13},{2,14},{3,15},{4,8},{5,9},{6,10},{7,11},{8,4},{9,5},... | collective-permute-start | bytes 3145736 | tf_op jit(solution)/shard_map/ppermute | solution.py:584
  122.4 10.4 %collective-permute-done.23 = f32[256,1024]{1,0:T(8,128)} collective-permute-done((f32[256,1024]{1,0:T(8,128)}, f32[256,1024]{1,0:T(8,128)}, u32[]{:S(2)}, u32[]{:S(2)}) %collective-permute-start.23) | collective-permute-done | bytes 1048608 | tf_op jit(solution)/shard_map/ppermute | solution.py:574
  132.8 1.8 broadcast_select_fusion.1
  135.3 1.4 collective-permute-done.22.refs_6_
  136.7 1.5 collective-permute-start.28
  138.2 1.4 collective-permute-start.24
  139.6 1.5 collective-permute-start.26
  141.1 9.5 %extend.1.front = f32[2,1024,1024]{2,1,0:T(8,128)} custom-call(s32[64]{0:T(128)S(1)} %get-tuple-element.59.table, f32[2,1024,1024]{2,1,0:T(8,128)} %bitcast.18, f32[10,2,128,640]{3,2,1,0:T(8,128)} %bitcast.14, f32[10,2,128,640]{3,2,1,0:T(8,128)} %bitcast.15, f32[10,2,128,640]{3,2,1,0:T(8,128)} %bitcast.16, f32[10,2,128,640]{3,2,1,0:T(8,128)} %bitcast.17, ...), custom_call_target="tpu_custom_call" | custom-call | bytes 23068672 | tf_op jit(solution)/shard_map/extend/pallas_call | solution.py:396
  150.6 2.0 %corners.1 = (bf16[3,512,512]{2,1,0:T(8,128)(2,1)S(1)}, bf16[3,512,512]{2,1,0:T(8,128)(2,1)S(1)}, f32[512,512]{1,0:T(8,128)S(1)}) custom-call(s32[64]{0:T(128)S(1)} %get-tuple-element.59.table, f32[8,256,128]{2,1,0:T(8,128)S(1)} %pad_maximum_fusion.3.own, f32[8,256,128]{2,1,0:T(8,128)S(1)} %collective-permute-done.27.swapped, f32[2,512,512]{2,1,0:T(8,128)S(1)} %copy-done), custom_call_target="tpu_custom_call" | custom-call | flops 805306368 | bytes 8388608 | tf_op jit(solution)/shard_map/corners/pallas_call | solution.py:315
  152.6 4.4 %collective-permute-done.26.got_b = f32[10,128,128]{2,1,0:T(8,128)S(1)} collective-permute-done((f32[10,128,128]{2,1,0:T(8,128)S(1)}, f32[10,128,128]{2,1,0:T(8,128)S(1)}, u32[]{:S(2)}, u32[]{:S(2)}) %collective-permute-start.26) | collective-permute-done | bytes 655392 | tf_op jit(solution)/shard_map/ppermute | solution.py:540
  157.9 2.2 %collective-permute-start.30 = (f32[10,128,128]{2,1,0:T(8,128)S(1)}, f32[10,128,128]{2,1,0:T(8,128)S(1)}, u32[]{:S(2)}, u32[]{:S(2)}) collective-permute-start(f32[10,128,128]{2,1,0:T(8,128)S(1)} %copy-done.12), channel_id=1, source_target_pairs={{0,64},{16,80},{32,96},{48,112},{64,0},{80,16},{96,32},{112,48},{1... | collective-permute-start | bytes 1966088 | tf_op jit(solution)/shard_map/ppermute | solution.py:540
  160.1 2.6 %uppers.1 = (bf16[1024,1024]{1,0:T(8,128)(2,1)S(1)}, bf16[1024,1024]{1,0:T(8,128)(2,1)S(1)}) custom-call(s32[64]{0:T(128)S(1)} %get-tuple-element.59.table, f32[512,1024]{1,0:T(8,128)S(1)} %pad_maximum_fusion.own, f32[512,1024]{1,0:T(8,128)S(1)} %collective-permute-done.28.swapped, f32[512,512]{1,0:T(8,128)S(1)} %get-tuple-element.106.cross), custom_call_target="tpu_custom_call" | custom-call | flops 1610612736 | bytes 9437184 | tf_op jit(solution)/shard_map/uppers/pallas_call | solution.py:346
  162.8 30.7 %update.1 = f32[2,1024,1024]{2,1,0:T(8,128)} custom-call(s32[64]{0:T(128)S(1)} %get-tuple-element.59.table, f32[2,1024,1024]{2,1,0:T(8,128)} %extend.1.front, f32[4,512,128]{2,1,0:T(8,128)S(1)} %pad_maximum_fusion.1.refs_0_, f32[4,512,128]{2,1,0:T(8,128)} %collective-permute-done.17.refs_1_, f32[4,512,128]{2,1,0:T(8,128)} %collective-permute-done.21.refs_2_, ...), custom_call_target="tpu_custom_call" | custom-call | flops 22548578304 | bytes 37748736 | tf_op jit(solution)/shard_map/update/pallas_call | solution.py:469
  193.5 3.3 %finish.1 = f32[2048,1024]{1,0:T(8,128)} custom-call(s32[64]{0:T(128)S(1)} %get-tuple-element.59.table, f32[2048,1024]{1,0:T(8,128)} %bitcast.19, f32[10,128,128]{2,1,0:T(8,128)S(1)} %collective-permute-done.26.got_b, f32[10,128,128]{2,1,0:T(8,128)S(1)} %collective-permute-done.29.got_c, ...), custom_call_target="tpu_custom_call", output_to_operand_aliasing={{}: (1, {})} | custom-call | bytes 6291456 | tf_op jit(solution)/shard_map/finish/pallas_call | solution.py:521
  (83 shorter events, 14.7 us)
Async XLA Ops:
  6.3 19.7 %copy-start.11 = (f32[10,128,128]{2,1,0:T(8,128)}, f32[10,128,128]{2,1,0:T(8,128)S(1)}, u32[]{:S(2)}) copy-start(f32[10,128,128]{2,1,0:T(8,128)S(1)} %get-tuple-element.112) | copy-start | bytes 1966084
  6.3 19.7 %copy-start.13 = (f32[10,128,128]{2,1,0:T(8,128)}, f32[10,128,128]{2,1,0:T(8,128)S(1)}, u32[]{:S(2)}) copy-start(f32[10,128,128]{2,1,0:T(8,128)S(1)} %get-tuple-element.111) | copy-start | bytes 1966084
  6.4 19.7 %copy-start.15 = (f32[10,128,128]{2,1,0:T(8,128)}, f32[10,128,128]{2,1,0:T(8,128)S(1)}, u32[]{:S(2)}) copy-start(f32[10,128,128]{2,1,0:T(8,128)S(1)} %get-tuple-element.96) | copy-start | bytes 1966084
  6.4 25.4 %collective-permute-start = (f32[10,128,128]{2,1,0:T(8,128)S(1)}, f32[10,128,128]{2,1,0:T(8,128)S(1)}, u32[]{:S(2)}, u32[]{:S(2)}) collective-permute-start(f32[10,128,128]{2,1,0:T(8,128)S(1)} %get-tuple-element.60), channel_id=1, source_target_pairs={{0,64},{16,80},{32,96},{48,112},{64,0},{80,16},{96,32},{112,48},{1... | collective-permute-start | bytes 1966088 | tf_op jit(solution)/shard_map/ppermute | solution.py:540
  10.9 1.9 collective-permute-start.1
  12.8 15.4 %collective-permute-start.4 = (f32[256,128]{1,0:T(8,128)S(1)}, f32[256,128]{1,0:T(8,128)S(1)}, u32[]{:S(2)}, u32[]{:S(2)}) collective-permute-start(f32[256,128]{1,0:T(8,128)S(1)} %add.44), channel_id=1, source_target_pairs={{0,64},{16,80},{32,96},{48,112},{64,0},{80,16},{96,32},{112,48},{1... | collective-permute-start | bytes 393224 | tf_op jit(solution)/shard_map/ppermute | solution.py:540
  12.9 18.8 %collective-permute-start.3 = (f32[256,128]{1,0:T(8,128)S(1)}, f32[256,128]{1,0:T(8,128)S(1)}, u32[]{:S(2)}, u32[]{:S(2)}) collective-permute-start(f32[256,128]{1,0:T(8,128)S(1)} %add.44), channel_id=1, source_target_pairs={{0,96},{16,112},{32,64},{48,80},{64,32},{80,48},{96,0},{112,16},{1... | collective-permute-start | bytes 393224 | tf_op jit(solution)/shard_map/ppermute | solution.py:540
  16.0 15.7 %collective-permute-start.2 = (f32[256,128]{1,0:T(8,128)S(1)}, f32[256,128]{1,0:T(8,128)S(1)}, u32[]{:S(2)}, u32[]{:S(2)}) collective-permute-start(f32[256,128]{1,0:T(8,128)S(1)} %add.44), channel_id=1, source_target_pairs={{0,32},{16,48},{32,0},{48,16},{64,96},{80,112},{96,64},{112,80},{1... | collective-permute-start | bytes 393224 | tf_op jit(solution)/shard_map/ppermute | solution.py:540
  26.1 1.0 copy-start.1
  27.1 18.0 %copy-start.6 = (s32[1024]{0:T(1024)S(1)}, s32[1024]{0:T(1024)}, u32[]{:S(2)}) copy-start(s32[1024]{0:T(1024)} %pivots.3) | copy-start | bytes 12292
  27.1 18.0 %copy-start.8 = (s32[2,80]{1,0:T(2,128)S(1)}, s32[2,80]{1,0:T(2,128)}, u32[]{:S(2)}) copy-start(s32[2,80]{1,0:T(2,128)} %maps.5) | copy-start | bytes 1924
  31.8 26.9 %collective-permute-start.7 = (f32[512,1024]{1,0:T(8,128)}, f32[512,1024]{1,0:T(8,128)}, u32[]{:S(2)}, u32[]{:S(2)}) collective-permute-start(f32[512,1024]{1,0:T(8,128)} %get-tuple-element.73), channel_id=1, source_target_pairs={{0,16},{16,0},{32,48},{48,32},{64,80},{80,64},{96,112},{112,96},{1... | collective-permute-start | bytes 6291464 | tf_op jit(solution)/shard_map/ppermute | solution.py:540
  35.5 20.1 %collective-permute-start.5 = (f32[1024,128]{1,0:T(8,128)}, f32[1024,128]{1,0:T(8,128)}, u32[]{:S(2)}, u32[]{:S(2)}) collective-permute-start(f32[1024,128]{1,0:T(8,128)} %get-tuple-element.69), channel_id=1, source_target_pairs={{0,12},{1,13},{2,14},{3,15},{4,8},{5,9},{6,10},{7,11},{16,28},{17,... | collective-permute-start | bytes 1572872 | tf_op jit(solution)/shard_map/ppermute | solution.py:544
  40.9 17.7 %collective-permute-start.8 = (f32[10,128,128]{2,1,0:T(8,128)}, f32[10,128,128]{2,1,0:T(8,128)S(1)}, u32[]{:S(2)}, u32[]{:S(2)}) collective-permute-start(f32[10,128,128]{2,1,0:T(8,128)} %get-tuple-element.74), channel_id=1, source_target_pairs={{0,64},{16,80},{32,96},{48,112},{64,0},{80,16},{96,32},{112,48},{1... | collective-permute-start | bytes 1966088 | tf_op jit(solution)/shard_map/ppermute | solution.py:540
  43.1 11.7 %collective-permute-start.6 = (f32[256,128]{1,0:T(8,128)S(1)}, f32[256,128]{1,0:T(8,128)}, u32[]{:S(2)}, u32[]{:S(2)}) collective-permute-start(f32[256,128]{1,0:T(8,128)S(1)} %add_add_fusion.1), channel_id=1, source_target_pairs={{0,12},{1,13},{2,14},{3,15},{4,8},{5,9},{6,10},{7,11},{16,28},{17,... | collective-permute-start | bytes 393224 | tf_op jit(solution)/shard_map/ppermute | solution.py:544
  45.1 1.2 copy-start.2
  46.3 9.3 %copy-start.4 = (f32[1024,128]{1,0:T(8,128)S(1)}, f32[1024,128]{1,0:T(8,128)}, u32[]{:S(2)}) copy-start(f32[1024,128]{1,0:T(8,128)} %copy-done.3) | copy-start | bytes 1572868
  54.8 3.9 %copy-start.9 = (f32[2048,128]{1,0:T(8,128)}, f32[2048,128]{1,0:T(8,128)S(1)}, u32[]{:S(2)}) copy-start(f32[2048,128]{1,0:T(8,128)S(1)} %get-tuple-element.109) | copy-start | bytes 3145732
  61.0 15.4 %collective-permute-start.12 = (f32[256,1024]{1,0:T(8,128)}, f32[256,1024]{1,0:T(8,128)}, u32[]{:S(2)}, u32[]{:S(2)}) collective-permute-start(f32[256,1024]{1,0:T(8,128)} %dynamic-slice_add_fusion), channel_id=1, source_target_pairs={{0,32},{16,112},{32,0},{48,80},{64,96},{80,48},{96,64},{112,16},{1... | collective-permute-start | bytes 3145736 | tf_op jit(solution)/shard_map/ppermute | solution.py:570
  64.2 8.5 %collective-permute-start.10 = (f32[1,512,128]{2,1,0:T(8,128)}, f32[1,512,128]{2,1,0:T(8,128)}, u32[]{:S(2)}, u32[]{:S(2)}) collective-permute-start(f32[1,512,128]{2,1,0:T(8,128)} %get-tuple-element.117), channel_id=1, source_target_pairs={{0,3},{1,2},{2,1},{3,0},{4,7},{5,6},{6,5},{7,4},{8,11},{9,10},{10,... | collective-permute-start | bytes 786440 | tf_op jit(solution)/shard_map/ppermute | solution.py:584
  66.2 4.8 %collective-permute-start.11 = (f32[1,256,128]{2,1,0:T(8,128)}, f32[1,256,128]{2,1,0:T(8,128)S(1)}, u32[]{:S(2)}, u32[]{:S(2)}) collective-permute-start(f32[1,256,128]{2,1,0:T(8,128)} %select_bitcast_fusion), channel_id=1, source_target_pairs={{0,4},{1,5},{2,6},{3,7},{4,0},{5,1},{6,2},{7,3},{8,12},{9,13},{10,... | collective-permute-start | bytes 393224 | tf_op jit(solution)/shard_map/ppermute | solution.py:608
  67.4 7.1 %collective-permute-start.9 = (f32[1,512,128]{2,1,0:T(8,128)}, f32[1,512,128]{2,1,0:T(8,128)}, u32[]{:S(2)}, u32[]{:S(2)}) collective-permute-start(f32[1,512,128]{2,1,0:T(8,128)} %get-tuple-element.118), channel_id=1, source_target_pairs={{0,1},{1,0},{2,3},{3,2},{4,5},{5,4},{6,7},{7,6},{8,9},{9,8},{10,11... | collective-permute-start | bytes 786440 | tf_op jit(solution)/shard_map/ppermute | solution.py:584
  79.2 11.9 %collective-permute-start.13 = (f32[2,512,128]{2,1,0:T(8,128)}, f32[2,512,128]{2,1,0:T(8,128)}, u32[]{:S(2)}, u32[]{:S(2)}) collective-permute-start(f32[2,512,128]{2,1,0:T(8,128)} %pad_maximum_fusion.5), channel_id=1, source_target_pairs={{0,3},{1,2},{2,1},{3,0},{4,7},{5,6},{6,5},{7,4},{8,11},{9,10},{10,... | collective-permute-start | bytes 1572872 | tf_op jit(solution)/shard_map/ppermute | solution.py:584
  81.0 9.1 %collective-permute-start.15 = (f32[2,256,128]{2,1,0:T(8,128)}, f32[2,256,128]{2,1,0:T(8,128)S(1)}, u32[]{:S(2)}, u32[]{:S(2)}) collective-permute-start(f32[2,256,128]{2,1,0:T(8,128)} %pad_maximum_fusion.8), channel_id=1, source_target_pairs={{0,1},{1,0},{2,3},{3,2},{4,5},{5,4},{6,7},{7,6},{8,9},{9,8},{10,11... | collective-permute-start | bytes 786440 | tf_op jit(solution)/shard_map/ppermute | solution.py:608
  83.5 9.2 %collective-permute-start.14 = (f32[2,512,128]{2,1,0:T(8,128)}, f32[2,512,128]{2,1,0:T(8,128)}, u32[]{:S(2)}, u32[]{:S(2)}) collective-permute-start(f32[2,512,128]{2,1,0:T(8,128)} %pad_maximum_fusion.6), channel_id=1, source_target_pairs={{0,1},{1,0},{2,3},{3,2},{4,5},{5,4},{6,7},{7,6},{8,9},{9,8},{10,11... | collective-permute-start | bytes 1572872 | tf_op jit(solution)/shard_map/ppermute | solution.py:584
  84.6 10.4 %collective-permute-start.16 = (f32[128,1024]{1,0:T(8,128)S(1)}, f32[128,1024]{1,0:T(8,128)}, u32[]{:S(2)}, u32[]{:S(2)}) collective-permute-start(f32[128,1024]{1,0:T(8,128)S(1)} %constant_dynamic-slice_fusion), channel_id=1, source_target_pairs={{0,96},{16,48},{32,64},{48,16},{64,32},{80,112},{96,0},{112,80},{1... | collective-permute-start | bytes 1572872 | tf_op jit(solution)/shard_map/ppermute | solution.py:570
  91.2 8.3 %copy-start.18 = (f32[4,256,128]{2,1,0:T(8,128)}, f32[4,256,128]{2,1,0:T(8,128)S(1)}, u32[]{:S(2)}) copy-start(f32[4,256,128]{2,1,0:T(8,128)S(1)} %pad_maximum_fusion.7) | copy-start | bytes 1572868
  91.2 3.8 %copy-start.17 = (f32[256,1024]{1,0:T(8,128)S(1)}, f32[256,1024]{1,0:T(8,128)}, u32[]{:S(2)}) copy-start(f32[256,1024]{1,0:T(8,128)} %add_add_fusion) | copy-start | bytes 3145732
  96.1 8.5 %collective-permute-start.20 = (f32[128,1024]{1,0:T(8,128)S(1)}, f32[128,1024]{1,0:T(8,128)}, u32[]{:S(2)}, u32[]{:S(2)}) collective-permute-start(f32[128,1024]{1,0:T(8,128)S(1)} %dynamic-slice_add_fusion.1), channel_id=1, source_target_pairs={{0,96},{16,48},{32,64},{48,16},{64,32},{80,112},{96,0},{112,80},{1... | collective-permute-start | bytes 1572872 | tf_op jit(solution)/shard_map/ppermute | solution.py:574
  96.2 16.0 %collective-permute-start.17 = (f32[4,512,128]{2,1,0:T(8,128)S(1)}, f32[4,512,128]{2,1,0:T(8,128)}, u32[]{:S(2)}, u32[]{:S(2)}) collective-permute-start(f32[4,512,128]{2,1,0:T(8,128)S(1)} %pad_maximum_fusion.1.refs_0_), channel_id=1, source_target_pairs={{0,4},{1,5},{2,6},{3,7},{4,0},{5,1},{6,2},{7,3},{8,12},{9,13},{10,... | collective-permute-start | bytes 3145736 | tf_op jit(solution)/shard_map/ppermute | solution.py:584
  96.9 20.3 %collective-permute-start.18 = (f32[4,512,128]{2,1,0:T(8,128)}, f32[4,512,128]{2,1,0:T(8,128)}, u32[]{:S(2)}, u32[]{:S(2)}) collective-permute-start(f32[4,512,128]{2,1,0:T(8,128)} %pad_maximum_fusion.2.refs_4_), channel_id=1, source_target_pairs={{0,12},{1,13},{2,14},{3,15},{4,8},{5,9},{6,10},{7,11},{8,4},{9,5},... | collective-permute-start | bytes 3145736 | tf_op jit(solution)/shard_map/ppermute | solution.py:584
  99.5 11.5 %collective-permute-start.19 = (f32[4,256,128]{2,1,0:T(8,128)S(1)}, f32[4,256,128]{2,1,0:T(8,128)}, u32[]{:S(2)}, u32[]{:S(2)}) collective-permute-start(f32[4,256,128]{2,1,0:T(8,128)S(1)} %pad_maximum_fusion.7), channel_id=1, source_target_pairs={{0,3},{1,2},{2,1},{3,0},{4,7},{5,6},{6,5},{7,4},{8,11},{9,10},{10,... | collective-permute-start | bytes 1572872 | tf_op jit(solution)/shard_map/ppermute | solution.py:608
  99.5 11.5 %copy-start.19 = (f32[4,256,128]{2,1,0:T(8,128)S(1)}, f32[4,256,128]{2,1,0:T(8,128)}, u32[]{:S(2)}) copy-start(f32[4,256,128]{2,1,0:T(8,128)} %copy-done.18) | copy-start | bytes 1572868
  117.2 15.7 %collective-permute-start.23 = (f32[256,1024]{1,0:T(8,128)}, f32[256,1024]{1,0:T(8,128)}, u32[]{:S(2)}, u32[]{:S(2)}) collective-permute-start(f32[256,1024]{1,0:T(8,128)} %pad_maximum_fusion.4), channel_id=1, source_target_pairs={{0,32},{16,112},{32,0},{48,80},{64,96},{80,48},{96,64},{112,16},{1... | collective-permute-start | bytes 3145736 | tf_op jit(solution)/shard_map/ppermute | solution.py:574
  120.0 15.3 %collective-permute-start.21 = (f32[4,512,128]{2,1,0:T(8,128)S(1)}, f32[4,512,128]{2,1,0:T(8,128)}, u32[]{:S(2)}, u32[]{:S(2)}) collective-permute-start(f32[4,512,128]{2,1,0:T(8,128)S(1)} %pad_maximum_fusion.1.refs_0_), channel_id=1, source_target_pairs={{0,12},{1,13},{2,14},{3,15},{4,8},{5,9},{6,10},{7,11},{8,4},{9,5},... | collective-permute-start | bytes 3145736 | tf_op jit(solution)/shard_map/ppermute | solution.py:584
  122.4 14.3 %collective-permute-start.22 = (f32[4,512,128]{2,1,0:T(8,128)}, f32[4,512,128]{2,1,0:T(8,128)}, u32[]{:S(2)}, u32[]{:S(2)}) collective-permute-start(f32[4,512,128]{2,1,0:T(8,128)} %pad_maximum_fusion.2.refs_4_), channel_id=1, source_target_pairs={{0,4},{1,5},{2,6},{3,7},{4,0},{5,1},{6,2},{7,3},{8,12},{9,13},{10,... | collective-permute-start | bytes 3145736 | tf_op jit(solution)/shard_map/ppermute | solution.py:584
  134.7 4.9 %copy-start.16 = (f32[10,128,128]{2,1,0:T(8,128)S(1)}, f32[10,128,128]{2,1,0:T(8,128)}, u32[]{:S(2)}) copy-start(f32[10,128,128]{2,1,0:T(8,128)} %copy-done.15) | copy-start | bytes 1966084
  136.7 23.4 %collective-permute-start.28 = (f32[512,1024]{1,0:T(8,128)S(1)}, f32[512,1024]{1,0:T(8,128)S(1)}, u32[]{:S(2)}, u32[]{:S(2)}) collective-permute-start(f32[512,1024]{1,0:T(8,128)S(1)} %pad_maximum_fusion.own), channel_id=1, source_target_pairs={{0,16},{16,0},{32,48},{48,32},{64,80},{80,64},{96,112},{112,96},{1... | collective-permute-start | bytes 6291464 | tf_op jit(solution)/shard_map/ppermute | solution.py:540
  138.2 12.4 %collective-permute-start.27 = (f32[8,256,128]{2,1,0:T(8,128)S(1)}, f32[8,256,128]{2,1,0:T(8,128)S(1)}, u32[]{:S(2)}, u32[]{:S(2)}) collective-permute-start(f32[8,256,128]{2,1,0:T(8,128)S(1)} %pad_maximum_fusion.3.own), channel_id=1, source_target_pairs={{0,16},{16,0},{32,48},{48,32},{64,80},{80,64},{96,112},{112,96},{1... | collective-permute-start | bytes 3145736 | tf_op jit(solution)/shard_map/ppermute | solution.py:540
  138.2 18.8 %collective-permute-start.24 = (f32[4,512,128]{2,1,0:T(8,128)}, f32[4,512,128]{2,1,0:T(8,128)S(1)}, u32[]{:S(2)}, u32[]{:S(2)}) collective-permute-start(f32[4,512,128]{2,1,0:T(8,128)} %collective-permute-done.17.refs_1_), channel_id=1, source_target_pairs={{0,12},{1,13},{2,14},{3,15},{4,8},{5,9},{6,10},{7,11},{8,4},{9,5},... | collective-permute-start | bytes 3145736 | tf_op jit(solution)/shard_map/ppermute | solution.py:584
  139.6 17.5 %collective-permute-start.25 = (f32[4,512,128]{2,1,0:T(8,128)}, f32[4,512,128]{2,1,0:T(8,128)S(1)}, u32[]{:S(2)}, u32[]{:S(2)}) collective-permute-start(f32[4,512,128]{2,1,0:T(8,128)} %collective-permute-done.18.refs_5_), channel_id=1, source_target_pairs={{0,4},{1,5},{2,6},{3,7},{4,0},{5,1},{6,2},{7,3},{8,12},{9,13},{10,... | collective-permute-start | bytes 3145736 | tf_op jit(solution)/shard_map/ppermute | solution.py:584
  139.6 17.5 %collective-permute-start.26 = (f32[10,128,128]{2,1,0:T(8,128)S(1)}, f32[10,128,128]{2,1,0:T(8,128)S(1)}, u32[]{:S(2)}, u32[]{:S(2)}) collective-permute-start(f32[10,128,128]{2,1,0:T(8,128)S(1)} %copy-done.16), channel_id=1, source_target_pairs={{0,64},{16,80},{32,96},{48,112},{64,0},{80,16},{96,32},{112,48},{1... | collective-permute-start | bytes 1966088 | tf_op jit(solution)/shard_map/ppermute | solution.py:540
  141.1 9.6 %copy-start = (f32[2,512,512]{2,1,0:T(8,128)S(1)}, f32[2,512,512]{2,1,0:T(8,128)}, u32[]{:S(2)}) copy-start(f32[2,512,512]{2,1,0:T(8,128)} %inverses.1) | copy-start | bytes 6291460
  150.6 6.5 %copy-start.14 = (f32[10,128,128]{2,1,0:T(8,128)S(1)}, f32[10,128,128]{2,1,0:T(8,128)}, u32[]{:S(2)}) copy-start(f32[10,128,128]{2,1,0:T(8,128)} %copy-done.13) | copy-start | bytes 1966084
  150.6 7.3 %copy-start.12 = (f32[10,128,128]{2,1,0:T(8,128)S(1)}, f32[10,128,128]{2,1,0:T(8,128)}, u32[]{:S(2)}) copy-start(f32[10,128,128]{2,1,0:T(8,128)} %copy-done.11) | copy-start | bytes 1966084
  157.1 36.4 %collective-permute-start.29 = (f32[10,128,128]{2,1,0:T(8,128)S(1)}, f32[10,128,128]{2,1,0:T(8,128)S(1)}, u32[]{:S(2)}, u32[]{:S(2)}) collective-permute-start(f32[10,128,128]{2,1,0:T(8,128)S(1)} %copy-done.14), channel_id=1, source_target_pairs={{0,64},{16,80},{32,96},{48,112},{64,0},{80,16},{96,32},{112,48},{1... | collective-permute-start | bytes 1966088 | tf_op jit(solution)/shard_map/ppermute | solution.py:540
  157.9 35.6 %collective-permute-start.30 = (f32[10,128,128]{2,1,0:T(8,128)S(1)}, f32[10,128,128]{2,1,0:T(8,128)S(1)}, u32[]{:S(2)}, u32[]{:S(2)}) collective-permute-start(f32[10,128,128]{2,1,0:T(8,128)S(1)} %copy-done.12), channel_id=1, source_target_pairs={{0,64},{16,80},{32,96},{48,112},{64,0},{80,16},{96,32},{112,48},{1... | collective-permute-start | bytes 1966088 | tf_op jit(solution)/shard_map/ppermute | solution.py:540
  160.1 2.6 %copy-start.10 = (f32[2048,128]{1,0:T(8,128)S(1)}, f32[2048,128]{1,0:T(8,128)}, u32[]{:S(2)}) copy-start(f32[2048,128]{1,0:T(8,128)} %copy-done.9) | copy-start | bytes 3145732
  (3 other events, 2.1 us)

commit v3 on v2

--- a/solution.py
+++ b/solution.py
@@ -55,7 +55,7 @@
 
 
 def prepare_kernel(
-    maps, pivots, front, pieces, first, rest_a, rest_b, rest_c, rest_d, panel, own, away, table,
+    maps, pivots, front, pieces, first, rest_a, rest_b, rest_c, rest_d, rest_e, panel, own, away, table,
     sending, kept, total, sem,
 ):
     here_row, here_col = lax.axis_index("row"), lax.axis_index("col")
@@ -73,9 +73,11 @@
         pltpu.make_async_copy(front.at[:, pl.ds(0, BLK)], panel, sem.at[2]),
     ]
     writes = []
-    for j, target in enumerate((rest_a, rest_b, rest_c, rest_d)):
+    targets = (0, 0, rest_a), (1, 0, rest_b), (1, 5, rest_c), (2, 0, rest_d), (3, 0, rest_e)
+    for n, (j, start, target) in enumerate(targets):
         d = j + (j >= place).astype(jnp.int32)
-        writes.append(pltpu.make_async_copy(sending.at[:, :, columns(d)], target, sem.at[3 + j]))
+        source = sending.at[pl.ds(start, target.shape[0]), :, columns(d)]
+        writes.append(pltpu.make_async_copy(source, target, sem.at[3 + n]))
     for copy in reads:
         copy.start()
     for kk in range(16):
@@ -140,12 +142,14 @@
 
 def prepare(maps, pivots, front, pieces):
     column = jax.ShapeDtypeStruct((10, BLK, BLK), F32)
+    half = jax.ShapeDtypeStruct((5, BLK, BLK), F32)
     return pl.pallas_call(
         prepare_kernel,
         out_shape=[
             column,
             column,
-            column,
+            half,
+            half,
             column,
             column,
             jax.ShapeDtypeStruct((2048, BLK), F32),
@@ -154,21 +158,21 @@
             jax.ShapeDtypeStruct((64,), jnp.int32),
         ],
         in_specs=[SMEM, VMEM, HBM, HBM],
-        out_specs=[VMEM, HBM, HBM, HBM, HBM, VMEM, VMEM, VMEM, SMEM],
+        out_specs=[VMEM, HBM, HBM, HBM, HBM, HBM, VMEM, VMEM, VMEM, SMEM],
         scratch_shapes=[
             pltpu.VMEM((10, BLK, 640), F32),
             pltpu.VMEM((10, BLK, BLK), F32),
             pltpu.VMEM((PANEL, BLK), F32),
-            pltpu.SemaphoreType.DMA((7,)),
+            pltpu.SemaphoreType.DMA((8,)),
         ],
         compiler_params=params(24),
         cost_estimate=cost(0, 9 * MIB),
         name="prepare",
-    )(maps, pivots.reshape(8, BLK), in_hbm(front), in_hbm(pieces))
+    )(in_hbm(maps), in_hbm(pivots.reshape(8, BLK)), in_hbm(front), in_hbm(pieces))
 
 
 def pivot_kernel(mine_half, maps, pivots, front, children, *refs):
-    rows, marks, spread, inverse, front_list, child_list, sem, child_sem = refs[-8:]
+    rows, marks, front_list, spread, inverse, child_list, sem, child_sem = refs[-8:]
     rows[...] = jnp.zeros_like(rows)
     marks[...] = refs[0][...] if mine_half else jnp.zeros_like(marks)
     here_row, here_col = lax.axis_index("row"), lax.axis_index("col")
@@ -195,6 +199,7 @@
         return counts[0] + mine.astype(jnp.int32), counts[1] + shared.astype(jnp.int32)
 
     counts = lax.fori_loop(0, PANEL, visit, (jnp.int32(0), jnp.int32(0)), unroll=8)
+    front_list[PANEL] = counts[0]
     mark = jnp.full((1, BLK), half + 1, jnp.int32).astype(F32)
 
     def take_front(n, carry):
@@ -239,13 +244,13 @@
         out_shape=[
             jax.ShapeDtypeStruct((PANEL, 1024), F32),
             jax.ShapeDtypeStruct((2048, BLK), F32),
+            jax.ShapeDtypeStruct((PANEL + 1,), jnp.int32),
         ],
         in_specs=[SMEM, SMEM, HBM, HBM] + [VMEM] * len(before),
-        out_specs=[VMEM, VMEM],
+        out_specs=[VMEM, VMEM, SMEM],
         scratch_shapes=[
             pltpu.VMEM((PANEL, 640), F32),
             pltpu.SMEM((128,), jnp.int32),
-            pltpu.SMEM((PANEL + 1,), jnp.int32),
             pltpu.SMEM((PANEL + 1,), jnp.int32),
             pltpu.SemaphoreType.DMA(()),
             pltpu.SemaphoreType.DMA(()),
@@ -253,7 +258,7 @@
         compiler_params=params(12),
         cost_estimate=cost(0, 24 * MIB),
         name="pivot_terms_mine" if mine_half else "pivot_terms_other",
-    )(maps, pivots, in_hbm(front), in_hbm(children), *before)
+    )(in_hbm(maps), in_hbm(pivots), in_hbm(front), in_hbm(children), *before)
 
 
 def panel_kernel(table, panel, got, top, bottom):
@@ -327,85 +332,103 @@
     )(table, own, swapped, inverses)
 
 
-def upper_kernel(table, own, swapped, cross, high, low):
+def factor_kernel(table, own, swapped, factor_h, factor_l, cross, high, low, patch):
     here_row, col = table[ROW], table[COL]
-    core = here_row % 2
+    core, slot = here_row % 2, col % 4
     inside = lax.broadcasted_iota(jnp.int32, (PANEL, 1024), 1) < BLK
+
+    def mine(x):
+        out = x[:, :BLK]
+        for s in range(1, 4):
+            out = jnp.where(slot == s, x[:, s * BLK : (s + 1) * BLK], out)
+        return out
+
+    def begin_with(block, x):
+        return jnp.concatenate([block, x[:, BLK:]], axis=1)
+
+    def factor(n):
+        return factor_h[n], factor_l[n]
+
+    def factor_columns(n):
+        return mine(factor_h[n].astype(F32)) + mine(factor_l[n].astype(F32))
+
     first = jnp.where(core == 0, own[...], swapped[...])
     first = jnp.where(inside & (col < 4), 0.0, first)
-    terms = split(first)
-    high[:PANEL], low[:PANEL] = terms
     second = jnp.where(core == 0, swapped[...], own[...])
-    second = second - dot3(split(cross[...]), terms)
+    second = second - dot3(split(cross[...]), split(first))
+    patch[...] = begin_with(jnp.where(col < 4, mine(cross[...]), second[:, :BLK]), second)
     second = jnp.where(inside & (col < 8), 0.0, second)
-    high[PANEL:], low[PANEL:] = split(second)
-
-
-def uppers(table, own, swapped, cross):
+    right = dot3(factor(1), split(second))
+    in_second = (col >= 4) & (col < 8)
+    right = begin_with(jnp.where(in_second, factor_columns(1), right[:, :BLK]), right)
+    terms = split(right)
+    high[PANEL:], low[PANEL:] = terms
+    first = jnp.where(inside & (col < 8), 0.0, first)
+    left = dot3(factor(0), split(first - dot3(factor(2), terms)))
+    left = begin_with(jnp.where(col < 4, factor_columns(0), left[:, :BLK]), left)
+    high[:PANEL], low[:PANEL] = split(left)
+
+
+def right_factor(table, own, swapped, factors, cross):
     shape = jax.ShapeDtypeStruct((1024, 1024), BF16)
     return pl.pallas_call(
-        upper_kernel,
-        out_shape=[shape, shape],
-        in_specs=[SMEM, VMEM, VMEM, VMEM],
-        out_specs=[VMEM, VMEM],
-        compiler_params=params(28),
-        cost_estimate=cost(6 * PANEL * PANEL * 1024, 9 * MIB),
-        name="uppers",
-    )(table, own, swapped, cross)
-
-
-def block_at(base, part, t, s):
-    return jnp.maximum(s[base + part // 2 * 8 + 2 * t + part % 2], 0)
-
-
-TILE = pl.BlockSpec((2, 256, 1024), lambda t, s: (0, t, 0))
+        factor_kernel,
+        out_shape=[shape, shape, jax.ShapeDtypeStruct((PANEL, 1024), F32)],
+        in_specs=[SMEM] + [VMEM] * 5,
+        out_specs=[VMEM] * 3,
+        compiler_params=params(34),
+        cost_estimate=cost(4 * 6 * PANEL * PANEL * 1024, 14 * MIB),
+        name="right_factor",
+    )(table, own, swapped, *factors, cross)
+
+
+def block_at(base, half, t, s):
+    return jnp.maximum(s[base + half * 8 + t], 0)
 
 
 def extend_kernel(columns, table, front, *refs):
     out, refs = refs[-1], refs[:-1]
-    kept, *got = (refs[4 * k : 4 * k + 4] for k in range(1 + columns))
+    kept, *got = (refs[2 * k : 2 * k + 2] for k in range(1 + columns))
     step = pl.program_id(0)
     out[...] = front[...]
-    for part in range(4):
-        half, rest = part // 2, part % 2
-        span = slice(rest * BLK, (rest + 1) * BLK)
-        kk = half * 8 + 2 * step + rest
-
-        @pl.when(table[KEPT_AT + kk] >= 0)
-        def _(half=half, span=span, part=part):
+    for half in range(2):
+
+        @pl.when(table[KEPT_AT + half * 8 + step] >= 0)
+        def _(half=half):
             for d in range(5):
                 to = pl.ds(pl.multiple_of(table[KEPT_COL + d] * BLK, BLK), BLK)
-                out[half, span, to] += kept[part][0, 0, :, d * BLK : (d + 1) * BLK]
-
-        @pl.when(table[GOT_AT + kk] >= 0)
-        def _(half=half, span=span, part=part):
+                out[half, :, to] += kept[half][0, 0, :, d * BLK : (d + 1) * BLK]
+
+        @pl.when(table[GOT_AT + half * 8 + step] >= 0)
+        def _(half=half):
             for j in range(columns):
                 to = pl.ds(pl.multiple_of(table[GOT_COL + j] * BLK, BLK), BLK)
-                out[half, span, to] += got[j][part][0]
+                out[half, :, to] += got[j][half][0]
 
 
 def extend(table, front, pieces, got):
-    def kept_at(part):
-        return lambda t, s: (block_at(KEPT_AT, part, t, s), s[SIDE], 0, 0)
-
-    def got_at(part):
-        return lambda t, s: (block_at(GOT_AT, part, t, s), 0, 0)
-
-    kept_specs = [pl.BlockSpec((1, 1, BLK, 640), kept_at(part)) for part in range(4)]
-    got_specs = [pl.BlockSpec((1, BLK, BLK), got_at(part)) for part in range(4)]
+    def kept_at(half):
+        return lambda t, s: (block_at(KEPT_AT, half, t, s), s[SIDE], 0, 0)
+
+    def got_at(half):
+        return lambda t, s: (block_at(GOT_AT, half, t, s), 0, 0)
+
+    tile = pl.BlockSpec((2, BLK, 1024), lambda t, s: (0, t, 0))
+    kept_specs = [pl.BlockSpec((1, 1, BLK, 640), kept_at(half)) for half in range(2)]
+    got_specs = [pl.BlockSpec((1, BLK, BLK), got_at(half)) for half in range(2)]
     return pl.pallas_call(
         functools.partial(extend_kernel, len(got)),
         out_shape=pltpu.HBM((2, 1024, 1024), F32),
         grid_spec=pltpu.PrefetchScalarGridSpec(
             num_scalar_prefetch=1,
-            grid=(4,),
-            in_specs=[TILE, *kept_specs, *got_specs * len(got)],
-            out_specs=TILE,
+            grid=(8,),
+            in_specs=[tile, *kept_specs, *got_specs * len(got)],
+            out_specs=tile,
         ),
         compiler_params=params(20),
         cost_estimate=cost(0, 22 * MIB),
         name="extend",
-    )(table, in_hbm(front.reshape(2, 1024, 1024)), *[in_hbm(pieces)] * 4, *[g for g in got for _ in range(4)])
+    )(table, in_hbm(front.reshape(2, 1024, 1024)), *[in_hbm(pieces)] * 2, *[g for g in got for _ in range(2)])
 
 
 ORDERS = ((1, 3, 4, 12), (3, 1, 12, 4)), ((4, 12, 1, 3), (12, 4, 3, 1))
@@ -413,7 +436,7 @@
 
 def update_kernel(table, front, *refs):
     blocks = refs[:4], refs[4:8]
-    factor_h, factor_l, upper_h, upper_l, marks, out, panels, lower_h, lower_l = refs[8:]
+    right_h, right_l, marks, out, panels = refs[8:]
     step = pl.program_id(0)
     col, core = table[COL], table[ROW] % 2
 
@@ -432,40 +455,31 @@
             block = jnp.where(far, far_block, near_block)
             y, x = c // 4, c % 4
             rows = slice(0, 256) if y < 2 else slice(256, PANEL)
-            panels[min(y, 3 - y), rows, x * BLK : (x + 1) * BLK] = block
+            first = min(y, 3 - y) * PANEL + x * BLK
+            columns = slice(first, first + BLK)
+            panels[0, rows, columns], panels[1, rows, columns] = split(block)
 
     for which in range(2):
         pl.when(step // 2 == which)(functools.partial(assemble, which))
 
-    mark = jnp.concatenate([marks[...].reshape(PANEL, BLK)] * 4, axis=1)
-    lower = dot3(split(panels[0]), (factor_h[0], factor_l[0]))
-    lower = jnp.where(mark != 1, lower, 0.0)
-    terms = split(lower)
-    lower_h[:, :PANEL], lower_l[:, :PANEL] = terms
-    second = panels[1] - dot3(terms, (factor_h[2], factor_l[2]))
-    later = dot3(split(second), (factor_h[1], factor_l[1]))
-    later = jnp.where(mark == 0, later, 0.0)
-    lower_h[:, PANEL:], lower_l[:, PANEL:] = split(later)
-    change = dot3((lower_h[...], lower_l[...]), (upper_h[...], upper_l[...]))
-    out[...] = front[...] - change.reshape(2, 256, 1024)
-
-    @pl.when(col < 8)
-    def _():
-        chosen = jnp.where(col < 4, lower, later)
-        fresh = chosen[:, :BLK]
-        for s in range(1, 4):
-            fresh = jnp.where(col % 4 == s, chosen[:, s * BLK : (s + 1) * BLK], fresh)
-        active = jnp.where(col < 4, (marks[...] != 1).astype(F32), (marks[...] == 0).astype(F32))
-        out[:, :, :BLK] = jnp.where(active > 0, fresh.reshape(2, 256, BLK), out[:, :, :BLK])
-
-
-def update(table, front, blocks, factors, upper, marks):
+    change = dot3((panels[0], panels[1]), (right_h[...], right_l[...])).reshape(2, 256, 1024)
+    active = marks[...] == 0
+    for j in range(8):
+        columns = slice(j * BLK, (j + 1) * BLK)
+        before, part = front[:, :, columns], change[:, :, columns]
+        after = before - part
+        if j == 0:
+            after = jnp.where(col < 8, part, after)
+        out[:, :, columns] = jnp.where(active, after, before)
+
+
+def update(table, front, blocks, right, marks):
     def whole(x):
         return pl.BlockSpec(x.shape, lambda t, s: (0,) * x.ndim, pipeline_mode=pl.Buffered(1))
 
     first = pl.BlockSpec((4, 256, BLK), lambda t, s: (0, jnp.minimum(t, 1), 0))
     second = pl.BlockSpec((4, 256, BLK), lambda t, s: (0, jnp.maximum(t - 2, 0), 0))
-    constants = *factors, *upper
+    tile = pl.BlockSpec((2, 256, 1024), lambda t, s: (0, t, 0))
     return pl.pallas_call(
         update_kernel,
         out_shape=pltpu.HBM((2, 1024, 1024), F32),
@@ -473,66 +487,80 @@
             num_scalar_prefetch=1,
             grid=(4,),
             in_specs=[
-                TILE,
+                tile,
                 *[first] * 4,
                 *[second] * 4,
-                *[whole(x) for x in constants],
+                *[whole(x) for x in right],
                 pl.BlockSpec((2, 256, BLK), lambda t, s: (0, t, 0)),
             ],
-            out_specs=TILE,
-            scratch_shapes=[
-                pltpu.VMEM((2, PANEL, PANEL), F32),
-                pltpu.VMEM((PANEL, 1024), BF16),
-                pltpu.VMEM((PANEL, 1024), BF16),
-            ],
+            out_specs=tile,
+            scratch_shapes=[pltpu.VMEM((2, PANEL, 1024), BF16)],
         ),
         compiler_params=params(34),
-        cost_estimate=cost(6 * 2048 * 1024 * 1024 + 3 * 6 * 2048 * PANEL * PANEL, 36 * MIB),
+        cost_estimate=cost(6 * 2048 * 1024 * 1024, 32 * MIB),
         name="update",
-    )(table, in_hbm(front), *blocks[0], *blocks[1], *constants, marks.reshape(2, 1024, BLK))
-
-
-def finish_kernel(table, front, got_b, got_c, got_d, out, held, read_sem, write_sem):
+    )(table, in_hbm(front), *blocks[0], *blocks[1], *right, marks.reshape(2, 1024, BLK))
+
+
+def finish_kernel(
+    table, list_other, list_mine, front, got_b, got_c, got_d, got_e, patch,
+    out, held, read_sem, write_sem, sem,
+):
     del front
-    got = got_b, got_c, got_d
+    core = table[ROW] % 2
     copies = []
-    for j in range(3):
-        for m in range(10):
-            rows = pl.ds(pl.multiple_of(table[GOT_ROW + m] * BLK, BLK), BLK)
-            columns = pl.ds(pl.multiple_of(table[GOT_COL + 2 + j] * BLK, BLK), BLK)
-            there, here = out.at[rows, columns], held.at[j, m]
-            copies.append(
-                (
-                    pltpu.make_async_copy(there, here, read_sem.at[j, m]),
-                    pltpu.make_async_copy(here, there, write_sem.at[j, m]),
-                )
-            )
-    for read, _ in copies:
+    for n, (column, first, got) in enumerate(
+        [(2, 0, got_b), (2, 5, got_c), (3, 0, got_d), (4, 0, got_e)]
+    ):
+        columns = pl.ds(pl.multiple_of(table[GOT_COL + column] * BLK, BLK), BLK)
+        for m in range(got.shape[0]):
+            rows = pl.ds(pl.multiple_of(table[GOT_ROW + first + m] * BLK, BLK), BLK)
+            there, here = out.at[rows, columns], held.at[n, m]
+            read = pltpu.make_async_copy(there, here, read_sem.at[n, m])
+            write = pltpu.make_async_copy(here, there, write_sem.at[n, m])
+            copies.append((read, write, n, m, got))
+    for read, *_ in copies:
         read.start()
-    for n, (read, write) in enumerate(copies):
+    for read, write, n, m, got in copies:
         read.wait()
-        held[n // 10, n % 10] += got[n // 10][n % 10]
+        held[n, m] += got[m]
         write.start()
-    for _, write in copies:
+    for _, write, *_ in copies:
         write.wait()
 
-
-def finish(table, front, *got):
+    def entry(n):
+        return jnp.where(core == 0, list_other[n], list_mine[n])
+
+    def place(n, carry):
+        at, p = entry(n) >> 9, entry(n) & 511
+        pltpu.make_async_copy(patch.at[pl.ds(p, 1), :], out.at[pl.ds(at, 1), :], sem).start()
+        return carry
+
+    def wait(_, carry):
+        pltpu.make_async_copy(patch.at[pl.ds(0, 1), :], out.at[pl.ds(0, 1), :], sem).wait()
+        return carry
+
+    lax.fori_loop(0, entry(PANEL), place, 0)
+    lax.fori_loop(0, entry(PANEL), wait, 0)
+
+
+def finish(table, lists, front, got, patch):
     return pl.pallas_call(
         finish_kernel,
         out_shape=jax.ShapeDtypeStruct((2048, 1024), F32),
-        in_specs=[SMEM, HBM, VMEM, VMEM, VMEM],
+        in_specs=[SMEM, SMEM, SMEM, HBM] + [VMEM] * 5,
         out_specs=HBM,
         scratch_shapes=[
-            pltpu.VMEM((3, 10, BLK, BLK), F32),
-            pltpu.SemaphoreType.DMA((3, 10)),
-            pltpu.SemaphoreType.DMA((3, 10)),
+            pltpu.VMEM((4, 10, BLK, BLK), F32),
+            pltpu.SemaphoreType.DMA((4, 10)),
+            pltpu.SemaphoreType.DMA((4, 10)),
+            pltpu.SemaphoreType.DMA(()),
         ],
-        input_output_aliases={1: 0},
-        compiler_params=params(8),
-        cost_estimate=cost(0, 6 * MIB),
+        input_output_aliases={3: 0},
+        compiler_params=params(12),
+        cost_estimate=cost(0, 8 * MIB),
         name="finish",
-    )(table, front, *got)
+    )(table, *lists, front, *got, patch)
 
 
 def swap(block, axis, partner):
@@ -540,14 +568,14 @@
     return lax.ppermute(block, axis, [(i, partner(i)) for i in range(count)])
 
 
-def fold(block, here_col):
+def fold(block, near):
     came = lax.ppermute(block[1], "col", [(c, c ^ 12) for c in range(8)])
-    return jnp.where(here_col < 8, block[0], came)
+    return jnp.where(near, block[0], came)
 
 
 def local(front, children, child_maps, pivots, diag_inverses):
     here_row, here_col = lax.axis_index("row"), lax.axis_index("col")
-    chip = here_row // 2
+    chip = here_row >> 1
     together = lax.optimization_barrier
     pieces = children.reshape(10, 2, BLK, 640)
 
@@ -559,21 +587,19 @@
 
     bits = (chip ^ (chip >> 1)) & 1, chip >> 1
     rings = [[(r, r ^ ((2, 6), (6, 2))[r % 2][k]) for r in range(8)] for k in range(2)]
-    bits = [jnp.where(here_row % 2 == 0, bits[k], bits[1 - k]) for k in range(2)]
-
-    def halve(terms, step):
-        size = terms[0].shape[0] // 2
-
-        def half(bit):
-            return sum(lax.dynamic_slice_in_dim(term, bit * size, size, 0) for term in terms)
-
-        came = lax.ppermute(half(1 - bits[step]), "row", rings[step])
-        return half(bits[step]) + came
+    low = [jnp.where(here_row & 1 == 0, bits[k], bits[1 - k]) == 0 for k in range(2)]
+    pivots, near, low = together((pivots, here_col < 8, low))
+
+    def halve(part, step):
+        size = part.shape[0] // 2
+        leave = jnp.where(low[step], part[size:], part[:size])
+        stay = jnp.where(low[step], part[:size], part[size:])
+        return stay + lax.ppermute(leave, "row", rings[step])
 
     def double(part, step):
         came = lax.ppermute(part, "row", rings[step])
-        low, high = jnp.where(bits[step] == 0, part, came), jnp.where(bits[step] == 0, came, part)
-        return jnp.concatenate([low, high], axis=0)
+        first, second = jnp.where(low[step], part, came), jnp.where(low[step], came, part)
+        return jnp.concatenate([first, second], axis=0)
 
     def gather_step(block, which, step):
         route = [
@@ -583,21 +609,22 @@
         ]
         return lax.ppermute(block, ("row", "col"), route)
 
-    first, rest_a, rest_b, rest_c, rest_d, panel, corner, away, table = prepare(
+    first, rest_a, rest_b, rest_c, rest_d, rest_e, panel, corner, away, table = prepare(
         child_maps, pivots, front, pieces
     )
     got0 = by_row(first, 4)
     corner = corner + by_row(away, 1)
-    corner = corner + (by_row(corner, 2) + (by_row(corner, 6) + by_row(corner, 4)))
-    away_rows, marks = pivot_terms(child_maps, pivots, front, children)
+    for k in range(2):
+        corner = corner + lax.ppermute(corner, "row", rings[k])
+    away_rows, marks, list_other = pivot_terms(child_maps, pivots, front, children)
     got0, away_rows, rest_a, marks, corner = together((got0, away_rows, rest_a, marks, corner))
 
     top, bottom = whole_panel(table, panel, got0)
-    mine = fold((top, bottom), here_col)
-    corner = fold((corner, corner), here_col)[None]
+    mine = fold((top, bottom), near)
+    corner = fold((corner, corner), near)[None]
     got_a = by_row(rest_a, 4)
-    own_rows, marks = pivot_terms(child_maps, pivots, front, children, marks)
-    total = own_rows, by_row(away_rows, 1)
+    own_rows, marks, list_mine = pivot_terms(child_maps, pivots, front, children, marks)
+    total = own_rows + by_row(away_rows, 1)
     mine, corner, total, got_a, rest_b = together((mine, corner, total, got_a, rest_b))
 
     def corner_step(block, step):
@@ -612,26 +639,32 @@
         came = [gather_step(held[w], w, k) for w in range(2)]
         held = [jnp.concatenate([h, c], axis=0) for h, c in zip(held, came)]
         corner = corner_step(corner, k)
-        total = halve(total if k == 0 else (total,), k)
-        held, corner, total = together((held, corner, total))
+        total = halve(total, k)
+        if k == 0:
+            held, corner, total, rest_b = together((held, corner, total, rest_b))
+            got_b = by_row(rest_b, 4)
+        else:
+            held, corner, total, got_b, rest_c = together((held, corner, total, got_b, rest_c))
     came = [gather_step(held[w], w, 2) for w in range(2)]
     corner = corner_step(corner, 2)
     total = double(total, 1)
-    came, corner, total = together((came, corner, total))
+    got_c = by_row(rest_c, 4)
+    came, corner, total, got_c = together((came, corner, total, got_c))
     held_far = [gather_step(held[w], w, 3) for w in range(2)]
-    factors = corners(table, corner, by_row(corner, 1), diag_inverses)
+    *factors, cross = corners(table, corner, by_row(corner, 1), diag_inverses)
     total = double(total, 0)
-    came, held_far, total, rest_b = together((came, held_far, total, rest_b))
+    front = extend(table, front, pieces, (got0, got_a))
+    came, held_far, total, rest_d, factors, cross, front = together(
+        (came, held_far, total, rest_d, factors, cross, front)
+    )
     came_far = [gather_step(came[w], w, 3) for w in range(2)]
-    got_b = by_row(rest_b, 4)
-    upper = uppers(table, total, by_row(total, 1), factors[2])
-    front = extend(table, front, pieces, (got0, got_a))
-    came_far, got_b, rest_c, rest_d = together((came_far, got_b, rest_c, rest_d))
-    got_c = by_row(rest_c, 4)
     got_d = by_row(rest_d, 4)
+    *right, patch = right_factor(table, total, by_row(total, 1), factors, cross)
+    came_far, got_d, rest_e, right, patch = together((came_far, got_d, rest_e, right, patch))
+    got_e = by_row(rest_e, 4)
     blocks = [(held[w], came[w], held_far[w], came_far[w]) for w in range(2)]
-    front = update(table, front, blocks, factors[:2], upper, marks)
-    return finish(table, front.reshape(2048, 1024), got_b, got_c, got_d)
+    front = update(table, front, blocks, right, marks).reshape(2048, 1024)
+    return finish(table, (list_other, list_mine), front, (got_b, got_c, got_d, got_e), patch)
 
 
 def solution(mesh):

time: 198 us -> 182 us (0.919)
  other arithmetic: 22.7 us -> 1.93 us
  waiting for transfers between devices: 48.6 us -> 68.3 us
  starting transfers between devices: 45.5 us -> 39 us
  local copies, waits for them, and re-layouts: 6.3 us -> 0.04 us
  Pallas kernels: 73.3 us -> 70.1 us
    ppermute x2 -> x4, waiting for transfers between devices: 0.01 us -> 17.9 us  [the longest x2 13.9 us: local(): corner = corner + lax.ppermute(corner, 'row', rings[k])]
    ppermute x12 -> x10, waiting for transfers between devices: 13.1 us -> 23.8 us  [swap(): return lax.ppermute(block, axis, [(i, partner(i)) for i in range(count)])]
    pallas_call x1, Pallas kernels: 30.7 us -> 20.4 us  [update(): pl.pallas_call(update_kernel, out_shape=pltpu.HBM((2, 1024, 1024), F32),...]
    ppermute x2, waiting for transfers between devices: 15.5 us -> 5.75 us  [double(): came = lax.ppermute(part, 'row', rings[step])]
    ppermute x10, starting transfers between devices: 10.8 us -> 2.87 us  [gather_step(): return lax.ppermute(block, ('row', 'col'), route)]
    ppermute x10, waiting for transfers between devices: 6.78 us -> 14 us  [gather_step(): return lax.ppermute(block, ('row', 'col'), route)]
    concatenate x4, other arithmetic: 7.46 us -> 0.21 us  [local(): held = [jnp.concatenate([h, c], axis=0) for h, c in zip(held, came)]]
    ppermute x3, waiting for transfers between devices: 13.2 us -> 6.69 us  [corner_step(): lax.ppermute(block, ('row', 'col'), route)]
  transfers between devices with their start and end apart: 31 -> 31, of which waited for: 13 -> 22; matrix products, arithmetic and copies ran while one was open for 9% -> 1% of each run, Pallas kernels for 33% -> 34%
where the time goes in v3:
time: 182 us; the launch traced here: 180 us
  Pallas kernels  70.1 us (39%)
  waiting for transfers between devices  68.3 us (38%)
  starting transfers between devices  39 us (21%)
  other arithmetic  1.93 us (1%)
    ppermute x10, waiting for transfers between devices, swap(): return lax.ppermute(block, axis, [(i, partner(i)) for i in range(count)])  23.8 us
    pallas_call x1, Pallas kernels, update(): pl.pallas_call(update_kernel, out_shape=pltpu.HBM((2, 1024, 1024), F32),...  20.4 us
    ppermute x10, starting transfers between devices, swap(): return lax.ppermute(block, axis, [(i, partner(i)) for i in range(count)])  18.9 us
    pallas_call x2, Pallas kernels, pivot_terms(): pl.pallas_call(functools.partial(pivot_kernel, mine_half), out_shape=[jax...  18.3 us
    ppermute x10, waiting for transfers between devices, gather_step(): return lax.ppermute(block, ('row', 'col'), route)  14 us
    ppermute x2, waiting for transfers between devices, local(): corner = corner + lax.ppermute(corner, 'row', rings[k])  13.9 us
    pallas_call x1, Pallas kernels, extend(): pl.pallas_call(functools.partial(extend_kernel, len(got)), out_shape=pltp...  10.9 us
    pallas_call x1, Pallas kernels, right_factor(): pl.pallas_call(factor_kernel, out_shape=[shape, shape, jax.ShapeDtypeStru...  7.95 us
  transfers between devices with their start and end apart: 31, of which 22 were waited for; matrix products, arithmetic and copies ran while one was open for 1% of the time, Pallas kernels for 34%

profile of v3, /device:TPU:1, one launch (start us, length us, event | category | flops | bytes accessed | tf_op | source)
XLA Modules:
  0.0 179.8 jit_solution(15111897075295799128)
XLA Ops:
  0.0 5.1 %prepare.1 = (f32[10,128,128]{2,1,0:T(8,128)S(1)}, f32[10,128,128]{2,1,0:T(8,128)S(1)}, f32[5,128,128]{2,1,0:T(8,128)S(1)}, f32[5,128,128]{2,1,0:T(8,128)S(1)}, ...) custom-call(s32[2,80]{1,0:T(2,128)} %maps.5, ...), custom_call_target="tpu_custom_call" | custom-call | bytes 9437184 | tf_op jit(solution)/shard_map/prepare/pallas_call | solution.py:146
  5.1 4.5 %collective-permute-start = (f32[10,128,128]{2,1,0:T(8,128)S(1)}, f32[10,128,128]{2,1,0:T(8,128)S(1)}, u32[]{:S(2)}, u32[]{:S(2)}) collective-permute-start(f32[10,128,128]{2,1,0:T(8,128)S(1)} %get-tuple-element.79), channel_id=1, source_target_pairs={{0,64},{16,80},{32,96},{48,112},{64,0},{80,16},{96,32},{112,48},{1... | collective-permute-start | bytes 1966088 | tf_op jit(solution)/shard_map/ppermute | solution.py:568
  9.6 1.0 collective-permute-start.1
  10.6 1.0 collective-permute-done.1
  11.6 0.5 collective-permute-start.2
  12.1 13.9 %collective-permute-done.2 = f32[256,128]{1,0:T(8,128)S(1)} collective-permute-done((f32[256,128]{1,0:T(8,128)S(1)}, f32[256,128]{1,0:T(8,128)S(1)}, u32[]{:S(2)}, u32[]{:S(2)}) %collective-permute-start.2) | collective-permute-done | bytes 131104 | tf_op jit(solution)/shard_map/ppermute | solution.py:618
  26.0 1.4 collective-permute-start.3
  27.4 9.1 %pivot_terms_other.1 = (f32[512,1024]{1,0:T(8,128)S(1)}, f32[2048,128]{1,0:T(8,128)S(1)}, s32[513]{0:T(1024)S(1)}) custom-call(s32[2,80]{1,0:T(2,128)} %maps.5, s32[1024]{0:T(1024)} %pivots.1, f32[2048,1024]{1,0:T(8,128)} %front.5, f32[2560,640]{1,0:T(8,128)} %children.3), custom_call_target="tpu_custom_call" | custom-call | bytes 25165824 | tf_op jit(solution)/shard_map/pivot_terms_other/pallas_call | solution.py:242
  36.9 0.8 whole_panel.1
  37.7 4.4 %collective-permute-start.4 = (f32[1024,128]{1,0:T(8,128)S(1)}, f32[1024,128]{1,0:T(8,128)S(1)}, u32[]{:S(2)}, u32[]{:S(2)}) collective-permute-start(f32[1024,128]{1,0:T(8,128)S(1)} %get-tuple-element.91), channel_id=1, source_target_pairs={{0,12},{1,13},{2,14},{3,15},{4,8},{5,9},{6,10},{7,11},{16,28},{17,... | collective-permute-start | bytes 1572872 | tf_op jit(solution)/shard_map/ppermute | solution.py:572
  42.1 3.1 %collective-permute-start.7 = (f32[10,128,128]{2,1,0:T(8,128)S(1)}, f32[10,128,128]{2,1,0:T(8,128)S(1)}, u32[]{:S(2)}, u32[]{:S(2)}) collective-permute-start(f32[10,128,128]{2,1,0:T(8,128)S(1)} %get-tuple-element.95), channel_id=1, source_target_pairs={{0,64},{16,80},{32,96},{48,112},{64,0},{80,16},{96,32},{112,48},{1... | collective-permute-start | bytes 1966088 | tf_op jit(solution)/shard_map/ppermute | solution.py:568
  45.3 1.3 collective-permute-start.5
  46.6 9.2 %pivot_terms_mine.1 = (f32[512,1024]{1,0:T(8,128)S(1)}, f32[2048,128]{1,0:T(8,128)S(1)}, s32[513]{0:T(1024)S(1)}) custom-call(s32[2,80]{1,0:T(2,128)} %maps.5, s32[1024]{0:T(1024)} %pivots.1, f32[2048,1024]{1,0:T(8,128)} %front.5, f32[2560,640]{1,0:T(8,128)} %children.3, f32[2048,128]{1,0:T(8,128)S(1)} %get-tuple-element.85.refs_0_), custom_call_target="tpu_custom_call" | custom-call | bytes 25165824 | tf_op jit(solution)/shard_map/pivot_terms_mine/pallas_call | solution.py:242
  56.4 3.2 %collective-permute-done.7.refs_4_.refs_5_ = f32[10,128,128]{2,1,0:T(8,128)S(1)} collective-permute-done((f32[10,128,128]{2,1,0:T(8,128)S(1)}, f32[10,128,128]{2,1,0:T(8,128)S(1)}, u32[]{:S(2)}, u32[]{:S(2)}) %collective-permute-start.7) | collective-permute-done | bytes 655392 | tf_op jit(solution)/shard_map/ppermute | solution.py:568
  59.8 3.5 %collective-permute-start.11 = (f32[256,1024]{1,0:T(8,128)S(1)}, f32[256,1024]{1,0:T(8,128)S(1)}, u32[]{:S(2)}, u32[]{:S(2)}) collective-permute-start(f32[256,1024]{1,0:T(8,128)S(1)} %slice_select_fusion), channel_id=1, source_target_pairs={{0,32},{16,112},{32,0},{48,80},{64,96},{80,48},{96,64},{112,16},{1... | collective-permute-start | bytes 3145736 | tf_op jit(solution)/shard_map/ppermute | solution.py:597
  63.3 0.5 collective-permute-start.9
  63.8 1.1 collective-permute-start.10
  64.9 3.0 %collective-permute-done.10 = f32[1,256,128]{2,1,0:T(8,128)S(1)} collective-permute-done((f32[1,256,128]{2,1,0:T(8,128)S(1)}, f32[1,256,128]{2,1,0:T(8,128)S(1)}, u32[]{:S(2)}, u32[]{:S(2)}) %collective-permute-start.10) | collective-permute-done | bytes 131104 | tf_op jit(solution)/shard_map/ppermute | solution.py:635
  67.9 1.9 %collective-permute-done.9 = f32[1,512,128]{2,1,0:T(8,128)S(1)} collective-permute-done((f32[1,512,128]{2,1,0:T(8,128)S(1)}, f32[1,512,128]{2,1,0:T(8,128)S(1)}, u32[]{:S(2)}, u32[]{:S(2)}) %collective-permute-start.9) | collective-permute-done | bytes 262176 | tf_op jit(solution)/shard_map/ppermute | solution.py:610
  69.8 2.0 %collective-permute-done.8 = f32[1,512,128]{2,1,0:T(8,128)S(1)} collective-permute-done((f32[1,512,128]{2,1,0:T(8,128)S(1)}, f32[1,512,128]{2,1,0:T(8,128)S(1)}, u32[]{:S(2)}, u32[]{:S(2)}) %collective-permute-start.8) | collective-permute-done | bytes 262176 | tf_op jit(solution)/shard_map/ppermute | solution.py:610
  71.9 3.6 %collective-permute-done.11 = f32[256,1024]{1,0:T(8,128)S(1)} collective-permute-done((f32[256,1024]{1,0:T(8,128)S(1)}, f32[256,1024]{1,0:T(8,128)S(1)}, u32[]{:S(2)}, u32[]{:S(2)}) %collective-permute-start.11) | collective-permute-done | bytes 1048608 | tf_op jit(solution)/shard_map/ppermute | solution.py:597
  76.2 2.4 %collective-permute-start.14 = (f32[2,256,128]{2,1,0:T(8,128)S(1)}, f32[2,256,128]{2,1,0:T(8,128)S(1)}, u32[]{:S(2)}, u32[]{:S(2)}) collective-permute-start(f32[2,256,128]{2,1,0:T(8,128)S(1)} %pad_maximum_fusion.8), channel_id=1, source_target_pairs={{0,1},{1,0},{2,3},{3,2},{4,5},{5,4},{6,7},{7,6},{8,9},{9,8},{10,11... | collective-permute-start | bytes 786440 | tf_op jit(solution)/shard_map/ppermute | solution.py:635
  78.8 3.8 %collective-permute-start.16 = (f32[5,128,128]{2,1,0:T(8,128)S(1)}, f32[5,128,128]{2,1,0:T(8,128)S(1)}, u32[]{:S(2)}, u32[]{:S(2)}) collective-permute-start(f32[5,128,128]{2,1,0:T(8,128)S(1)} %get-tuple-element.107), channel_id=1, source_target_pairs={{0,64},{16,80},{32,96},{48,112},{64,0},{80,16},{96,32},{112,48},{1... | collective-permute-start | bytes 983048 | tf_op jit(solution)/shard_map/ppermute | solution.py:568
  82.6 2.6 %collective-permute-done.14 = f32[2,256,128]{2,1,0:T(8,128)S(1)} collective-permute-done((f32[2,256,128]{2,1,0:T(8,128)S(1)}, f32[2,256,128]{2,1,0:T(8,128)S(1)}, u32[]{:S(2)}, u32[]{:S(2)}) %collective-permute-start.14) | collective-permute-done | bytes 262176 | tf_op jit(solution)/shard_map/ppermute | solution.py:635
  85.4 1.5 collective-permute-done.13
  87.4 9.0 %collective-permute-done.16.got_b = f32[5,128,128]{2,1,0:T(8,128)S(1)} collective-permute-done((f32[5,128,128]{2,1,0:T(8,128)S(1)}, f32[5,128,128]{2,1,0:T(8,128)S(1)}, u32[]{:S(2)}, u32[]{:S(2)}) %collective-permute-start.16) | collective-permute-done | bytes 327712 | tf_op jit(solution)/shard_map/ppermute | solution.py:568
  96.5 0.8 collective-permute-start.18
  97.2 1.3 collective-permute-start.19
  98.6 1.2 collective-permute-start.21
  99.7 5.0 %collective-permute-done.20 = f32[128,1024]{1,0:T(8,128)S(1)} collective-permute-done((f32[128,1024]{1,0:T(8,128)S(1)}, f32[128,1024]{1,0:T(8,128)S(1)}, u32[]{:S(2)}, u32[]{:S(2)}) %collective-permute-start.20) | collective-permute-done | bytes 524320 | tf_op jit(solution)/shard_map/ppermute | solution.py:600
  104.9 1.1 collective-permute-done.19
  106.1 2.1 %collective-permute-done.21.got_c = f32[5,128,128]{2,1,0:T(8,128)S(1)} collective-permute-done((f32[5,128,128]{2,1,0:T(8,128)S(1)}, f32[5,128,128]{2,1,0:T(8,128)S(1)}, u32[]{:S(2)}, u32[]{:S(2)}) %collective-permute-start.21) | collective-permute-done | bytes 327712 | tf_op jit(solution)/shard_map/ppermute | solution.py:568
  108.2 2.2 %collective-permute-done.17.refs_1_ = f32[4,512,128]{2,1,0:T(8,128)S(1)} collective-permute-done((f32[4,512,128]{2,1,0:T(8,128)S(1)}, f32[4,512,128]{2,1,0:T(8,128)S(1)}, u32[]{:S(2)}, u32[]{:S(2)}) %collective-permute-start.17) | collective-permute-done | bytes 1048608 | tf_op jit(solution)/shard_map/ppermute | solution.py:610
  110.4 5.6 %collective-permute-done.18.refs_5_ = f32[4,512,128]{2,1,0:T(8,128)S(1)} collective-permute-done((f32[4,512,128]{2,1,0:T(8,128)S(1)}, f32[4,512,128]{2,1,0:T(8,128)S(1)}, u32[]{:S(2)}, u32[]{:S(2)}) %collective-permute-start.18) | collective-permute-done | bytes 1048608 | tf_op jit(solution)/shard_map/ppermute | solution.py:610
  116.0 2.5 %collective-permute-start.25 = (f32[8,256,128]{2,1,0:T(8,128)S(1)}, f32[8,256,128]{2,1,0:T(8,128)S(1)}, u32[]{:S(2)}, u32[]{:S(2)}) collective-permute-start(f32[8,256,128]{2,1,0:T(8,128)S(1)} %pad_maximum_fusion.3.own), channel_id=1, source_target_pairs={{0,16},{16,0},{32,48},{48,32},{64,80},{80,64},{96,112},{112,96},{1... | collective-permute-start | bytes 3145736 | tf_op jit(solution)/shard_map/ppermute | solution.py:568
  118.6 1.2 collective-permute-start.24
  120.0 10.9 %extend.1.front = f32[2,1024,1024]{2,1,0:T(8,128)} custom-call(s32[64]{0:T(128)S(1)} %get-tuple-element.77.table, f32[2,1024,1024]{2,1,0:T(8,128)} %bitcast.15, f32[10,2,128,640]{3,2,1,0:T(8,128)} %bitcast.13, f32[10,2,128,640]{3,2,1,0:T(8,128)} %bitcast.14, f32[10,128,128]{2,1,0:T(8,128)S(1)} %collective-permute-done.got.refs_2_.refs_3_, ...), custom_call_target="tpu_custom_call" | custom-call | bytes 23068672 | tf_op jit(solution)/shard_map/extend/pallas_call | solution.py:419
  131.0 2.0 %corners.1 = (bf16[3,512,512]{2,1,0:T(8,128)(2,1)S(1)}, bf16[3,512,512]{2,1,0:T(8,128)(2,1)S(1)}, f32[512,512]{1,0:T(8,128)S(1)}) custom-call(s32[64]{0:T(128)S(1)} %get-tuple-element.77.table, f32[8,256,128]{2,1,0:T(8,128)S(1)} %pad_maximum_fusion.3.own, f32[8,256,128]{2,1,0:T(8,128)S(1)} %collective-permute-done.25.swapped, f32[2,512,512]{2,1,0:T(8,128)S(1)} %copy-done), custom_call_target="tpu_custom_call" | custom-call | flops 805306368 | bytes 8388608 | tf_op jit(solution)/shard_map/corners/pallas_call | solution.py:320
  133.0 0.7 collective-permute-done.24
  134.1 0.7 collective-permute-done.22.refs_2_
  134.8 1.6 collective-permute-start.29
  136.4 0.8 collective-permute-start.26
  137.2 0.8 collective-permute-start.28
  138.0 2.2 %collective-permute-done.29.swapped = f32[512,1024]{1,0:T(8,128)S(1)} collective-permute-done((f32[512,1024]{1,0:T(8,128)S(1)}, f32[512,1024]{1,0:T(8,128)S(1)}, u32[]{:S(2)}, u32[]{:S(2)}) %collective-permute-start.29) | collective-permute-done | bytes 2097184 | tf_op jit(solution)/shard_map/ppermute | solution.py:568
  140.2 8.0 %right_factor.1 = (bf16[1024,1024]{1,0:T(8,128)(2,1)S(1)}, bf16[1024,1024]{1,0:T(8,128)(2,1)S(1)}, f32[512,1024]{1,0:T(8,128)S(1)}) custom-call(s32[64]{0:T(128)S(1)} %get-tuple-element.77.table, f32[512,1024]{1,0:T(8,128)S(1)} %pad_maximum_fusion.own, f32[512,1024]{1,0:T(8,128)S(1)} %collective-permute-done.29.swapped, ...), custom_call_target="tpu_custom_call" | custom-call | flops 6442450944 | bytes 14680064 | tf_op jit(solution)/shard_map/right_factor/pallas_call | solution.py:374
  148.2 6.3 %collective-permute-done.28.got_d = f32[10,128,128]{2,1,0:T(8,128)S(1)} collective-permute-done((f32[10,128,128]{2,1,0:T(8,128)S(1)}, f32[10,128,128]{2,1,0:T(8,128)S(1)}, u32[]{:S(2)}, u32[]{:S(2)}) %collective-permute-start.28) | collective-permute-done | bytes 655392 | tf_op jit(solution)/shard_map/ppermute | solution.py:568
  154.5 20.4 %update.1 = f32[2,1024,1024]{2,1,0:T(8,128)} custom-call(s32[64]{0:T(128)S(1)} %get-tuple-element.77.table, f32[2,1024,1024]{2,1,0:T(8,128)} %extend.1.front, f32[4,512,128]{2,1,0:T(8,128)S(1)} %pad_maximum_fusion.1.refs_0_, f32[4,512,128]{2,1,0:T(8,128)S(1)} %collective-permute-done.17.refs_1_, f32[4,512,128]{2,1,0:T(8,128)S(1)} %collective-permute-done.22.refs_2_, ...), custom_call_target="tpu_custom_call" | custom-call | flops 12884901888 | bytes 33554432 | tf_op jit(solution)/shard_map/update/pallas_call | solution.py:483
  174.9 4.7 %finish.1 = f32[2048,1024]{1,0:T(8,128)} custom-call(s32[64]{0:T(128)S(1)} %get-tuple-element.77.table, s32[513]{0:T(1024)S(1)} %get-tuple-element.78.list_other, s32[513]{0:T(1024)S(1)} %get-tuple-element.86.list_mine, f32[2048,1024]{1,0:T(8,128)} %bitcast.16, f32[5,128,128]{2,1,0:T(8,128)S(1)} %collective-permute-done.16.got_b, ...), custom_call_target="tpu_custom_call", output_to_operand_aliasing={{}: (3, {})} | custom-call | bytes 8388608 | tf_op jit(solution)/shard_map/finish/pallas_call | solution.py:548
  (47 shorter events, 3.9 us)
Async XLA Ops:
  5.1 31.5 %collective-permute-start = (f32[10,128,128]{2,1,0:T(8,128)S(1)}, f32[10,128,128]{2,1,0:T(8,128)S(1)}, u32[]{:S(2)}, u32[]{:S(2)}) collective-permute-start(f32[10,128,128]{2,1,0:T(8,128)S(1)} %get-tuple-element.79), channel_id=1, source_target_pairs={{0,64},{16,80},{32,96},{48,112},{64,0},{80,16},{96,32},{112,48},{1... | collective-permute-start | bytes 1966088 | tf_op jit(solution)/shard_map/ppermute | solution.py:568
  9.6 1.9 %collective-permute-start.1 = (f32[256,128]{1,0:T(8,128)S(1)}, f32[256,128]{1,0:T(8,128)S(1)}, u32[]{:S(2)}, u32[]{:S(2)}) collective-permute-start(f32[256,128]{1,0:T(8,128)S(1)} %get-tuple-element.84), channel_id=1, source_target_pairs={{0,16},{16,0},{32,48},{48,32},{64,80},{80,64},{96,112},{112,96},{1... | collective-permute-start | bytes 393224 | tf_op jit(solution)/shard_map/ppermute | solution.py:568
  11.6 14.5 %collective-permute-start.2 = (f32[256,128]{1,0:T(8,128)S(1)}, f32[256,128]{1,0:T(8,128)S(1)}, u32[]{:S(2)}, u32[]{:S(2)}) collective-permute-start(f32[256,128]{1,0:T(8,128)S(1)} %add.18), channel_id=1, source_target_pairs={{0,32},{16,112},{32,0},{48,80},{64,96},{80,48},{96,64},{112,16},{1... | collective-permute-start | bytes 393224 | tf_op jit(solution)/shard_map/ppermute | solution.py:618
  26.0 10.5 %collective-permute-start.3 = (f32[256,128]{1,0:T(8,128)S(1)}, f32[256,128]{1,0:T(8,128)S(1)}, u32[]{:S(2)}, u32[]{:S(2)}) collective-permute-start(f32[256,128]{1,0:T(8,128)S(1)} %add.19), channel_id=1, source_target_pairs={{0,96},{16,48},{32,64},{48,16},{64,32},{80,112},{96,0},{112,80},{1... | collective-permute-start | bytes 393224 | tf_op jit(solution)/shard_map/ppermute | solution.py:618
  36.6 19.4 %collective-permute-start.6 = (f32[512,1024]{1,0:T(8,128)S(1)}, f32[512,1024]{1,0:T(8,128)S(1)}, u32[]{:S(2)}, u32[]{:S(2)}) collective-permute-start(f32[512,1024]{1,0:T(8,128)S(1)} %get-tuple-element.94), channel_id=1, source_target_pairs={{0,16},{16,0},{32,48},{48,32},{64,80},{80,64},{96,112},{112,96},{1... | collective-permute-start | bytes 6291464 | tf_op jit(solution)/shard_map/ppermute | solution.py:568
  37.7 18.2 %collective-permute-start.4 = (f32[1024,128]{1,0:T(8,128)S(1)}, f32[1024,128]{1,0:T(8,128)S(1)}, u32[]{:S(2)}, u32[]{:S(2)}) collective-permute-start(f32[1024,128]{1,0:T(8,128)S(1)} %get-tuple-element.91), channel_id=1, source_target_pairs={{0,12},{1,13},{2,14},{3,15},{4,8},{5,9},{6,10},{7,11},{16,28},{17,... | collective-permute-start | bytes 1572872 | tf_op jit(solution)/shard_map/ppermute | solution.py:572
  42.1 17.5 %collective-permute-start.7 = (f32[10,128,128]{2,1,0:T(8,128)S(1)}, f32[10,128,128]{2,1,0:T(8,128)S(1)}, u32[]{:S(2)}, u32[]{:S(2)}) collective-permute-start(f32[10,128,128]{2,1,0:T(8,128)S(1)} %get-tuple-element.95), channel_id=1, source_target_pairs={{0,64},{16,80},{32,96},{48,112},{64,0},{80,16},{96,32},{112,48},{1... | collective-permute-start | bytes 1966088 | tf_op jit(solution)/shard_map/ppermute | solution.py:568
  45.3 10.6 %collective-permute-start.5 = (f32[256,128]{1,0:T(8,128)S(1)}, f32[256,128]{1,0:T(8,128)S(1)}, u32[]{:S(2)}, u32[]{:S(2)}) collective-permute-start(f32[256,128]{1,0:T(8,128)S(1)} %add.20), channel_id=1, source_target_pairs={{0,12},{1,13},{2,14},{3,15},{4,8},{5,9},{6,10},{7,11},{16,28},{17,... | collective-permute-start | bytes 393224 | tf_op jit(solution)/shard_map/ppermute | solution.py:572
  59.8 15.6 %collective-permute-start.11 = (f32[256,1024]{1,0:T(8,128)S(1)}, f32[256,1024]{1,0:T(8,128)S(1)}, u32[]{:S(2)}, u32[]{:S(2)}) collective-permute-start(f32[256,1024]{1,0:T(8,128)S(1)} %slice_select_fusion), channel_id=1, source_target_pairs={{0,32},{16,112},{32,0},{48,80},{64,96},{80,48},{96,64},{112,16},{1... | collective-permute-start | bytes 3145736 | tf_op jit(solution)/shard_map/ppermute | solution.py:597
  63.3 6.5 %collective-permute-start.9 = (f32[1,512,128]{2,1,0:T(8,128)S(1)}, f32[1,512,128]{2,1,0:T(8,128)S(1)}, u32[]{:S(2)}, u32[]{:S(2)}) collective-permute-start(f32[1,512,128]{2,1,0:T(8,128)S(1)} %get-tuple-element.151), channel_id=1, source_target_pairs={{0,3},{1,2},{2,1},{3,0},{4,7},{5,6},{6,5},{7,4},{8,11},{9,10},{10,... | collective-permute-start | bytes 786440 | tf_op jit(solution)/shard_map/ppermute | solution.py:610
  63.8 4.1 %collective-permute-start.10 = (f32[1,256,128]{2,1,0:T(8,128)S(1)}, f32[1,256,128]{2,1,0:T(8,128)S(1)}, u32[]{:S(2)}, u32[]{:S(2)}) collective-permute-start(f32[1,256,128]{2,1,0:T(8,128)S(1)} %select_bitcast_fusion), channel_id=1, source_target_pairs={{0,4},{1,5},{2,6},{3,7},{4,0},{5,1},{6,2},{7,3},{8,12},{9,13},{10,... | collective-permute-start | bytes 393224 | tf_op jit(solution)/shard_map/ppermute | solution.py:635
  64.9 6.9 %collective-permute-start.8 = (f32[1,512,128]{2,1,0:T(8,128)S(1)}, f32[1,512,128]{2,1,0:T(8,128)S(1)}, u32[]{:S(2)}, u32[]{:S(2)}) collective-permute-start(f32[1,512,128]{2,1,0:T(8,128)S(1)} %get-tuple-element.152), channel_id=1, source_target_pairs={{0,1},{1,0},{2,3},{3,2},{4,5},{5,4},{6,7},{7,6},{8,9},{9,8},{10,11... | collective-permute-start | bytes 786440 | tf_op jit(solution)/shard_map/ppermute | solution.py:610
  75.7 9.6 %collective-permute-start.12 = (f32[2,512,128]{2,1,0:T(8,128)S(1)}, f32[2,512,128]{2,1,0:T(8,128)S(1)}, u32[]{:S(2)}, u32[]{:S(2)}) collective-permute-start(f32[2,512,128]{2,1,0:T(8,128)S(1)} %pad_maximum_fusion.5), channel_id=1, source_target_pairs={{0,3},{1,2},{2,1},{3,0},{4,7},{5,6},{6,5},{7,4},{8,11},{9,10},{10,... | collective-permute-start | bytes 1572872 | tf_op jit(solution)/shard_map/ppermute | solution.py:610
  76.2 9.0 %collective-permute-start.14 = (f32[2,256,128]{2,1,0:T(8,128)S(1)}, f32[2,256,128]{2,1,0:T(8,128)S(1)}, u32[]{:S(2)}, u32[]{:S(2)}) collective-permute-start(f32[2,256,128]{2,1,0:T(8,128)S(1)} %pad_maximum_fusion.8), channel_id=1, source_target_pairs={{0,1},{1,0},{2,3},{3,2},{4,5},{5,4},{6,7},{7,6},{8,9},{9,8},{10,11... | collective-permute-start | bytes 786440 | tf_op jit(solution)/shard_map/ppermute | solution.py:635
  78.6 8.3 %collective-permute-start.13 = (f32[2,512,128]{2,1,0:T(8,128)S(1)}, f32[2,512,128]{2,1,0:T(8,128)S(1)}, u32[]{:S(2)}, u32[]{:S(2)}) collective-permute-start(f32[2,512,128]{2,1,0:T(8,128)S(1)} %pad_maximum_fusion.6), channel_id=1, source_target_pairs={{0,1},{1,0},{2,3},{3,2},{4,5},{5,4},{6,7},{7,6},{8,9},{9,8},{10,11... | collective-permute-start | bytes 1572872 | tf_op jit(solution)/shard_map/ppermute | solution.py:610
  78.7 8.7 %collective-permute-start.15 = (f32[128,1024]{1,0:T(8,128)S(1)}, f32[128,1024]{1,0:T(8,128)S(1)}, u32[]{:S(2)}, u32[]{:S(2)}) collective-permute-start(f32[128,1024]{1,0:T(8,128)S(1)} %slice_select_fusion.1), channel_id=1, source_target_pairs={{0,96},{16,48},{32,64},{48,16},{64,32},{80,112},{96,0},{112,80},{1... | collective-permute-start | bytes 1572872 | tf_op jit(solution)/shard_map/ppermute | solution.py:597
  78.8 17.7 %collective-permute-start.16 = (f32[5,128,128]{2,1,0:T(8,128)S(1)}, f32[5,128,128]{2,1,0:T(8,128)S(1)}, u32[]{:S(2)}, u32[]{:S(2)}) collective-permute-start(f32[5,128,128]{2,1,0:T(8,128)S(1)} %get-tuple-element.107), channel_id=1, source_target_pairs={{0,64},{16,80},{32,96},{48,112},{64,0},{80,16},{96,32},{112,48},{1... | collective-permute-start | bytes 983048 | tf_op jit(solution)/shard_map/ppermute | solution.py:568
  96.4 8.3 %collective-permute-start.20 = (f32[128,1024]{1,0:T(8,128)S(1)}, f32[128,1024]{1,0:T(8,128)S(1)}, u32[]{:S(2)}, u32[]{:S(2)}) collective-permute-start(f32[128,1024]{1,0:T(8,128)S(1)} %select_add_fusion.1), channel_id=1, source_target_pairs={{0,96},{16,48},{32,64},{48,16},{64,32},{80,112},{96,0},{112,80},{1... | collective-permute-start | bytes 1572872 | tf_op jit(solution)/shard_map/ppermute | solution.py:600
  96.4 13.9 %collective-permute-start.17 = (f32[4,512,128]{2,1,0:T(8,128)S(1)}, f32[4,512,128]{2,1,0:T(8,128)S(1)}, u32[]{:S(2)}, u32[]{:S(2)}) collective-permute-start(f32[4,512,128]{2,1,0:T(8,128)S(1)} %pad_maximum_fusion.1.refs_0_), channel_id=1, source_target_pairs={{0,4},{1,5},{2,6},{3,7},{4,0},{5,1},{6,2},{7,3},{8,12},{9,13},{10,... | collective-permute-start | bytes 3145736 | tf_op jit(solution)/shard_map/ppermute | solution.py:610
  96.5 19.5 %collective-permute-start.18 = (f32[4,512,128]{2,1,0:T(8,128)S(1)}, f32[4,512,128]{2,1,0:T(8,128)S(1)}, u32[]{:S(2)}, u32[]{:S(2)}) collective-permute-start(f32[4,512,128]{2,1,0:T(8,128)S(1)} %pad_maximum_fusion.2.refs_4_), channel_id=1, source_target_pairs={{0,12},{1,13},{2,14},{3,15},{4,8},{5,9},{6,10},{7,11},{8,4},{9,5},... | collective-permute-start | bytes 3145736 | tf_op jit(solution)/shard_map/ppermute | solution.py:610
  97.2 8.8 %collective-permute-start.19 = (f32[4,256,128]{2,1,0:T(8,128)S(1)}, f32[4,256,128]{2,1,0:T(8,128)S(1)}, u32[]{:S(2)}, u32[]{:S(2)}) collective-permute-start(f32[4,256,128]{2,1,0:T(8,128)S(1)} %pad_maximum_fusion.7), channel_id=1, source_target_pairs={{0,3},{1,2},{2,1},{3,0},{4,7},{5,6},{6,5},{7,4},{8,11},{9,10},{10,... | collective-permute-start | bytes 1572872 | tf_op jit(solution)/shard_map/ppermute | solution.py:635
  98.6 9.7 %collective-permute-start.21 = (f32[5,128,128]{2,1,0:T(8,128)S(1)}, f32[5,128,128]{2,1,0:T(8,128)S(1)}, u32[]{:S(2)}, u32[]{:S(2)}) collective-permute-start(f32[5,128,128]{2,1,0:T(8,128)S(1)} %get-tuple-element.113), channel_id=1, source_target_pairs={{0,64},{16,80},{32,96},{48,112},{64,0},{80,16},{96,32},{112,48},{1... | collective-permute-start | bytes 983048 | tf_op jit(solution)/shard_map/ppermute | solution.py:568
  116.0 14.9 %collective-permute-start.25 = (f32[8,256,128]{2,1,0:T(8,128)S(1)}, f32[8,256,128]{2,1,0:T(8,128)S(1)}, u32[]{:S(2)}, u32[]{:S(2)}) collective-permute-start(f32[8,256,128]{2,1,0:T(8,128)S(1)} %pad_maximum_fusion.3.own), channel_id=1, source_target_pairs={{0,16},{16,0},{32,48},{48,32},{64,80},{80,64},{96,112},{112,96},{1... | collective-permute-start | bytes 3145736 | tf_op jit(solution)/shard_map/ppermute | solution.py:568
  118.6 15.2 %collective-permute-start.24 = (f32[256,1024]{1,0:T(8,128)S(1)}, f32[256,1024]{1,0:T(8,128)S(1)}, u32[]{:S(2)}, u32[]{:S(2)}) collective-permute-start(f32[256,1024]{1,0:T(8,128)S(1)} %pad_maximum_fusion.4), channel_id=1, source_target_pairs={{0,32},{16,112},{32,0},{48,80},{64,96},{80,48},{96,64},{112,16},{1... | collective-permute-start | bytes 3145736 | tf_op jit(solution)/shard_map/ppermute | solution.py:600
  119.8 15.1 %collective-permute-start.22 = (f32[4,512,128]{2,1,0:T(8,128)S(1)}, f32[4,512,128]{2,1,0:T(8,128)S(1)}, u32[]{:S(2)}, u32[]{:S(2)}) collective-permute-start(f32[4,512,128]{2,1,0:T(8,128)S(1)} %pad_maximum_fusion.1.refs_0_), channel_id=1, source_target_pairs={{0,12},{1,13},{2,14},{3,15},{4,8},{5,9},{6,10},{7,11},{8,4},{9,5},... | collective-permute-start | bytes 3145736 | tf_op jit(solution)/shard_map/ppermute | solution.py:610
  120.0 14.8 %collective-permute-start.23 = (f32[4,512,128]{2,1,0:T(8,128)S(1)}, f32[4,512,128]{2,1,0:T(8,128)S(1)}, u32[]{:S(2)}, u32[]{:S(2)}) collective-permute-start(f32[4,512,128]{2,1,0:T(8,128)S(1)} %pad_maximum_fusion.2.refs_4_), channel_id=1, source_target_pairs={{0,4},{1,5},{2,6},{3,7},{4,0},{5,1},{6,2},{7,3},{8,12},{9,13},{10,... | collective-permute-start | bytes 3145736 | tf_op jit(solution)/shard_map/ppermute | solution.py:610
  120.0 10.9 %copy-start = (f32[2,512,512]{2,1,0:T(8,128)S(1)}, f32[2,512,512]{2,1,0:T(8,128)}, u32[]{:S(2)}) copy-start(f32[2,512,512]{2,1,0:T(8,128)} %inverses.1) | copy-start | bytes 6291460
  134.8 5.4 %collective-permute-start.29 = (f32[512,1024]{1,0:T(8,128)S(1)}, f32[512,1024]{1,0:T(8,128)S(1)}, u32[]{:S(2)}, u32[]{:S(2)}) collective-permute-start(f32[512,1024]{1,0:T(8,128)S(1)} %pad_maximum_fusion.own), channel_id=1, source_target_pairs={{0,16},{16,0},{32,48},{48,32},{64,80},{80,64},{96,112},{112,96},{1... | collective-permute-start | bytes 6291464 | tf_op jit(solution)/shard_map/ppermute | solution.py:568
  136.4 18.0 %collective-permute-start.26 = (f32[4,512,128]{2,1,0:T(8,128)S(1)}, f32[4,512,128]{2,1,0:T(8,128)S(1)}, u32[]{:S(2)}, u32[]{:S(2)}) collective-permute-start(f32[4,512,128]{2,1,0:T(8,128)S(1)} %collective-permute-done.17.refs_1_), channel_id=1, source_target_pairs={{0,12},{1,13},{2,14},{3,15},{4,8},{5,9},{6,10},{7,11},{8,4},{9,5},... | collective-permute-start | bytes 3145736 | tf_op jit(solution)/shard_map/ppermute | solution.py:610
  137.2 17.3 %collective-permute-start.27 = (f32[4,512,128]{2,1,0:T(8,128)S(1)}, f32[4,512,128]{2,1,0:T(8,128)S(1)}, u32[]{:S(2)}, u32[]{:S(2)}) collective-permute-start(f32[4,512,128]{2,1,0:T(8,128)S(1)} %collective-permute-done.18.refs_5_), channel_id=1, source_target_pairs={{0,4},{1,5},{2,6},{3,7},{4,0},{5,1},{6,2},{7,3},{8,12},{9,13},{10,... | collective-permute-start | bytes 3145736 | tf_op jit(solution)/shard_map/ppermute | solution.py:610
  137.2 17.2 %collective-permute-start.28 = (f32[10,128,128]{2,1,0:T(8,128)S(1)}, f32[10,128,128]{2,1,0:T(8,128)S(1)}, u32[]{:S(2)}, u32[]{:S(2)}) collective-permute-start(f32[10,128,128]{2,1,0:T(8,128)S(1)} %get-tuple-element.127), channel_id=1, source_target_pairs={{0,64},{16,80},{32,96},{48,112},{64,0},{80,16},{96,32},{112,48},{1... | collective-permute-start | bytes 1966088 | tf_op jit(solution)/shard_map/ppermute | solution.py:568
  154.5 20.4 %collective-permute-start.30 = (f32[10,128,128]{2,1,0:T(8,128)S(1)}, f32[10,128,128]{2,1,0:T(8,128)S(1)}, u32[]{:S(2)}, u32[]{:S(2)}) collective-permute-start(f32[10,128,128]{2,1,0:T(8,128)S(1)} %get-tuple-element.145), channel_id=1, source_target_pairs={{0,64},{16,80},{32,96},{48,112},{64,0},{80,16},{96,32},{112,48},{1... | collective-permute-start | bytes 1966088 | tf_op jit(solution)/shard_map/ppermute | solution.py:568

commit v4 on v3

--- a/solution.py
+++ b/solution.py
@@ -54,10 +54,32 @@
     return place, found
 
 
+def cut_kernel(maps, pieces, first, sem):
+    other = 1 - lax.axis_index("row") // 4
+    place, _ = first_block(maps, 1 - other, lax.axis_index("col"))
+    columns = pl.ds(pl.multiple_of(place * BLK, BLK), BLK)
+    copy = pltpu.make_async_copy(pieces.at[:, other, :, columns], first, sem)
+    copy.start()
+    copy.wait()
+
+
+def cut(maps, pieces):
+    return pl.pallas_call(
+        cut_kernel,
+        out_shape=jax.ShapeDtypeStruct((10, BLK, BLK), F32),
+        in_specs=[SMEM, HBM],
+        out_specs=VMEM,
+        scratch_shapes=[pltpu.SemaphoreType.DMA(())],
+        compiler_params=params(4),
+        cost_estimate=cost(0, MIB),
+        name="cut",
+    )(in_hbm(maps), in_hbm(pieces))
+
+
 def prepare_kernel(
-    maps, pivots, front, pieces, first, rest_a, rest_b, rest_c, rest_d, rest_e, panel, own, away, table,
-    sending, kept, total, sem,
+    maps, pivots, front, pieces, first, *refs,
 ):
+    *rests, panel, own, away, table, sending, kept, total, sem = refs
     here_row, here_col = lax.axis_index("row"), lax.axis_index("col")
     side, core = here_row // 4, here_row % 2
     other = 1 - side
@@ -73,8 +95,8 @@
         pltpu.make_async_copy(front.at[:, pl.ds(0, BLK)], panel, sem.at[2]),
     ]
     writes = []
-    targets = (0, 0, rest_a), (1, 0, rest_b), (1, 5, rest_c), (2, 0, rest_d), (3, 0, rest_e)
-    for n, (j, start, target) in enumerate(targets):
+    places = (0, 0), (1, 0), (1, 5), (2, 0), (2, 5), (3, 0)
+    for n, ((j, start), target) in enumerate(zip(places, rests)):
         d = j + (j >= place).astype(jnp.int32)
         source = sending.at[pl.ds(start, target.shape[0]), :, columns(d)]
         writes.append(pltpu.make_async_copy(source, target, sem.at[3 + n]))
@@ -111,7 +133,6 @@
     reads[0].wait()
     for copy in writes:
         copy.start()
-    first[...] = sending[:, :, columns(place)]
     reads[1].wait()
     reads[2].wait()
 
@@ -140,35 +161,35 @@
         copy.wait()
 
 
-def prepare(maps, pivots, front, pieces):
+def prepare(maps, pivots, front, pieces, first):
     column = jax.ShapeDtypeStruct((10, BLK, BLK), F32)
     half = jax.ShapeDtypeStruct((5, BLK, BLK), F32)
     return pl.pallas_call(
         prepare_kernel,
         out_shape=[
             column,
-            column,
             half,
             half,
-            column,
+            half,
+            half,
             column,
             jax.ShapeDtypeStruct((2048, BLK), F32),
             jax.ShapeDtypeStruct((256, BLK), F32),
             jax.ShapeDtypeStruct((256, BLK), F32),
             jax.ShapeDtypeStruct((64,), jnp.int32),
         ],
-        in_specs=[SMEM, VMEM, HBM, HBM],
-        out_specs=[VMEM, HBM, HBM, HBM, HBM, HBM, VMEM, VMEM, VMEM, SMEM],
+        in_specs=[SMEM, VMEM, HBM, HBM, VMEM],
+        out_specs=[HBM] * 6 + [VMEM, VMEM, VMEM, SMEM],
         scratch_shapes=[
             pltpu.VMEM((10, BLK, 640), F32),
             pltpu.VMEM((10, BLK, BLK), F32),
             pltpu.VMEM((PANEL, BLK), F32),
-            pltpu.SemaphoreType.DMA((8,)),
+            pltpu.SemaphoreType.DMA((9,)),
         ],
         compiler_params=params(24),
         cost_estimate=cost(0, 9 * MIB),
         name="prepare",
-    )(in_hbm(maps), in_hbm(pivots.reshape(8, BLK)), in_hbm(front), in_hbm(pieces))
+    )(in_hbm(maps), in_hbm(pivots.reshape(8, BLK)), in_hbm(front), in_hbm(pieces), first)
 
 
 def pivot_kernel(mine_half, maps, pivots, front, children, *refs):
@@ -426,7 +447,7 @@
             out_specs=tile,
         ),
         compiler_params=params(20),
-        cost_estimate=cost(0, 22 * MIB),
+        cost_estimate=cost(0, MIB),
         name="extend",
     )(table, in_hbm(front.reshape(2, 1024, 1024)), *[in_hbm(pieces)] * 2, *[g for g in got for _ in range(2)])
 
@@ -436,8 +457,9 @@
 
 def update_kernel(table, front, *refs):
     blocks = refs[:4], refs[4:8]
-    right_h, right_l, marks, out, panels = refs[8:]
+    right_h, right_l, marks, got_b, got_c, got_d, out, panels = refs[8:]
     step = pl.program_id(0)
+    span = pl.ds(pl.multiple_of(step % 2 * 256, 256), 256)
     col, core = table[COL], table[ROW] % 2
 
     def assemble(which):
@@ -450,8 +472,8 @@
             flip = [jnp.where(core == 0, bits[e], bits[o]) for e, o in zip(even, odd)]
             slot = flip[0] | (flip[1] << 1)
             later, far = flip[2] == 1, flip[3] == 1
-            near_block = jnp.where(later, came[slot], held[slot])
-            far_block = jnp.where(later, came_far[slot], held_far[slot])
+            near_block = jnp.where(later, came[slot, span, :], held[slot, span, :])
+            far_block = jnp.where(later, came_far[slot, span, :], held_far[slot, span, :])
             block = jnp.where(far, far_block, near_block)
             y, x = c // 4, c % 4
             rows = slice(0, 256) if y < 2 else slice(256, PANEL)
@@ -472,13 +494,25 @@
             after = jnp.where(col < 8, part, after)
         out[:, :, columns] = jnp.where(active, after, before)
 
-
-def update(table, front, blocks, right, marks):
-    def whole(x):
-        return pl.BlockSpec(x.shape, lambda t, s: (0,) * x.ndim, pipeline_mode=pl.Buffered(1))
-
-    first = pl.BlockSpec((4, 256, BLK), lambda t, s: (0, jnp.minimum(t, 1), 0))
-    second = pl.BlockSpec((4, 256, BLK), lambda t, s: (0, jnp.maximum(t - 2, 0), 0))
+    def columns_of(j):
+        return pl.ds(pl.multiple_of(table[GOT_COL + j] * BLK, BLK), BLK)
+
+    for part in range(4):
+        half, rest = part // 2, part % 2
+        rows = slice(rest * BLK, (rest + 1) * BLK)
+        m = table[GOT_AT + half * 8 + 2 * step + rest]
+
+        @pl.when((m >= 0) & (m < 5))
+        def _(half=half, rows=rows, m=m):
+            out[half, rows, columns_of(2)] += got_b[m]
+            out[half, rows, columns_of(3)] += got_d[m]
+
+        @pl.when(m >= 5)
+        def _(half=half, rows=rows, m=m):
+            out[half, rows, columns_of(2)] += got_c[m - 5]
+
+
+def update(table, front, blocks, right, marks, got):
     tile = pl.BlockSpec((2, 256, 1024), lambda t, s: (0, t, 0))
     return pl.pallas_call(
         update_kernel,
@@ -488,10 +522,9 @@
             grid=(4,),
             in_specs=[
                 tile,
-                *[first] * 4,
-                *[second] * 4,
-                *[whole(x) for x in right],
+                *[VMEM] * 10,
                 pl.BlockSpec((2, 256, BLK), lambda t, s: (0, t, 0)),
+                *[VMEM] * 3,
             ],
             out_specs=tile,
             scratch_shapes=[pltpu.VMEM((2, PANEL, 1024), BF16)],
@@ -499,19 +532,17 @@
         compiler_params=params(34),
         cost_estimate=cost(6 * 2048 * 1024 * 1024, 32 * MIB),
         name="update",
-    )(table, in_hbm(front), *blocks[0], *blocks[1], *right, marks.reshape(2, 1024, BLK))
+    )(table, in_hbm(front), *blocks[0], *blocks[1], *right, marks.reshape(2, 1024, BLK), *got)
 
 
 def finish_kernel(
-    table, list_other, list_mine, front, got_b, got_c, got_d, got_e, patch,
+    table, list_other, list_mine, front, got_e, got_f, patch,
     out, held, read_sem, write_sem, sem,
 ):
     del front
     core = table[ROW] % 2
     copies = []
-    for n, (column, first, got) in enumerate(
-        [(2, 0, got_b), (2, 5, got_c), (3, 0, got_d), (4, 0, got_e)]
-    ):
+    for n, (column, first, got) in enumerate([(3, 5, got_e), (4, 0, got_f)]):
         columns = pl.ds(pl.multiple_of(table[GOT_COL + column] * BLK, BLK), BLK)
         for m in range(got.shape[0]):
             rows = pl.ds(pl.multiple_of(table[GOT_ROW + first + m] * BLK, BLK), BLK)
@@ -548,12 +579,12 @@
     return pl.pallas_call(
         finish_kernel,
         out_shape=jax.ShapeDtypeStruct((2048, 1024), F32),
-        in_specs=[SMEM, SMEM, SMEM, HBM] + [VMEM] * 5,
+        in_specs=[SMEM, SMEM, SMEM, HBM] + [VMEM] * 3,
         out_specs=HBM,
         scratch_shapes=[
-            pltpu.VMEM((4, 10, BLK, BLK), F32),
-            pltpu.SemaphoreType.DMA((4, 10)),
-            pltpu.SemaphoreType.DMA((4, 10)),
+            pltpu.VMEM((2, 10, BLK, BLK), F32),
+            pltpu.SemaphoreType.DMA((2, 10)),
+            pltpu.SemaphoreType.DMA((2, 10)),
             pltpu.SemaphoreType.DMA(()),
         ],
         input_output_aliases={3: 0},
@@ -609,13 +640,12 @@
         ]
         return lax.ppermute(block, ("row", "col"), route)
 
-    first, rest_a, rest_b, rest_c, rest_d, rest_e, panel, corner, away, table = prepare(
-        child_maps, pivots, front, pieces
-    )
+    first = cut(child_maps, pieces)
     got0 = by_row(first, 4)
+    *rest, panel, corner, away, table = prepare(child_maps, pivots, front, pieces, first)
+    rest_a, rest_b, rest_c, rest_d, rest_e, rest_f = rest
     corner = corner + by_row(away, 1)
-    for k in range(2):
-        corner = corner + lax.ppermute(corner, "row", rings[k])
+    corner = corner + (by_row(corner, 2) + (by_row(corner, 6) + by_row(corner, 4)))
     away_rows, marks, list_other = pivot_terms(child_maps, pivots, front, children)
     got0, away_rows, rest_a, marks, corner = together((got0, away_rows, rest_a, marks, corner))
 
@@ -641,30 +671,31 @@
         corner = corner_step(corner, k)
         total = halve(total, k)
         if k == 0:
-            held, corner, total, rest_b = together((held, corner, total, rest_b))
-            got_b = by_row(rest_b, 4)
-        else:
-            held, corner, total, got_b, rest_c = together((held, corner, total, got_b, rest_c))
+            front = extend(table, front, pieces, (got0, got_a))
+        held, corner, total, rest_b, front = together((held, corner, total, rest_b, front))
     came = [gather_step(held[w], w, 2) for w in range(2)]
     corner = corner_step(corner, 2)
     total = double(total, 1)
-    got_c = by_row(rest_c, 4)
-    came, corner, total, got_c = together((came, corner, total, got_c))
+    got_b = by_row(rest_b, 4)
+    came, corner, total, got_b, rest_c = together((came, corner, total, got_b, rest_c))
     held_far = [gather_step(held[w], w, 3) for w in range(2)]
     *factors, cross = corners(table, corner, by_row(corner, 1), diag_inverses)
     total = double(total, 0)
-    front = extend(table, front, pieces, (got0, got_a))
-    came, held_far, total, rest_d, factors, cross, front = together(
-        (came, held_far, total, rest_d, factors, cross, front)
+    got_c = by_row(rest_c, 4)
+    came, held_far, total, got_c, rest_d, factors, cross = together(
+        (came, held_far, total, got_c, rest_d, factors, cross)
     )
     came_far = [gather_step(came[w], w, 3) for w in range(2)]
     got_d = by_row(rest_d, 4)
     *right, patch = right_factor(table, total, by_row(total, 1), factors, cross)
-    came_far, got_d, rest_e, right, patch = together((came_far, got_d, rest_e, right, patch))
-    got_e = by_row(rest_e, 4)
+    came_far, got_d, rest_e, rest_f, right, patch = together(
+        (came_far, got_d, rest_e, rest_f, right, patch)
+    )
+    got_e, got_f = by_row(rest_e, 4), by_row(rest_f, 4)
     blocks = [(held[w], came[w], held_far[w], came_far[w]) for w in range(2)]
-    front = update(table, front, blocks, right, marks).reshape(2048, 1024)
-    return finish(table, (list_other, list_mine), front, (got_b, got_c, got_d, got_e), patch)
+    front = update(table, front, blocks, right, marks, (got_b, got_c, got_d))
+    front = front.reshape(2048, 1024)
+    return finish(table, (list_other, list_mine), front, (got_e, got_f), patch)
 
 
 def solution(mesh):

time: 182 us -> 172 us (0.945)
  waiting for transfers between devices: 68.3 us -> 49 us
  starting transfers between devices: 39 us -> 44.4 us
  local copies, waits for them, and re-layouts: 0.04 us -> 2.94 us
    ppermute x10 -> x14, waiting for transfers between devices: 23.8 us -> 6.21 us  [swap(): return lax.ppermute(block, axis, [(i, partner(i)) for i in range(count)])]
    ppermute x2 -> x0, waiting for transfers between devices: 13.9 us -> none  [local(): corner = corner + lax.ppermute(corner, 'row', rings[k])]
    ppermute x2, waiting for transfers between devices: 5.75 us -> 17.9 us  [double(): came = lax.ppermute(part, 'row', rings[step])]
    ppermute x10, starting transfers between devices: 2.87 us -> 7.83 us  [gather_step(): return lax.ppermute(block, ('row', 'col'), route)]
    ppermute x2, waiting for transfers between devices: 3.92 us -> 0.46 us  [halve(): return stay + lax.ppermute(leave, 'row', rings[step])]
    unnamed x2 -> x6, local copies, waits for them, and re-layouts: 0.01 us -> 2.91 us
    ppermute x10, waiting for transfers between devices: 14 us -> 16.7 us  [gather_step(): return lax.ppermute(block, ('row', 'col'), route)]
    ppermute x10 -> x14, starting transfers between devices: 18.9 us -> 21.3 us  [swap(): return lax.ppermute(block, axis, [(i, partner(i)) for i in range(count)])]
  transfers between devices with their start and end apart: 31 -> 33, of which waited for: 22 -> 15; matrix products, arithmetic and copies ran while one was open for 1% -> 1% of each run, Pallas kernels for 34% -> 38%
where the time goes in v4:
time: 172 us; the launch traced here: 170 us
  Pallas kernels  71.1 us (41%)
  waiting for transfers between devices  49 us (28%)
  starting transfers between devices  44.4 us (26%)
  local copies, waits for them, and re-layouts  2.94 us (2%)
  other arithmetic  2.36 us (1%)
    ppermute x14, starting transfers between devices, swap(): return lax.ppermute(block, axis, [(i, partner(i)) for i in range(count)])  21.3 us
    pallas_call x1, Pallas kernels, update(): pl.pallas_call(update_kernel, out_shape=pltpu.HBM((2, 1024, 1024), F32),...  20.5 us
    pallas_call x2, Pallas kernels, pivot_terms(): pl.pallas_call(functools.partial(pivot_kernel, mine_half), out_shape=[jax...  18.2 us
    ppermute x2, waiting for transfers between devices, double(): came = lax.ppermute(part, 'row', rings[step])  17.9 us
    ppermute x10, waiting for transfers between devices, gather_step(): return lax.ppermute(block, ('row', 'col'), route)  16.7 us
    pallas_call x1, Pallas kernels, extend(): pl.pallas_call(functools.partial(extend_kernel, len(got)), out_shape=pltp...  10.7 us
    pallas_call x1, Pallas kernels, right_factor(): pl.pallas_call(factor_kernel, out_shape=[shape, shape, jax.ShapeDtypeStru...  7.86 us
    ppermute x10, starting transfers between devices, gather_step(): return lax.ppermute(block, ('row', 'col'), route)  7.83 us
  transfers between devices with their start and end apart: 33, of which 15 were waited for; matrix products, arithmetic and copies ran while one was open for 1% of the time, Pallas kernels for 38%

profile of v4, /device:TPU:1, one launch (start us, length us, event | category | flops | bytes accessed | tf_op | source)
XLA Modules:
  0.0 170.3 jit_solution(16856300562055463532)
XLA Ops:
  0.0 1.8 %cut.1.first = f32[10,128,128]{2,1,0:T(8,128)S(1)} custom-call(s32[2,80]{1,0:T(2,128)} %maps.7, f32[10,2,128,640]{3,2,1,0:T(8,128)} %bitcast.12), custom_call_target="tpu_custom_call" | custom-call | bytes 1048576 | tf_op jit(solution)/shard_map/cut/pallas_call | solution.py:67
  1.9 4.5 %collective-permute-start = (f32[10,128,128]{2,1,0:T(8,128)S(1)}, f32[10,128,128]{2,1,0:T(8,128)S(1)}, u32[]{:S(2)}, u32[]{:S(2)}) collective-permute-start(f32[10,128,128]{2,1,0:T(8,128)S(1)} %cut.1.first), channel_id=1, source_target_pairs={{0,64},{16,80},{32,96},{48,112},{64,0},{80,16},{96,32},{112,48},{1... | collective-permute-start | bytes 1966088 | tf_op jit(solution)/shard_map/ppermute | solution.py:599
  6.4 5.1 %prepare.1 = (f32[10,128,128]{2,1,0:T(8,128)S(1)}, f32[5,128,128]{2,1,0:T(8,128)S(1)}, f32[5,128,128]{2,1,0:T(8,128)S(1)}, f32[5,128,128]{2,1,0:T(8,128)S(1)}, f...) custom-call(s32[2,80]{1,0:T(2,128)} %maps.7, ...), custom_call_target="tpu_custom_call" | custom-call | bytes 9437184 | tf_op jit(solution)/shard_map/prepare/pallas_call | solution.py:167
  11.5 1.0 collective-permute-start.1
  12.5 1.0 collective-permute-done.1
  13.6 3.1 %collective-permute-start.3 = (f32[256,128]{1,0:T(8,128)S(1)}, f32[256,128]{1,0:T(8,128)S(1)}, u32[]{:S(2)}, u32[]{:S(2)}) collective-permute-start(f32[256,128]{1,0:T(8,128)S(1)} %add.21), channel_id=1, source_target_pairs={{0,96},{16,112},{32,64},{48,80},{64,32},{80,48},{96,0},{112,16},{1... | collective-permute-start | bytes 393224 | tf_op jit(solution)/shard_map/ppermute | solution.py:599
  16.7 9.1 %pivot_terms_other.1 = (f32[512,1024]{1,0:T(8,128)S(1)}, f32[2048,128]{1,0:T(8,128)S(1)}, s32[513]{0:T(1024)S(1)}) custom-call(s32[2,80]{1,0:T(2,128)} %maps.7, s32[1024]{0:T(1024)} %pivots.1, f32[2048,1024]{1,0:T(8,128)} %front.5, f32[2560,640]{1,0:T(8,128)} %children.3), custom_call_target="tpu_custom_call" | custom-call | bytes 25165824 | tf_op jit(solution)/shard_map/pivot_terms_other/pallas_call | solution.py:263
  25.8 1.4 collective-permute-done.3
  27.2 1.3 collective-permute-start.7
  28.6 0.8 whole_panel.1
  29.4 4.7 %collective-permute-start.5 = (f32[1024,128]{1,0:T(8,128)S(1)}, f32[1024,128]{1,0:T(8,128)S(1)}, u32[]{:S(2)}, u32[]{:S(2)}) collective-permute-start(f32[1024,128]{1,0:T(8,128)S(1)} %get-tuple-element.93), channel_id=1, source_target_pairs={{0,12},{1,13},{2,14},{3,15},{4,8},{5,9},{6,10},{7,11},{16,28},{17,... | collective-permute-start | bytes 1572872 | tf_op jit(solution)/shard_map/ppermute | solution.py:603
  34.0 2.1 %collective-permute-start.8 = (f32[10,128,128]{2,1,0:T(8,128)S(1)}, f32[10,128,128]{2,1,0:T(8,128)S(1)}, u32[]{:S(2)}, u32[]{:S(2)}) collective-permute-start(f32[10,128,128]{2,1,0:T(8,128)S(1)} %get-tuple-element.97), channel_id=1, source_target_pairs={{0,64},{16,80},{32,96},{48,112},{64,0},{80,16},{96,32},{112,48},{1... | collective-permute-start | bytes 1966088 | tf_op jit(solution)/shard_map/ppermute | solution.py:599
  36.1 1.3 collective-permute-start.6
  37.4 9.1 %pivot_terms_mine.1 = (f32[512,1024]{1,0:T(8,128)S(1)}, f32[2048,128]{1,0:T(8,128)S(1)}, s32[513]{0:T(1024)S(1)}) custom-call(s32[2,80]{1,0:T(2,128)} %maps.7, s32[1024]{0:T(1024)} %pivots.1, f32[2048,1024]{1,0:T(8,128)} %front.5, f32[2560,640]{1,0:T(8,128)} %children.3, f32[2048,128]{1,0:T(8,128)S(1)} %get-tuple-element.87.refs_0_), custom_call_target="tpu_custom_call" | custom-call | bytes 25165824 | tf_op jit(solution)/shard_map/pivot_terms_mine/pallas_call | solution.py:263
  46.5 1.6 collective-permute-done.6
  48.8 2.9 %collective-permute-done.8.refs_4_.refs_5_ = f32[10,128,128]{2,1,0:T(8,128)S(1)} collective-permute-done((f32[10,128,128]{2,1,0:T(8,128)S(1)}, f32[10,128,128]{2,1,0:T(8,128)S(1)}, u32[]{:S(2)}, u32[]{:S(2)}) %collective-permute-start.8) | collective-permute-done | bytes 655392 | tf_op jit(solution)/shard_map/ppermute | solution.py:599
  51.8 2.3 %collective-permute-start.12 = (f32[256,1024]{1,0:T(8,128)S(1)}, f32[256,1024]{1,0:T(8,128)S(1)}, u32[]{:S(2)}, u32[]{:S(2)}) collective-permute-start(f32[256,1024]{1,0:T(8,128)S(1)} %slice_select_fusion), channel_id=1, source_target_pairs={{0,32},{16,112},{32,0},{48,80},{64,96},{80,48},{96,64},{112,16},{1... | collective-permute-start | bytes 3145736 | tf_op jit(solution)/shard_map/ppermute | solution.py:628
  54.8 1.4 collective-permute-start.11
  56.2 10.7 %extend.1.front = f32[2,1024,1024]{2,1,0:T(8,128)} custom-call(s32[64]{0:T(128)S(1)} %get-tuple-element.80.table, f32[2,1024,1024]{2,1,0:T(8,128)} %bitcast.16, f32[10,2,128,640]{3,2,1,0:T(8,128)} %bitcast.14, f32[10,2,128,640]{3,2,1,0:T(8,128)} %bitcast.15, f32[10,128,128]{2,1,0:T(8,128)S(1)} %collective-permute-done.got.refs_2_.refs_3_, ...), custom_call_target="tpu_custom_call" | custom-call | bytes 1048576 | tf_op jit(solution)/shard_map/extend/pallas_call | solution.py:440
  67.4 2.3 %collective-permute-start.15 = (f32[2,256,128]{2,1,0:T(8,128)S(1)}, f32[2,256,128]{2,1,0:T(8,128)S(1)}, u32[]{:S(2)}, u32[]{:S(2)}) collective-permute-start(f32[2,256,128]{2,1,0:T(8,128)S(1)} %pad_maximum_fusion.8), channel_id=1, source_target_pairs={{0,1},{1,0},{2,3},{3,2},{4,5},{5,4},{6,7},{7,6},{8,9},{9,8},{10,11... | collective-permute-start | bytes 786440 | tf_op jit(solution)/shard_map/ppermute | solution.py:665
  69.7 1.6 collective-permute-start.13
  71.4 0.9 collective-permute-start.14
  72.3 1.6 collective-permute-done.15
  74.0 5.2 %collective-permute-done.13 = f32[2,512,128]{2,1,0:T(8,128)S(1)} collective-permute-done((f32[2,512,128]{2,1,0:T(8,128)S(1)}, f32[2,512,128]{2,1,0:T(8,128)S(1)}, u32[]{:S(2)}, u32[]{:S(2)}) %collective-permute-start.13) | collective-permute-done | bytes 524320 | tf_op jit(solution)/shard_map/ppermute | solution.py:641
  79.9 1.4 collective-permute-start.20
  81.7 0.7 collective-permute-start.18
  82.4 0.9 collective-permute-start.19
  83.9 4.4 %collective-permute-done.20 = f32[128,1024]{1,0:T(8,128)S(1)} collective-permute-done((f32[128,1024]{1,0:T(8,128)S(1)}, f32[128,1024]{1,0:T(8,128)S(1)}, u32[]{:S(2)}, u32[]{:S(2)}) %collective-permute-start.20) | collective-permute-done | bytes 524320 | tf_op jit(solution)/shard_map/ppermute | solution.py:631
  88.5 4.5 %collective-permute-done.19 = f32[4,256,128]{2,1,0:T(8,128)S(1)} collective-permute-done((f32[4,256,128]{2,1,0:T(8,128)S(1)}, f32[4,256,128]{2,1,0:T(8,128)S(1)}, u32[]{:S(2)}, u32[]{:S(2)}) %collective-permute-start.19) | collective-permute-done | bytes 524320 | tf_op jit(solution)/shard_map/ppermute | solution.py:665
  93.2 2.1 %collective-permute-done.17.refs_1_ = f32[4,512,128]{2,1,0:T(8,128)S(1)} collective-permute-done((f32[4,512,128]{2,1,0:T(8,128)S(1)}, f32[4,512,128]{2,1,0:T(8,128)S(1)}, u32[]{:S(2)}, u32[]{:S(2)}) %collective-permute-start.17) | collective-permute-done | bytes 1048608 | tf_op jit(solution)/shard_map/ppermute | solution.py:641
  95.3 6.8 %collective-permute-done.18.refs_5_ = f32[4,512,128]{2,1,0:T(8,128)S(1)} collective-permute-done((f32[4,512,128]{2,1,0:T(8,128)S(1)}, f32[4,512,128]{2,1,0:T(8,128)S(1)}, u32[]{:S(2)}, u32[]{:S(2)}) %collective-permute-start.18) | collective-permute-done | bytes 1048608 | tf_op jit(solution)/shard_map/ppermute | solution.py:641
  102.1 1.1 collective-permute-start.24
  103.2 2.1 %collective-permute-start.22 = (f32[4,512,128]{2,1,0:T(8,128)S(1)}, f32[4,512,128]{2,1,0:T(8,128)S(1)}, u32[]{:S(2)}, u32[]{:S(2)}) collective-permute-start(f32[4,512,128]{2,1,0:T(8,128)S(1)} %pad_maximum_fusion.1.refs_0_), channel_id=1, source_target_pairs={{0,12},{1,13},{2,14},{3,15},{4,8},{5,9},{6,10},{7,11},{8,4},{9,5},... | collective-permute-start | bytes 3145736 | tf_op jit(solution)/shard_map/ppermute | solution.py:641
  105.3 1.7 collective-permute-start.25
  107.0 13.5 %collective-permute-done.24 = f32[256,1024]{1,0:T(8,128)S(1)} collective-permute-done((f32[256,1024]{1,0:T(8,128)S(1)}, f32[256,1024]{1,0:T(8,128)S(1)}, u32[]{:S(2)}, u32[]{:S(2)}) %collective-permute-start.24) | collective-permute-done | bytes 1048608 | tf_op jit(solution)/shard_map/ppermute | solution.py:631
  120.8 2.0 %corners.1 = (bf16[3,512,512]{2,1,0:T(8,128)(2,1)S(1)}, bf16[3,512,512]{2,1,0:T(8,128)(2,1)S(1)}, f32[512,512]{1,0:T(8,128)S(1)}) custom-call(s32[64]{0:T(128)S(1)} %get-tuple-element.80.table, f32[8,256,128]{2,1,0:T(8,128)S(1)} %pad_maximum_fusion.3.own, f32[8,256,128]{2,1,0:T(8,128)S(1)} %collective-permute-done.26.swapped, f32[2,512,512]{2,1,0:T(8,128)S(1)} %copy-done), custom_call_target="tpu_custom_call" | custom-call | flops 805306368 | bytes 8388608 | tf_op jit(solution)/shard_map/corners/pallas_call | solution.py:341
  123.1 2.5 %collective-permute-start.30 = (f32[512,1024]{1,0:T(8,128)S(1)}, f32[512,1024]{1,0:T(8,128)S(1)}, u32[]{:S(2)}, u32[]{:S(2)}) collective-permute-start(f32[512,1024]{1,0:T(8,128)S(1)} %pad_maximum_fusion.own), channel_id=1, source_target_pairs={{0,16},{16,0},{32,48},{48,32},{64,80},{80,64},{96,112},{112,96},{1... | collective-permute-start | bytes 6291464 | tf_op jit(solution)/shard_map/ppermute | solution.py:599
  125.6 1.5 collective-permute-start.27
  127.1 1.3 collective-permute-start.29
  128.4 1.0 collective-permute-done.30.swapped
  129.4 7.9 %right_factor.1 = (bf16[1024,1024]{1,0:T(8,128)(2,1)S(1)}, bf16[1024,1024]{1,0:T(8,128)(2,1)S(1)}, f32[512,1024]{1,0:T(8,128)S(1)}) custom-call(s32[64]{0:T(128)S(1)} %get-tuple-element.80.table, f32[512,1024]{1,0:T(8,128)S(1)} %pad_maximum_fusion.own, f32[512,1024]{1,0:T(8,128)S(1)} %collective-permute-done.30.swapped, ...), custom_call_target="tpu_custom_call" | custom-call | flops 6442450944 | bytes 14680064 | tf_op jit(solution)/shard_map/right_factor/pallas_call | solution.py:395
  137.3 1.3 copy-done.1
  138.6 2.2 %collective-permute-done.27.refs_3_ = f32[4,512,128]{2,1,0:T(8,128)S(1)} collective-permute-done((f32[4,512,128]{2,1,0:T(8,128)S(1)}, f32[4,512,128]{2,1,0:T(8,128)S(1)}, u32[]{:S(2)}, u32[]{:S(2)}) %collective-permute-start.27) | collective-permute-done | bytes 1048608 | tf_op jit(solution)/shard_map/ppermute | solution.py:641
  141.0 1.3 collective-permute-start.31
  142.3 1.7 collective-permute-start.32
  144.0 1.6 copy-done.2
  145.6 20.5 %update.1 = f32[2,1024,1024]{2,1,0:T(8,128)} custom-call(s32[64]{0:T(128)S(1)} %get-tuple-element.80.table, f32[2,1024,1024]{2,1,0:T(8,128)} %extend.1.front, f32[4,512,128]{2,1,0:T(8,128)S(1)} %pad_maximum_fusion.1.refs_0_, f32[4,512,128]{2,1,0:T(8,128)S(1)} %collective-permute-done.17.refs_1_, f32[4,512,128]{2,1,0:T(8,128)S(1)} %collective-permute-done.22.refs_2_, ...), custom_call_target="tpu_custom_call" | custom-call | flops 12884901888 | bytes 33554432 | tf_op jit(solution)/shard_map/update/pallas_call | solution.py:517
  166.1 4.1 %finish.1 = f32[2048,1024]{1,0:T(8,128)} custom-call(s32[64]{0:T(128)S(1)} %get-tuple-element.80.table, s32[513]{0:T(1024)S(1)} %get-tuple-element.81.list_other, s32[513]{0:T(1024)S(1)} %get-tuple-element.88.list_mine, f32[2048,1024]{1,0:T(8,128)} %bitcast.17, f32[5,128,128]{2,1,0:T(8,128)S(1)} %collective-permute-done.31.got_e, ...), custom_call_target="tpu_custom_call", output_to_operand_aliasing={{}: (3, {})} | custom-call | bytes 8388608 | tf_op jit(solution)/shard_map/finish/pallas_call | solution.py:579
  (55 shorter events, 5.0 us)
Async XLA Ops:
  1.9 25.4 %collective-permute-start = (f32[10,128,128]{2,1,0:T(8,128)S(1)}, f32[10,128,128]{2,1,0:T(8,128)S(1)}, u32[]{:S(2)}, u32[]{:S(2)}) collective-permute-start(f32[10,128,128]{2,1,0:T(8,128)S(1)} %cut.1.first), channel_id=1, source_target_pairs={{0,64},{16,80},{32,96},{48,112},{64,0},{80,16},{96,32},{112,48},{1... | collective-permute-start | bytes 1966088 | tf_op jit(solution)/shard_map/ppermute | solution.py:599
  11.5 2.0 %collective-permute-start.1 = (f32[256,128]{1,0:T(8,128)S(1)}, f32[256,128]{1,0:T(8,128)S(1)}, u32[]{:S(2)}, u32[]{:S(2)}) collective-permute-start(f32[256,128]{1,0:T(8,128)S(1)} %get-tuple-element.86), channel_id=1, source_target_pairs={{0,16},{16,0},{32,48},{48,32},{64,80},{80,64},{96,112},{112,96},{1... | collective-permute-start | bytes 393224 | tf_op jit(solution)/shard_map/ppermute | solution.py:599
  13.5 12.3 %collective-permute-start.4 = (f32[256,128]{1,0:T(8,128)S(1)}, f32[256,128]{1,0:T(8,128)S(1)}, u32[]{:S(2)}, u32[]{:S(2)}) collective-permute-start(f32[256,128]{1,0:T(8,128)S(1)} %add.21), channel_id=1, source_target_pairs={{0,64},{16,80},{32,96},{48,112},{64,0},{80,16},{96,32},{112,48},{1... | collective-permute-start | bytes 393224 | tf_op jit(solution)/shard_map/ppermute | solution.py:599
  13.6 13.6 %collective-permute-start.3 = (f32[256,128]{1,0:T(8,128)S(1)}, f32[256,128]{1,0:T(8,128)S(1)}, u32[]{:S(2)}, u32[]{:S(2)}) collective-permute-start(f32[256,128]{1,0:T(8,128)S(1)} %add.21), channel_id=1, source_target_pairs={{0,96},{16,112},{32,64},{48,80},{64,32},{80,48},{96,0},{112,16},{1... | collective-permute-start | bytes 393224 | tf_op jit(solution)/shard_map/ppermute | solution.py:599
  16.7 10.5 %collective-permute-start.2 = (f32[256,128]{1,0:T(8,128)S(1)}, f32[256,128]{1,0:T(8,128)S(1)}, u32[]{:S(2)}, u32[]{:S(2)}) collective-permute-start(f32[256,128]{1,0:T(8,128)S(1)} %add.21), channel_id=1, source_target_pairs={{0,32},{16,48},{32,0},{48,16},{64,96},{80,112},{96,64},{112,80},{1... | collective-permute-start | bytes 393224 | tf_op jit(solution)/shard_map/ppermute | solution.py:599
  27.2 21.0 %collective-permute-start.7 = (f32[512,1024]{1,0:T(8,128)S(1)}, f32[512,1024]{1,0:T(8,128)S(1)}, u32[]{:S(2)}, u32[]{:S(2)}) collective-permute-start(f32[512,1024]{1,0:T(8,128)S(1)} %get-tuple-element.96), channel_id=1, source_target_pairs={{0,16},{16,0},{32,48},{48,32},{64,80},{80,64},{96,112},{112,96},{1... | collective-permute-start | bytes 6291464 | tf_op jit(solution)/shard_map/ppermute | solution.py:599
  29.4 18.8 %collective-permute-start.5 = (f32[1024,128]{1,0:T(8,128)S(1)}, f32[1024,128]{1,0:T(8,128)S(1)}, u32[]{:S(2)}, u32[]{:S(2)}) collective-permute-start(f32[1024,128]{1,0:T(8,128)S(1)} %get-tuple-element.93), channel_id=1, source_target_pairs={{0,12},{1,13},{2,14},{3,15},{4,8},{5,9},{6,10},{7,11},{16,28},{17,... | collective-permute-start | bytes 1572872 | tf_op jit(solution)/shard_map/ppermute | solution.py:603
  34.0 17.6 %collective-permute-start.8 = (f32[10,128,128]{2,1,0:T(8,128)S(1)}, f32[10,128,128]{2,1,0:T(8,128)S(1)}, u32[]{:S(2)}, u32[]{:S(2)}) collective-permute-start(f32[10,128,128]{2,1,0:T(8,128)S(1)} %get-tuple-element.97), channel_id=1, source_target_pairs={{0,64},{16,80},{32,96},{48,112},{64,0},{80,16},{96,32},{112,48},{1... | collective-permute-start | bytes 1966088 | tf_op jit(solution)/shard_map/ppermute | solution.py:599
  36.1 12.0 %collective-permute-start.6 = (f32[256,128]{1,0:T(8,128)S(1)}, f32[256,128]{1,0:T(8,128)S(1)}, u32[]{:S(2)}, u32[]{:S(2)}) collective-permute-start(f32[256,128]{1,0:T(8,128)S(1)} %add_add_fusion), channel_id=1, source_target_pairs={{0,12},{1,13},{2,14},{3,15},{4,8},{5,9},{6,10},{7,11},{16,28},{17,... | collective-permute-start | bytes 393224 | tf_op jit(solution)/shard_map/ppermute | solution.py:603
  51.8 15.2 %collective-permute-start.12 = (f32[256,1024]{1,0:T(8,128)S(1)}, f32[256,1024]{1,0:T(8,128)S(1)}, u32[]{:S(2)}, u32[]{:S(2)}) collective-permute-start(f32[256,1024]{1,0:T(8,128)S(1)} %slice_select_fusion), channel_id=1, source_target_pairs={{0,32},{16,112},{32,0},{48,80},{64,96},{80,48},{96,64},{112,16},{1... | collective-permute-start | bytes 3145736 | tf_op jit(solution)/shard_map/ppermute | solution.py:628
  54.1 12.8 %collective-permute-start.10 = (f32[1,512,128]{2,1,0:T(8,128)S(1)}, f32[1,512,128]{2,1,0:T(8,128)S(1)}, u32[]{:S(2)}, u32[]{:S(2)}) collective-permute-start(f32[1,512,128]{2,1,0:T(8,128)S(1)} %get-tuple-element.157), channel_id=1, source_target_pairs={{0,3},{1,2},{2,1},{3,0},{4,7},{5,6},{6,5},{7,4},{8,11},{9,10},{10,... | collective-permute-start | bytes 786440 | tf_op jit(solution)/shard_map/ppermute | solution.py:641
  54.8 12.1 %collective-permute-start.11 = (f32[1,256,128]{2,1,0:T(8,128)S(1)}, f32[1,256,128]{2,1,0:T(8,128)S(1)}, u32[]{:S(2)}, u32[]{:S(2)}) collective-permute-start(f32[1,256,128]{2,1,0:T(8,128)S(1)} %select_bitcast_fusion), channel_id=1, source_target_pairs={{0,4},{1,5},{2,6},{3,7},{4,0},{5,1},{6,2},{7,3},{8,12},{9,13},{10,... | collective-permute-start | bytes 393224 | tf_op jit(solution)/shard_map/ppermute | solution.py:665
  56.2 10.8 %collective-permute-start.9 = (f32[1,512,128]{2,1,0:T(8,128)S(1)}, f32[1,512,128]{2,1,0:T(8,128)S(1)}, u32[]{:S(2)}, u32[]{:S(2)}) collective-permute-start(f32[1,512,128]{2,1,0:T(8,128)S(1)} %get-tuple-element.158), channel_id=1, source_target_pairs={{0,1},{1,0},{2,3},{3,2},{4,5},{5,4},{6,7},{7,6},{8,9},{9,8},{10,11... | collective-permute-start | bytes 786440 | tf_op jit(solution)/shard_map/ppermute | solution.py:641
  67.4 6.5 %collective-permute-start.15 = (f32[2,256,128]{2,1,0:T(8,128)S(1)}, f32[2,256,128]{2,1,0:T(8,128)S(1)}, u32[]{:S(2)}, u32[]{:S(2)}) collective-permute-start(f32[2,256,128]{2,1,0:T(8,128)S(1)} %pad_maximum_fusion.8), channel_id=1, source_target_pairs={{0,1},{1,0},{2,3},{3,2},{4,5},{5,4},{6,7},{7,6},{8,9},{9,8},{10,11... | collective-permute-start | bytes 786440 | tf_op jit(solution)/shard_map/ppermute | solution.py:665
  69.7 9.5 %collective-permute-start.13 = (f32[2,512,128]{2,1,0:T(8,128)S(1)}, f32[2,512,128]{2,1,0:T(8,128)S(1)}, u32[]{:S(2)}, u32[]{:S(2)}) collective-permute-start(f32[2,512,128]{2,1,0:T(8,128)S(1)} %pad_maximum_fusion.5), channel_id=1, source_target_pairs={{0,3},{1,2},{2,1},{3,0},{4,7},{5,6},{6,5},{7,4},{8,11},{9,10},{10,... | collective-permute-start | bytes 1572872 | tf_op jit(solution)/shard_map/ppermute | solution.py:641
  71.3 8.4 %collective-permute-start.16 = (f32[128,1024]{1,0:T(8,128)S(1)}, f32[128,1024]{1,0:T(8,128)S(1)}, u32[]{:S(2)}, u32[]{:S(2)}) collective-permute-start(f32[128,1024]{1,0:T(8,128)S(1)} %slice_select_fusion.1), channel_id=1, source_target_pairs={{0,96},{16,48},{32,64},{48,16},{64,32},{80,112},{96,0},{112,80},{1... | collective-permute-start | bytes 1572872 | tf_op jit(solution)/shard_map/ppermute | solution.py:628
  71.4 8.4 %collective-permute-start.14 = (f32[2,512,128]{2,1,0:T(8,128)S(1)}, f32[2,512,128]{2,1,0:T(8,128)S(1)}, u32[]{:S(2)}, u32[]{:S(2)}) collective-permute-start(f32[2,512,128]{2,1,0:T(8,128)S(1)} %pad_maximum_fusion.6), channel_id=1, source_target_pairs={{0,1},{1,0},{2,3},{3,2},{4,5},{5,4},{6,7},{7,6},{8,9},{9,8},{10,11... | collective-permute-start | bytes 1572872 | tf_op jit(solution)/shard_map/ppermute | solution.py:641
  79.9 8.4 %collective-permute-start.20 = (f32[128,1024]{1,0:T(8,128)S(1)}, f32[128,1024]{1,0:T(8,128)S(1)}, u32[]{:S(2)}, u32[]{:S(2)}) collective-permute-start(f32[128,1024]{1,0:T(8,128)S(1)} %select_add_fusion.1), channel_id=1, source_target_pairs={{0,96},{16,48},{32,64},{48,16},{64,32},{80,112},{96,0},{112,80},{1... | collective-permute-start | bytes 1572872 | tf_op jit(solution)/shard_map/ppermute | solution.py:631
  81.3 13.9 %collective-permute-start.17 = (f32[4,512,128]{2,1,0:T(8,128)S(1)}, f32[4,512,128]{2,1,0:T(8,128)S(1)}, u32[]{:S(2)}, u32[]{:S(2)}) collective-permute-start(f32[4,512,128]{2,1,0:T(8,128)S(1)} %pad_maximum_fusion.1.refs_0_), channel_id=1, source_target_pairs={{0,4},{1,5},{2,6},{3,7},{4,0},{5,1},{6,2},{7,3},{8,12},{9,13},{10,... | collective-permute-start | bytes 3145736 | tf_op jit(solution)/shard_map/ppermute | solution.py:641
  81.7 20.5 %collective-permute-start.18 = (f32[4,512,128]{2,1,0:T(8,128)S(1)}, f32[4,512,128]{2,1,0:T(8,128)S(1)}, u32[]{:S(2)}, u32[]{:S(2)}) collective-permute-start(f32[4,512,128]{2,1,0:T(8,128)S(1)} %pad_maximum_fusion.2.refs_4_), channel_id=1, source_target_pairs={{0,12},{1,13},{2,14},{3,15},{4,8},{5,9},{6,10},{7,11},{8,4},{9,5},... | collective-permute-start | bytes 3145736 | tf_op jit(solution)/shard_map/ppermute | solution.py:641
  82.4 10.7 %collective-permute-start.19 = (f32[4,256,128]{2,1,0:T(8,128)S(1)}, f32[4,256,128]{2,1,0:T(8,128)S(1)}, u32[]{:S(2)}, u32[]{:S(2)}) collective-permute-start(f32[4,256,128]{2,1,0:T(8,128)S(1)} %pad_maximum_fusion.7), channel_id=1, source_target_pairs={{0,3},{1,2},{2,1},{3,0},{4,7},{5,6},{6,5},{7,4},{8,11},{9,10},{10,... | collective-permute-start | bytes 1572872 | tf_op jit(solution)/shard_map/ppermute | solution.py:665
  83.2 9.9 %collective-permute-start.21 = (f32[5,128,128]{2,1,0:T(8,128)S(1)}, f32[5,128,128]{2,1,0:T(8,128)S(1)}, u32[]{:S(2)}, u32[]{:S(2)}) collective-permute-start(f32[5,128,128]{2,1,0:T(8,128)S(1)} %get-tuple-element.117), channel_id=1, source_target_pairs={{0,64},{16,80},{32,96},{48,112},{64,0},{80,16},{96,32},{112,48},{1... | collective-permute-start | bytes 983048 | tf_op jit(solution)/shard_map/ppermute | solution.py:599
  102.1 18.6 %copy-start = (f32[2,512,512]{2,1,0:T(8,128)S(1)}, f32[2,512,512]{2,1,0:T(8,128)}, u32[]{:S(2)}) copy-start(f32[2,512,512]{2,1,0:T(8,128)} %inverses.1) | copy-start | bytes 6291460
  102.1 18.4 %collective-permute-start.24 = (f32[256,1024]{1,0:T(8,128)S(1)}, f32[256,1024]{1,0:T(8,128)S(1)}, u32[]{:S(2)}, u32[]{:S(2)}) collective-permute-start(f32[256,1024]{1,0:T(8,128)S(1)} %pad_maximum_fusion.4), channel_id=1, source_target_pairs={{0,32},{16,112},{32,0},{48,80},{64,96},{80,48},{96,64},{112,16},{1... | collective-permute-start | bytes 3145736 | tf_op jit(solution)/shard_map/ppermute | solution.py:631
  103.2 17.5 %collective-permute-start.26 = (f32[8,256,128]{2,1,0:T(8,128)S(1)}, f32[8,256,128]{2,1,0:T(8,128)S(1)}, u32[]{:S(2)}, u32[]{:S(2)}) collective-permute-start(f32[8,256,128]{2,1,0:T(8,128)S(1)} %pad_maximum_fusion.3.own), channel_id=1, source_target_pairs={{0,16},{16,0},{32,48},{48,32},{64,80},{80,64},{96,112},{112,96},{1... | collective-permute-start | bytes 3145736 | tf_op jit(solution)/shard_map/ppermute | solution.py:599
  103.2 19.8 %collective-permute-start.22 = (f32[4,512,128]{2,1,0:T(8,128)S(1)}, f32[4,512,128]{2,1,0:T(8,128)S(1)}, u32[]{:S(2)}, u32[]{:S(2)}) collective-permute-start(f32[4,512,128]{2,1,0:T(8,128)S(1)} %pad_maximum_fusion.1.refs_0_), channel_id=1, source_target_pairs={{0,12},{1,13},{2,14},{3,15},{4,8},{5,9},{6,10},{7,11},{8,4},{9,5},... | collective-permute-start | bytes 3145736 | tf_op jit(solution)/shard_map/ppermute | solution.py:641
  105.3 17.7 %collective-permute-start.23 = (f32[4,512,128]{2,1,0:T(8,128)S(1)}, f32[4,512,128]{2,1,0:T(8,128)S(1)}, u32[]{:S(2)}, u32[]{:S(2)}) collective-permute-start(f32[4,512,128]{2,1,0:T(8,128)S(1)} %pad_maximum_fusion.2.refs_4_), channel_id=1, source_target_pairs={{0,4},{1,5},{2,6},{3,7},{4,0},{5,1},{6,2},{7,3},{8,12},{9,13},{10,... | collective-permute-start | bytes 3145736 | tf_op jit(solution)/shard_map/ppermute | solution.py:641
  105.3 17.7 %collective-permute-start.25 = (f32[5,128,128]{2,1,0:T(8,128)S(1)}, f32[5,128,128]{2,1,0:T(8,128)S(1)}, u32[]{:S(2)}, u32[]{:S(2)}) collective-permute-start(f32[5,128,128]{2,1,0:T(8,128)S(1)} %get-tuple-element.122), channel_id=1, source_target_pairs={{0,64},{16,80},{32,96},{48,112},{64,0},{80,16},{96,32},{112,48},{1... | collective-permute-start | bytes 983048 | tf_op jit(solution)/shard_map/ppermute | solution.py:599
  123.1 6.3 %collective-permute-start.30 = (f32[512,1024]{1,0:T(8,128)S(1)}, f32[512,1024]{1,0:T(8,128)S(1)}, u32[]{:S(2)}, u32[]{:S(2)}) collective-permute-start(f32[512,1024]{1,0:T(8,128)S(1)} %pad_maximum_fusion.own), channel_id=1, source_target_pairs={{0,16},{16,0},{32,48},{48,32},{64,80},{80,64},{96,112},{112,96},{1... | collective-permute-start | bytes 6291464 | tf_op jit(solution)/shard_map/ppermute | solution.py:599
  125.6 15.2 %collective-permute-start.27 = (f32[4,512,128]{2,1,0:T(8,128)S(1)}, f32[4,512,128]{2,1,0:T(8,128)S(1)}, u32[]{:S(2)}, u32[]{:S(2)}) collective-permute-start(f32[4,512,128]{2,1,0:T(8,128)S(1)} %collective-permute-done.17.refs_1_), channel_id=1, source_target_pairs={{0,12},{1,13},{2,14},{3,15},{4,8},{5,9},{6,10},{7,11},{8,4},{9,5},... | collective-permute-start | bytes 3145736 | tf_op jit(solution)/shard_map/ppermute | solution.py:641
  127.1 13.9 %collective-permute-start.28 = (f32[4,512,128]{2,1,0:T(8,128)S(1)}, f32[4,512,128]{2,1,0:T(8,128)S(1)}, u32[]{:S(2)}, u32[]{:S(2)}) collective-permute-start(f32[4,512,128]{2,1,0:T(8,128)S(1)} %collective-permute-done.18.refs_5_), channel_id=1, source_target_pairs={{0,4},{1,5},{2,6},{3,7},{4,0},{5,1},{6,2},{7,3},{8,12},{9,13},{10,... | collective-permute-start | bytes 3145736 | tf_op jit(solution)/shard_map/ppermute | solution.py:641
  127.1 11.5 %collective-permute-start.29 = (f32[5,128,128]{2,1,0:T(8,128)S(1)}, f32[5,128,128]{2,1,0:T(8,128)S(1)}, u32[]{:S(2)}, u32[]{:S(2)}) collective-permute-start(f32[5,128,128]{2,1,0:T(8,128)S(1)} %get-tuple-element.131), channel_id=1, source_target_pairs={{0,64},{16,80},{32,96},{48,112},{64,0},{80,16},{96,32},{112,48},{1... | collective-permute-start | bytes 983048 | tf_op jit(solution)/shard_map/ppermute | solution.py:599
  137.2 1.3 copy-start.1
  141.0 25.1 %collective-permute-start.31 = (f32[5,128,128]{2,1,0:T(8,128)S(1)}, f32[5,128,128]{2,1,0:T(8,128)S(1)}, u32[]{:S(2)}, u32[]{:S(2)}) collective-permute-start(f32[5,128,128]{2,1,0:T(8,128)S(1)} %get-tuple-element.150), channel_id=1, source_target_pairs={{0,64},{16,80},{32,96},{48,112},{64,0},{80,16},{96,32},{112,48},{1... | collective-permute-start | bytes 983048 | tf_op jit(solution)/shard_map/ppermute | solution.py:599
  142.3 23.8 %collective-permute-start.32 = (f32[10,128,128]{2,1,0:T(8,128)S(1)}, f32[10,128,128]{2,1,0:T(8,128)S(1)}, u32[]{:S(2)}, u32[]{:S(2)}) collective-permute-start(f32[10,128,128]{2,1,0:T(8,128)S(1)} %get-tuple-element.151), channel_id=1, source_target_pairs={{0,64},{16,80},{32,96},{48,112},{64,0},{80,16},{96,32},{112,48},{1... | collective-permute-start | bytes 1966088 | tf_op jit(solution)/shard_map/ppermute | solution.py:599
  144.0 1.6 copy-start.2

commit v5 on v4

--- a/solution.py
+++ b/solution.py
@@ -95,8 +95,15 @@
         pltpu.make_async_copy(front.at[:, pl.ds(0, BLK)], panel, sem.at[2]),
     ]
     writes = []
-    places = (0, 0), (1, 0), (1, 5), (2, 0), (2, 5), (3, 0)
-    for n, ((j, start), target) in enumerate(zip(places, rests)):
+    rest_a, rest_b, rest_c = rests
+    parts = (
+        (0, 0, rest_a),
+        (1, 0, rest_b),
+        (1, 5, rest_c.at[pl.ds(0, 5)]),
+        (2, 0, rest_c.at[pl.ds(5, 10)]),
+        (3, 0, rest_c.at[pl.ds(15, 10)]),
+    )
+    for n, (j, start, target) in enumerate(parts):
         d = j + (j >= place).astype(jnp.int32)
         source = sending.at[pl.ds(start, target.shape[0]), :, columns(d)]
         writes.append(pltpu.make_async_copy(source, target, sem.at[3 + n]))
@@ -163,28 +170,24 @@
 
 def prepare(maps, pivots, front, pieces, first):
     column = jax.ShapeDtypeStruct((10, BLK, BLK), F32)
-    half = jax.ShapeDtypeStruct((5, BLK, BLK), F32)
     return pl.pallas_call(
         prepare_kernel,
         out_shape=[
             column,
-            half,
-            half,
-            half,
-            half,
-            column,
+            jax.ShapeDtypeStruct((5, BLK, BLK), F32),
+            jax.ShapeDtypeStruct((25, BLK, BLK), F32),
             jax.ShapeDtypeStruct((2048, BLK), F32),
             jax.ShapeDtypeStruct((256, BLK), F32),
             jax.ShapeDtypeStruct((256, BLK), F32),
             jax.ShapeDtypeStruct((64,), jnp.int32),
         ],
         in_specs=[SMEM, VMEM, HBM, HBM, VMEM],
-        out_specs=[HBM] * 6 + [VMEM, VMEM, VMEM, SMEM],
+        out_specs=[HBM] * 3 + [VMEM, VMEM, VMEM, SMEM],
         scratch_shapes=[
             pltpu.VMEM((10, BLK, 640), F32),
             pltpu.VMEM((10, BLK, BLK), F32),
             pltpu.VMEM((PANEL, BLK), F32),
-            pltpu.SemaphoreType.DMA((9,)),
+            pltpu.SemaphoreType.DMA((8,)),
         ],
         compiler_params=params(24),
         cost_estimate=cost(0, 9 * MIB),
@@ -397,7 +400,7 @@
         out_shape=[shape, shape, jax.ShapeDtypeStruct((PANEL, 1024), F32)],
         in_specs=[SMEM] + [VMEM] * 5,
         out_specs=[VMEM] * 3,
-        compiler_params=params(34),
+        compiler_params=params(24),
         cost_estimate=cost(4 * 6 * PANEL * PANEL * 1024, 14 * MIB),
         name="right_factor",
     )(table, own, swapped, *factors, cross)
@@ -457,7 +460,7 @@
 
 def update_kernel(table, front, *refs):
     blocks = refs[:4], refs[4:8]
-    right_h, right_l, marks, got_b, got_c, got_d, out, panels = refs[8:]
+    right_h, right_l, marks, got_b, out, panels = refs[8:]
     step = pl.program_id(0)
     span = pl.ds(pl.multiple_of(step % 2 * 256, 256), 256)
     col, core = table[COL], table[ROW] % 2
@@ -484,19 +487,20 @@
     for which in range(2):
         pl.when(step // 2 == which)(functools.partial(assemble, which))
 
-    change = dot3((panels[0], panels[1]), (right_h[...], right_l[...])).reshape(2, 256, 1024)
     active = marks[...] == 0
-    for j in range(8):
-        columns = slice(j * BLK, (j + 1) * BLK)
-        before, part = front[:, :, columns], change[:, :, columns]
-        after = before - part
-        if j == 0:
-            after = jnp.where(col < 8, part, after)
-        out[:, :, columns] = jnp.where(active, after, before)
-
-    def columns_of(j):
-        return pl.ds(pl.multiple_of(table[GOT_COL + j] * BLK, BLK), BLK)
-
+    for piece in range(4):
+        wide = slice(piece * 256, (piece + 1) * 256)
+        change = dot3((panels[0], panels[1]), (right_h[:, wide], right_l[:, wide]))
+        change = change.reshape(2, 256, 256)
+        for j in range(2):
+            columns = slice(piece * 256 + j * BLK, piece * 256 + (j + 1) * BLK)
+            before, part = front[:, :, columns], change[:, :, j * BLK : (j + 1) * BLK]
+            after = before - part
+            if piece == 0 and j == 0:
+                after = jnp.where(col < 8, part, after)
+            out[:, :, columns] = jnp.where(active, after, before)
+
+    columns_b = pl.ds(pl.multiple_of(table[GOT_COL + 2] * BLK, BLK), BLK)
     for part in range(4):
         half, rest = part // 2, part % 2
         rows = slice(rest * BLK, (rest + 1) * BLK)
@@ -504,15 +508,10 @@
 
         @pl.when((m >= 0) & (m < 5))
         def _(half=half, rows=rows, m=m):
-            out[half, rows, columns_of(2)] += got_b[m]
-            out[half, rows, columns_of(3)] += got_d[m]
-
-        @pl.when(m >= 5)
-        def _(half=half, rows=rows, m=m):
-            out[half, rows, columns_of(2)] += got_c[m - 5]
-
-
-def update(table, front, blocks, right, marks, got):
+            out[half, rows, columns_b] += got_b[m]
+
+
+def update(table, front, blocks, right, marks, got_b):
     tile = pl.BlockSpec((2, 256, 1024), lambda t, s: (0, t, 0))
     return pl.pallas_call(
         update_kernel,
@@ -524,39 +523,39 @@
                 tile,
                 *[VMEM] * 10,
                 pl.BlockSpec((2, 256, BLK), lambda t, s: (0, t, 0)),
-                *[VMEM] * 3,
+                VMEM,
             ],
             out_specs=tile,
             scratch_shapes=[pltpu.VMEM((2, PANEL, 1024), BF16)],
         ),
-        compiler_params=params(34),
+        compiler_params=params(24),
         cost_estimate=cost(6 * 2048 * 1024 * 1024, 32 * MIB),
         name="update",
-    )(table, in_hbm(front), *blocks[0], *blocks[1], *right, marks.reshape(2, 1024, BLK), *got)
+    )(table, in_hbm(front), *blocks[0], *blocks[1], *right, marks.reshape(2, 1024, BLK), got_b)
 
 
 def finish_kernel(
-    table, list_other, list_mine, front, got_e, got_f, patch,
+    table, list_other, list_mine, front, got, patch,
     out, held, read_sem, write_sem, sem,
 ):
     del front
     core = table[ROW] % 2
     copies = []
-    for n, (column, first, got) in enumerate([(3, 5, got_e), (4, 0, got_f)]):
+    places = [(2, m) for m in range(5, 10)] + [(j, m) for j in (3, 4) for m in range(10)]
+    for n, (column, m) in enumerate(places):
         columns = pl.ds(pl.multiple_of(table[GOT_COL + column] * BLK, BLK), BLK)
-        for m in range(got.shape[0]):
-            rows = pl.ds(pl.multiple_of(table[GOT_ROW + first + m] * BLK, BLK), BLK)
-            there, here = out.at[rows, columns], held.at[n, m]
-            read = pltpu.make_async_copy(there, here, read_sem.at[n, m])
-            write = pltpu.make_async_copy(here, there, write_sem.at[n, m])
-            copies.append((read, write, n, m, got))
-    for read, *_ in copies:
+        rows = pl.ds(pl.multiple_of(table[GOT_ROW + m] * BLK, BLK), BLK)
+        there, here = out.at[rows, columns], held.at[n]
+        read = pltpu.make_async_copy(there, here, read_sem.at[n])
+        write = pltpu.make_async_copy(here, there, write_sem.at[n])
+        copies.append((read, write))
+    for read, _ in copies:
         read.start()
-    for read, write, n, m, got in copies:
+    for n, (read, write) in enumerate(copies):
         read.wait()
-        held[n, m] += got[m]
+        held[n] += got[n]
         write.start()
-    for _, write, *_ in copies:
+    for _, write in copies:
         write.wait()
 
     def entry(n):
@@ -579,19 +578,19 @@
     return pl.pallas_call(
         finish_kernel,
         out_shape=jax.ShapeDtypeStruct((2048, 1024), F32),
-        in_specs=[SMEM, SMEM, SMEM, HBM] + [VMEM] * 3,
+        in_specs=[SMEM, SMEM, SMEM, HBM] + [VMEM] * 2,
         out_specs=HBM,
         scratch_shapes=[
-            pltpu.VMEM((2, 10, BLK, BLK), F32),
-            pltpu.SemaphoreType.DMA((2, 10)),
-            pltpu.SemaphoreType.DMA((2, 10)),
+            pltpu.VMEM((25, BLK, BLK), F32),
+            pltpu.SemaphoreType.DMA((25,)),
+            pltpu.SemaphoreType.DMA((25,)),
             pltpu.SemaphoreType.DMA(()),
         ],
         input_output_aliases={3: 0},
         compiler_params=params(12),
         cost_estimate=cost(0, 8 * MIB),
         name="finish",
-    )(table, *lists, front, *got, patch)
+    )(table, *lists, front, got, patch)
 
 
 def swap(block, axis, partner):
@@ -643,7 +642,7 @@
     first = cut(child_maps, pieces)
     got0 = by_row(first, 4)
     *rest, panel, corner, away, table = prepare(child_maps, pivots, front, pieces, first)
-    rest_a, rest_b, rest_c, rest_d, rest_e, rest_f = rest
+    rest_a, rest_b, rest_c = rest
     corner = corner + by_row(away, 1)
     corner = corner + (by_row(corner, 2) + (by_row(corner, 6) + by_row(corner, 4)))
     away_rows, marks, list_other = pivot_terms(child_maps, pivots, front, children)
@@ -672,30 +671,25 @@
         total = halve(total, k)
         if k == 0:
             front = extend(table, front, pieces, (got0, got_a))
-        held, corner, total, rest_b, front = together((held, corner, total, rest_b, front))
+        held, corner, total, front = together((held, corner, total, front))
     came = [gather_step(held[w], w, 2) for w in range(2)]
     corner = corner_step(corner, 2)
-    total = double(total, 1)
+    total, rest_b = together((double(total, 1), rest_b))
     got_b = by_row(rest_b, 4)
-    came, corner, total, got_b, rest_c = together((came, corner, total, got_b, rest_c))
+    came, corner, total, got_b = together((came, corner, total, got_b))
     held_far = [gather_step(held[w], w, 3) for w in range(2)]
     *factors, cross = corners(table, corner, by_row(corner, 1), diag_inverses)
     total = double(total, 0)
-    got_c = by_row(rest_c, 4)
-    came, held_far, total, got_c, rest_d, factors, cross = together(
-        (came, held_far, total, got_c, rest_d, factors, cross)
+    came, held_far, total, rest_c, factors, cross = together(
+        (came, held_far, total, rest_c, factors, cross)
     )
     came_far = [gather_step(came[w], w, 3) for w in range(2)]
-    got_d = by_row(rest_d, 4)
+    got_c = by_row(rest_c, 4)
     *right, patch = right_factor(table, total, by_row(total, 1), factors, cross)
-    came_far, got_d, rest_e, rest_f, right, patch = together(
-        (came_far, got_d, rest_e, rest_f, right, patch)
-    )
-    got_e, got_f = by_row(rest_e, 4), by_row(rest_f, 4)
+    came_far, right, patch = together((came_far, right, patch))
     blocks = [(held[w], came[w], held_far[w], came_far[w]) for w in range(2)]
-    front = update(table, front, blocks, right, marks, (got_b, got_c, got_d))
-    front = front.reshape(2048, 1024)
-    return finish(table, (list_other, list_mine), front, (got_e, got_f), patch)
+    front = update(table, front, blocks, right, marks, got_b).reshape(2048, 1024)
+    return finish(table, (list_other, list_mine), front, got_c, patch)
 
 
 def solution(mesh):

time: 172 us -> 168 us (0.977)
  local copies, waits for them, and re-layouts: 2.94 us -> 0.04 us
    ppermute x14 -> x11, waiting for transfers between devices: 6.21 us -> 11.9 us  [swap(): return lax.ppermute(block, axis, [(i, partner(i)) for i in range(count)])]
    unnamed x6 -> x2, local copies, waits for them, and re-layouts: 2.91 us -> 0.01 us
    ppermute x3, waiting for transfers between devices: 6.11 us -> 3.7 us  [corner_step(): lax.ppermute(block, ('row', 'col'), route)]
    ppermute x2, waiting for transfers between devices: 17.9 us -> 15.9 us  [double(): came = lax.ppermute(part, 'row', rings[step])]
    ppermute x10, waiting for transfers between devices: 16.7 us -> 14.9 us  [gather_step(): return lax.ppermute(block, ('row', 'col'), route)]
    ppermute x14 -> x11, starting transfers between devices: 21.3 us -> 21.6 us  [swap(): return lax.ppermute(block, axis, [(i, partner(i)) for i in range(count)])]
  transfers between devices with their start and end apart: 33 -> 30, of which waited for: 15 -> 18; matrix products, arithmetic and copies ran while one was open for 1% -> 1% of each run, Pallas kernels for 38% -> 39%
where the time goes in v5:
time: 168 us; the launch traced here: 166 us
  Pallas kernels  71.2 us (42%)
  waiting for transfers between devices  48.8 us (29%)
  starting transfers between devices  43.8 us (26%)
  other arithmetic  2.11 us (1%)
    ppermute x11, starting transfers between devices, swap(): return lax.ppermute(block, axis, [(i, partner(i)) for i in range(count)])  21.6 us
    pallas_call x1, Pallas kernels, update(): pl.pallas_call(update_kernel, out_shape=pltpu.HBM((2, 1024, 1024), F32),...  20.3 us
    pallas_call x2, Pallas kernels, pivot_terms(): pl.pallas_call(functools.partial(pivot_kernel, mine_half), out_shape=[jax...  18.2 us
    ppermute x2, waiting for transfers between devices, double(): came = lax.ppermute(part, 'row', rings[step])  15.9 us
    ppermute x10, waiting for transfers between devices, gather_step(): return lax.ppermute(block, ('row', 'col'), route)  14.9 us
    ppermute x11, waiting for transfers between devices, swap(): return lax.ppermute(block, axis, [(i, partner(i)) for i in range(count)])  11.9 us
    pallas_call x1, Pallas kernels, extend(): pl.pallas_call(functools.partial(extend_kernel, len(got)), out_shape=pltp...  10.8 us
    pallas_call x1, Pallas kernels, right_factor(): pl.pallas_call(factor_kernel, out_shape=[shape, shape, jax.ShapeDtypeStru...  7.86 us
  transfers between devices with their start and end apart: 30, of which 18 were waited for; matrix products, arithmetic and copies ran while one was open for 1% of the time, Pallas kernels for 39%

profile of v5, /device:TPU:1, one launch (start us, length us, event | category | flops | bytes accessed | tf_op | source)
XLA Modules:
  0.0 166.4 jit_solution(5264988651813664703)
XLA Ops:
  0.0 1.8 %cut.1.first = f32[10,128,128]{2,1,0:T(8,128)S(1)} custom-call(s32[2,80]{1,0:T(2,128)} %maps.7, f32[10,2,128,640]{3,2,1,0:T(8,128)} %bitcast.12), custom_call_target="tpu_custom_call" | custom-call | bytes 1048576 | tf_op jit(solution)/shard_map/cut/pallas_call | solution.py:67
  1.9 4.5 %collective-permute-start = (f32[10,128,128]{2,1,0:T(8,128)S(1)}, f32[10,128,128]{2,1,0:T(8,128)S(1)}, u32[]{:S(2)}, u32[]{:S(2)}) collective-permute-start(f32[10,128,128]{2,1,0:T(8,128)S(1)} %cut.1.first), channel_id=1, source_target_pairs={{0,64},{16,80},{32,96},{48,112},{64,0},{80,16},{96,32},{112,48},{1... | collective-permute-start | bytes 1966088 | tf_op jit(solution)/shard_map/ppermute | solution.py:598
  6.4 5.1 %prepare.1 = (f32[10,128,128]{2,1,0:T(8,128)S(1)}, f32[5,128,128]{2,1,0:T(8,128)S(1)}, f32[25,128,128]{2,1,0:T(8,128)S(1)}, f32[2048,128]{1,0:T(8,128)S(1)}, f32...) custom-call(s32[2,80]{1,0:T(2,128)} %maps.7, s32[8,128]{1,0:T(8,128)} %bitcast.18, f32[2048,1024]{1,0:T(8,128)} %front.5, ...), custom_call_target="tpu_custom_call" | custom-call | bytes 9437184 | tf_op jit(solution)/shard_map/prepare/pallas_call | solution.py:173
  11.5 1.0 collective-permute-start.1
  12.5 1.0 collective-permute-done.1
  13.6 3.1 %collective-permute-start.3 = (f32[256,128]{1,0:T(8,128)S(1)}, f32[256,128]{1,0:T(8,128)S(1)}, u32[]{:S(2)}, u32[]{:S(2)}) collective-permute-start(f32[256,128]{1,0:T(8,128)S(1)} %add.21), channel_id=1, source_target_pairs={{0,96},{16,112},{32,64},{48,80},{64,32},{80,48},{96,0},{112,16},{1... | collective-permute-start | bytes 393224 | tf_op jit(solution)/shard_map/ppermute | solution.py:598
  16.7 9.4 %pivot_terms_other.1 = (f32[512,1024]{1,0:T(8,128)S(1)}, f32[2048,128]{1,0:T(8,128)S(1)}, s32[513]{0:T(1024)S(1)}) custom-call(s32[2,80]{1,0:T(2,128)} %maps.7, s32[1024]{0:T(1024)} %pivots.1, f32[2048,1024]{1,0:T(8,128)} %front.5, f32[2560,640]{1,0:T(8,128)} %children.3), custom_call_target="tpu_custom_call" | custom-call | bytes 25165824 | tf_op jit(solution)/shard_map/pivot_terms_other/pallas_call | solution.py:266
  26.1 1.1 collective-permute-done.3
  27.2 1.3 collective-permute-start.7
  28.6 0.8 whole_panel.1
  29.4 4.5 %collective-permute-start.5 = (f32[1024,128]{1,0:T(8,128)S(1)}, f32[1024,128]{1,0:T(8,128)S(1)}, u32[]{:S(2)}, u32[]{:S(2)}) collective-permute-start(f32[1024,128]{1,0:T(8,128)S(1)} %get-tuple-element.85), channel_id=1, source_target_pairs={{0,12},{1,13},{2,14},{3,15},{4,8},{5,9},{6,10},{7,11},{16,28},{17,... | collective-permute-start | bytes 1572872 | tf_op jit(solution)/shard_map/ppermute | solution.py:602
  33.9 2.4 %collective-permute-start.8 = (f32[10,128,128]{2,1,0:T(8,128)S(1)}, f32[10,128,128]{2,1,0:T(8,128)S(1)}, u32[]{:S(2)}, u32[]{:S(2)}) collective-permute-start(f32[10,128,128]{2,1,0:T(8,128)S(1)} %get-tuple-element.89), channel_id=1, source_target_pairs={{0,64},{16,80},{32,96},{48,112},{64,0},{80,16},{96,32},{112,48},{1... | collective-permute-start | bytes 1966088 | tf_op jit(solution)/shard_map/ppermute | solution.py:598
  36.3 1.3 collective-permute-start.6
  37.6 8.8 %pivot_terms_mine.1 = (f32[512,1024]{1,0:T(8,128)S(1)}, f32[2048,128]{1,0:T(8,128)S(1)}, s32[513]{0:T(1024)S(1)}) custom-call(s32[2,80]{1,0:T(2,128)} %maps.7, s32[1024]{0:T(1024)} %pivots.1, f32[2048,1024]{1,0:T(8,128)} %front.5, f32[2560,640]{1,0:T(8,128)} %children.3, f32[2048,128]{1,0:T(8,128)S(1)} %get-tuple-element.79.refs_0_), custom_call_target="tpu_custom_call" | custom-call | bytes 25165824 | tf_op jit(solution)/shard_map/pivot_terms_mine/pallas_call | solution.py:266
  46.4 1.5 collective-permute-done.6
  48.1 0.4 add.25
  48.5 3.0 %collective-permute-done.8.refs_4_.refs_5_ = f32[10,128,128]{2,1,0:T(8,128)S(1)} collective-permute-done((f32[10,128,128]{2,1,0:T(8,128)S(1)}, f32[10,128,128]{2,1,0:T(8,128)S(1)}, u32[]{:S(2)}, u32[]{:S(2)}) %collective-permute-start.8) | collective-permute-done | bytes 655392 | tf_op jit(solution)/shard_map/ppermute | solution.py:598
  51.7 2.6 %collective-permute-start.12 = (f32[256,1024]{1,0:T(8,128)S(1)}, f32[256,1024]{1,0:T(8,128)S(1)}, u32[]{:S(2)}, u32[]{:S(2)}) collective-permute-start(f32[256,1024]{1,0:T(8,128)S(1)} %slice_select_fusion), channel_id=1, source_target_pairs={{0,32},{16,112},{32,0},{48,80},{64,96},{80,48},{96,64},{112,16},{1... | collective-permute-start | bytes 3145736 | tf_op jit(solution)/shard_map/ppermute | solution.py:627
  54.3 0.5 collective-permute-start.10
  54.8 1.2 collective-permute-start.11
  56.0 10.8 %extend.1.front = f32[2,1024,1024]{2,1,0:T(8,128)} custom-call(s32[64]{0:T(128)S(1)} %get-tuple-element.72.table, f32[2,1024,1024]{2,1,0:T(8,128)} %bitcast.16, f32[10,2,128,640]{3,2,1,0:T(8,128)} %bitcast.14, f32[10,2,128,640]{3,2,1,0:T(8,128)} %bitcast.15, f32[10,128,128]{2,1,0:T(8,128)S(1)} %collective-permute-done.got.refs_2_.refs_3_, ...), custom_call_target="tpu_custom_call" | custom-call | bytes 1048576 | tf_op jit(solution)/shard_map/extend/pallas_call | solution.py:443
  67.3 2.2 %collective-permute-start.15 = (f32[2,256,128]{2,1,0:T(8,128)S(1)}, f32[2,256,128]{2,1,0:T(8,128)S(1)}, u32[]{:S(2)}, u32[]{:S(2)}) collective-permute-start(f32[2,256,128]{2,1,0:T(8,128)S(1)} %pad_maximum_fusion.8), channel_id=1, source_target_pairs={{0,1},{1,0},{2,3},{3,2},{4,5},{5,4},{6,7},{7,6},{8,9},{9,8},{10,11... | collective-permute-start | bytes 786440 | tf_op jit(solution)/shard_map/ppermute | solution.py:664
  69.5 2.0 %collective-permute-start.13 = (f32[2,512,128]{2,1,0:T(8,128)S(1)}, f32[2,512,128]{2,1,0:T(8,128)S(1)}, u32[]{:S(2)}, u32[]{:S(2)}) collective-permute-start(f32[2,512,128]{2,1,0:T(8,128)S(1)} %pad_maximum_fusion.5), channel_id=1, source_target_pairs={{0,3},{1,2},{2,1},{3,0},{4,7},{5,6},{6,5},{7,4},{8,11},{9,10},{10,... | collective-permute-start | bytes 1572872 | tf_op jit(solution)/shard_map/ppermute | solution.py:640
  71.7 0.9 collective-permute-start.14
  72.6 1.2 collective-permute-done.15
  73.9 5.1 %collective-permute-done.13 = f32[2,512,128]{2,1,0:T(8,128)S(1)} collective-permute-done((f32[2,512,128]{2,1,0:T(8,128)S(1)}, f32[2,512,128]{2,1,0:T(8,128)S(1)}, u32[]{:S(2)}, u32[]{:S(2)}) %collective-permute-start.13) | collective-permute-done | bytes 524320 | tf_op jit(solution)/shard_map/ppermute | solution.py:640
  79.1 0.9 collective-permute-done.16
  80.2 1.4 collective-permute-start.20
  81.9 0.7 collective-permute-start.18
  82.6 0.9 collective-permute-start.19
  83.5 5.1 %collective-permute-done.20 = f32[128,1024]{1,0:T(8,128)S(1)} collective-permute-done((f32[128,1024]{1,0:T(8,128)S(1)}, f32[128,1024]{1,0:T(8,128)S(1)}, u32[]{:S(2)}, u32[]{:S(2)}) %collective-permute-start.20) | collective-permute-done | bytes 524320 | tf_op jit(solution)/shard_map/ppermute | solution.py:630
  88.8 2.1 %collective-permute-start.21 = (f32[5,128,128]{2,1,0:T(8,128)S(1)}, f32[5,128,128]{2,1,0:T(8,128)S(1)}, u32[]{:S(2)}, u32[]{:S(2)}) collective-permute-start(f32[5,128,128]{2,1,0:T(8,128)S(1)} %get-tuple-element.109), channel_id=1, source_target_pairs={{0,64},{16,80},{32,96},{48,112},{64,0},{80,16},{96,32},{112,48},{1... | collective-permute-start | bytes 983048 | tf_op jit(solution)/shard_map/ppermute | solution.py:598
  90.9 2.5 %collective-permute-done.19 = f32[4,256,128]{2,1,0:T(8,128)S(1)} collective-permute-done((f32[4,256,128]{2,1,0:T(8,128)S(1)}, f32[4,256,128]{2,1,0:T(8,128)S(1)}, u32[]{:S(2)}, u32[]{:S(2)}) %collective-permute-start.19) | collective-permute-done | bytes 524320 | tf_op jit(solution)/shard_map/ppermute | solution.py:664
  93.4 3.0 %collective-permute-done.21.refs_11_ = f32[5,128,128]{2,1,0:T(8,128)S(1)} collective-permute-done((f32[5,128,128]{2,1,0:T(8,128)S(1)}, f32[5,128,128]{2,1,0:T(8,128)S(1)}, u32[]{:S(2)}, u32[]{:S(2)}) %collective-permute-start.21) | collective-permute-done | bytes 327712 | tf_op jit(solution)/shard_map/ppermute | solution.py:598
  96.4 5.9 %collective-permute-done.18.refs_5_ = f32[4,512,128]{2,1,0:T(8,128)S(1)} collective-permute-done((f32[4,512,128]{2,1,0:T(8,128)S(1)}, f32[4,512,128]{2,1,0:T(8,128)S(1)}, u32[]{:S(2)}, u32[]{:S(2)}) %collective-permute-start.18) | collective-permute-done | bytes 1048608 | tf_op jit(solution)/shard_map/ppermute | solution.py:640
  102.4 4.4 %collective-permute-start.25 = (f32[8,256,128]{2,1,0:T(8,128)S(1)}, f32[8,256,128]{2,1,0:T(8,128)S(1)}, u32[]{:S(2)}, u32[]{:S(2)}) collective-permute-start(f32[8,256,128]{2,1,0:T(8,128)S(1)} %pad_maximum_fusion.3.own), channel_id=1, source_target_pairs={{0,16},{16,0},{32,48},{48,32},{64,80},{80,64},{96,112},{112,96},{1... | collective-permute-start | bytes 3145736 | tf_op jit(solution)/shard_map/ppermute | solution.py:598
  106.7 1.0 collective-permute-start.24
  107.8 1.3 collective-permute-start.22
  109.1 2.0 %corners.1 = (bf16[3,512,512]{2,1,0:T(8,128)(2,1)S(1)}, bf16[3,512,512]{2,1,0:T(8,128)(2,1)S(1)}, f32[512,512]{1,0:T(8,128)S(1)}) custom-call(s32[64]{0:T(128)S(1)} %get-tuple-element.72.table, f32[8,256,128]{2,1,0:T(8,128)S(1)} %pad_maximum_fusion.3.own, f32[8,256,128]{2,1,0:T(8,128)S(1)} %collective-permute-done.25.swapped, f32[2,512,512]{2,1,0:T(8,128)S(1)} %copy-done), custom_call_target="tpu_custom_call" | custom-call | flops 805306368 | bytes 8388608 | tf_op jit(solution)/shard_map/corners/pallas_call | solution.py:344
  111.1 10.8 %collective-permute-done.24 = f32[256,1024]{1,0:T(8,128)S(1)} collective-permute-done((f32[256,1024]{1,0:T(8,128)S(1)}, f32[256,1024]{1,0:T(8,128)S(1)}, u32[]{:S(2)}, u32[]{:S(2)}) %collective-permute-start.24) | collective-permute-done | bytes 1048608 | tf_op jit(solution)/shard_map/ppermute | solution.py:630
  122.3 0.3 collective-permute-done.22.refs_2_
  122.9 1.3 collective-permute-start.26
  124.2 2.4 %collective-permute-start.29 = (f32[25,128,128]{2,1,0:T(8,128)S(1)}, f32[25,128,128]{2,1,0:T(8,128)S(1)}, u32[]{:S(2)}, u32[]{:S(2)}) collective-permute-start(f32[25,128,128]{2,1,0:T(8,128)S(1)} %get-tuple-element.135), channel_id=1, source_target_pairs={{0,64},{16,80},{32,96},{48,112},{64,0},{80,16},{96,32},{112,48},{1... | collective-permute-start | bytes 4915208 | tf_op jit(solution)/shard_map/ppermute | solution.py:598
  126.9 7.9 %right_factor.1 = (bf16[1024,1024]{1,0:T(8,128)(2,1)S(1)}, bf16[1024,1024]{1,0:T(8,128)(2,1)S(1)}, f32[512,1024]{1,0:T(8,128)S(1)}) custom-call(s32[64]{0:T(128)S(1)} %get-tuple-element.72.table, f32[512,1024]{1,0:T(8,128)S(1)} %pad_maximum_fusion.own, f32[512,1024]{1,0:T(8,128)S(1)} %collective-permute-done.28.swapped, ...), custom_call_target="tpu_custom_call" | custom-call | flops 6442450944 | bytes 14680064 | tf_op jit(solution)/shard_map/right_factor/pallas_call | solution.py:398
  134.7 3.4 %collective-permute-done.26.refs_3_ = f32[4,512,128]{2,1,0:T(8,128)S(1)} collective-permute-done((f32[4,512,128]{2,1,0:T(8,128)S(1)}, f32[4,512,128]{2,1,0:T(8,128)S(1)}, u32[]{:S(2)}, u32[]{:S(2)}) %collective-permute-start.26) | collective-permute-done | bytes 1048608 | tf_op jit(solution)/shard_map/ppermute | solution.py:640
  138.1 20.3 %update.1 = f32[2,1024,1024]{2,1,0:T(8,128)} custom-call(s32[64]{0:T(128)S(1)} %get-tuple-element.72.table, f32[2,1024,1024]{2,1,0:T(8,128)} %extend.1.front, f32[4,512,128]{2,1,0:T(8,128)S(1)} %pad_maximum_fusion.1.refs_0_, f32[4,512,128]{2,1,0:T(8,128)S(1)} %collective-permute-done.17.refs_1_, f32[4,512,128]{2,1,0:T(8,128)S(1)} %collective-permute-done.22.refs_2_, ...), custom_call_target="tpu_custom_call" | custom-call | flops 12884901888 | bytes 33554432 | tf_op jit(solution)/shard_map/update/pallas_call | solution.py:516
  158.5 3.5 %collective-permute-done.29.got = f32[25,128,128]{2,1,0:T(8,128)S(1)} collective-permute-done((f32[25,128,128]{2,1,0:T(8,128)S(1)}, f32[25,128,128]{2,1,0:T(8,128)S(1)}, u32[]{:S(2)}, u32[]{:S(2)}) %collective-permute-start.29) | collective-permute-done | bytes 1638432 | tf_op jit(solution)/shard_map/ppermute | solution.py:598
  162.0 4.2 %finish.1 = f32[2048,1024]{1,0:T(8,128)} custom-call(s32[64]{0:T(128)S(1)} %get-tuple-element.72.table, s32[513]{0:T(1024)S(1)} %get-tuple-element.73.list_other, s32[513]{0:T(1024)S(1)} %get-tuple-element.80.list_mine, f32[2048,1024]{1,0:T(8,128)} %bitcast.17, f32[25,128,128]{2,1,0:T(8,128)S(1)} %collective-permute-done.29.got, ...), custom_call_target="tpu_custom_call", output_to_operand_aliasing={{}: (3, {})} | custom-call | bytes 8388608 | tf_op jit(solution)/shard_map/finish/pallas_call | solution.py:578
  (45 shorter events, 2.8 us)
Async XLA Ops:
  1.9 25.4 %collective-permute-start = (f32[10,128,128]{2,1,0:T(8,128)S(1)}, f32[10,128,128]{2,1,0:T(8,128)S(1)}, u32[]{:S(2)}, u32[]{:S(2)}) collective-permute-start(f32[10,128,128]{2,1,0:T(8,128)S(1)} %cut.1.first), channel_id=1, source_target_pairs={{0,64},{16,80},{32,96},{48,112},{64,0},{80,16},{96,32},{112,48},{1... | collective-permute-start | bytes 1966088 | tf_op jit(solution)/shard_map/ppermute | solution.py:598
  11.5 2.0 %collective-permute-start.1 = (f32[256,128]{1,0:T(8,128)S(1)}, f32[256,128]{1,0:T(8,128)S(1)}, u32[]{:S(2)}, u32[]{:S(2)}) collective-permute-start(f32[256,128]{1,0:T(8,128)S(1)} %get-tuple-element.78), channel_id=1, source_target_pairs={{0,16},{16,0},{32,48},{48,32},{64,80},{80,64},{96,112},{112,96},{1... | collective-permute-start | bytes 393224 | tf_op jit(solution)/shard_map/ppermute | solution.py:598
  13.5 12.6 %collective-permute-start.4 = (f32[256,128]{1,0:T(8,128)S(1)}, f32[256,128]{1,0:T(8,128)S(1)}, u32[]{:S(2)}, u32[]{:S(2)}) collective-permute-start(f32[256,128]{1,0:T(8,128)S(1)} %add.21), channel_id=1, source_target_pairs={{0,64},{16,80},{32,96},{48,112},{64,0},{80,16},{96,32},{112,48},{1... | collective-permute-start | bytes 393224 | tf_op jit(solution)/shard_map/ppermute | solution.py:598
  13.6 13.6 %collective-permute-start.3 = (f32[256,128]{1,0:T(8,128)S(1)}, f32[256,128]{1,0:T(8,128)S(1)}, u32[]{:S(2)}, u32[]{:S(2)}) collective-permute-start(f32[256,128]{1,0:T(8,128)S(1)} %add.21), channel_id=1, source_target_pairs={{0,96},{16,112},{32,64},{48,80},{64,32},{80,48},{96,0},{112,16},{1... | collective-permute-start | bytes 393224 | tf_op jit(solution)/shard_map/ppermute | solution.py:598
  16.7 10.5 %collective-permute-start.2 = (f32[256,128]{1,0:T(8,128)S(1)}, f32[256,128]{1,0:T(8,128)S(1)}, u32[]{:S(2)}, u32[]{:S(2)}) collective-permute-start(f32[256,128]{1,0:T(8,128)S(1)} %add.21), channel_id=1, source_target_pairs={{0,32},{16,48},{32,0},{48,16},{64,96},{80,112},{96,64},{112,80},{1... | collective-permute-start | bytes 393224 | tf_op jit(solution)/shard_map/ppermute | solution.py:598
  27.2 20.8 %collective-permute-start.7 = (f32[512,1024]{1,0:T(8,128)S(1)}, f32[512,1024]{1,0:T(8,128)S(1)}, u32[]{:S(2)}, u32[]{:S(2)}) collective-permute-start(f32[512,1024]{1,0:T(8,128)S(1)} %get-tuple-element.88), channel_id=1, source_target_pairs={{0,16},{16,0},{32,48},{48,32},{64,80},{80,64},{96,112},{112,96},{1... | collective-permute-start | bytes 6291464 | tf_op jit(solution)/shard_map/ppermute | solution.py:598
  29.4 18.6 %collective-permute-start.5 = (f32[1024,128]{1,0:T(8,128)S(1)}, f32[1024,128]{1,0:T(8,128)S(1)}, u32[]{:S(2)}, u32[]{:S(2)}) collective-permute-start(f32[1024,128]{1,0:T(8,128)S(1)} %get-tuple-element.85), channel_id=1, source_target_pairs={{0,12},{1,13},{2,14},{3,15},{4,8},{5,9},{6,10},{7,11},{16,28},{17,... | collective-permute-start | bytes 1572872 | tf_op jit(solution)/shard_map/ppermute | solution.py:602
  33.9 17.6 %collective-permute-start.8 = (f32[10,128,128]{2,1,0:T(8,128)S(1)}, f32[10,128,128]{2,1,0:T(8,128)S(1)}, u32[]{:S(2)}, u32[]{:S(2)}) collective-permute-start(f32[10,128,128]{2,1,0:T(8,128)S(1)} %get-tuple-element.89), channel_id=1, source_target_pairs={{0,64},{16,80},{32,96},{48,112},{64,0},{80,16},{96,32},{112,48},{1... | collective-permute-start | bytes 1966088 | tf_op jit(solution)/shard_map/ppermute | solution.py:598
  36.3 11.7 %collective-permute-start.6 = (f32[256,128]{1,0:T(8,128)S(1)}, f32[256,128]{1,0:T(8,128)S(1)}, u32[]{:S(2)}, u32[]{:S(2)}) collective-permute-start(f32[256,128]{1,0:T(8,128)S(1)} %add_add_fusion), channel_id=1, source_target_pairs={{0,12},{1,13},{2,14},{3,15},{4,8},{5,9},{6,10},{7,11},{16,28},{17,... | collective-permute-start | bytes 393224 | tf_op jit(solution)/shard_map/ppermute | solution.py:602
  51.7 15.3 %collective-permute-start.12 = (f32[256,1024]{1,0:T(8,128)S(1)}, f32[256,1024]{1,0:T(8,128)S(1)}, u32[]{:S(2)}, u32[]{:S(2)}) collective-permute-start(f32[256,1024]{1,0:T(8,128)S(1)} %slice_select_fusion), channel_id=1, source_target_pairs={{0,32},{16,112},{32,0},{48,80},{64,96},{80,48},{96,64},{112,16},{1... | collective-permute-start | bytes 3145736 | tf_op jit(solution)/shard_map/ppermute | solution.py:627
  54.3 12.6 %collective-permute-start.10 = (f32[1,512,128]{2,1,0:T(8,128)S(1)}, f32[1,512,128]{2,1,0:T(8,128)S(1)}, u32[]{:S(2)}, u32[]{:S(2)}) collective-permute-start(f32[1,512,128]{2,1,0:T(8,128)S(1)} %get-tuple-element.141), channel_id=1, source_target_pairs={{0,3},{1,2},{2,1},{3,0},{4,7},{5,6},{6,5},{7,4},{8,11},{9,10},{10,... | collective-permute-start | bytes 786440 | tf_op jit(solution)/shard_map/ppermute | solution.py:640
  54.8 12.1 %collective-permute-start.11 = (f32[1,256,128]{2,1,0:T(8,128)S(1)}, f32[1,256,128]{2,1,0:T(8,128)S(1)}, u32[]{:S(2)}, u32[]{:S(2)}) collective-permute-start(f32[1,256,128]{2,1,0:T(8,128)S(1)} %select_bitcast_fusion), channel_id=1, source_target_pairs={{0,4},{1,5},{2,6},{3,7},{4,0},{5,1},{6,2},{7,3},{8,12},{9,13},{10,... | collective-permute-start | bytes 393224 | tf_op jit(solution)/shard_map/ppermute | solution.py:664
  56.0 10.9 %collective-permute-start.9 = (f32[1,512,128]{2,1,0:T(8,128)S(1)}, f32[1,512,128]{2,1,0:T(8,128)S(1)}, u32[]{:S(2)}, u32[]{:S(2)}) collective-permute-start(f32[1,512,128]{2,1,0:T(8,128)S(1)} %get-tuple-element.142), channel_id=1, source_target_pairs={{0,1},{1,0},{2,3},{3,2},{4,5},{5,4},{6,7},{7,6},{8,9},{9,8},{10,11... | collective-permute-start | bytes 786440 | tf_op jit(solution)/shard_map/ppermute | solution.py:640
  67.3 6.5 %collective-permute-start.15 = (f32[2,256,128]{2,1,0:T(8,128)S(1)}, f32[2,256,128]{2,1,0:T(8,128)S(1)}, u32[]{:S(2)}, u32[]{:S(2)}) collective-permute-start(f32[2,256,128]{2,1,0:T(8,128)S(1)} %pad_maximum_fusion.8), channel_id=1, source_target_pairs={{0,1},{1,0},{2,3},{3,2},{4,5},{5,4},{6,7},{7,6},{8,9},{9,8},{10,11... | collective-permute-start | bytes 786440 | tf_op jit(solution)/shard_map/ppermute | solution.py:664
  69.5 9.5 %collective-permute-start.13 = (f32[2,512,128]{2,1,0:T(8,128)S(1)}, f32[2,512,128]{2,1,0:T(8,128)S(1)}, u32[]{:S(2)}, u32[]{:S(2)}) collective-permute-start(f32[2,512,128]{2,1,0:T(8,128)S(1)} %pad_maximum_fusion.5), channel_id=1, source_target_pairs={{0,3},{1,2},{2,1},{3,0},{4,7},{5,6},{6,5},{7,4},{8,11},{9,10},{10,... | collective-permute-start | bytes 1572872 | tf_op jit(solution)/shard_map/ppermute | solution.py:640
  71.6 8.4 %collective-permute-start.16 = (f32[128,1024]{1,0:T(8,128)S(1)}, f32[128,1024]{1,0:T(8,128)S(1)}, u32[]{:S(2)}, u32[]{:S(2)}) collective-permute-start(f32[128,1024]{1,0:T(8,128)S(1)} %slice_select_fusion.1), channel_id=1, source_target_pairs={{0,96},{16,48},{32,64},{48,16},{64,32},{80,112},{96,0},{112,80},{1... | collective-permute-start | bytes 1572872 | tf_op jit(solution)/shard_map/ppermute | solution.py:627
  71.7 8.4 %collective-permute-start.14 = (f32[2,512,128]{2,1,0:T(8,128)S(1)}, f32[2,512,128]{2,1,0:T(8,128)S(1)}, u32[]{:S(2)}, u32[]{:S(2)}) collective-permute-start(f32[2,512,128]{2,1,0:T(8,128)S(1)} %pad_maximum_fusion.6), channel_id=1, source_target_pairs={{0,1},{1,0},{2,3},{3,2},{4,5},{5,4},{6,7},{7,6},{8,9},{9,8},{10,11... | collective-permute-start | bytes 1572872 | tf_op jit(solution)/shard_map/ppermute | solution.py:640
  80.2 8.4 %collective-permute-start.20 = (f32[128,1024]{1,0:T(8,128)S(1)}, f32[128,1024]{1,0:T(8,128)S(1)}, u32[]{:S(2)}, u32[]{:S(2)}) collective-permute-start(f32[128,1024]{1,0:T(8,128)S(1)} %select_add_fusion.1), channel_id=1, source_target_pairs={{0,96},{16,48},{32,64},{48,16},{64,32},{80,112},{96,0},{112,80},{1... | collective-permute-start | bytes 1572872 | tf_op jit(solution)/shard_map/ppermute | solution.py:630
  81.6 14.8 %collective-permute-start.17 = (f32[4,512,128]{2,1,0:T(8,128)S(1)}, f32[4,512,128]{2,1,0:T(8,128)S(1)}, u32[]{:S(2)}, u32[]{:S(2)}) collective-permute-start(f32[4,512,128]{2,1,0:T(8,128)S(1)} %pad_maximum_fusion.1.refs_0_), channel_id=1, source_target_pairs={{0,4},{1,5},{2,6},{3,7},{4,0},{5,1},{6,2},{7,3},{8,12},{9,13},{10,... | collective-permute-start | bytes 3145736 | tf_op jit(solution)/shard_map/ppermute | solution.py:640
  81.9 20.5 %collective-permute-start.18 = (f32[4,512,128]{2,1,0:T(8,128)S(1)}, f32[4,512,128]{2,1,0:T(8,128)S(1)}, u32[]{:S(2)}, u32[]{:S(2)}) collective-permute-start(f32[4,512,128]{2,1,0:T(8,128)S(1)} %pad_maximum_fusion.2.refs_4_), channel_id=1, source_target_pairs={{0,12},{1,13},{2,14},{3,15},{4,8},{5,9},{6,10},{7,11},{8,4},{9,5},... | collective-permute-start | bytes 3145736 | tf_op jit(solution)/shard_map/ppermute | solution.py:640
  82.6 10.7 %collective-permute-start.19 = (f32[4,256,128]{2,1,0:T(8,128)S(1)}, f32[4,256,128]{2,1,0:T(8,128)S(1)}, u32[]{:S(2)}, u32[]{:S(2)}) collective-permute-start(f32[4,256,128]{2,1,0:T(8,128)S(1)} %pad_maximum_fusion.7), channel_id=1, source_target_pairs={{0,3},{1,2},{2,1},{3,0},{4,7},{5,6},{6,5},{7,4},{8,11},{9,10},{10,... | collective-permute-start | bytes 1572872 | tf_op jit(solution)/shard_map/ppermute | solution.py:664
  88.7 20.4 %copy-start = (f32[2,512,512]{2,1,0:T(8,128)S(1)}, f32[2,512,512]{2,1,0:T(8,128)}, u32[]{:S(2)}) copy-start(f32[2,512,512]{2,1,0:T(8,128)} %inverses.1) | copy-start | bytes 6291460
  88.8 7.6 %collective-permute-start.21 = (f32[5,128,128]{2,1,0:T(8,128)S(1)}, f32[5,128,128]{2,1,0:T(8,128)S(1)}, u32[]{:S(2)}, u32[]{:S(2)}) collective-permute-start(f32[5,128,128]{2,1,0:T(8,128)S(1)} %get-tuple-element.109), channel_id=1, source_target_pairs={{0,64},{16,80},{32,96},{48,112},{64,0},{80,16},{96,32},{112,48},{1... | collective-permute-start | bytes 983048 | tf_op jit(solution)/shard_map/ppermute | solution.py:598
  102.4 6.7 %collective-permute-start.25 = (f32[8,256,128]{2,1,0:T(8,128)S(1)}, f32[8,256,128]{2,1,0:T(8,128)S(1)}, u32[]{:S(2)}, u32[]{:S(2)}) collective-permute-start(f32[8,256,128]{2,1,0:T(8,128)S(1)} %pad_maximum_fusion.3.own), channel_id=1, source_target_pairs={{0,16},{16,0},{32,48},{48,32},{64,80},{80,64},{96,112},{112,96},{1... | collective-permute-start | bytes 3145736 | tf_op jit(solution)/shard_map/ppermute | solution.py:598
  106.7 15.2 %collective-permute-start.24 = (f32[256,1024]{1,0:T(8,128)S(1)}, f32[256,1024]{1,0:T(8,128)S(1)}, u32[]{:S(2)}, u32[]{:S(2)}) collective-permute-start(f32[256,1024]{1,0:T(8,128)S(1)} %pad_maximum_fusion.4), channel_id=1, source_target_pairs={{0,32},{16,112},{32,0},{48,80},{64,96},{80,48},{96,64},{112,16},{1... | collective-permute-start | bytes 3145736 | tf_op jit(solution)/shard_map/ppermute | solution.py:630
  107.8 14.9 %collective-permute-start.22 = (f32[4,512,128]{2,1,0:T(8,128)S(1)}, f32[4,512,128]{2,1,0:T(8,128)S(1)}, u32[]{:S(2)}, u32[]{:S(2)}) collective-permute-start(f32[4,512,128]{2,1,0:T(8,128)S(1)} %pad_maximum_fusion.1.refs_0_), channel_id=1, source_target_pairs={{0,12},{1,13},{2,14},{3,15},{4,8},{5,9},{6,10},{7,11},{8,4},{9,5},... | collective-permute-start | bytes 3145736 | tf_op jit(solution)/shard_map/ppermute | solution.py:640
  109.1 13.6 %collective-permute-start.23 = (f32[4,512,128]{2,1,0:T(8,128)S(1)}, f32[4,512,128]{2,1,0:T(8,128)S(1)}, u32[]{:S(2)}, u32[]{:S(2)}) collective-permute-start(f32[4,512,128]{2,1,0:T(8,128)S(1)} %pad_maximum_fusion.2.refs_4_), channel_id=1, source_target_pairs={{0,4},{1,5},{2,6},{3,7},{4,0},{5,1},{6,2},{7,3},{8,12},{9,13},{10,... | collective-permute-start | bytes 3145736 | tf_op jit(solution)/shard_map/ppermute | solution.py:640
  122.7 4.2 %collective-permute-start.28 = (f32[512,1024]{1,0:T(8,128)S(1)}, f32[512,1024]{1,0:T(8,128)S(1)}, u32[]{:S(2)}, u32[]{:S(2)}) collective-permute-start(f32[512,1024]{1,0:T(8,128)S(1)} %pad_maximum_fusion.own), channel_id=1, source_target_pairs={{0,16},{16,0},{32,48},{48,32},{64,80},{80,64},{96,112},{112,96},{1... | collective-permute-start | bytes 6291464 | tf_op jit(solution)/shard_map/ppermute | solution.py:598
  122.9 15.2 %collective-permute-start.26 = (f32[4,512,128]{2,1,0:T(8,128)S(1)}, f32[4,512,128]{2,1,0:T(8,128)S(1)}, u32[]{:S(2)}, u32[]{:S(2)}) collective-permute-start(f32[4,512,128]{2,1,0:T(8,128)S(1)} %collective-permute-done.17.refs_1_), channel_id=1, source_target_pairs={{0,12},{1,13},{2,14},{3,15},{4,8},{5,9},{6,10},{7,11},{8,4},{9,5},... | collective-permute-start | bytes 3145736 | tf_op jit(solution)/shard_map/ppermute | solution.py:640
  124.2 13.9 %collective-permute-start.27 = (f32[4,512,128]{2,1,0:T(8,128)S(1)}, f32[4,512,128]{2,1,0:T(8,128)S(1)}, u32[]{:S(2)}, u32[]{:S(2)}) collective-permute-start(f32[4,512,128]{2,1,0:T(8,128)S(1)} %collective-permute-done.18.refs_5_), channel_id=1, source_target_pairs={{0,4},{1,5},{2,6},{3,7},{4,0},{5,1},{6,2},{7,3},{8,12},{9,13},{10,... | collective-permute-start | bytes 3145736 | tf_op jit(solution)/shard_map/ppermute | solution.py:640
  124.2 37.8 %collective-permute-start.29 = (f32[25,128,128]{2,1,0:T(8,128)S(1)}, f32[25,128,128]{2,1,0:T(8,128)S(1)}, u32[]{:S(2)}, u32[]{:S(2)}) collective-permute-start(f32[25,128,128]{2,1,0:T(8,128)S(1)} %get-tuple-element.135), channel_id=1, source_target_pairs={{0,64},{16,80},{32,96},{48,112},{64,0},{80,16},{96,32},{112,48},{1... | collective-permute-start | bytes 4915208 | tf_op jit(solution)/shard_map/ppermute | solution.py:598

commit v6 on v5

--- a/solution.py
+++ b/solution.py
@@ -95,13 +95,13 @@
         pltpu.make_async_copy(front.at[:, pl.ds(0, BLK)], panel, sem.at[2]),
     ]
     writes = []
-    rest_a, rest_b, rest_c = rests
+    rest_a, rest_b = rests
     parts = (
         (0, 0, rest_a),
-        (1, 0, rest_b),
-        (1, 5, rest_c.at[pl.ds(0, 5)]),
-        (2, 0, rest_c.at[pl.ds(5, 10)]),
-        (3, 0, rest_c.at[pl.ds(15, 10)]),
+        (0, 5, rest_b.at[pl.ds(0, 5)]),
+        (1, 0, rest_b.at[pl.ds(5, 10)]),
+        (2, 0, rest_b.at[pl.ds(15, 10)]),
+        (3, 0, rest_b.at[pl.ds(25, 10)]),
     )
     for n, (j, start, target) in enumerate(parts):
         d = j + (j >= place).astype(jnp.int32)
@@ -169,20 +169,18 @@
 
 
 def prepare(maps, pivots, front, pieces, first):
-    column = jax.ShapeDtypeStruct((10, BLK, BLK), F32)
     return pl.pallas_call(
         prepare_kernel,
         out_shape=[
-            column,
             jax.ShapeDtypeStruct((5, BLK, BLK), F32),
-            jax.ShapeDtypeStruct((25, BLK, BLK), F32),
+            jax.ShapeDtypeStruct((35, BLK, BLK), F32),
             jax.ShapeDtypeStruct((2048, BLK), F32),
             jax.ShapeDtypeStruct((256, BLK), F32),
             jax.ShapeDtypeStruct((256, BLK), F32),
             jax.ShapeDtypeStruct((64,), jnp.int32),
         ],
         in_specs=[SMEM, VMEM, HBM, HBM, VMEM],
-        out_specs=[HBM] * 3 + [VMEM, VMEM, VMEM, SMEM],
+        out_specs=[HBM] * 2 + [VMEM, VMEM, VMEM, SMEM],
         scratch_shapes=[
             pltpu.VMEM((10, BLK, 640), F32),
             pltpu.VMEM((10, BLK, BLK), F32),
@@ -410,9 +408,9 @@
     return jnp.maximum(s[base + half * 8 + t], 0)
 
 
-def extend_kernel(columns, table, front, *refs):
+def extend_kernel(counts, table, front, *refs):
     out, refs = refs[-1], refs[:-1]
-    kept, *got = (refs[2 * k : 2 * k + 2] for k in range(1 + columns))
+    kept, *got = (refs[2 * k : 2 * k + 2] for k in range(1 + len(counts)))
     step = pl.program_id(0)
     out[...] = front[...]
     for half in range(2):
@@ -423,9 +421,11 @@
                 to = pl.ds(pl.multiple_of(table[KEPT_COL + d] * BLK, BLK), BLK)
                 out[half, :, to] += kept[half][0, 0, :, d * BLK : (d + 1) * BLK]
 
-        @pl.when(table[GOT_AT + half * 8 + step] >= 0)
-        def _(half=half):
-            for j in range(columns):
+        m = table[GOT_AT + half * 8 + step]
+        for j, count in enumerate(counts):
+
+            @pl.when((m >= 0) & (m < count))
+            def _(half=half, j=j):
                 to = pl.ds(pl.multiple_of(table[GOT_COL + j] * BLK, BLK), BLK)
                 out[half, :, to] += got[j][half][0]
 
@@ -434,19 +434,21 @@
     def kept_at(half):
         return lambda t, s: (block_at(KEPT_AT, half, t, s), s[SIDE], 0, 0)
 
-    def got_at(half):
-        return lambda t, s: (block_at(GOT_AT, half, t, s), 0, 0)
+    def got_at(half, count):
+        return lambda t, s: (jnp.minimum(block_at(GOT_AT, half, t, s), count - 1), 0, 0)
 
     tile = pl.BlockSpec((2, BLK, 1024), lambda t, s: (0, t, 0))
     kept_specs = [pl.BlockSpec((1, 1, BLK, 640), kept_at(half)) for half in range(2)]
-    got_specs = [pl.BlockSpec((1, BLK, BLK), got_at(half)) for half in range(2)]
-    return pl.pallas_call(
-        functools.partial(extend_kernel, len(got)),
+    got_specs = [
+        pl.BlockSpec((1, BLK, BLK), got_at(half, g.shape[0])) for g in got for half in range(2)
+    ]
+    return pl.pallas_call(
+        functools.partial(extend_kernel, [g.shape[0] for g in got]),
         out_shape=pltpu.HBM((2, 1024, 1024), F32),
         grid_spec=pltpu.PrefetchScalarGridSpec(
             num_scalar_prefetch=1,
             grid=(8,),
-            in_specs=[tile, *kept_specs, *got_specs * len(got)],
+            in_specs=[tile, *kept_specs, *got_specs],
             out_specs=tile,
         ),
         compiler_params=params(20),
@@ -460,7 +462,7 @@
 
 def update_kernel(table, front, *refs):
     blocks = refs[:4], refs[4:8]
-    right_h, right_l, marks, got_b, out, panels = refs[8:]
+    right_h, right_l, marks, out, panels = refs[8:]
     step = pl.program_id(0)
     span = pl.ds(pl.multiple_of(step % 2 * 256, 256), 256)
     col, core = table[COL], table[ROW] % 2
@@ -500,18 +502,8 @@
                 after = jnp.where(col < 8, part, after)
             out[:, :, columns] = jnp.where(active, after, before)
 
-    columns_b = pl.ds(pl.multiple_of(table[GOT_COL + 2] * BLK, BLK), BLK)
-    for part in range(4):
-        half, rest = part // 2, part % 2
-        rows = slice(rest * BLK, (rest + 1) * BLK)
-        m = table[GOT_AT + half * 8 + 2 * step + rest]
-
-        @pl.when((m >= 0) & (m < 5))
-        def _(half=half, rows=rows, m=m):
-            out[half, rows, columns_b] += got_b[m]
-
-
-def update(table, front, blocks, right, marks, got_b):
+
+def update(table, front, blocks, right, marks):
     tile = pl.BlockSpec((2, 256, 1024), lambda t, s: (0, t, 0))
     return pl.pallas_call(
         update_kernel,
@@ -523,7 +515,6 @@
                 tile,
                 *[VMEM] * 10,
                 pl.BlockSpec((2, 256, BLK), lambda t, s: (0, t, 0)),
-                VMEM,
             ],
             out_specs=tile,
             scratch_shapes=[pltpu.VMEM((2, PANEL, 1024), BF16)],
@@ -531,7 +522,7 @@
         compiler_params=params(24),
         cost_estimate=cost(6 * 2048 * 1024 * 1024, 32 * MIB),
         name="update",
-    )(table, in_hbm(front), *blocks[0], *blocks[1], *right, marks.reshape(2, 1024, BLK), got_b)
+    )(table, in_hbm(front), *blocks[0], *blocks[1], *right, marks.reshape(2, 1024, BLK))
 
 
 def finish_kernel(
@@ -541,7 +532,7 @@
     del front
     core = table[ROW] % 2
     copies = []
-    places = [(2, m) for m in range(5, 10)] + [(j, m) for j in (3, 4) for m in range(10)]
+    places = [(1, m) for m in range(5, 10)] + [(j, m) for j in (2, 3, 4) for m in range(10)]
     for n, (column, m) in enumerate(places):
         columns = pl.ds(pl.multiple_of(table[GOT_COL + column] * BLK, BLK), BLK)
         rows = pl.ds(pl.multiple_of(table[GOT_ROW + m] * BLK, BLK), BLK)
@@ -581,9 +572,9 @@
         in_specs=[SMEM, SMEM, SMEM, HBM] + [VMEM] * 2,
         out_specs=HBM,
         scratch_shapes=[
-            pltpu.VMEM((25, BLK, BLK), F32),
-            pltpu.SemaphoreType.DMA((25,)),
-            pltpu.SemaphoreType.DMA((25,)),
+            pltpu.VMEM((35, BLK, BLK), F32),
+            pltpu.SemaphoreType.DMA((35,)),
+            pltpu.SemaphoreType.DMA((35,)),
             pltpu.SemaphoreType.DMA(()),
         ],
         input_output_aliases={3: 0},
@@ -642,7 +633,7 @@
     first = cut(child_maps, pieces)
     got0 = by_row(first, 4)
     *rest, panel, corner, away, table = prepare(child_maps, pivots, front, pieces, first)
-    rest_a, rest_b, rest_c = rest
+    rest_a, rest_b = rest
     corner = corner + by_row(away, 1)
     corner = corner + (by_row(corner, 2) + (by_row(corner, 6) + by_row(corner, 4)))
     away_rows, marks, list_other = pivot_terms(child_maps, pivots, front, children)
@@ -669,27 +660,24 @@
         held = [jnp.concatenate([h, c], axis=0) for h, c in zip(held, came)]
         corner = corner_step(corner, k)
         total = halve(total, k)
+        if k == 1:
+            total = double(total, 1)
         if k == 0:
             front = extend(table, front, pieces, (got0, got_a))
         held, corner, total, front = together((held, corner, total, front))
     came = [gather_step(held[w], w, 2) for w in range(2)]
     corner = corner_step(corner, 2)
-    total, rest_b = together((double(total, 1), rest_b))
+    total = double(total, 0)
+    came, corner, total, rest_b = together((came, corner, total, rest_b))
     got_b = by_row(rest_b, 4)
-    came, corner, total, got_b = together((came, corner, total, got_b))
     held_far = [gather_step(held[w], w, 3) for w in range(2)]
+    came_far = [gather_step(came[w], w, 3) for w in range(2)]
     *factors, cross = corners(table, corner, by_row(corner, 1), diag_inverses)
-    total = double(total, 0)
-    came, held_far, total, rest_c, factors, cross = together(
-        (came, held_far, total, rest_c, factors, cross)
-    )
-    came_far = [gather_step(came[w], w, 3) for w in range(2)]
-    got_c = by_row(rest_c, 4)
     *right, patch = right_factor(table, total, by_row(total, 1), factors, cross)
-    came_far, right, patch = together((came_far, right, patch))
+    held_far, came_far, right, patch = together((held_far, came_far, right, patch))
     blocks = [(held[w], came[w], held_far[w], came_far[w]) for w in range(2)]
-    front = update(table, front, blocks, right, marks, got_b).reshape(2048, 1024)
-    return finish(table, (list_other, list_mine), front, got_c, patch)
+    front = update(table, front, blocks, right, marks).reshape(2048, 1024)
+    return finish(table, (list_other, list_mine), front, got_b, patch)
 
 
 def solution(mesh):

time: 168 us -> 168 us (level)
    ppermute x11 -> x10, waiting for transfers between devices: 11.9 us -> 3.64 us  [swap(): return lax.ppermute(block, axis, [(i, partner(i)) for i in range(count)])]
    ppermute x10, waiting for transfers between devices: 14.9 us -> 21.4 us  [gather_step(): return lax.ppermute(block, ('row', 'col'), route)]
    ppermute x10, starting transfers between devices: 6.95 us -> 12.7 us  [gather_step(): return lax.ppermute(block, ('row', 'col'), route)]
    ppermute x2, waiting for transfers between devices: 15.9 us -> 10.6 us  [double(): came = lax.ppermute(part, 'row', rings[step])]
    ppermute x11 -> x10, starting transfers between devices: 21.6 us -> 16.3 us  [swap(): return lax.ppermute(block, axis, [(i, partner(i)) for i in range(count)])]
    ppermute x2, waiting for transfers between devices: 0.88 us -> 4.68 us  [halve(): return stay + lax.ppermute(leave, 'row', rings[step])]
    ppermute x3, waiting for transfers between devices: 3.7 us -> 6.17 us  [corner_step(): lax.ppermute(block, ('row', 'col'), route)]
    ppermute x2, starting transfers between devices: 2.47 us -> 0.7 us  [double(): came = lax.ppermute(part, 'row', rings[step])]
  transfers between devices with their start and end apart: 30 -> 29, of which waited for: 18 -> 16; matrix products, arithmetic and copies ran while one was open for 1% -> 1% of each run, Pallas kernels for 39% -> 39%
where the time goes in v6:
time: 168 us; the launch traced here: 165 us
  Pallas kernels  71.8 us (43%)
  waiting for transfers between devices  47.7 us (28%)
  starting transfers between devices  43.4 us (26%)
  other arithmetic  2.04 us (1%)
    ppermute x10, waiting for transfers between devices, gather_step(): return lax.ppermute(block, ('row', 'col'), route)  21.4 us
    pallas_call x1, Pallas kernels, update(): pl.pallas_call(update_kernel, out_shape=pltpu.HBM((2, 1024, 1024), F32),...  20.3 us
    pallas_call x2, Pallas kernels, pivot_terms(): pl.pallas_call(functools.partial(pivot_kernel, mine_half), out_shape=[jax...  18.2 us
    ppermute x10, starting transfers between devices, swap(): return lax.ppermute(block, axis, [(i, partner(i)) for i in range(count)])  16.3 us
    ppermute x10, starting transfers between devices, gather_step(): return lax.ppermute(block, ('row', 'col'), route)  12.7 us
    pallas_call x1, Pallas kernels, extend(): pl.pallas_call(functools.partial(extend_kernel, [g.shape[0] for g in got]...  10.8 us
    ppermute x2, waiting for transfers between devices, double(): came = lax.ppermute(part, 'row', rings[step])  10.6 us
    pallas_call x1, Pallas kernels, right_factor(): pl.pallas_call(factor_kernel, out_shape=[shape, shape, jax.ShapeDtypeStru...  7.94 us
  transfers between devices with their start and end apart: 29, of which 16 were waited for; matrix products, arithmetic and copies ran while one was open for 1% of the time, Pallas kernels for 39%

profile of v6, /device:TPU:1, one launch (start us, length us, event | category | flops | bytes accessed | tf_op | source)
XLA Modules:
  0.0 165.4 jit_solution(1534916371420932868)
XLA Ops:
  0.0 1.8 %cut.1.first = f32[10,128,128]{2,1,0:T(8,128)S(1)} custom-call(s32[2,80]{1,0:T(2,128)} %maps.7, f32[10,2,128,640]{3,2,1,0:T(8,128)} %bitcast.12), custom_call_target="tpu_custom_call" | custom-call | bytes 1048576 | tf_op jit(solution)/shard_map/cut/pallas_call | solution.py:67
  1.9 4.5 %collective-permute-start = (f32[10,128,128]{2,1,0:T(8,128)S(1)}, f32[10,128,128]{2,1,0:T(8,128)S(1)}, u32[]{:S(2)}, u32[]{:S(2)}) collective-permute-start(f32[10,128,128]{2,1,0:T(8,128)S(1)} %cut.1.first), channel_id=1, source_target_pairs={{0,64},{16,80},{32,96},{48,112},{64,0},{80,16},{96,32},{112,48},{1... | collective-permute-start | bytes 1966088 | tf_op jit(solution)/shard_map/ppermute | solution.py:589
  6.4 5.1 %prepare.1 = (f32[5,128,128]{2,1,0:T(8,128)S(1)}, f32[35,128,128]{2,1,0:T(8,128)S(1)}, f32[2048,128]{1,0:T(8,128)S(1)}, f32[256,128]{1,0:T(8,128)S(1)}, f32[256,128]{1,0:T(8,128)S(1)}, /*index=5*/s32[64]{0:T(128)S(1)}) custom-call(s32[2,80]{1,0:T(2,128)} %maps.7, s32[8,128]{1,0:T(8,128)} %bitcast.18, f32[2048,1024]{1,0:T(8,128)} %front.5, ...), custom_call_target="tpu_custom_call" | custom-call | bytes 9437184 | tf_op jit(solution)/shard_map/prepare/pallas_call | solution.py:172
  11.5 1.0 collective-permute-start.1
  12.5 1.0 collective-permute-done.1
  13.6 3.1 %collective-permute-start.3 = (f32[256,128]{1,0:T(8,128)S(1)}, f32[256,128]{1,0:T(8,128)S(1)}, u32[]{:S(2)}, u32[]{:S(2)}) collective-permute-start(f32[256,128]{1,0:T(8,128)S(1)} %add.21), channel_id=1, source_target_pairs={{0,96},{16,112},{32,64},{48,80},{64,32},{80,48},{96,0},{112,16},{1... | collective-permute-start | bytes 393224 | tf_op jit(solution)/shard_map/ppermute | solution.py:589
  16.7 9.1 %pivot_terms_other.1 = (f32[512,1024]{1,0:T(8,128)S(1)}, f32[2048,128]{1,0:T(8,128)S(1)}, s32[513]{0:T(1024)S(1)}) custom-call(s32[2,80]{1,0:T(2,128)} %maps.7, s32[1024]{0:T(1024)} %pivots.1, f32[2048,1024]{1,0:T(8,128)} %front.5, f32[2560,640]{1,0:T(8,128)} %children.3), custom_call_target="tpu_custom_call" | custom-call | bytes 25165824 | tf_op jit(solution)/shard_map/pivot_terms_other/pallas_call | solution.py:264
  25.9 1.3 collective-permute-done.3
  27.2 1.3 collective-permute-start.7
  28.6 0.8 whole_panel.1
  29.4 4.5 %collective-permute-start.5 = (f32[1024,128]{1,0:T(8,128)S(1)}, f32[1024,128]{1,0:T(8,128)S(1)}, u32[]{:S(2)}, u32[]{:S(2)}) collective-permute-start(f32[1024,128]{1,0:T(8,128)S(1)} %get-tuple-element.75), channel_id=1, source_target_pairs={{0,12},{1,13},{2,14},{3,15},{4,8},{5,9},{6,10},{7,11},{16,28},{17,... | collective-permute-start | bytes 1572872 | tf_op jit(solution)/shard_map/ppermute | solution.py:593
  33.9 1.3 collective-permute-start.6
  35.2 2.4 %collective-permute-start.8 = (f32[5,128,128]{2,1,0:T(8,128)S(1)}, f32[5,128,128]{2,1,0:T(8,128)S(1)}, u32[]{:S(2)}, u32[]{:S(2)}) collective-permute-start(f32[5,128,128]{2,1,0:T(8,128)S(1)} %get-tuple-element.79), channel_id=1, source_target_pairs={{0,64},{16,80},{32,96},{48,112},{64,0},{80,16},{96,32},{112,48},{1... | collective-permute-start | bytes 983048 | tf_op jit(solution)/shard_map/ppermute | solution.py:589
  37.6 9.1 %pivot_terms_mine.1 = (f32[512,1024]{1,0:T(8,128)S(1)}, f32[2048,128]{1,0:T(8,128)S(1)}, s32[513]{0:T(1024)S(1)}) custom-call(s32[2,80]{1,0:T(2,128)} %maps.7, s32[1024]{0:T(1024)} %pivots.1, f32[2048,1024]{1,0:T(8,128)} %front.5, f32[2560,640]{1,0:T(8,128)} %children.3, f32[2048,128]{1,0:T(8,128)S(1)} %get-tuple-element.69.refs_0_), custom_call_target="tpu_custom_call" | custom-call | bytes 25165824 | tf_op jit(solution)/shard_map/pivot_terms_mine/pallas_call | solution.py:264
  46.7 1.3 collective-permute-done.6
  48.1 0.4 add.25
  48.6 2.6 %collective-permute-start.12 = (f32[256,1024]{1,0:T(8,128)S(1)}, f32[256,1024]{1,0:T(8,128)S(1)}, u32[]{:S(2)}, u32[]{:S(2)}) collective-permute-start(f32[256,1024]{1,0:T(8,128)S(1)} %slice_select_fusion), channel_id=1, source_target_pairs={{0,32},{16,112},{32,0},{48,80},{64,96},{80,48},{96,64},{112,16},{1... | collective-permute-start | bytes 3145736 | tf_op jit(solution)/shard_map/ppermute | solution.py:618
  51.3 3.5 %collective-permute-start.10 = (f32[1,512,128]{2,1,0:T(8,128)S(1)}, f32[1,512,128]{2,1,0:T(8,128)S(1)}, u32[]{:S(2)}, u32[]{:S(2)}) collective-permute-start(f32[1,512,128]{2,1,0:T(8,128)S(1)} %get-tuple-element.121), channel_id=1, source_target_pairs={{0,3},{1,2},{2,1},{3,0},{4,7},{5,6},{6,5},{7,4},{8,11},{9,10},{10,... | collective-permute-start | bytes 786440 | tf_op jit(solution)/shard_map/ppermute | solution.py:631
  54.8 1.0 collective-permute-start.11
  55.8 10.8 %extend.1.front = f32[2,1024,1024]{2,1,0:T(8,128)} custom-call(s32[64]{0:T(128)S(1)} %get-tuple-element.62.table, f32[2,1024,1024]{2,1,0:T(8,128)} %bitcast.16, f32[10,2,128,640]{3,2,1,0:T(8,128)} %bitcast.14, f32[10,2,128,640]{3,2,1,0:T(8,128)} %bitcast.15, f32[10,128,128]{2,1,0:T(8,128)S(1)} %collective-permute-done.got.refs_2_.refs_3_, ...), custom_call_target="tpu_custom_call" | custom-call | bytes 1048576 | tf_op jit(solution)/shard_map/extend/pallas_call | solution.py:445
  67.2 0.3 collective-permute-start.13
  67.5 2.7 %collective-permute-start.15 = (f32[2,256,128]{2,1,0:T(8,128)S(1)}, f32[2,256,128]{2,1,0:T(8,128)S(1)}, u32[]{:S(2)}, u32[]{:S(2)}) collective-permute-start(f32[2,256,128]{2,1,0:T(8,128)S(1)} %pad_maximum_fusion.8), channel_id=1, source_target_pairs={{0,1},{1,0},{2,3},{3,2},{4,5},{5,4},{6,7},{7,6},{8,9},{9,8},{10,11... | collective-permute-start | bytes 786440 | tf_op jit(solution)/shard_map/ppermute | solution.py:655
  70.1 0.7 collective-permute-start.14
  70.8 4.7 %collective-permute-done.16 = f32[128,1024]{1,0:T(8,128)S(1)} collective-permute-done((f32[128,1024]{1,0:T(8,128)S(1)}, f32[128,1024]{1,0:T(8,128)S(1)}, u32[]{:S(2)}, u32[]{:S(2)}) %collective-permute-start.16) | collective-permute-done | bytes 524320 | tf_op jit(solution)/shard_map/ppermute | solution.py:618
  75.7 0.9 collective-permute-done.15
  76.9 1.6 collective-permute-done.14
  78.5 5.5 %collective-permute-done.17 = f32[128,1024]{1,0:T(8,128)S(1)} collective-permute-done((f32[128,1024]{1,0:T(8,128)S(1)}, f32[128,1024]{1,0:T(8,128)S(1)}, u32[]{:S(2)}, u32[]{:S(2)}) %collective-permute-start.17) | collective-permute-done | bytes 524320 | tf_op jit(solution)/shard_map/ppermute | solution.py:621
  84.3 0.6 collective-permute-start.21
  84.9 1.5 collective-permute-start.20
  86.4 2.7 %collective-permute-start.19 = (f32[4,512,128]{2,1,0:T(8,128)S(1)}, f32[4,512,128]{2,1,0:T(8,128)S(1)}, u32[]{:S(2)}, u32[]{:S(2)}) collective-permute-start(f32[4,512,128]{2,1,0:T(8,128)S(1)} %pad_maximum_fusion.2.refs_4_), channel_id=1, source_target_pairs={{0,12},{1,13},{2,14},{3,15},{4,8},{5,9},{6,10},{7,11},{8,4},{9,5},... | collective-permute-start | bytes 3145736 | tf_op jit(solution)/shard_map/ppermute | solution.py:631
  89.1 5.3 %collective-permute-done.20 = f32[4,256,128]{2,1,0:T(8,128)S(1)} collective-permute-done((f32[4,256,128]{2,1,0:T(8,128)S(1)}, f32[4,256,128]{2,1,0:T(8,128)S(1)}, u32[]{:S(2)}, u32[]{:S(2)}) %collective-permute-start.20) | collective-permute-done | bytes 524320 | tf_op jit(solution)/shard_map/ppermute | solution.py:655
  94.4 5.1 %collective-permute-done.21 = f32[256,1024]{1,0:T(8,128)S(1)} collective-permute-done((f32[256,1024]{1,0:T(8,128)S(1)}, f32[256,1024]{1,0:T(8,128)S(1)}, u32[]{:S(2)}, u32[]{:S(2)}) %collective-permute-start.21) | collective-permute-done | bytes 1048608 | tf_op jit(solution)/shard_map/ppermute | solution.py:621
  99.9 0.4 collective-permute-done.18.refs_1_
  100.3 6.6 %collective-permute-done.19.refs_5_ = f32[4,512,128]{2,1,0:T(8,128)S(1)} collective-permute-done((f32[4,512,128]{2,1,0:T(8,128)S(1)}, f32[4,512,128]{2,1,0:T(8,128)S(1)}, u32[]{:S(2)}, u32[]{:S(2)}) %collective-permute-start.19) | collective-permute-done | bytes 1048608 | tf_op jit(solution)/shard_map/ppermute | solution.py:631
  106.9 0.5 collective-permute-start.27
  107.4 3.3 %collective-permute-start.28 = (f32[35,128,128]{2,1,0:T(8,128)S(1)}, f32[35,128,128]{2,1,0:T(8,128)S(1)}, u32[]{:S(2)}, u32[]{:S(2)}) collective-permute-start(f32[35,128,128]{2,1,0:T(8,128)S(1)} %get-tuple-element.115), channel_id=1, source_target_pairs={{0,64},{16,80},{32,96},{48,112},{64,0},{80,16},{96,32},{112,48},{1... | collective-permute-start | bytes 6881288 | tf_op jit(solution)/shard_map/ppermute | solution.py:589
  110.7 3.0 %collective-permute-start.22 = (f32[4,512,128]{2,1,0:T(8,128)S(1)}, f32[4,512,128]{2,1,0:T(8,128)S(1)}, u32[]{:S(2)}, u32[]{:S(2)}) collective-permute-start(f32[4,512,128]{2,1,0:T(8,128)S(1)} %pad_maximum_fusion.1.refs_0_), channel_id=1, source_target_pairs={{0,12},{1,13},{2,14},{3,15},{4,8},{5,9},{6,10},{7,11},{8,4},{9,5},... | collective-permute-start | bytes 3145736 | tf_op jit(solution)/shard_map/ppermute | solution.py:631
  113.7 1.2 collective-permute-start.23
  114.9 0.6 collective-permute-start.24
  115.5 0.7 collective-permute-start.25
  116.2 2.0 %corners.1 = (bf16[3,512,512]{2,1,0:T(8,128)(2,1)S(1)}, bf16[3,512,512]{2,1,0:T(8,128)(2,1)S(1)}, f32[512,512]{1,0:T(8,128)S(1)}) custom-call(s32[64]{0:T(128)S(1)} %get-tuple-element.62.table, f32[8,256,128]{2,1,0:T(8,128)S(1)} %pad_maximum_fusion.4.own, f32[8,256,128]{2,1,0:T(8,128)S(1)} %collective-permute-done.27.swapped, f32[2,512,512]{2,1,0:T(8,128)S(1)} %copy-done), custom_call_target="tpu_custom_call" | custom-call | flops 805306368 | bytes 8388608 | tf_op jit(solution)/shard_map/corners/pallas_call | solution.py:342
  118.3 7.9 %right_factor.1 = (bf16[1024,1024]{1,0:T(8,128)(2,1)S(1)}, bf16[1024,1024]{1,0:T(8,128)(2,1)S(1)}, f32[512,1024]{1,0:T(8,128)S(1)}) custom-call(s32[64]{0:T(128)S(1)} %get-tuple-element.62.table, f32[512,1024]{1,0:T(8,128)S(1)} %pad_maximum_fusion.own, f32[512,1024]{1,0:T(8,128)S(1)} %collective-permute-done.26.swapped, ...), custom_call_target="tpu_custom_call" | custom-call | flops 6442450944 | bytes 14680064 | tf_op jit(solution)/shard_map/right_factor/pallas_call | solution.py:396
  126.2 1.4 collective-permute-done.23.refs_6_
  127.6 9.8 %collective-permute-done.24.refs_3_ = f32[4,512,128]{2,1,0:T(8,128)S(1)} collective-permute-done((f32[4,512,128]{2,1,0:T(8,128)S(1)}, f32[4,512,128]{2,1,0:T(8,128)S(1)}, u32[]{:S(2)}, u32[]{:S(2)}) %collective-permute-start.24) | collective-permute-done | bytes 1048608 | tf_op jit(solution)/shard_map/ppermute | solution.py:631
  137.4 1.5 collective-permute-done.25.refs_7_
  138.9 20.3 %update.1 = f32[2,1024,1024]{2,1,0:T(8,128)} custom-call(s32[64]{0:T(128)S(1)} %get-tuple-element.62.table, f32[2,1024,1024]{2,1,0:T(8,128)} %extend.1.front, f32[4,512,128]{2,1,0:T(8,128)S(1)} %pad_maximum_fusion.1.refs_0_, f32[4,512,128]{2,1,0:T(8,128)S(1)} %collective-permute-done.18.refs_1_, f32[4,512,128]{2,1,0:T(8,128)S(1)} %collective-permute-done.22.refs_2_, ...), custom_call_target="tpu_custom_call" | custom-call | flops 12884901888 | bytes 33554432 | tf_op jit(solution)/shard_map/update/pallas_call | solution.py:508
  159.2 1.3 collective-permute-done.28.got
  160.5 4.7 %finish.1 = f32[2048,1024]{1,0:T(8,128)} custom-call(s32[64]{0:T(128)S(1)} %get-tuple-element.62.table, s32[513]{0:T(1024)S(1)} %get-tuple-element.63.list_other, s32[513]{0:T(1024)S(1)} %get-tuple-element.70.list_mine, f32[2048,1024]{1,0:T(8,128)} %bitcast.17, f32[35,128,128]{2,1,0:T(8,128)S(1)} %collective-permute-done.28.got, ...), custom_call_target="tpu_custom_call", output_to_operand_aliasing={{}: (3, {})} | custom-call | bytes 8388608 | tf_op jit(solution)/shard_map/finish/pallas_call | solution.py:569
  (43 shorter events, 2.2 us)
Async XLA Ops:
  1.9 25.4 %collective-permute-start = (f32[10,128,128]{2,1,0:T(8,128)S(1)}, f32[10,128,128]{2,1,0:T(8,128)S(1)}, u32[]{:S(2)}, u32[]{:S(2)}) collective-permute-start(f32[10,128,128]{2,1,0:T(8,128)S(1)} %cut.1.first), channel_id=1, source_target_pairs={{0,64},{16,80},{32,96},{48,112},{64,0},{80,16},{96,32},{112,48},{1... | collective-permute-start | bytes 1966088 | tf_op jit(solution)/shard_map/ppermute | solution.py:589
  11.5 2.0 %collective-permute-start.1 = (f32[256,128]{1,0:T(8,128)S(1)}, f32[256,128]{1,0:T(8,128)S(1)}, u32[]{:S(2)}, u32[]{:S(2)}) collective-permute-start(f32[256,128]{1,0:T(8,128)S(1)} %get-tuple-element.68), channel_id=1, source_target_pairs={{0,16},{16,0},{32,48},{48,32},{64,80},{80,64},{96,112},{112,96},{1... | collective-permute-start | bytes 393224 | tf_op jit(solution)/shard_map/ppermute | solution.py:589
  13.5 12.4 %collective-permute-start.4 = (f32[256,128]{1,0:T(8,128)S(1)}, f32[256,128]{1,0:T(8,128)S(1)}, u32[]{:S(2)}, u32[]{:S(2)}) collective-permute-start(f32[256,128]{1,0:T(8,128)S(1)} %add.21), channel_id=1, source_target_pairs={{0,64},{16,80},{32,96},{48,112},{64,0},{80,16},{96,32},{112,48},{1... | collective-permute-start | bytes 393224 | tf_op jit(solution)/shard_map/ppermute | solution.py:589
  13.6 13.6 %collective-permute-start.3 = (f32[256,128]{1,0:T(8,128)S(1)}, f32[256,128]{1,0:T(8,128)S(1)}, u32[]{:S(2)}, u32[]{:S(2)}) collective-permute-start(f32[256,128]{1,0:T(8,128)S(1)} %add.21), channel_id=1, source_target_pairs={{0,96},{16,112},{32,64},{48,80},{64,32},{80,48},{96,0},{112,16},{1... | collective-permute-start | bytes 393224 | tf_op jit(solution)/shard_map/ppermute | solution.py:589
  16.7 10.5 %collective-permute-start.2 = (f32[256,128]{1,0:T(8,128)S(1)}, f32[256,128]{1,0:T(8,128)S(1)}, u32[]{:S(2)}, u32[]{:S(2)}) collective-permute-start(f32[256,128]{1,0:T(8,128)S(1)} %add.21), channel_id=1, source_target_pairs={{0,32},{16,48},{32,0},{48,16},{64,96},{80,112},{96,64},{112,80},{1... | collective-permute-start | bytes 393224 | tf_op jit(solution)/shard_map/ppermute | solution.py:589
  27.2 20.8 %collective-permute-start.7 = (f32[512,1024]{1,0:T(8,128)S(1)}, f32[512,1024]{1,0:T(8,128)S(1)}, u32[]{:S(2)}, u32[]{:S(2)}) collective-permute-start(f32[512,1024]{1,0:T(8,128)S(1)} %get-tuple-element.78), channel_id=1, source_target_pairs={{0,16},{16,0},{32,48},{48,32},{64,80},{80,64},{96,112},{112,96},{1... | collective-permute-start | bytes 6291464 | tf_op jit(solution)/shard_map/ppermute | solution.py:589
  29.4 18.6 %collective-permute-start.5 = (f32[1024,128]{1,0:T(8,128)S(1)}, f32[1024,128]{1,0:T(8,128)S(1)}, u32[]{:S(2)}, u32[]{:S(2)}) collective-permute-start(f32[1024,128]{1,0:T(8,128)S(1)} %get-tuple-element.75), channel_id=1, source_target_pairs={{0,12},{1,13},{2,14},{3,15},{4,8},{5,9},{6,10},{7,11},{16,28},{17,... | collective-permute-start | bytes 1572872 | tf_op jit(solution)/shard_map/ppermute | solution.py:593
  33.9 14.1 %collective-permute-start.6 = (f32[256,128]{1,0:T(8,128)S(1)}, f32[256,128]{1,0:T(8,128)S(1)}, u32[]{:S(2)}, u32[]{:S(2)}) collective-permute-start(f32[256,128]{1,0:T(8,128)S(1)} %add_add_fusion), channel_id=1, source_target_pairs={{0,12},{1,13},{2,14},{3,15},{4,8},{5,9},{6,10},{7,11},{16,28},{17,... | collective-permute-start | bytes 393224 | tf_op jit(solution)/shard_map/ppermute | solution.py:593
  35.2 13.3 %collective-permute-start.8 = (f32[5,128,128]{2,1,0:T(8,128)S(1)}, f32[5,128,128]{2,1,0:T(8,128)S(1)}, u32[]{:S(2)}, u32[]{:S(2)}) collective-permute-start(f32[5,128,128]{2,1,0:T(8,128)S(1)} %get-tuple-element.79), channel_id=1, source_target_pairs={{0,64},{16,80},{32,96},{48,112},{64,0},{80,16},{96,32},{112,48},{1... | collective-permute-start | bytes 983048 | tf_op jit(solution)/shard_map/ppermute | solution.py:589
  48.6 18.1 %collective-permute-start.12 = (f32[256,1024]{1,0:T(8,128)S(1)}, f32[256,1024]{1,0:T(8,128)S(1)}, u32[]{:S(2)}, u32[]{:S(2)}) collective-permute-start(f32[256,1024]{1,0:T(8,128)S(1)} %slice_select_fusion), channel_id=1, source_target_pairs={{0,32},{16,112},{32,0},{48,80},{64,96},{80,48},{96,64},{112,16},{1... | collective-permute-start | bytes 3145736 | tf_op jit(solution)/shard_map/ppermute | solution.py:618
  51.3 15.4 %collective-permute-start.10 = (f32[1,512,128]{2,1,0:T(8,128)S(1)}, f32[1,512,128]{2,1,0:T(8,128)S(1)}, u32[]{:S(2)}, u32[]{:S(2)}) collective-permute-start(f32[1,512,128]{2,1,0:T(8,128)S(1)} %get-tuple-element.121), channel_id=1, source_target_pairs={{0,3},{1,2},{2,1},{3,0},{4,7},{5,6},{6,5},{7,4},{8,11},{9,10},{10,... | collective-permute-start | bytes 786440 | tf_op jit(solution)/shard_map/ppermute | solution.py:631
  54.8 11.9 %collective-permute-start.11 = (f32[1,256,128]{2,1,0:T(8,128)S(1)}, f32[1,256,128]{2,1,0:T(8,128)S(1)}, u32[]{:S(2)}, u32[]{:S(2)}) collective-permute-start(f32[1,256,128]{2,1,0:T(8,128)S(1)} %select_bitcast_fusion), channel_id=1, source_target_pairs={{0,4},{1,5},{2,6},{3,7},{4,0},{5,1},{6,2},{7,3},{8,12},{9,13},{10,... | collective-permute-start | bytes 393224 | tf_op jit(solution)/shard_map/ppermute | solution.py:655
  55.8 10.9 %collective-permute-start.9 = (f32[1,512,128]{2,1,0:T(8,128)S(1)}, f32[1,512,128]{2,1,0:T(8,128)S(1)}, u32[]{:S(2)}, u32[]{:S(2)}) collective-permute-start(f32[1,512,128]{2,1,0:T(8,128)S(1)} %get-tuple-element.122), channel_id=1, source_target_pairs={{0,1},{1,0},{2,3},{3,2},{4,5},{5,4},{6,7},{7,6},{8,9},{9,8},{10,11... | collective-permute-start | bytes 786440 | tf_op jit(solution)/shard_map/ppermute | solution.py:631
  67.1 8.4 %collective-permute-start.16 = (f32[128,1024]{1,0:T(8,128)S(1)}, f32[128,1024]{1,0:T(8,128)S(1)}, u32[]{:S(2)}, u32[]{:S(2)}) collective-permute-start(f32[128,1024]{1,0:T(8,128)S(1)} %slice_select_fusion.1), channel_id=1, source_target_pairs={{0,96},{16,48},{32,64},{48,16},{64,32},{80,112},{96,0},{112,80},{1... | collective-permute-start | bytes 1572872 | tf_op jit(solution)/shard_map/ppermute | solution.py:618
  67.2 9.6 %collective-permute-start.13 = (f32[2,512,128]{2,1,0:T(8,128)S(1)}, f32[2,512,128]{2,1,0:T(8,128)S(1)}, u32[]{:S(2)}, u32[]{:S(2)}) collective-permute-start(f32[2,512,128]{2,1,0:T(8,128)S(1)} %pad_maximum_fusion.5), channel_id=1, source_target_pairs={{0,3},{1,2},{2,1},{3,0},{4,7},{5,6},{6,5},{7,4},{8,11},{9,10},{10,... | collective-permute-start | bytes 1572872 | tf_op jit(solution)/shard_map/ppermute | solution.py:631
  67.5 9.1 %collective-permute-start.15 = (f32[2,256,128]{2,1,0:T(8,128)S(1)}, f32[2,256,128]{2,1,0:T(8,128)S(1)}, u32[]{:S(2)}, u32[]{:S(2)}) collective-permute-start(f32[2,256,128]{2,1,0:T(8,128)S(1)} %pad_maximum_fusion.8), channel_id=1, source_target_pairs={{0,1},{1,0},{2,3},{3,2},{4,5},{5,4},{6,7},{7,6},{8,9},{9,8},{10,11... | collective-permute-start | bytes 786440 | tf_op jit(solution)/shard_map/ppermute | solution.py:655
  70.1 8.3 %collective-permute-start.14 = (f32[2,512,128]{2,1,0:T(8,128)S(1)}, f32[2,512,128]{2,1,0:T(8,128)S(1)}, u32[]{:S(2)}, u32[]{:S(2)}) collective-permute-start(f32[2,512,128]{2,1,0:T(8,128)S(1)} %pad_maximum_fusion.6), channel_id=1, source_target_pairs={{0,1},{1,0},{2,3},{3,2},{4,5},{5,4},{6,7},{7,6},{8,9},{9,8},{10,11... | collective-permute-start | bytes 1572872 | tf_op jit(solution)/shard_map/ppermute | solution.py:631
  75.6 8.4 %collective-permute-start.17 = (f32[128,1024]{1,0:T(8,128)S(1)}, f32[128,1024]{1,0:T(8,128)S(1)}, u32[]{:S(2)}, u32[]{:S(2)}) collective-permute-start(f32[128,1024]{1,0:T(8,128)S(1)} %select_add_fusion.1), channel_id=1, source_target_pairs={{0,96},{16,48},{32,64},{48,16},{64,32},{80,112},{96,0},{112,80},{1... | collective-permute-start | bytes 1572872 | tf_op jit(solution)/shard_map/ppermute | solution.py:621
  84.3 15.2 %collective-permute-start.21 = (f32[256,1024]{1,0:T(8,128)S(1)}, f32[256,1024]{1,0:T(8,128)S(1)}, u32[]{:S(2)}, u32[]{:S(2)}) collective-permute-start(f32[256,1024]{1,0:T(8,128)S(1)} %pad_maximum_fusion.3), channel_id=1, source_target_pairs={{0,32},{16,112},{32,0},{48,80},{64,96},{80,48},{96,64},{112,16},{1... | collective-permute-start | bytes 3145736 | tf_op jit(solution)/shard_map/ppermute | solution.py:621
  84.9 9.5 %collective-permute-start.20 = (f32[4,256,128]{2,1,0:T(8,128)S(1)}, f32[4,256,128]{2,1,0:T(8,128)S(1)}, u32[]{:S(2)}, u32[]{:S(2)}) collective-permute-start(f32[4,256,128]{2,1,0:T(8,128)S(1)} %pad_maximum_fusion.7), channel_id=1, source_target_pairs={{0,3},{1,2},{2,1},{3,0},{4,7},{5,6},{6,5},{7,4},{8,11},{9,10},{10,... | collective-permute-start | bytes 1572872 | tf_op jit(solution)/shard_map/ppermute | solution.py:655
  86.4 13.9 %collective-permute-start.18 = (f32[4,512,128]{2,1,0:T(8,128)S(1)}, f32[4,512,128]{2,1,0:T(8,128)S(1)}, u32[]{:S(2)}, u32[]{:S(2)}) collective-permute-start(f32[4,512,128]{2,1,0:T(8,128)S(1)} %pad_maximum_fusion.1.refs_0_), channel_id=1, source_target_pairs={{0,4},{1,5},{2,6},{3,7},{4,0},{5,1},{6,2},{7,3},{8,12},{9,13},{10,... | collective-permute-start | bytes 3145736 | tf_op jit(solution)/shard_map/ppermute | solution.py:631
  86.4 20.5 %collective-permute-start.19 = (f32[4,512,128]{2,1,0:T(8,128)S(1)}, f32[4,512,128]{2,1,0:T(8,128)S(1)}, u32[]{:S(2)}, u32[]{:S(2)}) collective-permute-start(f32[4,512,128]{2,1,0:T(8,128)S(1)} %pad_maximum_fusion.2.refs_4_), channel_id=1, source_target_pairs={{0,12},{1,13},{2,14},{3,15},{4,8},{5,9},{6,10},{7,11},{8,4},{9,5},... | collective-permute-start | bytes 3145736 | tf_op jit(solution)/shard_map/ppermute | solution.py:631
  99.7 16.5 %copy-start = (f32[2,512,512]{2,1,0:T(8,128)S(1)}, f32[2,512,512]{2,1,0:T(8,128)}, u32[]{:S(2)}) copy-start(f32[2,512,512]{2,1,0:T(8,128)} %inverses.1) | copy-start | bytes 6291460
  106.9 8.6 %collective-permute-start.26 = (f32[512,1024]{1,0:T(8,128)S(1)}, f32[512,1024]{1,0:T(8,128)S(1)}, u32[]{:S(2)}, u32[]{:S(2)}) collective-permute-start(f32[512,1024]{1,0:T(8,128)S(1)} %pad_maximum_fusion.own), channel_id=1, source_target_pairs={{0,16},{16,0},{32,48},{48,32},{64,80},{80,64},{96,112},{112,96},{1... | collective-permute-start | bytes 6291464 | tf_op jit(solution)/shard_map/ppermute | solution.py:589
  106.9 8.0 %collective-permute-start.27 = (f32[8,256,128]{2,1,0:T(8,128)S(1)}, f32[8,256,128]{2,1,0:T(8,128)S(1)}, u32[]{:S(2)}, u32[]{:S(2)}) collective-permute-start(f32[8,256,128]{2,1,0:T(8,128)S(1)} %pad_maximum_fusion.4.own), channel_id=1, source_target_pairs={{0,16},{16,0},{32,48},{48,32},{64,80},{80,64},{96,112},{112,96},{1... | collective-permute-start | bytes 3145736 | tf_op jit(solution)/shard_map/ppermute | solution.py:589
  107.4 53.1 %collective-permute-start.28 = (f32[35,128,128]{2,1,0:T(8,128)S(1)}, f32[35,128,128]{2,1,0:T(8,128)S(1)}, u32[]{:S(2)}, u32[]{:S(2)}) collective-permute-start(f32[35,128,128]{2,1,0:T(8,128)S(1)} %get-tuple-element.115), channel_id=1, source_target_pairs={{0,64},{16,80},{32,96},{48,112},{64,0},{80,16},{96,32},{112,48},{1... | collective-permute-start | bytes 6881288 | tf_op jit(solution)/shard_map/ppermute | solution.py:589
  110.7 15.5 %collective-permute-start.22 = (f32[4,512,128]{2,1,0:T(8,128)S(1)}, f32[4,512,128]{2,1,0:T(8,128)S(1)}, u32[]{:S(2)}, u32[]{:S(2)}) collective-permute-start(f32[4,512,128]{2,1,0:T(8,128)S(1)} %pad_maximum_fusion.1.refs_0_), channel_id=1, source_target_pairs={{0,12},{1,13},{2,14},{3,15},{4,8},{5,9},{6,10},{7,11},{8,4},{9,5},... | collective-permute-start | bytes 3145736 | tf_op jit(solution)/shard_map/ppermute | solution.py:631
  113.7 13.9 %collective-permute-start.23 = (f32[4,512,128]{2,1,0:T(8,128)S(1)}, f32[4,512,128]{2,1,0:T(8,128)S(1)}, u32[]{:S(2)}, u32[]{:S(2)}) collective-permute-start(f32[4,512,128]{2,1,0:T(8,128)S(1)} %pad_maximum_fusion.2.refs_4_), channel_id=1, source_target_pairs={{0,4},{1,5},{2,6},{3,7},{4,0},{5,1},{6,2},{7,3},{8,12},{9,13},{10,... | collective-permute-start | bytes 3145736 | tf_op jit(solution)/shard_map/ppermute | solution.py:631
  114.9 22.5 %collective-permute-start.24 = (f32[4,512,128]{2,1,0:T(8,128)S(1)}, f32[4,512,128]{2,1,0:T(8,128)S(1)}, u32[]{:S(2)}, u32[]{:S(2)}) collective-permute-start(f32[4,512,128]{2,1,0:T(8,128)S(1)} %collective-permute-done.18.refs_1_), channel_id=1, source_target_pairs={{0,12},{1,13},{2,14},{3,15},{4,8},{5,9},{6,10},{7,11},{8,4},{9,5},... | collective-permute-start | bytes 3145736 | tf_op jit(solution)/shard_map/ppermute | solution.py:631
  115.5 23.3 %collective-permute-start.25 = (f32[4,512,128]{2,1,0:T(8,128)S(1)}, f32[4,512,128]{2,1,0:T(8,128)S(1)}, u32[]{:S(2)}, u32[]{:S(2)}) collective-permute-start(f32[4,512,128]{2,1,0:T(8,128)S(1)} %collective-permute-done.19.refs_5_), channel_id=1, source_target_pairs={{0,4},{1,5},{2,6},{3,7},{4,0},{5,1},{6,2},{7,3},{8,12},{9,13},{10,... | collective-permute-start | bytes 3145736 | tf_op jit(solution)/shard_map/ppermute | solution.py:631

commit v7 on v6

--- a/solution.py
+++ b/solution.py
@@ -98,10 +98,9 @@
     rest_a, rest_b = rests
     parts = (
         (0, 0, rest_a),
-        (0, 5, rest_b.at[pl.ds(0, 5)]),
-        (1, 0, rest_b.at[pl.ds(5, 10)]),
-        (2, 0, rest_b.at[pl.ds(15, 10)]),
-        (3, 0, rest_b.at[pl.ds(25, 10)]),
+        (1, 0, rest_b.at[pl.ds(0, 10)]),
+        (2, 0, rest_b.at[pl.ds(10, 10)]),
+        (3, 0, rest_b.at[pl.ds(20, 10)]),
     )
     for n, (j, start, target) in enumerate(parts):
         d = j + (j >= place).astype(jnp.int32)
@@ -172,8 +171,8 @@
     return pl.pallas_call(
         prepare_kernel,
         out_shape=[
-            jax.ShapeDtypeStruct((5, BLK, BLK), F32),
-            jax.ShapeDtypeStruct((35, BLK, BLK), F32),
+            jax.ShapeDtypeStruct((10, BLK, BLK), F32),
+            jax.ShapeDtypeStruct((30, BLK, BLK), F32),
             jax.ShapeDtypeStruct((2048, BLK), F32),
             jax.ShapeDtypeStruct((256, BLK), F32),
             jax.ShapeDtypeStruct((256, BLK), F32),
@@ -185,7 +184,7 @@
             pltpu.VMEM((10, BLK, 640), F32),
             pltpu.VMEM((10, BLK, BLK), F32),
             pltpu.VMEM((PANEL, BLK), F32),
-            pltpu.SemaphoreType.DMA((8,)),
+            pltpu.SemaphoreType.DMA((7,)),
         ],
         compiler_params=params(24),
         cost_estimate=cost(0, 9 * MIB),
@@ -532,7 +531,7 @@
     del front
     core = table[ROW] % 2
     copies = []
-    places = [(1, m) for m in range(5, 10)] + [(j, m) for j in (2, 3, 4) for m in range(10)]
+    places = [(j, m) for j in (2, 3, 4) for m in range(10)]
     for n, (column, m) in enumerate(places):
         columns = pl.ds(pl.multiple_of(table[GOT_COL + column] * BLK, BLK), BLK)
         rows = pl.ds(pl.multiple_of(table[GOT_ROW + m] * BLK, BLK), BLK)
@@ -572,9 +571,9 @@
         in_specs=[SMEM, SMEM, SMEM, HBM] + [VMEM] * 2,
         out_specs=HBM,
         scratch_shapes=[
-            pltpu.VMEM((35, BLK, BLK), F32),
-            pltpu.SemaphoreType.DMA((35,)),
-            pltpu.SemaphoreType.DMA((35,)),
+            pltpu.VMEM((30, BLK, BLK), F32),
+            pltpu.SemaphoreType.DMA((30,)),
+            pltpu.SemaphoreType.DMA((30,)),
             pltpu.SemaphoreType.DMA(()),
         ],
         input_output_aliases={3: 0},
@@ -659,22 +658,22 @@
         came = [gather_step(held[w], w, k) for w in range(2)]
         held = [jnp.concatenate([h, c], axis=0) for h, c in zip(held, came)]
         corner = corner_step(corner, k)
-        total = halve(total, k)
-        if k == 1:
-            total = double(total, 1)
-        if k == 0:
-            front = extend(table, front, pieces, (got0, got_a))
-        held, corner, total, front = together((held, corner, total, front))
+    total = halve(total, 0)
+    held, corner, total = together((held, corner, total))
     came = [gather_step(held[w], w, 2) for w in range(2)]
     corner = corner_step(corner, 2)
-    total = double(total, 0)
-    came, corner, total, rest_b = together((came, corner, total, rest_b))
+    total = double(halve(total, 1), 1)
+    came, corner, total, front = together((came, corner, total, front))
+    held_far = [gather_step(held[w], w, 3) for w in range(2)]
+    front = extend(table, front, pieces, (got0, got_a))
+    *factors, cross = corners(table, corner, by_row(corner, 1), diag_inverses)
+    came, held_far, total, rest_b, factors, cross, front = together(
+        (came, held_far, double(total, 0), rest_b, factors, cross, front)
+    )
+    came_far = [gather_step(came[w], w, 3) for w in range(2)]
     got_b = by_row(rest_b, 4)
-    held_far = [gather_step(held[w], w, 3) for w in range(2)]
-    came_far = [gather_step(came[w], w, 3) for w in range(2)]
-    *factors, cross = corners(table, corner, by_row(corner, 1), diag_inverses)
     *right, patch = right_factor(table, total, by_row(total, 1), factors, cross)
-    held_far, came_far, right, patch = together((held_far, came_far, right, patch))
+    came_far, right, patch = together((came_far, right, patch))
     blocks = [(held[w], came[w], held_far[w], came_far[w]) for w in range(2)]
     front = update(table, front, blocks, right, marks).reshape(2048, 1024)
     return finish(table, (list_other, list_mine), front, got_b, patch)

time: 168 us -> 166 us (0.988); the launches traced: 165 us -> 166 us
  starting transfers between devices: 43.4 us -> 37.4 us
  waiting for transfers between devices: 47.7 us -> 53.7 us
    ppermute x10, waiting for transfers between devices: 3.64 us -> 17.1 us  [swap(): return lax.ppermute(block, axis, [(i, partner(i)) for i in range(count)])]
    ppermute x10, starting transfers between devices: 12.7 us -> 5.4 us  [gather_step(): return lax.ppermute(block, ('row', 'col'), route)]
    ppermute x10, waiting for transfers between devices: 21.4 us -> 15.7 us  [gather_step(): return lax.ppermute(block, ('row', 'col'), route)]
    ppermute x2, waiting for transfers between devices: 4.68 us -> 7.53 us  [halve(): return stay + lax.ppermute(leave, 'row', rings[step])]
    ppermute x2, waiting for transfers between devices: 10.6 us -> 8.23 us  [double(): came = lax.ppermute(part, 'row', rings[step])]
    ppermute x3, waiting for transfers between devices: 6.17 us -> 3.84 us  [corner_step(): lax.ppermute(block, ('row', 'col'), route)]
where the time goes in v7:
time: 166 us
  Pallas kernels  71.5 us (43%)
  waiting for transfers between devices  53.7 us (32%)
  starting transfers between devices  37.4 us (23%)
  other arithmetic  2.39 us (1%)
    pallas_call x1, Pallas kernels, update(): pl.pallas_call(update_kernel, out_shape=pltpu.HBM((2, 1024, 1024), F32),...  20.3 us
    pallas_call x2, Pallas kernels, pivot_terms(): pl.pallas_call(functools.partial(pivot_kernel, mine_half), out_shape=[jax...  18.1 us
    ppermute x10, starting transfers between devices, swap(): return lax.ppermute(block, axis, [(i, partner(i)) for i in range(count)])  17.8 us
    ppermute x10, waiting for transfers between devices, swap(): return lax.ppermute(block, axis, [(i, partner(i)) for i in range(count)])  17.1 us
    ppermute x10, waiting for transfers between devices, gather_step(): return lax.ppermute(block, ('row', 'col'), route)  15.7 us
    pallas_call x1, Pallas kernels, extend(): pl.pallas_call(functools.partial(extend_kernel, [g.shape[0] for g in got]...  11 us
    ppermute x2, waiting for transfers between devices, double(): came = lax.ppermute(part, 'row', rings[step])  8.23 us
    pallas_call x1, Pallas kernels, right_factor(): pl.pallas_call(factor_kernel, out_shape=[shape, shape, jax.ShapeDtypeStru...  7.86 us
  transfers between devices with their start and end apart: 29, of which 16 were waited for; matrix products, arithmetic and copies ran while one was open for 1% of the time, Pallas kernels for 39%

profile of v7, /device:TPU:1, one launch (start us, length us, event | category | flops | bytes accessed | tf_op | source)
XLA Modules:
  0.0 165.6 jit_solution(7827792192311367618)
XLA Ops:
  0.0 1.8 %cut.1.first = f32[10,128,128]{2,1,0:T(8,128)S(1)} custom-call(s32[2,80]{1,0:T(2,128)} %maps.7, f32[10,2,128,640]{3,2,1,0:T(8,128)} %bitcast.12), custom_call_target="tpu_custom_call" | custom-call | bytes 1048576 | tf_op jit(solution)/shard_map/cut/pallas_call | solution.py:67
  1.9 4.5 %collective-permute-start = (f32[10,128,128]{2,1,0:T(8,128)S(1)}, f32[10,128,128]{2,1,0:T(8,128)S(1)}, u32[]{:S(2)}, u32[]{:S(2)}) collective-permute-start(f32[10,128,128]{2,1,0:T(8,128)S(1)} %cut.1.first), channel_id=1, source_target_pairs={{0,64},{16,80},{32,96},{48,112},{64,0},{80,16},{96,32},{112,48},{1... | collective-permute-start | bytes 1966088 | tf_op jit(solution)/shard_map/ppermute | solution.py:588
  6.4 5.1 %prepare.1 = (f32[10,128,128]{2,1,0:T(8,128)S(1)}, f32[30,128,128]{2,1,0:T(8,128)S(1)}, f32[2048,128]{1,0:T(8,128)S(1)}, f32[256,128]{1,0:T(8,128)S(1)}, f32[256,128]{1,0:T(8,128)S(1)}, /*index=5*/s32[64]{0:T(128)S(1)}) custom-call(s32[2,80]{1,0:T(2,128)} %maps.7, s32[8,128]{1,0:T(8,128)} %bitcast.18, f32[2048,1024]{1,0:T(8,128)} %front.5, ...), custom_call_target="tpu_custom_call" | custom-call | bytes 9437184 | tf_op jit(solution)/shard_map/prepare/pallas_call | solution.py:171
  11.5 1.0 collective-permute-start.1
  12.5 1.0 collective-permute-done.1
  13.6 3.1 %collective-permute-start.3 = (f32[256,128]{1,0:T(8,128)S(1)}, f32[256,128]{1,0:T(8,128)S(1)}, u32[]{:S(2)}, u32[]{:S(2)}) collective-permute-start(f32[256,128]{1,0:T(8,128)S(1)} %add.21), channel_id=1, source_target_pairs={{0,96},{16,112},{32,64},{48,80},{64,32},{80,48},{96,0},{112,16},{1... | collective-permute-start | bytes 393224 | tf_op jit(solution)/shard_map/ppermute | solution.py:588
  16.7 9.0 %pivot_terms_other.1 = (f32[512,1024]{1,0:T(8,128)S(1)}, f32[2048,128]{1,0:T(8,128)S(1)}, s32[513]{0:T(1024)S(1)}) custom-call(s32[2,80]{1,0:T(2,128)} %maps.7, s32[1024]{0:T(1024)} %pivots.1, f32[2048,1024]{1,0:T(8,128)} %front.5, f32[2560,640]{1,0:T(8,128)} %children.3), custom_call_target="tpu_custom_call" | custom-call | bytes 25165824 | tf_op jit(solution)/shard_map/pivot_terms_other/pallas_call | solution.py:263
  25.8 1.4 collective-permute-done.3
  27.2 1.3 collective-permute-start.7
  28.6 0.8 whole_panel.1
  29.4 4.5 %collective-permute-start.5 = (f32[1024,128]{1,0:T(8,128)S(1)}, f32[1024,128]{1,0:T(8,128)S(1)}, u32[]{:S(2)}, u32[]{:S(2)}) collective-permute-start(f32[1024,128]{1,0:T(8,128)S(1)} %get-tuple-element.77), channel_id=1, source_target_pairs={{0,12},{1,13},{2,14},{3,15},{4,8},{5,9},{6,10},{7,11},{16,28},{17,... | collective-permute-start | bytes 1572872 | tf_op jit(solution)/shard_map/ppermute | solution.py:592
  33.9 2.4 %collective-permute-start.8 = (f32[10,128,128]{2,1,0:T(8,128)S(1)}, f32[10,128,128]{2,1,0:T(8,128)S(1)}, u32[]{:S(2)}, u32[]{:S(2)}) collective-permute-start(f32[10,128,128]{2,1,0:T(8,128)S(1)} %get-tuple-element.81), channel_id=1, source_target_pairs={{0,64},{16,80},{32,96},{48,112},{64,0},{80,16},{96,32},{112,48},{1... | collective-permute-start | bytes 1966088 | tf_op jit(solution)/shard_map/ppermute | solution.py:588
  36.3 1.3 collective-permute-start.6
  37.6 9.1 %pivot_terms_mine.1 = (f32[512,1024]{1,0:T(8,128)S(1)}, f32[2048,128]{1,0:T(8,128)S(1)}, s32[513]{0:T(1024)S(1)}) custom-call(s32[2,80]{1,0:T(2,128)} %maps.7, s32[1024]{0:T(1024)} %pivots.1, f32[2048,1024]{1,0:T(8,128)} %front.5, f32[2560,640]{1,0:T(8,128)} %children.3, f32[2048,128]{1,0:T(8,128)S(1)} %get-tuple-element.71.refs_0_), custom_call_target="tpu_custom_call" | custom-call | bytes 25165824 | tf_op jit(solution)/shard_map/pivot_terms_mine/pallas_call | solution.py:263
  46.7 1.3 collective-permute-done.6
  48.1 0.6 add.25
  48.6 2.9 %collective-permute-done.8.refs_4_.refs_5_ = f32[10,128,128]{2,1,0:T(8,128)S(1)} collective-permute-done((f32[10,128,128]{2,1,0:T(8,128)S(1)}, f32[10,128,128]{2,1,0:T(8,128)S(1)}, u32[]{:S(2)}, u32[]{:S(2)}) %collective-permute-start.8) | collective-permute-done | bytes 655392 | tf_op jit(solution)/shard_map/ppermute | solution.py:588
  51.5 0.7 collective-permute-start.11
  52.4 2.6 %collective-permute-start.15 = (f32[256,1024]{1,0:T(8,128)S(1)}, f32[256,1024]{1,0:T(8,128)S(1)}, u32[]{:S(2)}, u32[]{:S(2)}) collective-permute-start(f32[256,1024]{1,0:T(8,128)S(1)} %slice_select_fusion), channel_id=1, source_target_pairs={{0,32},{16,112},{32,0},{48,80},{64,96},{80,48},{96,64},{112,16},{1... | collective-permute-start | bytes 3145736 | tf_op jit(solution)/shard_map/ppermute | solution.py:617
  55.0 1.0 collective-permute-start.13
  56.0 2.3 %collective-permute-done.11 = f32[1,512,128]{2,1,0:T(8,128)S(1)} collective-permute-done((f32[1,512,128]{2,1,0:T(8,128)S(1)}, f32[1,512,128]{2,1,0:T(8,128)S(1)}, u32[]{:S(2)}, u32[]{:S(2)}) %collective-permute-start.11) | collective-permute-done | bytes 262176 | tf_op jit(solution)/shard_map/ppermute | solution.py:630
  58.5 0.9 collective-permute-done.13
  59.4 3.6 %collective-permute-start.14 = (f32[2,256,128]{2,1,0:T(8,128)S(1)}, f32[2,256,128]{2,1,0:T(8,128)S(1)}, u32[]{:S(2)}, u32[]{:S(2)}) collective-permute-start(f32[2,256,128]{2,1,0:T(8,128)S(1)} %pad_maximum_fusion.8), channel_id=1, source_target_pairs={{0,1},{1,0},{2,3},{3,2},{4,5},{5,4},{6,7},{7,6},{8,9},{9,8},{10,11... | collective-permute-start | bytes 786440 | tf_op jit(solution)/shard_map/ppermute | solution.py:654
  63.0 0.8 collective-permute-start.10
  63.7 3.0 %collective-permute-done.14 = f32[2,256,128]{2,1,0:T(8,128)S(1)} collective-permute-done((f32[2,256,128]{2,1,0:T(8,128)S(1)}, f32[2,256,128]{2,1,0:T(8,128)S(1)}, u32[]{:S(2)}, u32[]{:S(2)}) %collective-permute-start.14) | collective-permute-done | bytes 262176 | tf_op jit(solution)/shard_map/ppermute | solution.py:654
  66.7 0.4 collective-permute-done.12
  67.2 5.3 %collective-permute-done.10 = f32[2,512,128]{2,1,0:T(8,128)S(1)} collective-permute-done((f32[2,512,128]{2,1,0:T(8,128)S(1)}, f32[2,512,128]{2,1,0:T(8,128)S(1)}, u32[]{:S(2)}, u32[]{:S(2)}) %collective-permute-start.10) | collective-permute-done | bytes 524320 | tf_op jit(solution)/shard_map/ppermute | solution.py:630
  72.7 0.3 select_add_fusion
  73.3 0.6 collective-permute-start.17
  73.9 7.5 %collective-permute-done.19 = f32[128,1024]{1,0:T(8,128)S(1)} collective-permute-done((f32[128,1024]{1,0:T(8,128)S(1)}, f32[128,1024]{1,0:T(8,128)S(1)}, u32[]{:S(2)}, u32[]{:S(2)}) %collective-permute-start.19) | collective-permute-done | bytes 524320 | tf_op jit(solution)/shard_map/ppermute | solution.py:617
  81.7 8.2 %collective-permute-done.20 = f32[128,1024]{1,0:T(8,128)S(1)} collective-permute-done((f32[128,1024]{1,0:T(8,128)S(1)}, f32[128,1024]{1,0:T(8,128)S(1)}, u32[]{:S(2)}, u32[]{:S(2)}) %collective-permute-start.20) | collective-permute-done | bytes 524320 | tf_op jit(solution)/shard_map/ppermute | solution.py:620
  90.2 4.0 %collective-permute-done.17.refs_5_ = f32[4,512,128]{2,1,0:T(8,128)S(1)} collective-permute-done((f32[4,512,128]{2,1,0:T(8,128)S(1)}, f32[4,512,128]{2,1,0:T(8,128)S(1)}, u32[]{:S(2)}, u32[]{:S(2)}) %collective-permute-start.17) | collective-permute-done | bytes 1048608 | tf_op jit(solution)/shard_map/ppermute | solution.py:630
  94.1 3.3 %collective-permute-start.24 = (f32[8,256,128]{2,1,0:T(8,128)S(1)}, f32[8,256,128]{2,1,0:T(8,128)S(1)}, u32[]{:S(2)}, u32[]{:S(2)}) collective-permute-start(f32[8,256,128]{2,1,0:T(8,128)S(1)} %pad_maximum_fusion.3.own), channel_id=1, source_target_pairs={{0,16},{16,0},{32,48},{48,32},{64,80},{80,64},{96,112},{112,96},{1... | collective-permute-start | bytes 3145736 | tf_op jit(solution)/shard_map/ppermute | solution.py:588
  97.4 0.9 collective-permute-start.23
  98.3 1.4 collective-permute-start.21
  99.7 11.0 %extend.1.front = f32[2,1024,1024]{2,1,0:T(8,128)} custom-call(s32[64]{0:T(128)S(1)} %get-tuple-element.64.table, f32[2,1024,1024]{2,1,0:T(8,128)} %bitcast.16, f32[10,2,128,640]{3,2,1,0:T(8,128)} %bitcast.14, f32[10,2,128,640]{3,2,1,0:T(8,128)} %bitcast.15, f32[10,128,128]{2,1,0:T(8,128)S(1)} %collective-permute-done.got.refs_2_.refs_3_, ...), custom_call_target="tpu_custom_call" | custom-call | bytes 1048576 | tf_op jit(solution)/shard_map/extend/pallas_call | solution.py:444
  110.7 2.0 %corners.1 = (bf16[3,512,512]{2,1,0:T(8,128)(2,1)S(1)}, bf16[3,512,512]{2,1,0:T(8,128)(2,1)S(1)}, f32[512,512]{1,0:T(8,128)S(1)}) custom-call(s32[64]{0:T(128)S(1)} %get-tuple-element.64.table, f32[8,256,128]{2,1,0:T(8,128)S(1)} %pad_maximum_fusion.3.own, f32[8,256,128]{2,1,0:T(8,128)S(1)} %collective-permute-done.24.swapped, f32[2,512,512]{2,1,0:T(8,128)S(1)} %copy-done), custom_call_target="tpu_custom_call" | custom-call | flops 805306368 | bytes 8388608 | tf_op jit(solution)/shard_map/corners/pallas_call | solution.py:341
  112.7 0.3 broadcast_select_fusion.1
  113.4 0.4 collective-permute-start.27
  113.8 0.9 collective-permute-start.25
  114.7 0.9 collective-permute-start.26
  115.6 1.7 %collective-permute-start.28 = (f32[30,128,128]{2,1,0:T(8,128)S(1)}, f32[30,128,128]{2,1,0:T(8,128)S(1)}, u32[]{:S(2)}, u32[]{:S(2)}) collective-permute-start(f32[30,128,128]{2,1,0:T(8,128)S(1)} %get-tuple-element.119), channel_id=1, source_target_pairs={{0,64},{16,80},{32,96},{48,112},{64,0},{80,16},{96,32},{112,48},{1... | collective-permute-start | bytes 5898248 | tf_op jit(solution)/shard_map/ppermute | solution.py:588
  117.3 0.3 collective-permute-done.27.swapped
  117.6 7.9 %right_factor.1 = (bf16[1024,1024]{1,0:T(8,128)(2,1)S(1)}, bf16[1024,1024]{1,0:T(8,128)(2,1)S(1)}, f32[512,1024]{1,0:T(8,128)S(1)}) custom-call(s32[64]{0:T(128)S(1)} %get-tuple-element.64.table, f32[512,1024]{1,0:T(8,128)S(1)} %pad_maximum_fusion.own, f32[512,1024]{1,0:T(8,128)S(1)} %collective-permute-done.27.swapped, ...), custom_call_target="tpu_custom_call" | custom-call | flops 6442450944 | bytes 14680064 | tf_op jit(solution)/shard_map/right_factor/pallas_call | solution.py:395
  125.5 3.5 %collective-permute-done.25.refs_3_ = f32[4,512,128]{2,1,0:T(8,128)S(1)} collective-permute-done((f32[4,512,128]{2,1,0:T(8,128)S(1)}, f32[4,512,128]{2,1,0:T(8,128)S(1)}, u32[]{:S(2)}, u32[]{:S(2)}) %collective-permute-start.25) | collective-permute-done | bytes 1048608 | tf_op jit(solution)/shard_map/ppermute | solution.py:630
  129.0 20.3 %update.1 = f32[2,1024,1024]{2,1,0:T(8,128)} custom-call(s32[64]{0:T(128)S(1)} %get-tuple-element.64.table, f32[2,1024,1024]{2,1,0:T(8,128)} %extend.1.front, f32[4,512,128]{2,1,0:T(8,128)S(1)} %pad_maximum_fusion.1.refs_0_, f32[4,512,128]{2,1,0:T(8,128)S(1)} %collective-permute-done.16.refs_1_, f32[4,512,128]{2,1,0:T(8,128)S(1)} %collective-permute-done.21.refs_2_, ...), custom_call_target="tpu_custom_call" | custom-call | flops 12884901888 | bytes 33554432 | tf_op jit(solution)/shard_map/update/pallas_call | solution.py:507
  149.2 11.6 %collective-permute-done.28.got = f32[30,128,128]{2,1,0:T(8,128)S(1)} collective-permute-done((f32[30,128,128]{2,1,0:T(8,128)S(1)}, f32[30,128,128]{2,1,0:T(8,128)S(1)}, u32[]{:S(2)}, u32[]{:S(2)}) %collective-permute-start.28) | collective-permute-done | bytes 1966112 | tf_op jit(solution)/shard_map/ppermute | solution.py:588
  160.8 4.6 %finish.1 = f32[2048,1024]{1,0:T(8,128)} custom-call(s32[64]{0:T(128)S(1)} %get-tuple-element.64.table, s32[513]{0:T(1024)S(1)} %get-tuple-element.65.list_other, s32[513]{0:T(1024)S(1)} %get-tuple-element.72.list_mine, f32[2048,1024]{1,0:T(8,128)} %bitcast.17, f32[30,128,128]{2,1,0:T(8,128)S(1)} %collective-permute-done.28.got, ...), custom_call_target="tpu_custom_call", output_to_operand_aliasing={{}: (3, {})} | custom-call | bytes 8388608 | tf_op jit(solution)/shard_map/finish/pallas_call | solution.py:568
  (43 shorter events, 2.0 us)
Async XLA Ops:
  1.9 25.4 %collective-permute-start = (f32[10,128,128]{2,1,0:T(8,128)S(1)}, f32[10,128,128]{2,1,0:T(8,128)S(1)}, u32[]{:S(2)}, u32[]{:S(2)}) collective-permute-start(f32[10,128,128]{2,1,0:T(8,128)S(1)} %cut.1.first), channel_id=1, source_target_pairs={{0,64},{16,80},{32,96},{48,112},{64,0},{80,16},{96,32},{112,48},{1... | collective-permute-start | bytes 1966088 | tf_op jit(solution)/shard_map/ppermute | solution.py:588
  11.5 2.0 %collective-permute-start.1 = (f32[256,128]{1,0:T(8,128)S(1)}, f32[256,128]{1,0:T(8,128)S(1)}, u32[]{:S(2)}, u32[]{:S(2)}) collective-permute-start(f32[256,128]{1,0:T(8,128)S(1)} %get-tuple-element.70), channel_id=1, source_target_pairs={{0,16},{16,0},{32,48},{48,32},{64,80},{80,64},{96,112},{112,96},{1... | collective-permute-start | bytes 393224 | tf_op jit(solution)/shard_map/ppermute | solution.py:588
  13.5 12.3 %collective-permute-start.4 = (f32[256,128]{1,0:T(8,128)S(1)}, f32[256,128]{1,0:T(8,128)S(1)}, u32[]{:S(2)}, u32[]{:S(2)}) collective-permute-start(f32[256,128]{1,0:T(8,128)S(1)} %add.21), channel_id=1, source_target_pairs={{0,64},{16,80},{32,96},{48,112},{64,0},{80,16},{96,32},{112,48},{1... | collective-permute-start | bytes 393224 | tf_op jit(solution)/shard_map/ppermute | solution.py:588
  13.6 13.6 %collective-permute-start.3 = (f32[256,128]{1,0:T(8,128)S(1)}, f32[256,128]{1,0:T(8,128)S(1)}, u32[]{:S(2)}, u32[]{:S(2)}) collective-permute-start(f32[256,128]{1,0:T(8,128)S(1)} %add.21), channel_id=1, source_target_pairs={{0,96},{16,112},{32,64},{48,80},{64,32},{80,48},{96,0},{112,16},{1... | collective-permute-start | bytes 393224 | tf_op jit(solution)/shard_map/ppermute | solution.py:588
  16.7 10.5 %collective-permute-start.2 = (f32[256,128]{1,0:T(8,128)S(1)}, f32[256,128]{1,0:T(8,128)S(1)}, u32[]{:S(2)}, u32[]{:S(2)}) collective-permute-start(f32[256,128]{1,0:T(8,128)S(1)} %add.21), channel_id=1, source_target_pairs={{0,32},{16,48},{32,0},{48,16},{64,96},{80,112},{96,64},{112,80},{1... | collective-permute-start | bytes 393224 | tf_op jit(solution)/shard_map/ppermute | solution.py:588
  27.2 20.8 %collective-permute-start.7 = (f32[512,1024]{1,0:T(8,128)S(1)}, f32[512,1024]{1,0:T(8,128)S(1)}, u32[]{:S(2)}, u32[]{:S(2)}) collective-permute-start(f32[512,1024]{1,0:T(8,128)S(1)} %get-tuple-element.80), channel_id=1, source_target_pairs={{0,16},{16,0},{32,48},{48,32},{64,80},{80,64},{96,112},{112,96},{1... | collective-permute-start | bytes 6291464 | tf_op jit(solution)/shard_map/ppermute | solution.py:588
  29.4 18.6 %collective-permute-start.5 = (f32[1024,128]{1,0:T(8,128)S(1)}, f32[1024,128]{1,0:T(8,128)S(1)}, u32[]{:S(2)}, u32[]{:S(2)}) collective-permute-start(f32[1024,128]{1,0:T(8,128)S(1)} %get-tuple-element.77), channel_id=1, source_target_pairs={{0,12},{1,13},{2,14},{3,15},{4,8},{5,9},{6,10},{7,11},{16,28},{17,... | collective-permute-start | bytes 1572872 | tf_op jit(solution)/shard_map/ppermute | solution.py:592
  33.9 17.6 %collective-permute-start.8 = (f32[10,128,128]{2,1,0:T(8,128)S(1)}, f32[10,128,128]{2,1,0:T(8,128)S(1)}, u32[]{:S(2)}, u32[]{:S(2)}) collective-permute-start(f32[10,128,128]{2,1,0:T(8,128)S(1)} %get-tuple-element.81), channel_id=1, source_target_pairs={{0,64},{16,80},{32,96},{48,112},{64,0},{80,16},{96,32},{112,48},{1... | collective-permute-start | bytes 1966088 | tf_op jit(solution)/shard_map/ppermute | solution.py:588
  36.3 11.7 %collective-permute-start.6 = (f32[256,128]{1,0:T(8,128)S(1)}, f32[256,128]{1,0:T(8,128)S(1)}, u32[]{:S(2)}, u32[]{:S(2)}) collective-permute-start(f32[256,128]{1,0:T(8,128)S(1)} %add_add_fusion), channel_id=1, source_target_pairs={{0,12},{1,13},{2,14},{3,15},{4,8},{5,9},{6,10},{7,11},{16,28},{17,... | collective-permute-start | bytes 393224 | tf_op jit(solution)/shard_map/ppermute | solution.py:592
  51.5 6.8 %collective-permute-start.11 = (f32[1,512,128]{2,1,0:T(8,128)S(1)}, f32[1,512,128]{2,1,0:T(8,128)S(1)}, u32[]{:S(2)}, u32[]{:S(2)}) collective-permute-start(f32[1,512,128]{2,1,0:T(8,128)S(1)} %get-tuple-element.125), channel_id=1, source_target_pairs={{0,3},{1,2},{2,1},{3,0},{4,7},{5,6},{6,5},{7,4},{8,11},{9,10},{10,... | collective-permute-start | bytes 786440 | tf_op jit(solution)/shard_map/ppermute | solution.py:630
  52.2 10.7 %collective-permute-start.9 = (f32[1,512,128]{2,1,0:T(8,128)S(1)}, f32[1,512,128]{2,1,0:T(8,128)S(1)}, u32[]{:S(2)}, u32[]{:S(2)}) collective-permute-start(f32[1,512,128]{2,1,0:T(8,128)S(1)} %get-tuple-element.126), channel_id=1, source_target_pairs={{0,1},{1,0},{2,3},{3,2},{4,5},{5,4},{6,7},{7,6},{8,9},{9,8},{10,11... | collective-permute-start | bytes 786440 | tf_op jit(solution)/shard_map/ppermute | solution.py:630
  52.4 20.3 %collective-permute-start.15 = (f32[256,1024]{1,0:T(8,128)S(1)}, f32[256,1024]{1,0:T(8,128)S(1)}, u32[]{:S(2)}, u32[]{:S(2)}) collective-permute-start(f32[256,1024]{1,0:T(8,128)S(1)} %slice_select_fusion), channel_id=1, source_target_pairs={{0,32},{16,112},{32,0},{48,80},{64,96},{80,48},{96,64},{112,16},{1... | collective-permute-start | bytes 3145736 | tf_op jit(solution)/shard_map/ppermute | solution.py:617
  55.0 4.4 %collective-permute-start.13 = (f32[1,256,128]{2,1,0:T(8,128)S(1)}, f32[1,256,128]{2,1,0:T(8,128)S(1)}, u32[]{:S(2)}, u32[]{:S(2)}) collective-permute-start(f32[1,256,128]{2,1,0:T(8,128)S(1)} %select_bitcast_fusion), channel_id=1, source_target_pairs={{0,4},{1,5},{2,6},{3,7},{4,0},{5,1},{6,2},{7,3},{8,12},{9,13},{10,... | collective-permute-start | bytes 393224 | tf_op jit(solution)/shard_map/ppermute | solution.py:654
  58.4 8.8 %collective-permute-start.12 = (f32[2,512,128]{2,1,0:T(8,128)S(1)}, f32[2,512,128]{2,1,0:T(8,128)S(1)}, u32[]{:S(2)}, u32[]{:S(2)}) collective-permute-start(f32[2,512,128]{2,1,0:T(8,128)S(1)} %pad_maximum_fusion.6), channel_id=1, source_target_pairs={{0,1},{1,0},{2,3},{3,2},{4,5},{5,4},{6,7},{7,6},{8,9},{9,8},{10,11... | collective-permute-start | bytes 1572872 | tf_op jit(solution)/shard_map/ppermute | solution.py:630
  59.4 7.3 %collective-permute-start.14 = (f32[2,256,128]{2,1,0:T(8,128)S(1)}, f32[2,256,128]{2,1,0:T(8,128)S(1)}, u32[]{:S(2)}, u32[]{:S(2)}) collective-permute-start(f32[2,256,128]{2,1,0:T(8,128)S(1)} %pad_maximum_fusion.8), channel_id=1, source_target_pairs={{0,1},{1,0},{2,3},{3,2},{4,5},{5,4},{6,7},{7,6},{8,9},{9,8},{10,11... | collective-permute-start | bytes 786440 | tf_op jit(solution)/shard_map/ppermute | solution.py:654
  63.0 9.6 %collective-permute-start.10 = (f32[2,512,128]{2,1,0:T(8,128)S(1)}, f32[2,512,128]{2,1,0:T(8,128)S(1)}, u32[]{:S(2)}, u32[]{:S(2)}) collective-permute-start(f32[2,512,128]{2,1,0:T(8,128)S(1)} %pad_maximum_fusion.5), channel_id=1, source_target_pairs={{0,3},{1,2},{2,1},{3,0},{4,7},{5,6},{6,5},{7,4},{8,11},{9,10},{10,... | collective-permute-start | bytes 1572872 | tf_op jit(solution)/shard_map/ppermute | solution.py:630
  73.0 8.4 %collective-permute-start.19 = (f32[128,1024]{1,0:T(8,128)S(1)}, f32[128,1024]{1,0:T(8,128)S(1)}, u32[]{:S(2)}, u32[]{:S(2)}) collective-permute-start(f32[128,1024]{1,0:T(8,128)S(1)} %slice_select_fusion.1), channel_id=1, source_target_pairs={{0,96},{16,48},{32,64},{48,16},{64,32},{80,112},{96,0},{112,80},{1... | collective-permute-start | bytes 1572872 | tf_op jit(solution)/shard_map/ppermute | solution.py:617
  73.1 8.5 %collective-permute-start.18 = (f32[4,256,128]{2,1,0:T(8,128)S(1)}, f32[4,256,128]{2,1,0:T(8,128)S(1)}, u32[]{:S(2)}, u32[]{:S(2)}) collective-permute-start(f32[4,256,128]{2,1,0:T(8,128)S(1)} %pad_maximum_fusion.7), channel_id=1, source_target_pairs={{0,3},{1,2},{2,1},{3,0},{4,7},{5,6},{6,5},{7,4},{8,11},{9,10},{10,... | collective-permute-start | bytes 1572872 | tf_op jit(solution)/shard_map/ppermute | solution.py:654
  73.2 17.0 %collective-permute-start.16 = (f32[4,512,128]{2,1,0:T(8,128)S(1)}, f32[4,512,128]{2,1,0:T(8,128)S(1)}, u32[]{:S(2)}, u32[]{:S(2)}) collective-permute-start(f32[4,512,128]{2,1,0:T(8,128)S(1)} %pad_maximum_fusion.1.refs_0_), channel_id=1, source_target_pairs={{0,4},{1,5},{2,6},{3,7},{4,0},{5,1},{6,2},{7,3},{8,12},{9,13},{10,... | collective-permute-start | bytes 3145736 | tf_op jit(solution)/shard_map/ppermute | solution.py:630
  73.3 20.9 %collective-permute-start.17 = (f32[4,512,128]{2,1,0:T(8,128)S(1)}, f32[4,512,128]{2,1,0:T(8,128)S(1)}, u32[]{:S(2)}, u32[]{:S(2)}) collective-permute-start(f32[4,512,128]{2,1,0:T(8,128)S(1)} %pad_maximum_fusion.2.refs_4_), channel_id=1, source_target_pairs={{0,12},{1,13},{2,14},{3,15},{4,8},{5,9},{6,10},{7,11},{8,4},{9,5},... | collective-permute-start | bytes 3145736 | tf_op jit(solution)/shard_map/ppermute | solution.py:630
  81.5 8.4 %collective-permute-start.20 = (f32[128,1024]{1,0:T(8,128)S(1)}, f32[128,1024]{1,0:T(8,128)S(1)}, u32[]{:S(2)}, u32[]{:S(2)}) collective-permute-start(f32[128,1024]{1,0:T(8,128)S(1)} %select_add_fusion.1), channel_id=1, source_target_pairs={{0,96},{16,48},{32,64},{48,16},{64,32},{80,112},{96,0},{112,80},{1... | collective-permute-start | bytes 1572872 | tf_op jit(solution)/shard_map/ppermute | solution.py:620
  94.1 16.5 %collective-permute-start.24 = (f32[8,256,128]{2,1,0:T(8,128)S(1)}, f32[8,256,128]{2,1,0:T(8,128)S(1)}, u32[]{:S(2)}, u32[]{:S(2)}) collective-permute-start(f32[8,256,128]{2,1,0:T(8,128)S(1)} %pad_maximum_fusion.3.own), channel_id=1, source_target_pairs={{0,16},{16,0},{32,48},{48,32},{64,80},{80,64},{96,112},{112,96},{1... | collective-permute-start | bytes 3145736 | tf_op jit(solution)/shard_map/ppermute | solution.py:588
  97.4 15.3 %collective-permute-start.23 = (f32[256,1024]{1,0:T(8,128)S(1)}, f32[256,1024]{1,0:T(8,128)S(1)}, u32[]{:S(2)}, u32[]{:S(2)}) collective-permute-start(f32[256,1024]{1,0:T(8,128)S(1)} %pad_maximum_fusion.4), channel_id=1, source_target_pairs={{0,32},{16,112},{32,0},{48,80},{64,96},{80,48},{96,64},{112,16},{1... | collective-permute-start | bytes 3145736 | tf_op jit(solution)/shard_map/ppermute | solution.py:620
  98.3 15.1 %collective-permute-start.21 = (f32[4,512,128]{2,1,0:T(8,128)S(1)}, f32[4,512,128]{2,1,0:T(8,128)S(1)}, u32[]{:S(2)}, u32[]{:S(2)}) collective-permute-start(f32[4,512,128]{2,1,0:T(8,128)S(1)} %pad_maximum_fusion.1.refs_0_), channel_id=1, source_target_pairs={{0,12},{1,13},{2,14},{3,15},{4,8},{5,9},{6,10},{7,11},{8,4},{9,5},... | collective-permute-start | bytes 3145736 | tf_op jit(solution)/shard_map/ppermute | solution.py:630
  99.7 13.7 %collective-permute-start.22 = (f32[4,512,128]{2,1,0:T(8,128)S(1)}, f32[4,512,128]{2,1,0:T(8,128)S(1)}, u32[]{:S(2)}, u32[]{:S(2)}) collective-permute-start(f32[4,512,128]{2,1,0:T(8,128)S(1)} %pad_maximum_fusion.2.refs_4_), channel_id=1, source_target_pairs={{0,4},{1,5},{2,6},{3,7},{4,0},{5,1},{6,2},{7,3},{8,12},{9,13},{10,... | collective-permute-start | bytes 3145736 | tf_op jit(solution)/shard_map/ppermute | solution.py:630
  99.7 11.0 %copy-start = (f32[2,512,512]{2,1,0:T(8,128)S(1)}, f32[2,512,512]{2,1,0:T(8,128)}, u32[]{:S(2)}) copy-start(f32[2,512,512]{2,1,0:T(8,128)} %inverses.1) | copy-start | bytes 6291460
  113.4 4.2 %collective-permute-start.27 = (f32[512,1024]{1,0:T(8,128)S(1)}, f32[512,1024]{1,0:T(8,128)S(1)}, u32[]{:S(2)}, u32[]{:S(2)}) collective-permute-start(f32[512,1024]{1,0:T(8,128)S(1)} %pad_maximum_fusion.own), channel_id=1, source_target_pairs={{0,16},{16,0},{32,48},{48,32},{64,80},{80,64},{96,112},{112,96},{1... | collective-permute-start | bytes 6291464 | tf_op jit(solution)/shard_map/ppermute | solution.py:588
  113.8 15.2 %collective-permute-start.25 = (f32[4,512,128]{2,1,0:T(8,128)S(1)}, f32[4,512,128]{2,1,0:T(8,128)S(1)}, u32[]{:S(2)}, u32[]{:S(2)}) collective-permute-start(f32[4,512,128]{2,1,0:T(8,128)S(1)} %collective-permute-done.16.refs_1_), channel_id=1, source_target_pairs={{0,12},{1,13},{2,14},{3,15},{4,8},{5,9},{6,10},{7,11},{8,4},{9,5},... | collective-permute-start | bytes 3145736 | tf_op jit(solution)/shard_map/ppermute | solution.py:630
  114.7 14.2 %collective-permute-start.26 = (f32[4,512,128]{2,1,0:T(8,128)S(1)}, f32[4,512,128]{2,1,0:T(8,128)S(1)}, u32[]{:S(2)}, u32[]{:S(2)}) collective-permute-start(f32[4,512,128]{2,1,0:T(8,128)S(1)} %collective-permute-done.17.refs_5_), channel_id=1, source_target_pairs={{0,4},{1,5},{2,6},{3,7},{4,0},{5,1},{6,2},{7,3},{8,12},{9,13},{10,... | collective-permute-start | bytes 3145736 | tf_op jit(solution)/shard_map/ppermute | solution.py:630
  115.6 45.2 %collective-permute-start.28 = (f32[30,128,128]{2,1,0:T(8,128)S(1)}, f32[30,128,128]{2,1,0:T(8,128)S(1)}, u32[]{:S(2)}, u32[]{:S(2)}) collective-permute-start(f32[30,128,128]{2,1,0:T(8,128)S(1)} %get-tuple-element.119), channel_id=1, source_target_pairs={{0,64},{16,80},{32,96},{48,112},{64,0},{80,16},{96,32},{112,48},{1... | collective-permute-start | bytes 5898248 | tf_op jit(solution)/shard_map/ppermute | solution.py:588

commit v8 on v7

--- a/solution.py
+++ b/solution.py
@@ -95,12 +95,13 @@
         pltpu.make_async_copy(front.at[:, pl.ds(0, BLK)], panel, sem.at[2]),
     ]
     writes = []
-    rest_a, rest_b = rests
+    rest_a, rest_b, rest_c, rest_d = rests
     parts = (
         (0, 0, rest_a),
-        (1, 0, rest_b.at[pl.ds(0, 10)]),
-        (2, 0, rest_b.at[pl.ds(10, 10)]),
-        (3, 0, rest_b.at[pl.ds(20, 10)]),
+        (1, 0, rest_b),
+        (1, 5, rest_c),
+        (2, 0, rest_d.at[pl.ds(0, 10)]),
+        (3, 0, rest_d.at[pl.ds(10, 10)]),
     )
     for n, (j, start, target) in enumerate(parts):
         d = j + (j >= place).astype(jnp.int32)
@@ -172,19 +173,21 @@
         prepare_kernel,
         out_shape=[
             jax.ShapeDtypeStruct((10, BLK, BLK), F32),
-            jax.ShapeDtypeStruct((30, BLK, BLK), F32),
+            jax.ShapeDtypeStruct((5, BLK, BLK), F32),
+            jax.ShapeDtypeStruct((5, BLK, BLK), F32),
+            jax.ShapeDtypeStruct((20, BLK, BLK), F32),
             jax.ShapeDtypeStruct((2048, BLK), F32),
             jax.ShapeDtypeStruct((256, BLK), F32),
             jax.ShapeDtypeStruct((256, BLK), F32),
             jax.ShapeDtypeStruct((64,), jnp.int32),
         ],
         in_specs=[SMEM, VMEM, HBM, HBM, VMEM],
-        out_specs=[HBM] * 2 + [VMEM, VMEM, VMEM, SMEM],
+        out_specs=[HBM] * 4 + [VMEM, VMEM, VMEM, SMEM],
         scratch_shapes=[
             pltpu.VMEM((10, BLK, 640), F32),
             pltpu.VMEM((10, BLK, BLK), F32),
             pltpu.VMEM((PANEL, BLK), F32),
-            pltpu.SemaphoreType.DMA((7,)),
+            pltpu.SemaphoreType.DMA((8,)),
         ],
         compiler_params=params(24),
         cost_estimate=cost(0, 9 * MIB),
@@ -407,9 +410,12 @@
     return jnp.maximum(s[base + half * 8 + t], 0)
 
 
-def extend_kernel(counts, table, front, *refs):
+ARRIVED = (0, 0, 10), (1, 0, 10), (2, 0, 5)
+
+
+def extend_kernel(table, front, *refs):
     out, refs = refs[-1], refs[:-1]
-    kept, *got = (refs[2 * k : 2 * k + 2] for k in range(1 + len(counts)))
+    kept, *got = (refs[2 * k : 2 * k + 2] for k in range(1 + len(ARRIVED)))
     step = pl.program_id(0)
     out[...] = front[...]
     for half in range(2):
@@ -421,11 +427,11 @@
                 out[half, :, to] += kept[half][0, 0, :, d * BLK : (d + 1) * BLK]
 
         m = table[GOT_AT + half * 8 + step]
-        for j, count in enumerate(counts):
-
-            @pl.when((m >= 0) & (m < count))
-            def _(half=half, j=j):
-                to = pl.ds(pl.multiple_of(table[GOT_COL + j] * BLK, BLK), BLK)
+        for j, (column, start, count) in enumerate(ARRIVED):
+
+            @pl.when((m >= start) & (m < start + count))
+            def _(half=half, j=j, column=column):
+                to = pl.ds(pl.multiple_of(table[GOT_COL + column] * BLK, BLK), BLK)
                 out[half, :, to] += got[j][half][0]
 
 
@@ -433,16 +439,20 @@
     def kept_at(half):
         return lambda t, s: (block_at(KEPT_AT, half, t, s), s[SIDE], 0, 0)
 
-    def got_at(half, count):
-        return lambda t, s: (jnp.minimum(block_at(GOT_AT, half, t, s), count - 1), 0, 0)
+    def got_at(half, start, count):
+        return lambda t, s: (
+            jnp.clip(s[GOT_AT + half * 8 + t] - start, 0, count - 1), 0, 0
+        )
 
     tile = pl.BlockSpec((2, BLK, 1024), lambda t, s: (0, t, 0))
     kept_specs = [pl.BlockSpec((1, 1, BLK, 640), kept_at(half)) for half in range(2)]
     got_specs = [
-        pl.BlockSpec((1, BLK, BLK), got_at(half, g.shape[0])) for g in got for half in range(2)
+        pl.BlockSpec((1, BLK, BLK), got_at(half, start, count))
+        for _, start, count in ARRIVED
+        for half in range(2)
     ]
     return pl.pallas_call(
-        functools.partial(extend_kernel, [g.shape[0] for g in got]),
+        extend_kernel,
         out_shape=pltpu.HBM((2, 1024, 1024), F32),
         grid_spec=pltpu.PrefetchScalarGridSpec(
             num_scalar_prefetch=1,
@@ -525,13 +535,13 @@
 
 
 def finish_kernel(
-    table, list_other, list_mine, front, got, patch,
+    table, list_other, list_mine, front, got_c, got_d, patch,
     out, held, read_sem, write_sem, sem,
 ):
     del front
     core = table[ROW] % 2
     copies = []
-    places = [(j, m) for j in (2, 3, 4) for m in range(10)]
+    places = [(2, m) for m in range(5, 10)] + [(j, m) for j in (3, 4) for m in range(10)]
     for n, (column, m) in enumerate(places):
         columns = pl.ds(pl.multiple_of(table[GOT_COL + column] * BLK, BLK), BLK)
         rows = pl.ds(pl.multiple_of(table[GOT_ROW + m] * BLK, BLK), BLK)
@@ -543,7 +553,7 @@
         read.start()
     for n, (read, write) in enumerate(copies):
         read.wait()
-        held[n] += got[n]
+        held[n] += got_c[n] if n < 5 else got_d[n - 5]
         write.start()
     for _, write in copies:
         write.wait()
@@ -568,19 +578,19 @@
     return pl.pallas_call(
         finish_kernel,
         out_shape=jax.ShapeDtypeStruct((2048, 1024), F32),
-        in_specs=[SMEM, SMEM, SMEM, HBM] + [VMEM] * 2,
+        in_specs=[SMEM, SMEM, SMEM, HBM] + [VMEM] * 3,
         out_specs=HBM,
         scratch_shapes=[
-            pltpu.VMEM((30, BLK, BLK), F32),
-            pltpu.SemaphoreType.DMA((30,)),
-            pltpu.SemaphoreType.DMA((30,)),
+            pltpu.VMEM((25, BLK, BLK), F32),
+            pltpu.SemaphoreType.DMA((25,)),
+            pltpu.SemaphoreType.DMA((25,)),
             pltpu.SemaphoreType.DMA(()),
         ],
         input_output_aliases={3: 0},
         compiler_params=params(12),
         cost_estimate=cost(0, 8 * MIB),
         name="finish",
-    )(table, *lists, front, got, patch)
+    )(table, *lists, front, *got, patch)
 
 
 def swap(block, axis, partner):
@@ -632,7 +642,7 @@
     first = cut(child_maps, pieces)
     got0 = by_row(first, 4)
     *rest, panel, corner, away, table = prepare(child_maps, pivots, front, pieces, first)
-    rest_a, rest_b = rest
+    rest_a, rest_b, rest_c, rest_d = rest
     corner = corner + by_row(away, 1)
     corner = corner + (by_row(corner, 2) + (by_row(corner, 6) + by_row(corner, 4)))
     away_rows, marks, list_other = pivot_terms(child_maps, pivots, front, children)
@@ -659,24 +669,26 @@
         held = [jnp.concatenate([h, c], axis=0) for h, c in zip(held, came)]
         corner = corner_step(corner, k)
     total = halve(total, 0)
-    held, corner, total = together((held, corner, total))
+    got_b = by_row(rest_b, 4)
+    held, corner, total, got_b, rest_c = together((held, corner, total, got_b, rest_c))
     came = [gather_step(held[w], w, 2) for w in range(2)]
     corner = corner_step(corner, 2)
     total = double(halve(total, 1), 1)
-    came, corner, total, front = together((came, corner, total, front))
+    got_c = by_row(rest_c, 4)
+    front = extend(table, front, pieces, (got0, got_a, got_b))
+    came, corner, total, front, got_c = together((came, corner, total, front, got_c))
     held_far = [gather_step(held[w], w, 3) for w in range(2)]
-    front = extend(table, front, pieces, (got0, got_a))
     *factors, cross = corners(table, corner, by_row(corner, 1), diag_inverses)
-    came, held_far, total, rest_b, factors, cross, front = together(
-        (came, held_far, double(total, 0), rest_b, factors, cross, front)
+    came, held_far, total, rest_d, factors, cross, front = together(
+        (came, held_far, double(total, 0), rest_d, factors, cross, front)
     )
     came_far = [gather_step(came[w], w, 3) for w in range(2)]
-    got_b = by_row(rest_b, 4)
+    got_d = by_row(rest_d, 4)
     *right, patch = right_factor(table, total, by_row(total, 1), factors, cross)
     came_far, right, patch = together((came_far, right, patch))
     blocks = [(held[w], came[w], held_far[w], came_far[w]) for w in range(2)]
     front = update(table, front, blocks, right, marks).reshape(2048, 1024)
-    return finish(table, (list_other, list_mine), front, got_b, patch)
+    return finish(table, (list_other, list_mine), front, (got_c, got_d), patch)
 
 
 def solution(mesh):

time: 166 us -> 165 us (level)
  waiting for transfers between devices: 53.7 us -> 39.7 us
  starting transfers between devices: 37.4 us -> 48.8 us
    ppermute x10 -> x12, waiting for transfers between devices: 17.1 us -> 7.98 us  [swap(): return lax.ppermute(block, axis, [(i, partner(i)) for i in range(count)])]
    ppermute x10 -> x12, starting transfers between devices: 17.8 us -> 26.7 us  [swap(): return lax.ppermute(block, axis, [(i, partner(i)) for i in range(count)])]
    ppermute x10, waiting for transfers between devices: 15.7 us -> 12.1 us  [gather_step(): return lax.ppermute(block, ('row', 'col'), route)]
    ppermute x2, waiting for transfers between devices: 8.23 us -> 10.8 us  [double(): came = lax.ppermute(part, 'row', rings[step])]
    ppermute x3, waiting for transfers between devices: 3.84 us -> 1.81 us  [corner_step(): lax.ppermute(block, ('row', 'col'), route)]
    ppermute x2, waiting for transfers between devices: 7.53 us -> 5.75 us  [halve(): return stay + lax.ppermute(leave, 'row', rings[step])]
  transfers between devices with their start and end apart: 29 -> 31, of which waited for: 16 -> 17; matrix products, arithmetic and copies ran while one was open for 1% -> 1% of each run, Pallas kernels for 39% -> 40%
where the time goes in v8:
time: 165 us; the launch traced here: 164 us
  Pallas kernels  72.3 us (44%)
  starting transfers between devices  48.8 us (30%)
  waiting for transfers between devices  39.7 us (24%)
  other arithmetic  2.32 us (1%)
    ppermute x12, starting transfers between devices, swap(): return lax.ppermute(block, axis, [(i, partner(i)) for i in range(count)])  26.7 us
    pallas_call x1, Pallas kernels, update(): pl.pallas_call(update_kernel, out_shape=pltpu.HBM((2, 1024, 1024), F32),...  20.3 us
    pallas_call x2, Pallas kernels, pivot_terms(): pl.pallas_call(functools.partial(pivot_kernel, mine_half), out_shape=[jax...  18.7 us
    ppermute x10, waiting for transfers between devices, gather_step(): return lax.ppermute(block, ('row', 'col'), route)  12.1 us
    pallas_call x1, Pallas kernels, extend(): pl.pallas_call(extend_kernel, out_shape=pltpu.HBM((2, 1024, 1024), F32),...  11.1 us
    ppermute x2, waiting for transfers between devices, double(): came = lax.ppermute(part, 'row', rings[step])  10.8 us
    ppermute x12, waiting for transfers between devices, swap(): return lax.ppermute(block, axis, [(i, partner(i)) for i in range(count)])  7.98 us
    pallas_call x1, Pallas kernels, right_factor(): pl.pallas_call(factor_kernel, out_shape=[shape, shape, jax.ShapeDtypeStru...  7.86 us
  transfers between devices with their start and end apart: 31, of which 17 were waited for; matrix products, arithmetic and copies ran while one was open for 1% of the time, Pallas kernels for 40%

profile of v8, /device:TPU:1, one launch (start us, length us, event | category | flops | bytes accessed | tf_op | source)
XLA Modules:
  0.0 163.7 jit_solution(1556492236838730586)
XLA Ops:
  0.0 1.8 %cut.1.first = f32[10,128,128]{2,1,0:T(8,128)S(1)} custom-call(s32[2,80]{1,0:T(2,128)} %maps.7, f32[10,2,128,640]{3,2,1,0:T(8,128)} %bitcast.12), custom_call_target="tpu_custom_call" | custom-call | bytes 1048576 | tf_op jit(solution)/shard_map/cut/pallas_call | solution.py:67
  1.9 4.5 %collective-permute-start = (f32[10,128,128]{2,1,0:T(8,128)S(1)}, f32[10,128,128]{2,1,0:T(8,128)S(1)}, u32[]{:S(2)}, u32[]{:S(2)}) collective-permute-start(f32[10,128,128]{2,1,0:T(8,128)S(1)} %cut.1.first), channel_id=1, source_target_pairs={{0,64},{16,80},{32,96},{48,112},{64,0},{80,16},{96,32},{112,48},{1... | collective-permute-start | bytes 1966088 | tf_op jit(solution)/shard_map/ppermute | solution.py:598
  6.4 5.1 %prepare.1 = (f32[10,128,128]{2,1,0:T(8,128)S(1)}, f32[5,128,128]{2,1,0:T(8,128)S(1)}, f32[5,128,128]{2,1,0:T(8,128)S(1)}, f32[20,128,128]{2,1,0:T(8,128)S(1)}, ...) custom-call(s32[2,80]{1,0:T(2,128)} %maps.7, s32[8,128]{1,0:T(8,128)} %bitcast.18, ...), custom_call_target="tpu_custom_call" | custom-call | bytes 9437184 | tf_op jit(solution)/shard_map/prepare/pallas_call | solution.py:172
  11.5 1.0 collective-permute-start.1
  12.5 1.0 collective-permute-done.1
  13.6 3.1 %collective-permute-start.3 = (f32[256,128]{1,0:T(8,128)S(1)}, f32[256,128]{1,0:T(8,128)S(1)}, u32[]{:S(2)}, u32[]{:S(2)}) collective-permute-start(f32[256,128]{1,0:T(8,128)S(1)} %add.21), channel_id=1, source_target_pairs={{0,96},{16,112},{32,64},{48,80},{64,32},{80,48},{96,0},{112,16},{1... | collective-permute-start | bytes 393224 | tf_op jit(solution)/shard_map/ppermute | solution.py:598
  16.7 9.2 %pivot_terms_other.1 = (f32[512,1024]{1,0:T(8,128)S(1)}, f32[2048,128]{1,0:T(8,128)S(1)}, s32[513]{0:T(1024)S(1)}) custom-call(s32[2,80]{1,0:T(2,128)} %maps.7, s32[1024]{0:T(1024)} %pivots.1, f32[2048,1024]{1,0:T(8,128)} %front.5, f32[2560,640]{1,0:T(8,128)} %children.3), custom_call_target="tpu_custom_call" | custom-call | bytes 25165824 | tf_op jit(solution)/shard_map/pivot_terms_other/pallas_call | solution.py:266
  26.0 1.2 collective-permute-done.3
  27.3 1.3 collective-permute-start.7
  28.6 0.8 whole_panel.1
  29.4 4.7 %collective-permute-start.5 = (f32[1024,128]{1,0:T(8,128)S(1)}, f32[1024,128]{1,0:T(8,128)S(1)}, u32[]{:S(2)}, u32[]{:S(2)}) collective-permute-start(f32[1024,128]{1,0:T(8,128)S(1)} %get-tuple-element.82), channel_id=1, source_target_pairs={{0,12},{1,13},{2,14},{3,15},{4,8},{5,9},{6,10},{7,11},{16,28},{17,... | collective-permute-start | bytes 1572872 | tf_op jit(solution)/shard_map/ppermute | solution.py:602
  34.0 2.1 %collective-permute-start.8 = (f32[10,128,128]{2,1,0:T(8,128)S(1)}, f32[10,128,128]{2,1,0:T(8,128)S(1)}, u32[]{:S(2)}, u32[]{:S(2)}) collective-permute-start(f32[10,128,128]{2,1,0:T(8,128)S(1)} %get-tuple-element.86), channel_id=1, source_target_pairs={{0,64},{16,80},{32,96},{48,112},{64,0},{80,16},{96,32},{112,48},{1... | collective-permute-start | bytes 1966088 | tf_op jit(solution)/shard_map/ppermute | solution.py:598
  36.1 1.3 collective-permute-start.6
  37.4 9.5 %pivot_terms_mine.1 = (f32[512,1024]{1,0:T(8,128)S(1)}, f32[2048,128]{1,0:T(8,128)S(1)}, s32[513]{0:T(1024)S(1)}) custom-call(s32[2,80]{1,0:T(2,128)} %maps.7, s32[1024]{0:T(1024)} %pivots.1, f32[2048,1024]{1,0:T(8,128)} %front.5, f32[2560,640]{1,0:T(8,128)} %children.3, f32[2048,128]{1,0:T(8,128)S(1)} %get-tuple-element.76.refs_0_), custom_call_target="tpu_custom_call" | custom-call | bytes 25165824 | tf_op jit(solution)/shard_map/pivot_terms_mine/pallas_call | solution.py:266
  46.9 1.2 collective-permute-done.6
  48.2 0.6 add.25
  48.8 2.9 %collective-permute-done.8.refs_4_.refs_5_ = f32[10,128,128]{2,1,0:T(8,128)S(1)} collective-permute-done((f32[10,128,128]{2,1,0:T(8,128)S(1)}, f32[10,128,128]{2,1,0:T(8,128)S(1)}, u32[]{:S(2)}, u32[]{:S(2)}) %collective-permute-start.8) | collective-permute-done | bytes 655392 | tf_op jit(solution)/shard_map/ppermute | solution.py:598
  51.7 0.7 collective-permute-start.11
  52.5 2.3 %collective-permute-start.15 = (f32[256,1024]{1,0:T(8,128)S(1)}, f32[256,1024]{1,0:T(8,128)S(1)}, u32[]{:S(2)}, u32[]{:S(2)}) collective-permute-start(f32[256,1024]{1,0:T(8,128)S(1)} %slice_select_fusion), channel_id=1, source_target_pairs={{0,32},{16,112},{32,0},{48,80},{64,96},{80,48},{96,64},{112,16},{1... | collective-permute-start | bytes 3145736 | tf_op jit(solution)/shard_map/ppermute | solution.py:627
  54.8 1.2 collective-permute-start.13
  56.0 2.5 %collective-permute-done.11 = f32[1,512,128]{2,1,0:T(8,128)S(1)} collective-permute-done((f32[1,512,128]{2,1,0:T(8,128)S(1)}, f32[1,512,128]{2,1,0:T(8,128)S(1)}, u32[]{:S(2)}, u32[]{:S(2)}) %collective-permute-start.11) | collective-permute-done | bytes 262176 | tf_op jit(solution)/shard_map/ppermute | solution.py:640
  58.6 0.7 collective-permute-done.13
  59.3 3.6 %collective-permute-start.14 = (f32[2,256,128]{2,1,0:T(8,128)S(1)}, f32[2,256,128]{2,1,0:T(8,128)S(1)}, u32[]{:S(2)}, u32[]{:S(2)}) collective-permute-start(f32[2,256,128]{2,1,0:T(8,128)S(1)} %pad_maximum_fusion.8), channel_id=1, source_target_pairs={{0,1},{1,0},{2,3},{3,2},{4,5},{5,4},{6,7},{7,6},{8,9},{9,8},{10,11... | collective-permute-start | bytes 786440 | tf_op jit(solution)/shard_map/ppermute | solution.py:664
  63.0 0.8 collective-permute-start.10
  63.8 1.8 %collective-permute-start.16 = (f32[5,128,128]{2,1,0:T(8,128)S(1)}, f32[5,128,128]{2,1,0:T(8,128)S(1)}, u32[]{:S(2)}, u32[]{:S(2)}) collective-permute-start(f32[5,128,128]{2,1,0:T(8,128)S(1)} %get-tuple-element.92), channel_id=1, source_target_pairs={{0,64},{16,80},{32,96},{48,112},{64,0},{80,16},{96,32},{112,48},{1... | collective-permute-start | bytes 983048 | tf_op jit(solution)/shard_map/ppermute | solution.py:598
  65.5 1.2 collective-permute-done.14
  66.7 0.6 collective-permute-done.12
  67.4 5.2 %collective-permute-done.10 = f32[2,512,128]{2,1,0:T(8,128)S(1)} collective-permute-done((f32[2,512,128]{2,1,0:T(8,128)S(1)}, f32[2,512,128]{2,1,0:T(8,128)S(1)}, u32[]{:S(2)}, u32[]{:S(2)}) %collective-permute-start.10) | collective-permute-done | bytes 524320 | tf_op jit(solution)/shard_map/ppermute | solution.py:640
  73.0 1.8 %collective-permute-done.16.refs_6_.refs_7_ = f32[5,128,128]{2,1,0:T(8,128)S(1)} collective-permute-done((f32[5,128,128]{2,1,0:T(8,128)S(1)}, f32[5,128,128]{2,1,0:T(8,128)S(1)}, u32[]{:S(2)}, u32[]{:S(2)}) %collective-permute-start.16) | collective-permute-done | bytes 327712 | tf_op jit(solution)/shard_map/ppermute | solution.py:598
  74.8 1.1 collective-permute-start.20
  75.9 1.3 collective-permute-start.18
  77.2 5.8 %collective-permute-done.20 = f32[128,1024]{1,0:T(8,128)S(1)} collective-permute-done((f32[128,1024]{1,0:T(8,128)S(1)}, f32[128,1024]{1,0:T(8,128)S(1)}, u32[]{:S(2)}, u32[]{:S(2)}) %collective-permute-start.20) | collective-permute-done | bytes 524320 | tf_op jit(solution)/shard_map/ppermute | solution.py:627
  83.0 1.4 collective-permute-start.21
  84.4 2.4 %collective-permute-start.22 = (f32[5,128,128]{2,1,0:T(8,128)S(1)}, f32[5,128,128]{2,1,0:T(8,128)S(1)}, u32[]{:S(2)}, u32[]{:S(2)}) collective-permute-start(f32[5,128,128]{2,1,0:T(8,128)S(1)} %get-tuple-element.101), channel_id=1, source_target_pairs={{0,64},{16,80},{32,96},{48,112},{64,0},{80,16},{96,32},{112,48},{1... | collective-permute-start | bytes 983048 | tf_op jit(solution)/shard_map/ppermute | solution.py:598
  86.8 11.1 %extend.1.front = f32[2,1024,1024]{2,1,0:T(8,128)} custom-call(s32[64]{0:T(128)S(1)} %get-tuple-element.69.table, f32[2,1024,1024]{2,1,0:T(8,128)} %bitcast.16, f32[10,2,128,640]{3,2,1,0:T(8,128)} %bitcast.14, f32[10,2,128,640]{3,2,1,0:T(8,128)} %bitcast.15, f32[10,128,128]{2,1,0:T(8,128)S(1)} %collective-permute-done.got.refs_2_.refs_3_, ...), custom_call_target="tpu_custom_call" | custom-call | bytes 1048576 | tf_op jit(solution)/shard_map/extend/pallas_call | solution.py:454
  98.3 8.7 %collective-permute-start.26 = (f32[8,256,128]{2,1,0:T(8,128)S(1)}, f32[8,256,128]{2,1,0:T(8,128)S(1)}, u32[]{:S(2)}, u32[]{:S(2)}) collective-permute-start(f32[8,256,128]{2,1,0:T(8,128)S(1)} %pad_maximum_fusion.3.own), channel_id=1, source_target_pairs={{0,16},{16,0},{32,48},{48,32},{64,80},{80,64},{96,112},{112,96},{1... | collective-permute-start | bytes 3145736 | tf_op jit(solution)/shard_map/ppermute | solution.py:598
  107.2 1.5 collective-permute-start.23
  108.8 0.6 collective-permute-done.26.swapped
  109.3 2.0 %corners.1 = (bf16[3,512,512]{2,1,0:T(8,128)(2,1)S(1)}, bf16[3,512,512]{2,1,0:T(8,128)(2,1)S(1)}, f32[512,512]{1,0:T(8,128)S(1)}) custom-call(s32[64]{0:T(128)S(1)} %get-tuple-element.69.table, f32[8,256,128]{2,1,0:T(8,128)S(1)} %pad_maximum_fusion.3.own, f32[8,256,128]{2,1,0:T(8,128)S(1)} %collective-permute-done.26.swapped, f32[2,512,512]{2,1,0:T(8,128)S(1)} %copy-done), custom_call_target="tpu_custom_call" | custom-call | flops 805306368 | bytes 8388608 | tf_op jit(solution)/shard_map/corners/pallas_call | solution.py:344
  111.4 10.8 %collective-permute-done.25 = f32[256,1024]{1,0:T(8,128)S(1)} collective-permute-done((f32[256,1024]{1,0:T(8,128)S(1)}, f32[256,1024]{1,0:T(8,128)S(1)}, u32[]{:S(2)}, u32[]{:S(2)}) %collective-permute-start.25) | collective-permute-done | bytes 1048608 | tf_op jit(solution)/shard_map/ppermute | solution.py:630
  122.7 0.6 collective-permute-start.29
  123.2 1.5 collective-permute-start.27
  124.7 0.7 collective-permute-start.28
  125.4 1.1 collective-permute-start.30
  127.0 7.9 %right_factor.1 = (bf16[1024,1024]{1,0:T(8,128)(2,1)S(1)}, bf16[1024,1024]{1,0:T(8,128)(2,1)S(1)}, f32[512,1024]{1,0:T(8,128)S(1)}) custom-call(s32[64]{0:T(128)S(1)} %get-tuple-element.69.table, f32[512,1024]{1,0:T(8,128)S(1)} %pad_maximum_fusion.own, f32[512,1024]{1,0:T(8,128)S(1)} %collective-permute-done.29.swapped, ...), custom_call_target="tpu_custom_call" | custom-call | flops 6442450944 | bytes 14680064 | tf_op jit(solution)/shard_map/right_factor/pallas_call | solution.py:398
  134.9 3.5 %collective-permute-done.27.refs_3_ = f32[4,512,128]{2,1,0:T(8,128)S(1)} collective-permute-done((f32[4,512,128]{2,1,0:T(8,128)S(1)}, f32[4,512,128]{2,1,0:T(8,128)S(1)}, u32[]{:S(2)}, u32[]{:S(2)}) %collective-permute-start.27) | collective-permute-done | bytes 1048608 | tf_op jit(solution)/shard_map/ppermute | solution.py:640
  138.7 20.3 %update.1 = f32[2,1024,1024]{2,1,0:T(8,128)} custom-call(s32[64]{0:T(128)S(1)} %get-tuple-element.69.table, f32[2,1024,1024]{2,1,0:T(8,128)} %extend.1.front, f32[4,512,128]{2,1,0:T(8,128)S(1)} %pad_maximum_fusion.1.refs_0_, f32[4,512,128]{2,1,0:T(8,128)S(1)} %collective-permute-done.17.refs_1_, f32[4,512,128]{2,1,0:T(8,128)S(1)} %collective-permute-done.23.refs_2_, ...), custom_call_target="tpu_custom_call" | custom-call | flops 12884901888 | bytes 33554432 | tf_op jit(solution)/shard_map/update/pallas_call | solution.py:517
  158.9 4.6 %finish.1 = f32[2048,1024]{1,0:T(8,128)} custom-call(s32[64]{0:T(128)S(1)} %get-tuple-element.69.table, s32[513]{0:T(1024)S(1)} %get-tuple-element.70.list_other, s32[513]{0:T(1024)S(1)} %get-tuple-element.77.list_mine, f32[2048,1024]{1,0:T(8,128)} %bitcast.17, f32[5,128,128]{2,1,0:T(8,128)S(1)} %collective-permute-done.22.got_c, ...), custom_call_target="tpu_custom_call", output_to_operand_aliasing={{}: (3, {})} | custom-call | bytes 8388608 | tf_op jit(solution)/shard_map/finish/pallas_call | solution.py:578
  (47 shorter events, 3.1 us)
Async XLA Ops:
  1.9 25.4 %collective-permute-start = (f32[10,128,128]{2,1,0:T(8,128)S(1)}, f32[10,128,128]{2,1,0:T(8,128)S(1)}, u32[]{:S(2)}, u32[]{:S(2)}) collective-permute-start(f32[10,128,128]{2,1,0:T(8,128)S(1)} %cut.1.first), channel_id=1, source_target_pairs={{0,64},{16,80},{32,96},{48,112},{64,0},{80,16},{96,32},{112,48},{1... | collective-permute-start | bytes 1966088 | tf_op jit(solution)/shard_map/ppermute | solution.py:598
  11.5 2.0 %collective-permute-start.1 = (f32[256,128]{1,0:T(8,128)S(1)}, f32[256,128]{1,0:T(8,128)S(1)}, u32[]{:S(2)}, u32[]{:S(2)}) collective-permute-start(f32[256,128]{1,0:T(8,128)S(1)} %get-tuple-element.75), channel_id=1, source_target_pairs={{0,16},{16,0},{32,48},{48,32},{64,80},{80,64},{96,112},{112,96},{1... | collective-permute-start | bytes 393224 | tf_op jit(solution)/shard_map/ppermute | solution.py:598
  13.5 12.5 %collective-permute-start.4 = (f32[256,128]{1,0:T(8,128)S(1)}, f32[256,128]{1,0:T(8,128)S(1)}, u32[]{:S(2)}, u32[]{:S(2)}) collective-permute-start(f32[256,128]{1,0:T(8,128)S(1)} %add.21), channel_id=1, source_target_pairs={{0,64},{16,80},{32,96},{48,112},{64,0},{80,16},{96,32},{112,48},{1... | collective-permute-start | bytes 393224 | tf_op jit(solution)/shard_map/ppermute | solution.py:598
  13.6 13.6 %collective-permute-start.3 = (f32[256,128]{1,0:T(8,128)S(1)}, f32[256,128]{1,0:T(8,128)S(1)}, u32[]{:S(2)}, u32[]{:S(2)}) collective-permute-start(f32[256,128]{1,0:T(8,128)S(1)} %add.21), channel_id=1, source_target_pairs={{0,96},{16,112},{32,64},{48,80},{64,32},{80,48},{96,0},{112,16},{1... | collective-permute-start | bytes 393224 | tf_op jit(solution)/shard_map/ppermute | solution.py:598
  16.7 10.5 %collective-permute-start.2 = (f32[256,128]{1,0:T(8,128)S(1)}, f32[256,128]{1,0:T(8,128)S(1)}, u32[]{:S(2)}, u32[]{:S(2)}) collective-permute-start(f32[256,128]{1,0:T(8,128)S(1)} %add.21), channel_id=1, source_target_pairs={{0,32},{16,48},{32,0},{48,16},{64,96},{80,112},{96,64},{112,80},{1... | collective-permute-start | bytes 393224 | tf_op jit(solution)/shard_map/ppermute | solution.py:598
  27.3 21.0 %collective-permute-start.7 = (f32[512,1024]{1,0:T(8,128)S(1)}, f32[512,1024]{1,0:T(8,128)S(1)}, u32[]{:S(2)}, u32[]{:S(2)}) collective-permute-start(f32[512,1024]{1,0:T(8,128)S(1)} %get-tuple-element.85), channel_id=1, source_target_pairs={{0,16},{16,0},{32,48},{48,32},{64,80},{80,64},{96,112},{112,96},{1... | collective-permute-start | bytes 6291464 | tf_op jit(solution)/shard_map/ppermute | solution.py:598
  29.4 18.8 %collective-permute-start.5 = (f32[1024,128]{1,0:T(8,128)S(1)}, f32[1024,128]{1,0:T(8,128)S(1)}, u32[]{:S(2)}, u32[]{:S(2)}) collective-permute-start(f32[1024,128]{1,0:T(8,128)S(1)} %get-tuple-element.82), channel_id=1, source_target_pairs={{0,12},{1,13},{2,14},{3,15},{4,8},{5,9},{6,10},{7,11},{16,28},{17,... | collective-permute-start | bytes 1572872 | tf_op jit(solution)/shard_map/ppermute | solution.py:602
  34.0 17.6 %collective-permute-start.8 = (f32[10,128,128]{2,1,0:T(8,128)S(1)}, f32[10,128,128]{2,1,0:T(8,128)S(1)}, u32[]{:S(2)}, u32[]{:S(2)}) collective-permute-start(f32[10,128,128]{2,1,0:T(8,128)S(1)} %get-tuple-element.86), channel_id=1, source_target_pairs={{0,64},{16,80},{32,96},{48,112},{64,0},{80,16},{96,32},{112,48},{1... | collective-permute-start | bytes 1966088 | tf_op jit(solution)/shard_map/ppermute | solution.py:598
  36.1 12.0 %collective-permute-start.6 = (f32[256,128]{1,0:T(8,128)S(1)}, f32[256,128]{1,0:T(8,128)S(1)}, u32[]{:S(2)}, u32[]{:S(2)}) collective-permute-start(f32[256,128]{1,0:T(8,128)S(1)} %add_add_fusion), channel_id=1, source_target_pairs={{0,12},{1,13},{2,14},{3,15},{4,8},{5,9},{6,10},{7,11},{16,28},{17,... | collective-permute-start | bytes 393224 | tf_op jit(solution)/shard_map/ppermute | solution.py:602
  51.7 6.8 %collective-permute-start.11 = (f32[1,512,128]{2,1,0:T(8,128)S(1)}, f32[1,512,128]{2,1,0:T(8,128)S(1)}, u32[]{:S(2)}, u32[]{:S(2)}) collective-permute-start(f32[1,512,128]{2,1,0:T(8,128)S(1)} %get-tuple-element.135), channel_id=1, source_target_pairs={{0,3},{1,2},{2,1},{3,0},{4,7},{5,6},{6,5},{7,4},{8,11},{9,10},{10,... | collective-permute-start | bytes 786440 | tf_op jit(solution)/shard_map/ppermute | solution.py:640
  52.4 10.6 %collective-permute-start.9 = (f32[1,512,128]{2,1,0:T(8,128)S(1)}, f32[1,512,128]{2,1,0:T(8,128)S(1)}, u32[]{:S(2)}, u32[]{:S(2)}) collective-permute-start(f32[1,512,128]{2,1,0:T(8,128)S(1)} %get-tuple-element.136), channel_id=1, source_target_pairs={{0,1},{1,0},{2,3},{3,2},{4,5},{5,4},{6,7},{7,6},{8,9},{9,8},{10,11... | collective-permute-start | bytes 786440 | tf_op jit(solution)/shard_map/ppermute | solution.py:640
  52.5 20.1 %collective-permute-start.15 = (f32[256,1024]{1,0:T(8,128)S(1)}, f32[256,1024]{1,0:T(8,128)S(1)}, u32[]{:S(2)}, u32[]{:S(2)}) collective-permute-start(f32[256,1024]{1,0:T(8,128)S(1)} %slice_select_fusion), channel_id=1, source_target_pairs={{0,32},{16,112},{32,0},{48,80},{64,96},{80,48},{96,64},{112,16},{1... | collective-permute-start | bytes 3145736 | tf_op jit(solution)/shard_map/ppermute | solution.py:627
  54.8 4.5 %collective-permute-start.13 = (f32[1,256,128]{2,1,0:T(8,128)S(1)}, f32[1,256,128]{2,1,0:T(8,128)S(1)}, u32[]{:S(2)}, u32[]{:S(2)}) collective-permute-start(f32[1,256,128]{2,1,0:T(8,128)S(1)} %select_bitcast_fusion), channel_id=1, source_target_pairs={{0,4},{1,5},{2,6},{3,7},{4,0},{5,1},{6,2},{7,3},{8,12},{9,13},{10,... | collective-permute-start | bytes 393224 | tf_op jit(solution)/shard_map/ppermute | solution.py:664
  58.5 8.8 %collective-permute-start.12 = (f32[2,512,128]{2,1,0:T(8,128)S(1)}, f32[2,512,128]{2,1,0:T(8,128)S(1)}, u32[]{:S(2)}, u32[]{:S(2)}) collective-permute-start(f32[2,512,128]{2,1,0:T(8,128)S(1)} %pad_maximum_fusion.6), channel_id=1, source_target_pairs={{0,1},{1,0},{2,3},{3,2},{4,5},{5,4},{6,7},{7,6},{8,9},{9,8},{10,11... | collective-permute-start | bytes 1572872 | tf_op jit(solution)/shard_map/ppermute | solution.py:640
  59.3 7.3 %collective-permute-start.14 = (f32[2,256,128]{2,1,0:T(8,128)S(1)}, f32[2,256,128]{2,1,0:T(8,128)S(1)}, u32[]{:S(2)}, u32[]{:S(2)}) collective-permute-start(f32[2,256,128]{2,1,0:T(8,128)S(1)} %pad_maximum_fusion.8), channel_id=1, source_target_pairs={{0,1},{1,0},{2,3},{3,2},{4,5},{5,4},{6,7},{7,6},{8,9},{9,8},{10,11... | collective-permute-start | bytes 786440 | tf_op jit(solution)/shard_map/ppermute | solution.py:664
  63.0 9.6 %collective-permute-start.10 = (f32[2,512,128]{2,1,0:T(8,128)S(1)}, f32[2,512,128]{2,1,0:T(8,128)S(1)}, u32[]{:S(2)}, u32[]{:S(2)}) collective-permute-start(f32[2,512,128]{2,1,0:T(8,128)S(1)} %pad_maximum_fusion.5), channel_id=1, source_target_pairs={{0,3},{1,2},{2,1},{3,0},{4,7},{5,6},{6,5},{7,4},{8,11},{9,10},{10,... | collective-permute-start | bytes 1572872 | tf_op jit(solution)/shard_map/ppermute | solution.py:640
  63.8 11.0 %collective-permute-start.16 = (f32[5,128,128]{2,1,0:T(8,128)S(1)}, f32[5,128,128]{2,1,0:T(8,128)S(1)}, u32[]{:S(2)}, u32[]{:S(2)}) collective-permute-start(f32[5,128,128]{2,1,0:T(8,128)S(1)} %get-tuple-element.92), channel_id=1, source_target_pairs={{0,64},{16,80},{32,96},{48,112},{64,0},{80,16},{96,32},{112,48},{1... | collective-permute-start | bytes 983048 | tf_op jit(solution)/shard_map/ppermute | solution.py:598
  74.8 8.1 %collective-permute-start.20 = (f32[128,1024]{1,0:T(8,128)S(1)}, f32[128,1024]{1,0:T(8,128)S(1)}, u32[]{:S(2)}, u32[]{:S(2)}) collective-permute-start(f32[128,1024]{1,0:T(8,128)S(1)} %slice_select_fusion.1), channel_id=1, source_target_pairs={{0,96},{16,48},{32,64},{48,16},{64,32},{80,112},{96,0},{112,80},{1... | collective-permute-start | bytes 1572872 | tf_op jit(solution)/shard_map/ppermute | solution.py:627
  75.9 22.0 %collective-permute-start.19 = (f32[4,256,128]{2,1,0:T(8,128)S(1)}, f32[4,256,128]{2,1,0:T(8,128)S(1)}, u32[]{:S(2)}, u32[]{:S(2)}) collective-permute-start(f32[4,256,128]{2,1,0:T(8,128)S(1)} %pad_maximum_fusion.7), channel_id=1, source_target_pairs={{0,3},{1,2},{2,1},{3,0},{4,7},{5,6},{6,5},{7,4},{8,11},{9,10},{10,... | collective-permute-start | bytes 1572872 | tf_op jit(solution)/shard_map/ppermute | solution.py:664
  75.9 22.4 %collective-permute-start.17 = (f32[4,512,128]{2,1,0:T(8,128)S(1)}, f32[4,512,128]{2,1,0:T(8,128)S(1)}, u32[]{:S(2)}, u32[]{:S(2)}) collective-permute-start(f32[4,512,128]{2,1,0:T(8,128)S(1)} %pad_maximum_fusion.1.refs_0_), channel_id=1, source_target_pairs={{0,4},{1,5},{2,6},{3,7},{4,0},{5,1},{6,2},{7,3},{8,12},{9,13},{10,... | collective-permute-start | bytes 3145736 | tf_op jit(solution)/shard_map/ppermute | solution.py:640
  75.9 22.4 %collective-permute-start.18 = (f32[4,512,128]{2,1,0:T(8,128)S(1)}, f32[4,512,128]{2,1,0:T(8,128)S(1)}, u32[]{:S(2)}, u32[]{:S(2)}) collective-permute-start(f32[4,512,128]{2,1,0:T(8,128)S(1)} %pad_maximum_fusion.2.refs_4_), channel_id=1, source_target_pairs={{0,12},{1,13},{2,14},{3,15},{4,8},{5,9},{6,10},{7,11},{8,4},{9,5},... | collective-permute-start | bytes 3145736 | tf_op jit(solution)/shard_map/ppermute | solution.py:640
  83.0 15.0 %collective-permute-start.21 = (f32[128,1024]{1,0:T(8,128)S(1)}, f32[128,1024]{1,0:T(8,128)S(1)}, u32[]{:S(2)}, u32[]{:S(2)}) collective-permute-start(f32[128,1024]{1,0:T(8,128)S(1)} %select_add_fusion.1), channel_id=1, source_target_pairs={{0,96},{16,48},{32,64},{48,16},{64,32},{80,112},{96,0},{112,80},{1... | collective-permute-start | bytes 1572872 | tf_op jit(solution)/shard_map/ppermute | solution.py:630
  84.4 13.9 %collective-permute-start.22 = (f32[5,128,128]{2,1,0:T(8,128)S(1)}, f32[5,128,128]{2,1,0:T(8,128)S(1)}, u32[]{:S(2)}, u32[]{:S(2)}) collective-permute-start(f32[5,128,128]{2,1,0:T(8,128)S(1)} %get-tuple-element.101), channel_id=1, source_target_pairs={{0,64},{16,80},{32,96},{48,112},{64,0},{80,16},{96,32},{112,48},{1... | collective-permute-start | bytes 983048 | tf_op jit(solution)/shard_map/ppermute | solution.py:598
  98.0 11.3 %copy-start = (f32[2,512,512]{2,1,0:T(8,128)S(1)}, f32[2,512,512]{2,1,0:T(8,128)}, u32[]{:S(2)}) copy-start(f32[2,512,512]{2,1,0:T(8,128)} %inverses.1) | copy-start | bytes 6291460
  98.3 11.0 %collective-permute-start.26 = (f32[8,256,128]{2,1,0:T(8,128)S(1)}, f32[8,256,128]{2,1,0:T(8,128)S(1)}, u32[]{:S(2)}, u32[]{:S(2)}) collective-permute-start(f32[8,256,128]{2,1,0:T(8,128)S(1)} %pad_maximum_fusion.3.own), channel_id=1, source_target_pairs={{0,16},{16,0},{32,48},{48,32},{64,80},{80,64},{96,112},{112,96},{1... | collective-permute-start | bytes 3145736 | tf_op jit(solution)/shard_map/ppermute | solution.py:598
  107.0 15.2 %collective-permute-start.25 = (f32[256,1024]{1,0:T(8,128)S(1)}, f32[256,1024]{1,0:T(8,128)S(1)}, u32[]{:S(2)}, u32[]{:S(2)}) collective-permute-start(f32[256,1024]{1,0:T(8,128)S(1)} %pad_maximum_fusion.4), channel_id=1, source_target_pairs={{0,32},{16,112},{32,0},{48,80},{64,96},{80,48},{96,64},{112,16},{1... | collective-permute-start | bytes 3145736 | tf_op jit(solution)/shard_map/ppermute | solution.py:630
  107.2 15.4 %collective-permute-start.23 = (f32[4,512,128]{2,1,0:T(8,128)S(1)}, f32[4,512,128]{2,1,0:T(8,128)S(1)}, u32[]{:S(2)}, u32[]{:S(2)}) collective-permute-start(f32[4,512,128]{2,1,0:T(8,128)S(1)} %pad_maximum_fusion.1.refs_0_), channel_id=1, source_target_pairs={{0,12},{1,13},{2,14},{3,15},{4,8},{5,9},{6,10},{7,11},{8,4},{9,5},... | collective-permute-start | bytes 3145736 | tf_op jit(solution)/shard_map/ppermute | solution.py:640
  108.7 13.9 %collective-permute-start.24 = (f32[4,512,128]{2,1,0:T(8,128)S(1)}, f32[4,512,128]{2,1,0:T(8,128)S(1)}, u32[]{:S(2)}, u32[]{:S(2)}) collective-permute-start(f32[4,512,128]{2,1,0:T(8,128)S(1)} %pad_maximum_fusion.2.refs_4_), channel_id=1, source_target_pairs={{0,4},{1,5},{2,6},{3,7},{4,0},{5,1},{6,2},{7,3},{8,12},{9,13},{10,... | collective-permute-start | bytes 3145736 | tf_op jit(solution)/shard_map/ppermute | solution.py:640
  122.7 4.3 %collective-permute-start.29 = (f32[512,1024]{1,0:T(8,128)S(1)}, f32[512,1024]{1,0:T(8,128)S(1)}, u32[]{:S(2)}, u32[]{:S(2)}) collective-permute-start(f32[512,1024]{1,0:T(8,128)S(1)} %pad_maximum_fusion.own), channel_id=1, source_target_pairs={{0,16},{16,0},{32,48},{48,32},{64,80},{80,64},{96,112},{112,96},{1... | collective-permute-start | bytes 6291464 | tf_op jit(solution)/shard_map/ppermute | solution.py:598
  123.2 15.2 %collective-permute-start.27 = (f32[4,512,128]{2,1,0:T(8,128)S(1)}, f32[4,512,128]{2,1,0:T(8,128)S(1)}, u32[]{:S(2)}, u32[]{:S(2)}) collective-permute-start(f32[4,512,128]{2,1,0:T(8,128)S(1)} %collective-permute-done.17.refs_1_), channel_id=1, source_target_pairs={{0,12},{1,13},{2,14},{3,15},{4,8},{5,9},{6,10},{7,11},{8,4},{9,5},... | collective-permute-start | bytes 3145736 | tf_op jit(solution)/shard_map/ppermute | solution.py:640
  124.7 13.9 %collective-permute-start.28 = (f32[4,512,128]{2,1,0:T(8,128)S(1)}, f32[4,512,128]{2,1,0:T(8,128)S(1)}, u32[]{:S(2)}, u32[]{:S(2)}) collective-permute-start(f32[4,512,128]{2,1,0:T(8,128)S(1)} %collective-permute-done.18.refs_5_), channel_id=1, source_target_pairs={{0,4},{1,5},{2,6},{3,7},{4,0},{5,1},{6,2},{7,3},{8,12},{9,13},{10,... | collective-permute-start | bytes 3145736 | tf_op jit(solution)/shard_map/ppermute | solution.py:640
  125.4 33.5 %collective-permute-start.30 = (f32[20,128,128]{2,1,0:T(8,128)S(1)}, f32[20,128,128]{2,1,0:T(8,128)S(1)}, u32[]{:S(2)}, u32[]{:S(2)}) collective-permute-start(f32[20,128,128]{2,1,0:T(8,128)S(1)} %get-tuple-element.129), channel_id=1, source_target_pairs={{0,64},{16,80},{32,96},{48,112},{64,0},{80,16},{96,32},{112,48},{1... | collective-permute-start | bytes 3932168 | tf_op jit(solution)/shard_map/ppermute | solution.py:598

commit v9 on v8

--- a/solution.py
+++ b/solution.py
@@ -95,13 +95,13 @@
         pltpu.make_async_copy(front.at[:, pl.ds(0, BLK)], panel, sem.at[2]),
     ]
     writes = []
-    rest_a, rest_b, rest_c, rest_d = rests
+    rest_a, rest_b, rest_c = rests
     parts = (
         (0, 0, rest_a),
         (1, 0, rest_b),
-        (1, 5, rest_c),
-        (2, 0, rest_d.at[pl.ds(0, 10)]),
-        (3, 0, rest_d.at[pl.ds(10, 10)]),
+        (1, 5, rest_c.at[pl.ds(0, 5)]),
+        (2, 0, rest_c.at[pl.ds(5, 10)]),
+        (3, 0, rest_c.at[pl.ds(15, 10)]),
     )
     for n, (j, start, target) in enumerate(parts):
         d = j + (j >= place).astype(jnp.int32)
@@ -174,15 +174,14 @@
         out_shape=[
             jax.ShapeDtypeStruct((10, BLK, BLK), F32),
             jax.ShapeDtypeStruct((5, BLK, BLK), F32),
-            jax.ShapeDtypeStruct((5, BLK, BLK), F32),
-            jax.ShapeDtypeStruct((20, BLK, BLK), F32),
+            jax.ShapeDtypeStruct((25, BLK, BLK), F32),
             jax.ShapeDtypeStruct((2048, BLK), F32),
             jax.ShapeDtypeStruct((256, BLK), F32),
             jax.ShapeDtypeStruct((256, BLK), F32),
             jax.ShapeDtypeStruct((64,), jnp.int32),
         ],
         in_specs=[SMEM, VMEM, HBM, HBM, VMEM],
-        out_specs=[HBM] * 4 + [VMEM, VMEM, VMEM, SMEM],
+        out_specs=[HBM] * 3 + [VMEM, VMEM, VMEM, SMEM],
         scratch_shapes=[
             pltpu.VMEM((10, BLK, 640), F32),
             pltpu.VMEM((10, BLK, BLK), F32),
@@ -535,7 +534,7 @@
 
 
 def finish_kernel(
-    table, list_other, list_mine, front, got_c, got_d, patch,
+    table, list_other, list_mine, front, got, patch,
     out, held, read_sem, write_sem, sem,
 ):
     del front
@@ -553,7 +552,7 @@
         read.start()
     for n, (read, write) in enumerate(copies):
         read.wait()
-        held[n] += got_c[n] if n < 5 else got_d[n - 5]
+        held[n] += got[n]
         write.start()
     for _, write in copies:
         write.wait()
@@ -578,7 +577,7 @@
     return pl.pallas_call(
         finish_kernel,
         out_shape=jax.ShapeDtypeStruct((2048, 1024), F32),
-        in_specs=[SMEM, SMEM, SMEM, HBM] + [VMEM] * 3,
+        in_specs=[SMEM, SMEM, SMEM, HBM] + [VMEM] * 2,
         out_specs=HBM,
         scratch_shapes=[
             pltpu.VMEM((25, BLK, BLK), F32),
@@ -590,7 +589,7 @@
         compiler_params=params(12),
         cost_estimate=cost(0, 8 * MIB),
         name="finish",
-    )(table, *lists, front, *got, patch)
+    )(table, *lists, front, got, patch)
 
 
 def swap(block, axis, partner):
@@ -642,7 +641,7 @@
     first = cut(child_maps, pieces)
     got0 = by_row(first, 4)
     *rest, panel, corner, away, table = prepare(child_maps, pivots, front, pieces, first)
-    rest_a, rest_b, rest_c, rest_d = rest
+    rest_a, rest_b, rest_c = rest
     corner = corner + by_row(away, 1)
     corner = corner + (by_row(corner, 2) + (by_row(corner, 6) + by_row(corner, 4)))
     away_rows, marks, list_other = pivot_terms(child_maps, pivots, front, children)
@@ -669,26 +668,25 @@
         held = [jnp.concatenate([h, c], axis=0) for h, c in zip(held, came)]
         corner = corner_step(corner, k)
     total = halve(total, 0)
-    got_b = by_row(rest_b, 4)
-    held, corner, total, got_b, rest_c = together((held, corner, total, got_b, rest_c))
+    held, corner, total, rest_b = together((held, corner, total, rest_b))
     came = [gather_step(held[w], w, 2) for w in range(2)]
     corner = corner_step(corner, 2)
     total = double(halve(total, 1), 1)
-    got_c = by_row(rest_c, 4)
+    got_b = by_row(rest_b, 4)
+    came, corner, total, got_b = together((came, corner, total, got_b))
+    held_far = [gather_step(held[w], w, 3) for w in range(2)]
     front = extend(table, front, pieces, (got0, got_a, got_b))
-    came, corner, total, front, got_c = together((came, corner, total, front, got_c))
-    held_far = [gather_step(held[w], w, 3) for w in range(2)]
     *factors, cross = corners(table, corner, by_row(corner, 1), diag_inverses)
-    came, held_far, total, rest_d, factors, cross, front = together(
-        (came, held_far, double(total, 0), rest_d, factors, cross, front)
+    came, held_far, total, rest_c, factors, cross, front = together(
+        (came, held_far, double(total, 0), rest_c, factors, cross, front)
     )
     came_far = [gather_step(came[w], w, 3) for w in range(2)]
-    got_d = by_row(rest_d, 4)
+    got_c = by_row(rest_c, 4)
     *right, patch = right_factor(table, total, by_row(total, 1), factors, cross)
     came_far, right, patch = together((came_far, right, patch))
     blocks = [(held[w], came[w], held_far[w], came_far[w]) for w in range(2)]
     front = update(table, front, blocks, right, marks).reshape(2048, 1024)
-    return finish(table, (list_other, list_mine), front, (got_c, got_d), patch)
+    return finish(table, (list_other, list_mine), front, got_c, patch)
 
 
 def solution(mesh):

time: 165 us -> 168 us (1.018)
  waiting for transfers between devices: 39.7 us -> 48.2 us
  starting transfers between devices: 48.8 us -> 43.8 us
    ppermute x12 -> x11, waiting for transfers between devices: 7.98 us -> 15.8 us  [swap(): return lax.ppermute(block, axis, [(i, partner(i)) for i in range(count)])]
    ppermute x2, waiting for transfers between devices: 10.8 us -> 6.57 us  [double(): came = lax.ppermute(part, 'row', rings[step])]
    ppermute x12 -> x11, starting transfers between devices: 26.7 us -> 23.7 us  [swap(): return lax.ppermute(block, axis, [(i, partner(i)) for i in range(count)])]
    ppermute x2, waiting for transfers between devices: 5.75 us -> 7.69 us  [halve(): return stay + lax.ppermute(leave, 'row', rings[step])]
    ppermute x3, waiting for transfers between devices: 1.81 us -> 3.65 us  [corner_step(): lax.ppermute(block, ('row', 'col'), route)]
    ppermute x10, starting transfers between devices: 6.47 us -> 4.71 us  [gather_step(): return lax.ppermute(block, ('row', 'col'), route)]
  transfers between devices with their start and end apart: 31 -> 30, of which waited for: 17 -> 17; matrix products, arithmetic and copies ran while one was open for 1% -> 1% of each run, Pallas kernels for 40% -> 39%
where the time goes in v9:
time: 168 us; the launch traced here: 167 us
  Pallas kernels  71.9 us (43%)
  waiting for transfers between devices  48.2 us (29%)
  starting transfers between devices  43.8 us (26%)
  other arithmetic  2.34 us (1%)
    ppermute x11, starting transfers between devices, swap(): return lax.ppermute(block, axis, [(i, partner(i)) for i in range(count)])  23.7 us
    pallas_call x1, Pallas kernels, update(): pl.pallas_call(update_kernel, out_shape=pltpu.HBM((2, 1024, 1024), F32),...  20.7 us
    pallas_call x2, Pallas kernels, pivot_terms(): pl.pallas_call(functools.partial(pivot_kernel, mine_half), out_shape=[jax...  18.2 us
    ppermute x11, waiting for transfers between devices, swap(): return lax.ppermute(block, axis, [(i, partner(i)) for i in range(count)])  15.8 us
    ppermute x10, waiting for transfers between devices, gather_step(): return lax.ppermute(block, ('row', 'col'), route)  13 us
    pallas_call x1, Pallas kernels, extend(): pl.pallas_call(extend_kernel, out_shape=pltpu.HBM((2, 1024, 1024), F32),...  11 us
    pallas_call x1, Pallas kernels, right_factor(): pl.pallas_call(factor_kernel, out_shape=[shape, shape, jax.ShapeDtypeStru...  7.77 us
    ppermute x2, waiting for transfers between devices, halve(): return stay + lax.ppermute(leave, 'row', rings[step])  7.69 us
  transfers between devices with their start and end apart: 30, of which 17 were waited for; matrix products, arithmetic and copies ran while one was open for 1% of the time, Pallas kernels for 39%

profile of v9, /device:TPU:1, one launch (start us, length us, event | category | flops | bytes accessed | tf_op | source)
XLA Modules:
  0.0 166.8 jit_solution(2897527559573113347)
XLA Ops:
  0.0 1.8 %cut.1.first = f32[10,128,128]{2,1,0:T(8,128)S(1)} custom-call(s32[2,80]{1,0:T(2,128)} %maps.7, f32[10,2,128,640]{3,2,1,0:T(8,128)} %bitcast.12), custom_call_target="tpu_custom_call" | custom-call | bytes 1048576 | tf_op jit(solution)/shard_map/cut/pallas_call | solution.py:67
  1.9 4.5 %collective-permute-start = (f32[10,128,128]{2,1,0:T(8,128)S(1)}, f32[10,128,128]{2,1,0:T(8,128)S(1)}, u32[]{:S(2)}, u32[]{:S(2)}) collective-permute-start(f32[10,128,128]{2,1,0:T(8,128)S(1)} %cut.1.first), channel_id=1, source_target_pairs={{0,64},{16,80},{32,96},{48,112},{64,0},{80,16},{96,32},{112,48},{1... | collective-permute-start | bytes 1966088 | tf_op jit(solution)/shard_map/ppermute | solution.py:597
  6.4 5.1 %prepare.1 = (f32[10,128,128]{2,1,0:T(8,128)S(1)}, f32[5,128,128]{2,1,0:T(8,128)S(1)}, f32[25,128,128]{2,1,0:T(8,128)S(1)}, f32[2048,128]{1,0:T(8,128)S(1)}, f32...) custom-call(s32[2,80]{1,0:T(2,128)} %maps.7, s32[8,128]{1,0:T(8,128)} %bitcast.18, f32[2048,1024]{1,0:T(8,128)} %front.5, ...), custom_call_target="tpu_custom_call" | custom-call | bytes 9437184 | tf_op jit(solution)/shard_map/prepare/pallas_call | solution.py:172
  11.5 1.0 collective-permute-start.1
  12.5 1.0 collective-permute-done.1
  13.6 3.1 %collective-permute-start.3 = (f32[256,128]{1,0:T(8,128)S(1)}, f32[256,128]{1,0:T(8,128)S(1)}, u32[]{:S(2)}, u32[]{:S(2)}) collective-permute-start(f32[256,128]{1,0:T(8,128)S(1)} %add.21), channel_id=1, source_target_pairs={{0,96},{16,112},{32,64},{48,80},{64,32},{80,48},{96,0},{112,16},{1... | collective-permute-start | bytes 393224 | tf_op jit(solution)/shard_map/ppermute | solution.py:597
  16.7 9.1 %pivot_terms_other.1 = (f32[512,1024]{1,0:T(8,128)S(1)}, f32[2048,128]{1,0:T(8,128)S(1)}, s32[513]{0:T(1024)S(1)}) custom-call(s32[2,80]{1,0:T(2,128)} %maps.7, s32[1024]{0:T(1024)} %pivots.1, f32[2048,1024]{1,0:T(8,128)} %front.5, f32[2560,640]{1,0:T(8,128)} %children.3), custom_call_target="tpu_custom_call" | custom-call | bytes 25165824 | tf_op jit(solution)/shard_map/pivot_terms_other/pallas_call | solution.py:265
  25.8 1.4 collective-permute-done.3
  27.2 1.3 collective-permute-start.7
  28.6 0.8 whole_panel.1
  29.4 4.7 %collective-permute-start.5 = (f32[1024,128]{1,0:T(8,128)S(1)}, f32[1024,128]{1,0:T(8,128)S(1)}, u32[]{:S(2)}, u32[]{:S(2)}) collective-permute-start(f32[1024,128]{1,0:T(8,128)S(1)} %get-tuple-element.79), channel_id=1, source_target_pairs={{0,12},{1,13},{2,14},{3,15},{4,8},{5,9},{6,10},{7,11},{16,28},{17,... | collective-permute-start | bytes 1572872 | tf_op jit(solution)/shard_map/ppermute | solution.py:601
  34.0 2.1 %collective-permute-start.8 = (f32[10,128,128]{2,1,0:T(8,128)S(1)}, f32[10,128,128]{2,1,0:T(8,128)S(1)}, u32[]{:S(2)}, u32[]{:S(2)}) collective-permute-start(f32[10,128,128]{2,1,0:T(8,128)S(1)} %get-tuple-element.83), channel_id=1, source_target_pairs={{0,64},{16,80},{32,96},{48,112},{64,0},{80,16},{96,32},{112,48},{1... | collective-permute-start | bytes 1966088 | tf_op jit(solution)/shard_map/ppermute | solution.py:597
  36.1 1.3 collective-permute-start.6
  37.4 9.2 %pivot_terms_mine.1 = (f32[512,1024]{1,0:T(8,128)S(1)}, f32[2048,128]{1,0:T(8,128)S(1)}, s32[513]{0:T(1024)S(1)}) custom-call(s32[2,80]{1,0:T(2,128)} %maps.7, s32[1024]{0:T(1024)} %pivots.1, f32[2048,1024]{1,0:T(8,128)} %front.5, f32[2560,640]{1,0:T(8,128)} %children.3, f32[2048,128]{1,0:T(8,128)S(1)} %get-tuple-element.73.refs_0_), custom_call_target="tpu_custom_call" | custom-call | bytes 25165824 | tf_op jit(solution)/shard_map/pivot_terms_mine/pallas_call | solution.py:265
  46.6 1.5 collective-permute-done.6
  48.2 0.6 add.25
  48.8 2.9 %collective-permute-done.8.refs_4_.refs_5_ = f32[10,128,128]{2,1,0:T(8,128)S(1)} collective-permute-done((f32[10,128,128]{2,1,0:T(8,128)S(1)}, f32[10,128,128]{2,1,0:T(8,128)S(1)}, u32[]{:S(2)}, u32[]{:S(2)}) %collective-permute-start.8) | collective-permute-done | bytes 655392 | tf_op jit(solution)/shard_map/ppermute | solution.py:597
  51.7 0.7 collective-permute-start.11
  52.5 2.3 %collective-permute-start.15 = (f32[256,1024]{1,0:T(8,128)S(1)}, f32[256,1024]{1,0:T(8,128)S(1)}, u32[]{:S(2)}, u32[]{:S(2)}) collective-permute-start(f32[256,1024]{1,0:T(8,128)S(1)} %slice_select_fusion), channel_id=1, source_target_pairs={{0,32},{16,112},{32,0},{48,80},{64,96},{80,48},{96,64},{112,16},{1... | collective-permute-start | bytes 3145736 | tf_op jit(solution)/shard_map/ppermute | solution.py:626
  54.8 1.2 collective-permute-start.13
  56.0 2.5 %collective-permute-done.11 = f32[1,512,128]{2,1,0:T(8,128)S(1)} collective-permute-done((f32[1,512,128]{2,1,0:T(8,128)S(1)}, f32[1,512,128]{2,1,0:T(8,128)S(1)}, u32[]{:S(2)}, u32[]{:S(2)}) %collective-permute-start.11) | collective-permute-done | bytes 262176 | tf_op jit(solution)/shard_map/ppermute | solution.py:639
  58.6 0.7 collective-permute-done.13
  59.3 3.7 %collective-permute-start.14 = (f32[2,256,128]{2,1,0:T(8,128)S(1)}, f32[2,256,128]{2,1,0:T(8,128)S(1)}, u32[]{:S(2)}, u32[]{:S(2)}) collective-permute-start(f32[2,256,128]{2,1,0:T(8,128)S(1)} %pad_maximum_fusion.8), channel_id=1, source_target_pairs={{0,1},{1,0},{2,3},{3,2},{4,5},{5,4},{6,7},{7,6},{8,9},{9,8},{10,11... | collective-permute-start | bytes 786440 | tf_op jit(solution)/shard_map/ppermute | solution.py:663
  63.1 0.8 collective-permute-start.10
  63.9 3.0 %collective-permute-done.14 = f32[2,256,128]{2,1,0:T(8,128)S(1)} collective-permute-done((f32[2,256,128]{2,1,0:T(8,128)S(1)}, f32[2,256,128]{2,1,0:T(8,128)S(1)}, u32[]{:S(2)}, u32[]{:S(2)}) %collective-permute-start.14) | collective-permute-done | bytes 262176 | tf_op jit(solution)/shard_map/ppermute | solution.py:663
  66.9 0.3 collective-permute-done.12
  67.2 5.5 %collective-permute-done.10 = f32[2,512,128]{2,1,0:T(8,128)S(1)} collective-permute-done((f32[2,512,128]{2,1,0:T(8,128)S(1)}, f32[2,512,128]{2,1,0:T(8,128)S(1)}, u32[]{:S(2)}, u32[]{:S(2)}) %collective-permute-start.10) | collective-permute-done | bytes 524320 | tf_op jit(solution)/shard_map/ppermute | solution.py:639
  72.8 0.3 select_add_fusion
  73.5 0.4 collective-permute-start.17
  73.9 7.7 %collective-permute-done.19 = f32[128,1024]{1,0:T(8,128)S(1)} collective-permute-done((f32[128,1024]{1,0:T(8,128)S(1)}, f32[128,1024]{1,0:T(8,128)S(1)}, u32[]{:S(2)}, u32[]{:S(2)}) %collective-permute-start.19) | collective-permute-done | bytes 524320 | tf_op jit(solution)/shard_map/ppermute | solution.py:626
  81.8 1.7 %collective-permute-start.21 = (f32[5,128,128]{2,1,0:T(8,128)S(1)}, f32[5,128,128]{2,1,0:T(8,128)S(1)}, u32[]{:S(2)}, u32[]{:S(2)}) collective-permute-start(f32[5,128,128]{2,1,0:T(8,128)S(1)} %get-tuple-element.95), channel_id=1, source_target_pairs={{0,64},{16,80},{32,96},{48,112},{64,0},{80,16},{96,32},{112,48},{1... | collective-permute-start | bytes 983048 | tf_op jit(solution)/shard_map/ppermute | solution.py:597
  83.6 6.6 %collective-permute-done.20 = f32[128,1024]{1,0:T(8,128)S(1)} collective-permute-done((f32[128,1024]{1,0:T(8,128)S(1)}, f32[128,1024]{1,0:T(8,128)S(1)}, u32[]{:S(2)}, u32[]{:S(2)}) %collective-permute-start.20) | collective-permute-done | bytes 524320 | tf_op jit(solution)/shard_map/ppermute | solution.py:629
  90.3 4.4 %collective-permute-done.21.refs_6_.refs_7_ = f32[5,128,128]{2,1,0:T(8,128)S(1)} collective-permute-done((f32[5,128,128]{2,1,0:T(8,128)S(1)}, f32[5,128,128]{2,1,0:T(8,128)S(1)}, u32[]{:S(2)}, u32[]{:S(2)}) %collective-permute-start.21) | collective-permute-done | bytes 327712 | tf_op jit(solution)/shard_map/ppermute | solution.py:597
  94.8 8.9 %collective-permute-start.25 = (f32[8,256,128]{2,1,0:T(8,128)S(1)}, f32[8,256,128]{2,1,0:T(8,128)S(1)}, u32[]{:S(2)}, u32[]{:S(2)}) collective-permute-start(f32[8,256,128]{2,1,0:T(8,128)S(1)} %pad_maximum_fusion.3.own), channel_id=1, source_target_pairs={{0,16},{16,0},{32,48},{48,32},{64,80},{80,64},{96,112},{112,96},{1... | collective-permute-start | bytes 3145736 | tf_op jit(solution)/shard_map/ppermute | solution.py:597
  103.7 2.0 %collective-permute-start.24 = (f32[256,1024]{1,0:T(8,128)S(1)}, f32[256,1024]{1,0:T(8,128)S(1)}, u32[]{:S(2)}, u32[]{:S(2)}) collective-permute-start(f32[256,1024]{1,0:T(8,128)S(1)} %pad_maximum_fusion.4), channel_id=1, source_target_pairs={{0,32},{16,112},{32,0},{48,80},{64,96},{80,48},{96,64},{112,16},{1... | collective-permute-start | bytes 3145736 | tf_op jit(solution)/shard_map/ppermute | solution.py:629
  105.9 11.0 %extend.1.front = f32[2,1024,1024]{2,1,0:T(8,128)} custom-call(s32[64]{0:T(128)S(1)} %get-tuple-element.66.table, f32[2,1024,1024]{2,1,0:T(8,128)} %bitcast.16, f32[10,2,128,640]{3,2,1,0:T(8,128)} %bitcast.14, f32[10,2,128,640]{3,2,1,0:T(8,128)} %bitcast.15, f32[10,128,128]{2,1,0:T(8,128)S(1)} %collective-permute-done.got.refs_2_.refs_3_, ...), custom_call_target="tpu_custom_call" | custom-call | bytes 1048576 | tf_op jit(solution)/shard_map/extend/pallas_call | solution.py:453
  116.9 2.0 %corners.1 = (bf16[3,512,512]{2,1,0:T(8,128)(2,1)S(1)}, bf16[3,512,512]{2,1,0:T(8,128)(2,1)S(1)}, f32[512,512]{1,0:T(8,128)S(1)}) custom-call(s32[64]{0:T(128)S(1)} %get-tuple-element.66.table, f32[8,256,128]{2,1,0:T(8,128)S(1)} %pad_maximum_fusion.3.own, f32[8,256,128]{2,1,0:T(8,128)S(1)} %collective-permute-done.25.swapped, f32[2,512,512]{2,1,0:T(8,128)S(1)} %copy-done), custom_call_target="tpu_custom_call" | custom-call | flops 805306368 | bytes 8388608 | tf_op jit(solution)/shard_map/corners/pallas_call | solution.py:343
  119.5 1.1 collective-permute-done.22.refs_2_
  120.6 1.6 collective-permute-start.26
  122.2 0.9 collective-permute-start.27
  123.1 0.9 collective-permute-start.29
  124.0 0.7 collective-permute-done.28.swapped
  124.8 7.8 %right_factor.1 = (bf16[1024,1024]{1,0:T(8,128)(2,1)S(1)}, bf16[1024,1024]{1,0:T(8,128)(2,1)S(1)}, f32[512,1024]{1,0:T(8,128)S(1)}) custom-call(s32[64]{0:T(128)S(1)} %get-tuple-element.66.table, f32[512,1024]{1,0:T(8,128)S(1)} %pad_maximum_fusion.own, f32[512,1024]{1,0:T(8,128)S(1)} %collective-permute-done.28.swapped, ...), custom_call_target="tpu_custom_call" | custom-call | flops 6442450944 | bytes 14680064 | tf_op jit(solution)/shard_map/right_factor/pallas_call | solution.py:397
  132.5 3.2 %collective-permute-done.26.refs_3_ = f32[4,512,128]{2,1,0:T(8,128)S(1)} collective-permute-done((f32[4,512,128]{2,1,0:T(8,128)S(1)}, f32[4,512,128]{2,1,0:T(8,128)S(1)}, u32[]{:S(2)}, u32[]{:S(2)}) %collective-permute-start.26) | collective-permute-done | bytes 1048608 | tf_op jit(solution)/shard_map/ppermute | solution.py:639
  135.8 0.4 collective-permute-done.27.refs_7_
  136.2 20.7 %update.1 = f32[2,1024,1024]{2,1,0:T(8,128)} custom-call(s32[64]{0:T(128)S(1)} %get-tuple-element.66.table, f32[2,1024,1024]{2,1,0:T(8,128)} %extend.1.front, f32[4,512,128]{2,1,0:T(8,128)S(1)} %pad_maximum_fusion.1.refs_0_, f32[4,512,128]{2,1,0:T(8,128)S(1)} %collective-permute-done.16.refs_1_, f32[4,512,128]{2,1,0:T(8,128)S(1)} %collective-permute-done.22.refs_2_, ...), custom_call_target="tpu_custom_call" | custom-call | flops 12884901888 | bytes 33554432 | tf_op jit(solution)/shard_map/update/pallas_call | solution.py:516
  156.9 5.3 %collective-permute-done.29.got = f32[25,128,128]{2,1,0:T(8,128)S(1)} collective-permute-done((f32[25,128,128]{2,1,0:T(8,128)S(1)}, f32[25,128,128]{2,1,0:T(8,128)S(1)}, u32[]{:S(2)}, u32[]{:S(2)}) %collective-permute-start.29) | collective-permute-done | bytes 1638432 | tf_op jit(solution)/shard_map/ppermute | solution.py:597
  162.2 4.4 %finish.1 = f32[2048,1024]{1,0:T(8,128)} custom-call(s32[64]{0:T(128)S(1)} %get-tuple-element.66.table, s32[513]{0:T(1024)S(1)} %get-tuple-element.67.list_other, s32[513]{0:T(1024)S(1)} %get-tuple-element.74.list_mine, f32[2048,1024]{1,0:T(8,128)} %bitcast.17, f32[25,128,128]{2,1,0:T(8,128)S(1)} %collective-permute-done.29.got, ...), custom_call_target="tpu_custom_call", output_to_operand_aliasing={{}: (3, {})} | custom-call | bytes 8388608 | tf_op jit(solution)/shard_map/finish/pallas_call | solution.py:577
  (45 shorter events, 2.2 us)
Async XLA Ops:
  1.9 25.4 %collective-permute-start = (f32[10,128,128]{2,1,0:T(8,128)S(1)}, f32[10,128,128]{2,1,0:T(8,128)S(1)}, u32[]{:S(2)}, u32[]{:S(2)}) collective-permute-start(f32[10,128,128]{2,1,0:T(8,128)S(1)} %cut.1.first), channel_id=1, source_target_pairs={{0,64},{16,80},{32,96},{48,112},{64,0},{80,16},{96,32},{112,48},{1... | collective-permute-start | bytes 1966088 | tf_op jit(solution)/shard_map/ppermute | solution.py:597
  11.5 2.0 %collective-permute-start.1 = (f32[256,128]{1,0:T(8,128)S(1)}, f32[256,128]{1,0:T(8,128)S(1)}, u32[]{:S(2)}, u32[]{:S(2)}) collective-permute-start(f32[256,128]{1,0:T(8,128)S(1)} %get-tuple-element.72), channel_id=1, source_target_pairs={{0,16},{16,0},{32,48},{48,32},{64,80},{80,64},{96,112},{112,96},{1... | collective-permute-start | bytes 393224 | tf_op jit(solution)/shard_map/ppermute | solution.py:597
  13.5 12.3 %collective-permute-start.4 = (f32[256,128]{1,0:T(8,128)S(1)}, f32[256,128]{1,0:T(8,128)S(1)}, u32[]{:S(2)}, u32[]{:S(2)}) collective-permute-start(f32[256,128]{1,0:T(8,128)S(1)} %add.21), channel_id=1, source_target_pairs={{0,64},{16,80},{32,96},{48,112},{64,0},{80,16},{96,32},{112,48},{1... | collective-permute-start | bytes 393224 | tf_op jit(solution)/shard_map/ppermute | solution.py:597
  13.6 13.6 %collective-permute-start.3 = (f32[256,128]{1,0:T(8,128)S(1)}, f32[256,128]{1,0:T(8,128)S(1)}, u32[]{:S(2)}, u32[]{:S(2)}) collective-permute-start(f32[256,128]{1,0:T(8,128)S(1)} %add.21), channel_id=1, source_target_pairs={{0,96},{16,112},{32,64},{48,80},{64,32},{80,48},{96,0},{112,16},{1... | collective-permute-start | bytes 393224 | tf_op jit(solution)/shard_map/ppermute | solution.py:597
  16.7 10.5 %collective-permute-start.2 = (f32[256,128]{1,0:T(8,128)S(1)}, f32[256,128]{1,0:T(8,128)S(1)}, u32[]{:S(2)}, u32[]{:S(2)}) collective-permute-start(f32[256,128]{1,0:T(8,128)S(1)} %add.21), channel_id=1, source_target_pairs={{0,32},{16,48},{32,0},{48,16},{64,96},{80,112},{96,64},{112,80},{1... | collective-permute-start | bytes 393224 | tf_op jit(solution)/shard_map/ppermute | solution.py:597
  27.2 21.0 %collective-permute-start.7 = (f32[512,1024]{1,0:T(8,128)S(1)}, f32[512,1024]{1,0:T(8,128)S(1)}, u32[]{:S(2)}, u32[]{:S(2)}) collective-permute-start(f32[512,1024]{1,0:T(8,128)S(1)} %get-tuple-element.82), channel_id=1, source_target_pairs={{0,16},{16,0},{32,48},{48,32},{64,80},{80,64},{96,112},{112,96},{1... | collective-permute-start | bytes 6291464 | tf_op jit(solution)/shard_map/ppermute | solution.py:597
  29.4 18.8 %collective-permute-start.5 = (f32[1024,128]{1,0:T(8,128)S(1)}, f32[1024,128]{1,0:T(8,128)S(1)}, u32[]{:S(2)}, u32[]{:S(2)}) collective-permute-start(f32[1024,128]{1,0:T(8,128)S(1)} %get-tuple-element.79), channel_id=1, source_target_pairs={{0,12},{1,13},{2,14},{3,15},{4,8},{5,9},{6,10},{7,11},{16,28},{17,... | collective-permute-start | bytes 1572872 | tf_op jit(solution)/shard_map/ppermute | solution.py:601
  34.0 17.6 %collective-permute-start.8 = (f32[10,128,128]{2,1,0:T(8,128)S(1)}, f32[10,128,128]{2,1,0:T(8,128)S(1)}, u32[]{:S(2)}, u32[]{:S(2)}) collective-permute-start(f32[10,128,128]{2,1,0:T(8,128)S(1)} %get-tuple-element.83), channel_id=1, source_target_pairs={{0,64},{16,80},{32,96},{48,112},{64,0},{80,16},{96,32},{112,48},{1... | collective-permute-start | bytes 1966088 | tf_op jit(solution)/shard_map/ppermute | solution.py:597
  36.1 12.0 %collective-permute-start.6 = (f32[256,128]{1,0:T(8,128)S(1)}, f32[256,128]{1,0:T(8,128)S(1)}, u32[]{:S(2)}, u32[]{:S(2)}) collective-permute-start(f32[256,128]{1,0:T(8,128)S(1)} %add_add_fusion), channel_id=1, source_target_pairs={{0,12},{1,13},{2,14},{3,15},{4,8},{5,9},{6,10},{7,11},{16,28},{17,... | collective-permute-start | bytes 393224 | tf_op jit(solution)/shard_map/ppermute | solution.py:601
  51.7 6.8 %collective-permute-start.11 = (f32[1,512,128]{2,1,0:T(8,128)S(1)}, f32[1,512,128]{2,1,0:T(8,128)S(1)}, u32[]{:S(2)}, u32[]{:S(2)}) collective-permute-start(f32[1,512,128]{2,1,0:T(8,128)S(1)} %get-tuple-element.129), channel_id=1, source_target_pairs={{0,3},{1,2},{2,1},{3,0},{4,7},{5,6},{6,5},{7,4},{8,11},{9,10},{10,... | collective-permute-start | bytes 786440 | tf_op jit(solution)/shard_map/ppermute | solution.py:639
  52.3 10.7 %collective-permute-start.9 = (f32[1,512,128]{2,1,0:T(8,128)S(1)}, f32[1,512,128]{2,1,0:T(8,128)S(1)}, u32[]{:S(2)}, u32[]{:S(2)}) collective-permute-start(f32[1,512,128]{2,1,0:T(8,128)S(1)} %get-tuple-element.130), channel_id=1, source_target_pairs={{0,1},{1,0},{2,3},{3,2},{4,5},{5,4},{6,7},{7,6},{8,9},{9,8},{10,11... | collective-permute-start | bytes 786440 | tf_op jit(solution)/shard_map/ppermute | solution.py:639
  52.5 20.3 %collective-permute-start.15 = (f32[256,1024]{1,0:T(8,128)S(1)}, f32[256,1024]{1,0:T(8,128)S(1)}, u32[]{:S(2)}, u32[]{:S(2)}) collective-permute-start(f32[256,1024]{1,0:T(8,128)S(1)} %slice_select_fusion), channel_id=1, source_target_pairs={{0,32},{16,112},{32,0},{48,80},{64,96},{80,48},{96,64},{112,16},{1... | collective-permute-start | bytes 3145736 | tf_op jit(solution)/shard_map/ppermute | solution.py:626
  54.8 4.5 %collective-permute-start.13 = (f32[1,256,128]{2,1,0:T(8,128)S(1)}, f32[1,256,128]{2,1,0:T(8,128)S(1)}, u32[]{:S(2)}, u32[]{:S(2)}) collective-permute-start(f32[1,256,128]{2,1,0:T(8,128)S(1)} %select_bitcast_fusion), channel_id=1, source_target_pairs={{0,4},{1,5},{2,6},{3,7},{4,0},{5,1},{6,2},{7,3},{8,12},{9,13},{10,... | collective-permute-start | bytes 393224 | tf_op jit(solution)/shard_map/ppermute | solution.py:663
  58.5 8.6 %collective-permute-start.12 = (f32[2,512,128]{2,1,0:T(8,128)S(1)}, f32[2,512,128]{2,1,0:T(8,128)S(1)}, u32[]{:S(2)}, u32[]{:S(2)}) collective-permute-start(f32[2,512,128]{2,1,0:T(8,128)S(1)} %pad_maximum_fusion.6), channel_id=1, source_target_pairs={{0,1},{1,0},{2,3},{3,2},{4,5},{5,4},{6,7},{7,6},{8,9},{9,8},{10,11... | collective-permute-start | bytes 1572872 | tf_op jit(solution)/shard_map/ppermute | solution.py:639
  59.3 7.5 %collective-permute-start.14 = (f32[2,256,128]{2,1,0:T(8,128)S(1)}, f32[2,256,128]{2,1,0:T(8,128)S(1)}, u32[]{:S(2)}, u32[]{:S(2)}) collective-permute-start(f32[2,256,128]{2,1,0:T(8,128)S(1)} %pad_maximum_fusion.8), channel_id=1, source_target_pairs={{0,1},{1,0},{2,3},{3,2},{4,5},{5,4},{6,7},{7,6},{8,9},{9,8},{10,11... | collective-permute-start | bytes 786440 | tf_op jit(solution)/shard_map/ppermute | solution.py:663
  63.1 9.6 %collective-permute-start.10 = (f32[2,512,128]{2,1,0:T(8,128)S(1)}, f32[2,512,128]{2,1,0:T(8,128)S(1)}, u32[]{:S(2)}, u32[]{:S(2)}) collective-permute-start(f32[2,512,128]{2,1,0:T(8,128)S(1)} %pad_maximum_fusion.5), channel_id=1, source_target_pairs={{0,3},{1,2},{2,1},{3,0},{4,7},{5,6},{6,5},{7,4},{8,11},{9,10},{10,... | collective-permute-start | bytes 1572872 | tf_op jit(solution)/shard_map/ppermute | solution.py:639
  73.2 8.4 %collective-permute-start.19 = (f32[128,1024]{1,0:T(8,128)S(1)}, f32[128,1024]{1,0:T(8,128)S(1)}, u32[]{:S(2)}, u32[]{:S(2)}) collective-permute-start(f32[128,1024]{1,0:T(8,128)S(1)} %slice_select_fusion.1), channel_id=1, source_target_pairs={{0,96},{16,48},{32,64},{48,16},{64,32},{80,112},{96,0},{112,80},{1... | collective-permute-start | bytes 1572872 | tf_op jit(solution)/shard_map/ppermute | solution.py:626
  73.3 10.2 %collective-permute-start.18 = (f32[4,256,128]{2,1,0:T(8,128)S(1)}, f32[4,256,128]{2,1,0:T(8,128)S(1)}, u32[]{:S(2)}, u32[]{:S(2)}) collective-permute-start(f32[4,256,128]{2,1,0:T(8,128)S(1)} %pad_maximum_fusion.7), channel_id=1, source_target_pairs={{0,3},{1,2},{2,1},{3,0},{4,7},{5,6},{6,5},{7,4},{8,11},{9,10},{10,... | collective-permute-start | bytes 1572872 | tf_op jit(solution)/shard_map/ppermute | solution.py:663
  73.4 21.4 %collective-permute-start.16 = (f32[4,512,128]{2,1,0:T(8,128)S(1)}, f32[4,512,128]{2,1,0:T(8,128)S(1)}, u32[]{:S(2)}, u32[]{:S(2)}) collective-permute-start(f32[4,512,128]{2,1,0:T(8,128)S(1)} %pad_maximum_fusion.1.refs_0_), channel_id=1, source_target_pairs={{0,4},{1,5},{2,6},{3,7},{4,0},{5,1},{6,2},{7,3},{8,12},{9,13},{10,... | collective-permute-start | bytes 3145736 | tf_op jit(solution)/shard_map/ppermute | solution.py:639
  73.5 21.3 %collective-permute-start.17 = (f32[4,512,128]{2,1,0:T(8,128)S(1)}, f32[4,512,128]{2,1,0:T(8,128)S(1)}, u32[]{:S(2)}, u32[]{:S(2)}) collective-permute-start(f32[4,512,128]{2,1,0:T(8,128)S(1)} %pad_maximum_fusion.2.refs_4_), channel_id=1, source_target_pairs={{0,12},{1,13},{2,14},{3,15},{4,8},{5,9},{6,10},{7,11},{8,4},{9,5},... | collective-permute-start | bytes 3145736 | tf_op jit(solution)/shard_map/ppermute | solution.py:639
  81.7 8.4 %collective-permute-start.20 = (f32[128,1024]{1,0:T(8,128)S(1)}, f32[128,1024]{1,0:T(8,128)S(1)}, u32[]{:S(2)}, u32[]{:S(2)}) collective-permute-start(f32[128,1024]{1,0:T(8,128)S(1)} %select_add_fusion.1), channel_id=1, source_target_pairs={{0,96},{16,48},{32,64},{48,16},{64,32},{80,112},{96,0},{112,80},{1... | collective-permute-start | bytes 1572872 | tf_op jit(solution)/shard_map/ppermute | solution.py:629
  81.8 13.0 %collective-permute-start.21 = (f32[5,128,128]{2,1,0:T(8,128)S(1)}, f32[5,128,128]{2,1,0:T(8,128)S(1)}, u32[]{:S(2)}, u32[]{:S(2)}) collective-permute-start(f32[5,128,128]{2,1,0:T(8,128)S(1)} %get-tuple-element.95), channel_id=1, source_target_pairs={{0,64},{16,80},{32,96},{48,112},{64,0},{80,16},{96,32},{112,48},{1... | collective-permute-start | bytes 983048 | tf_op jit(solution)/shard_map/ppermute | solution.py:597
  94.8 22.1 %collective-permute-start.25 = (f32[8,256,128]{2,1,0:T(8,128)S(1)}, f32[8,256,128]{2,1,0:T(8,128)S(1)}, u32[]{:S(2)}, u32[]{:S(2)}) collective-permute-start(f32[8,256,128]{2,1,0:T(8,128)S(1)} %pad_maximum_fusion.3.own), channel_id=1, source_target_pairs={{0,16},{16,0},{32,48},{48,32},{64,80},{80,64},{96,112},{112,96},{1... | collective-permute-start | bytes 3145736 | tf_op jit(solution)/shard_map/ppermute | solution.py:597
  103.7 15.3 %collective-permute-start.24 = (f32[256,1024]{1,0:T(8,128)S(1)}, f32[256,1024]{1,0:T(8,128)S(1)}, u32[]{:S(2)}, u32[]{:S(2)}) collective-permute-start(f32[256,1024]{1,0:T(8,128)S(1)} %pad_maximum_fusion.4), channel_id=1, source_target_pairs={{0,32},{16,112},{32,0},{48,80},{64,96},{80,48},{96,64},{112,16},{1... | collective-permute-start | bytes 3145736 | tf_op jit(solution)/shard_map/ppermute | solution.py:629
  105.7 14.9 %collective-permute-start.22 = (f32[4,512,128]{2,1,0:T(8,128)S(1)}, f32[4,512,128]{2,1,0:T(8,128)S(1)}, u32[]{:S(2)}, u32[]{:S(2)}) collective-permute-start(f32[4,512,128]{2,1,0:T(8,128)S(1)} %pad_maximum_fusion.1.refs_0_), channel_id=1, source_target_pairs={{0,12},{1,13},{2,14},{3,15},{4,8},{5,9},{6,10},{7,11},{8,4},{9,5},... | collective-permute-start | bytes 3145736 | tf_op jit(solution)/shard_map/ppermute | solution.py:639
  105.9 14.7 %collective-permute-start.23 = (f32[4,512,128]{2,1,0:T(8,128)S(1)}, f32[4,512,128]{2,1,0:T(8,128)S(1)}, u32[]{:S(2)}, u32[]{:S(2)}) collective-permute-start(f32[4,512,128]{2,1,0:T(8,128)S(1)} %pad_maximum_fusion.2.refs_4_), channel_id=1, source_target_pairs={{0,4},{1,5},{2,6},{3,7},{4,0},{5,1},{6,2},{7,3},{8,12},{9,13},{10,... | collective-permute-start | bytes 3145736 | tf_op jit(solution)/shard_map/ppermute | solution.py:639
  105.9 11.0 %copy-start = (f32[2,512,512]{2,1,0:T(8,128)S(1)}, f32[2,512,512]{2,1,0:T(8,128)}, u32[]{:S(2)}) copy-start(f32[2,512,512]{2,1,0:T(8,128)} %inverses.1) | copy-start | bytes 6291460
  120.6 4.2 %collective-permute-start.28 = (f32[512,1024]{1,0:T(8,128)S(1)}, f32[512,1024]{1,0:T(8,128)S(1)}, u32[]{:S(2)}, u32[]{:S(2)}) collective-permute-start(f32[512,1024]{1,0:T(8,128)S(1)} %pad_maximum_fusion.own), channel_id=1, source_target_pairs={{0,16},{16,0},{32,48},{48,32},{64,80},{80,64},{96,112},{112,96},{1... | collective-permute-start | bytes 6291464 | tf_op jit(solution)/shard_map/ppermute | solution.py:597
  120.6 15.2 %collective-permute-start.26 = (f32[4,512,128]{2,1,0:T(8,128)S(1)}, f32[4,512,128]{2,1,0:T(8,128)S(1)}, u32[]{:S(2)}, u32[]{:S(2)}) collective-permute-start(f32[4,512,128]{2,1,0:T(8,128)S(1)} %collective-permute-done.16.refs_1_), channel_id=1, source_target_pairs={{0,12},{1,13},{2,14},{3,15},{4,8},{5,9},{6,10},{7,11},{8,4},{9,5},... | collective-permute-start | bytes 3145736 | tf_op jit(solution)/shard_map/ppermute | solution.py:639
  122.2 13.9 %collective-permute-start.27 = (f32[4,512,128]{2,1,0:T(8,128)S(1)}, f32[4,512,128]{2,1,0:T(8,128)S(1)}, u32[]{:S(2)}, u32[]{:S(2)}) collective-permute-start(f32[4,512,128]{2,1,0:T(8,128)S(1)} %collective-permute-done.17.refs_5_), channel_id=1, source_target_pairs={{0,4},{1,5},{2,6},{3,7},{4,0},{5,1},{6,2},{7,3},{8,12},{9,13},{10,... | collective-permute-start | bytes 3145736 | tf_op jit(solution)/shard_map/ppermute | solution.py:639
  123.1 39.1 %collective-permute-start.29 = (f32[25,128,128]{2,1,0:T(8,128)S(1)}, f32[25,128,128]{2,1,0:T(8,128)S(1)}, u32[]{:S(2)}, u32[]{:S(2)}) collective-permute-start(f32[25,128,128]{2,1,0:T(8,128)S(1)} %get-tuple-element.123), channel_id=1, source_target_pairs={{0,64},{16,80},{32,96},{48,112},{64,0},{80,16},{96,32},{112,48},{1... | collective-permute-start | bytes 4915208 | tf_op jit(solution)/shard_map/ppermute | solution.py:597

commit v10 on v9

--- a/solution.py
+++ b/solution.py
@@ -95,13 +95,13 @@
         pltpu.make_async_copy(front.at[:, pl.ds(0, BLK)], panel, sem.at[2]),
     ]
     writes = []
-    rest_a, rest_b, rest_c = rests
+    rest_a, rest_b = rests
     parts = (
-        (0, 0, rest_a),
-        (1, 0, rest_b),
-        (1, 5, rest_c.at[pl.ds(0, 5)]),
-        (2, 0, rest_c.at[pl.ds(5, 10)]),
-        (3, 0, rest_c.at[pl.ds(15, 10)]),
+        (0, 0, rest_a.at[pl.ds(0, 10)]),
+        (1, 0, rest_a.at[pl.ds(10, 5)]),
+        (1, 5, rest_b.at[pl.ds(0, 5)]),
+        (2, 0, rest_b.at[pl.ds(5, 10)]),
+        (3, 0, rest_b.at[pl.ds(15, 10)]),
     )
     for n, (j, start, target) in enumerate(parts):
         d = j + (j >= place).astype(jnp.int32)
@@ -172,8 +172,7 @@
     return pl.pallas_call(
         prepare_kernel,
         out_shape=[
-            jax.ShapeDtypeStruct((10, BLK, BLK), F32),
-            jax.ShapeDtypeStruct((5, BLK, BLK), F32),
+            jax.ShapeDtypeStruct((15, BLK, BLK), F32),
             jax.ShapeDtypeStruct((25, BLK, BLK), F32),
             jax.ShapeDtypeStruct((2048, BLK), F32),
             jax.ShapeDtypeStruct((256, BLK), F32),
@@ -181,7 +180,7 @@
             jax.ShapeDtypeStruct((64,), jnp.int32),
         ],
         in_specs=[SMEM, VMEM, HBM, HBM, VMEM],
-        out_specs=[HBM] * 3 + [VMEM, VMEM, VMEM, SMEM],
+        out_specs=[HBM] * 2 + [VMEM, VMEM, VMEM, SMEM],
         scratch_shapes=[
             pltpu.VMEM((10, BLK, 640), F32),
             pltpu.VMEM((10, BLK, BLK), F32),
@@ -409,7 +408,7 @@
     return jnp.maximum(s[base + half * 8 + t], 0)
 
 
-ARRIVED = (0, 0, 10), (1, 0, 10), (2, 0, 5)
+ARRIVED = (0, 0, 10, 0), (1, 0, 10, 0), (2, 0, 5, 10)
 
 
 def extend_kernel(table, front, *refs):
@@ -426,7 +425,7 @@
                 out[half, :, to] += kept[half][0, 0, :, d * BLK : (d + 1) * BLK]
 
         m = table[GOT_AT + half * 8 + step]
-        for j, (column, start, count) in enumerate(ARRIVED):
+        for j, (column, start, count, _) in enumerate(ARRIVED):
 
             @pl.when((m >= start) & (m < start + count))
             def _(half=half, j=j, column=column):
@@ -438,16 +437,16 @@
     def kept_at(half):
         return lambda t, s: (block_at(KEPT_AT, half, t, s), s[SIDE], 0, 0)
 
-    def got_at(half, start, count):
+    def got_at(half, start, count, slot):
         return lambda t, s: (
-            jnp.clip(s[GOT_AT + half * 8 + t] - start, 0, count - 1), 0, 0
+            jnp.clip(s[GOT_AT + half * 8 + t] - start, 0, count - 1) + slot, 0, 0
         )
 
     tile = pl.BlockSpec((2, BLK, 1024), lambda t, s: (0, t, 0))
     kept_specs = [pl.BlockSpec((1, 1, BLK, 640), kept_at(half)) for half in range(2)]
     got_specs = [
-        pl.BlockSpec((1, BLK, BLK), got_at(half, start, count))
-        for _, start, count in ARRIVED
+        pl.BlockSpec((1, BLK, BLK), got_at(half, start, count, slot))
+        for _, start, count, slot in ARRIVED
         for half in range(2)
     ]
     return pl.pallas_call(
@@ -641,7 +640,7 @@
     first = cut(child_maps, pieces)
     got0 = by_row(first, 4)
     *rest, panel, corner, away, table = prepare(child_maps, pivots, front, pieces, first)
-    rest_a, rest_b, rest_c = rest
+    rest_a, rest_b = rest
     corner = corner + by_row(away, 1)
     corner = corner + (by_row(corner, 2) + (by_row(corner, 6) + by_row(corner, 4)))
     away_rows, marks, list_other = pivot_terms(child_maps, pivots, front, children)
@@ -653,7 +652,7 @@
     got_a = by_row(rest_a, 4)
     own_rows, marks, list_mine = pivot_terms(child_maps, pivots, front, children, marks)
     total = own_rows + by_row(away_rows, 1)
-    mine, corner, total, got_a, rest_b = together((mine, corner, total, got_a, rest_b))
+    mine, corner, total, got_a = together((mine, corner, total, got_a))
 
     def corner_step(block, step):
         masks = ((4, 1, 3), (1, 3, 4))
@@ -668,25 +667,24 @@
         held = [jnp.concatenate([h, c], axis=0) for h, c in zip(held, came)]
         corner = corner_step(corner, k)
     total = halve(total, 0)
-    held, corner, total, rest_b = together((held, corner, total, rest_b))
+    held, corner, total = together((held, corner, total))
     came = [gather_step(held[w], w, 2) for w in range(2)]
     corner = corner_step(corner, 2)
     total = double(halve(total, 1), 1)
-    got_b = by_row(rest_b, 4)
-    came, corner, total, got_b = together((came, corner, total, got_b))
+    came, corner, total = together((came, corner, total))
     held_far = [gather_step(held[w], w, 3) for w in range(2)]
-    front = extend(table, front, pieces, (got0, got_a, got_b))
+    front = extend(table, front, pieces, (got0, got_a, got_a))
     *factors, cross = corners(table, corner, by_row(corner, 1), diag_inverses)
-    came, held_far, total, rest_c, factors, cross, front = together(
-        (came, held_far, double(total, 0), rest_c, factors, cross, front)
+    came, held_far, total, rest_b, factors, cross, front = together(
+        (came, held_far, double(total, 0), rest_b, factors, cross, front)
     )
     came_far = [gather_step(came[w], w, 3) for w in range(2)]
-    got_c = by_row(rest_c, 4)
+    got_b = by_row(rest_b, 4)
     *right, patch = right_factor(table, total, by_row(total, 1), factors, cross)
     came_far, right, patch = together((came_far, right, patch))
     blocks = [(held[w], came[w], held_far[w], came_far[w]) for w in range(2)]
     front = update(table, front, blocks, right, marks).reshape(2048, 1024)
-    return finish(table, (list_other, list_mine), front, got_c, patch)
+    return finish(table, (list_other, list_mine), front, got_b, patch)
 
 
 def solution(mesh):

time: 168 us -> 162 us (0.964)
  waiting for transfers between devices: 48.2 us -> 45.4 us
  starting transfers between devices: 43.8 us -> 41.2 us
    ppermute x11 -> x10, waiting for transfers between devices: 15.8 us -> 8.96 us  [swap(): return lax.ppermute(block, axis, [(i, partner(i)) for i in range(count)])]
    ppermute x10, starting transfers between devices: 4.71 us -> 11.1 us  [gather_step(): return lax.ppermute(block, ('row', 'col'), route)]
    ppermute x11 -> x10, starting transfers between devices: 23.7 us -> 17.9 us  [swap(): return lax.ppermute(block, axis, [(i, partner(i)) for i in range(count)])]
    ppermute x3, waiting for transfers between devices: 3.65 us -> 6.76 us  [corner_step(): lax.ppermute(block, ('row', 'col'), route)]
    ppermute x3, starting transfers between devices: 5.02 us -> 2.66 us  [corner_step(): lax.ppermute(block, ('row', 'col'), route)]
    ppermute x2, waiting for transfers between devices: 1.53 us -> 3.29 us  [fold(): came = lax.ppermute(block[1], 'col', [(c, c ^ 12) for c in range(8)])]
  transfers between devices with their start and end apart: 30 -> 29, of which waited for: 17 -> 15; matrix products, arithmetic and copies ran while one was open for 1% -> 1% of each run, Pallas kernels for 39% -> 41%
where the time goes in v10:
time: 162 us; the launch traced here: 161 us
  Pallas kernels  71.9 us (44%)
  waiting for transfers between devices  45.4 us (28%)
  starting transfers between devices  41.2 us (25%)
  other arithmetic  2.3 us (1%)
    pallas_call x1, Pallas kernels, update(): pl.pallas_call(update_kernel, out_shape=pltpu.HBM((2, 1024, 1024), F32),...  20.7 us
    pallas_call x2, Pallas kernels, pivot_terms(): pl.pallas_call(functools.partial(pivot_kernel, mine_half), out_shape=[jax...  18.1 us
    ppermute x10, starting transfers between devices, swap(): return lax.ppermute(block, axis, [(i, partner(i)) for i in range(count)])  17.9 us
    ppermute x10, waiting for transfers between devices, gather_step(): return lax.ppermute(block, ('row', 'col'), route)  11.7 us
    pallas_call x1, Pallas kernels, extend(): pl.pallas_call(extend_kernel, out_shape=pltpu.HBM((2, 1024, 1024), F32),...  11.2 us
    ppermute x10, starting transfers between devices, gather_step(): return lax.ppermute(block, ('row', 'col'), route)  11.1 us
    ppermute x10, waiting for transfers between devices, swap(): return lax.ppermute(block, axis, [(i, partner(i)) for i in range(count)])  8.96 us
    ppermute x2, waiting for transfers between devices, double(): came = lax.ppermute(part, 'row', rings[step])  8.22 us
  transfers between devices with their start and end apart: 29, of which 15 were waited for; matrix products, arithmetic and copies ran while one was open for 1% of the time, Pallas kernels for 41%

profile of v10, /device:TPU:1, one launch (start us, length us, event | category | flops | bytes accessed | tf_op | source)
XLA Modules:
  0.0 161.2 jit_solution(17532203698325776756)
XLA Ops:
  0.0 1.8 %cut.1.first = f32[10,128,128]{2,1,0:T(8,128)S(1)} custom-call(s32[2,80]{1,0:T(2,128)} %maps.7, f32[10,2,128,640]{3,2,1,0:T(8,128)} %bitcast.12), custom_call_target="tpu_custom_call" | custom-call | bytes 1048576 | tf_op jit(solution)/shard_map/cut/pallas_call | solution.py:67
  1.9 4.5 %collective-permute-start = (f32[10,128,128]{2,1,0:T(8,128)S(1)}, f32[10,128,128]{2,1,0:T(8,128)S(1)}, u32[]{:S(2)}, u32[]{:S(2)}) collective-permute-start(f32[10,128,128]{2,1,0:T(8,128)S(1)} %cut.1.first), channel_id=1, source_target_pairs={{0,64},{16,80},{32,96},{48,112},{64,0},{80,16},{96,32},{112,48},{1... | collective-permute-start | bytes 1966088 | tf_op jit(solution)/shard_map/ppermute | solution.py:596
  6.4 5.1 %prepare.1 = (f32[15,128,128]{2,1,0:T(8,128)S(1)}, f32[25,128,128]{2,1,0:T(8,128)S(1)}, f32[2048,128]{1,0:T(8,128)S(1)}, f32[256,128]{1,0:T(8,128)S(1)}, f32[256,128]{1,0:T(8,128)S(1)}, /*index=5*/s32[64]{0:T(128)S(1)}) custom-call(s32[2,80]{1,0:T(2,128)} %maps.7, s32[8,128]{1,0:T(8,128)} %bitcast.18, f32[2048,1024]{1,0:T(8,128)} %front.5, ...), custom_call_target="tpu_custom_call" | custom-call | bytes 9437184 | tf_op jit(solution)/shard_map/prepare/pallas_call | solution.py:172
  11.5 1.0 collective-permute-start.1
  12.5 1.0 collective-permute-done.1
  13.6 3.1 %collective-permute-start.3 = (f32[256,128]{1,0:T(8,128)S(1)}, f32[256,128]{1,0:T(8,128)S(1)}, u32[]{:S(2)}, u32[]{:S(2)}) collective-permute-start(f32[256,128]{1,0:T(8,128)S(1)} %add.21), channel_id=1, source_target_pairs={{0,96},{16,112},{32,64},{48,80},{64,32},{80,48},{96,0},{112,16},{1... | collective-permute-start | bytes 393224 | tf_op jit(solution)/shard_map/ppermute | solution.py:596
  16.7 9.0 %pivot_terms_other.1 = (f32[512,1024]{1,0:T(8,128)S(1)}, f32[2048,128]{1,0:T(8,128)S(1)}, s32[513]{0:T(1024)S(1)}) custom-call(s32[2,80]{1,0:T(2,128)} %maps.7, s32[1024]{0:T(1024)} %pivots.1, f32[2048,1024]{1,0:T(8,128)} %front.5, f32[2560,640]{1,0:T(8,128)} %children.3), custom_call_target="tpu_custom_call" | custom-call | bytes 25165824 | tf_op jit(solution)/shard_map/pivot_terms_other/pallas_call | solution.py:264
  25.8 1.4 collective-permute-done.3
  27.2 1.3 collective-permute-start.7
  28.6 2.2 %collective-permute-start.8 = (f32[15,128,128]{2,1,0:T(8,128)S(1)}, f32[15,128,128]{2,1,0:T(8,128)S(1)}, u32[]{:S(2)}, u32[]{:S(2)}) collective-permute-start(f32[15,128,128]{2,1,0:T(8,128)S(1)} %get-tuple-element.79), channel_id=1, source_target_pairs={{0,64},{16,80},{32,96},{48,112},{64,0},{80,16},{96,32},{112,48},{1... | collective-permute-start | bytes 2949128 | tf_op jit(solution)/shard_map/ppermute | solution.py:596
  30.8 0.8 whole_panel.1
  31.6 4.7 %collective-permute-start.5 = (f32[1024,128]{1,0:T(8,128)S(1)}, f32[1024,128]{1,0:T(8,128)S(1)}, u32[]{:S(2)}, u32[]{:S(2)}) collective-permute-start(f32[1024,128]{1,0:T(8,128)S(1)} %get-tuple-element.75), channel_id=1, source_target_pairs={{0,12},{1,13},{2,14},{3,15},{4,8},{5,9},{6,10},{7,11},{16,28},{17,... | collective-permute-start | bytes 1572872 | tf_op jit(solution)/shard_map/ppermute | solution.py:600
  36.2 1.3 collective-permute-start.6
  37.5 9.1 %pivot_terms_mine.1 = (f32[512,1024]{1,0:T(8,128)S(1)}, f32[2048,128]{1,0:T(8,128)S(1)}, s32[513]{0:T(1024)S(1)}) custom-call(s32[2,80]{1,0:T(2,128)} %maps.7, s32[1024]{0:T(1024)} %pivots.1, f32[2048,1024]{1,0:T(8,128)} %front.5, f32[2560,640]{1,0:T(8,128)} %children.3, f32[2048,128]{1,0:T(8,128)S(1)} %get-tuple-element.69.refs_0_), custom_call_target="tpu_custom_call" | custom-call | bytes 25165824 | tf_op jit(solution)/shard_map/pivot_terms_mine/pallas_call | solution.py:264
  46.7 3.3 %collective-permute-done.6 = f32[256,128]{1,0:T(8,128)S(1)} collective-permute-done((f32[256,128]{1,0:T(8,128)S(1)}, f32[256,128]{1,0:T(8,128)S(1)}, u32[]{:S(2)}, u32[]{:S(2)}) %collective-permute-start.6) | collective-permute-done | bytes 131104 | tf_op jit(solution)/shard_map/ppermute | solution.py:600
  50.1 0.6 add.25
  50.6 2.8 %collective-permute-done.8.refs_4_.refs_5_.refs_6_.refs_7_ = f32[15,128,128]{2,1,0:T(8,128)S(1)} collective-permute-done((f32[15,128,128]{2,1,0:T(8,128)S(1)}, f32[15,128,128]{2,1,0:T(8,128)S(1)}, u32[]{:S(2)}, u32[]{:S(2)}) %collective-permute-start.8) | collective-permute-done | bytes 983072 | tf_op jit(solution)/shard_map/ppermute | solution.py:596
  53.4 2.8 %collective-permute-start.11 = (f32[1,512,128]{2,1,0:T(8,128)S(1)}, f32[1,512,128]{2,1,0:T(8,128)S(1)}, u32[]{:S(2)}, u32[]{:S(2)}) collective-permute-start(f32[1,512,128]{2,1,0:T(8,128)S(1)} %get-tuple-element.121), channel_id=1, source_target_pairs={{0,3},{1,2},{2,1},{3,0},{4,7},{5,6},{6,5},{7,4},{8,11},{9,10},{10,... | collective-permute-start | bytes 786440 | tf_op jit(solution)/shard_map/ppermute | solution.py:638
  56.4 2.4 %collective-permute-start.15 = (f32[256,1024]{1,0:T(8,128)S(1)}, f32[256,1024]{1,0:T(8,128)S(1)}, u32[]{:S(2)}, u32[]{:S(2)}) collective-permute-start(f32[256,1024]{1,0:T(8,128)S(1)} %slice_select_fusion), channel_id=1, source_target_pairs={{0,32},{16,112},{32,0},{48,80},{64,96},{80,48},{96,64},{112,16},{1... | collective-permute-start | bytes 3145736 | tf_op jit(solution)/shard_map/ppermute | solution.py:625
  58.9 1.2 collective-permute-start.13
  60.3 1.3 collective-permute-start.12
  61.7 2.8 %collective-permute-done.13 = f32[1,256,128]{2,1,0:T(8,128)S(1)} collective-permute-done((f32[1,256,128]{2,1,0:T(8,128)S(1)}, f32[1,256,128]{2,1,0:T(8,128)S(1)}, u32[]{:S(2)}, u32[]{:S(2)}) %collective-permute-start.13) | collective-permute-done | bytes 131104 | tf_op jit(solution)/shard_map/ppermute | solution.py:662
  64.4 1.1 collective-permute-start.14
  65.6 2.1 %collective-permute-start.10 = (f32[2,512,128]{2,1,0:T(8,128)S(1)}, f32[2,512,128]{2,1,0:T(8,128)S(1)}, u32[]{:S(2)}, u32[]{:S(2)}) collective-permute-start(f32[2,512,128]{2,1,0:T(8,128)S(1)} %pad_maximum_fusion.5), channel_id=1, source_target_pairs={{0,3},{1,2},{2,1},{3,0},{4,7},{5,6},{6,5},{7,4},{8,11},{9,10},{10,... | collective-permute-start | bytes 1572872 | tf_op jit(solution)/shard_map/ppermute | solution.py:638
  67.7 4.0 %collective-permute-done.14 = f32[2,256,128]{2,1,0:T(8,128)S(1)} collective-permute-done((f32[2,256,128]{2,1,0:T(8,128)S(1)}, f32[2,256,128]{2,1,0:T(8,128)S(1)}, u32[]{:S(2)}, u32[]{:S(2)}) %collective-permute-start.14) | collective-permute-done | bytes 262176 | tf_op jit(solution)/shard_map/ppermute | solution.py:662
  71.8 3.4 %collective-permute-done.10 = f32[2,512,128]{2,1,0:T(8,128)S(1)} collective-permute-done((f32[2,512,128]{2,1,0:T(8,128)S(1)}, f32[2,512,128]{2,1,0:T(8,128)S(1)}, u32[]{:S(2)}, u32[]{:S(2)}) %collective-permute-start.10) | collective-permute-done | bytes 524320 | tf_op jit(solution)/shard_map/ppermute | solution.py:638
  75.3 0.3 select_add_fusion
  75.7 0.3 collective-permute-start.18
  76.1 1.6 collective-permute-start.17
  77.6 6.4 %collective-permute-done.19 = f32[128,1024]{1,0:T(8,128)S(1)} collective-permute-done((f32[128,1024]{1,0:T(8,128)S(1)}, f32[128,1024]{1,0:T(8,128)S(1)}, u32[]{:S(2)}, u32[]{:S(2)}) %collective-permute-start.19) | collective-permute-done | bytes 524320 | tf_op jit(solution)/shard_map/ppermute | solution.py:625
  84.3 8.2 %collective-permute-done.20 = f32[128,1024]{1,0:T(8,128)S(1)} collective-permute-done((f32[128,1024]{1,0:T(8,128)S(1)}, f32[128,1024]{1,0:T(8,128)S(1)}, u32[]{:S(2)}, u32[]{:S(2)}) %collective-permute-start.20) | collective-permute-done | bytes 524320 | tf_op jit(solution)/shard_map/ppermute | solution.py:628
  92.8 4.1 %collective-permute-done.17.refs_5_ = f32[4,512,128]{2,1,0:T(8,128)S(1)} collective-permute-done((f32[4,512,128]{2,1,0:T(8,128)S(1)}, f32[4,512,128]{2,1,0:T(8,128)S(1)}, u32[]{:S(2)}, u32[]{:S(2)}) %collective-permute-start.17) | collective-permute-done | bytes 1048608 | tf_op jit(solution)/shard_map/ppermute | solution.py:638
  96.8 2.2 %collective-permute-start.24 = (f32[8,256,128]{2,1,0:T(8,128)S(1)}, f32[8,256,128]{2,1,0:T(8,128)S(1)}, u32[]{:S(2)}, u32[]{:S(2)}) collective-permute-start(f32[8,256,128]{2,1,0:T(8,128)S(1)} %pad_maximum_fusion.3.own), channel_id=1, source_target_pairs={{0,16},{16,0},{32,48},{48,32},{64,80},{80,64},{96,112},{112,96},{1... | collective-permute-start | bytes 3145736 | tf_op jit(solution)/shard_map/ppermute | solution.py:596
  99.0 1.0 collective-permute-start.23
  100.1 1.6 collective-permute-start.21
  101.7 11.2 %extend.1.front = f32[2,1024,1024]{2,1,0:T(8,128)} custom-call(s32[64]{0:T(128)S(1)} %get-tuple-element.62.table, f32[2,1024,1024]{2,1,0:T(8,128)} %bitcast.16, f32[10,2,128,640]{3,2,1,0:T(8,128)} %bitcast.14, f32[10,2,128,640]{3,2,1,0:T(8,128)} %bitcast.15, f32[10,128,128]{2,1,0:T(8,128)S(1)} %collective-permute-done.got.refs_2_.refs_3_, ...), custom_call_target="tpu_custom_call" | custom-call | bytes 1048576 | tf_op jit(solution)/shard_map/extend/pallas_call | solution.py:452
  112.9 2.0 %corners.1 = (bf16[3,512,512]{2,1,0:T(8,128)(2,1)S(1)}, bf16[3,512,512]{2,1,0:T(8,128)(2,1)S(1)}, f32[512,512]{1,0:T(8,128)S(1)}) custom-call(s32[64]{0:T(128)S(1)} %get-tuple-element.62.table, f32[8,256,128]{2,1,0:T(8,128)S(1)} %pad_maximum_fusion.3.own, f32[8,256,128]{2,1,0:T(8,128)S(1)} %collective-permute-done.24.swapped, f32[2,512,512]{2,1,0:T(8,128)S(1)} %copy-done), custom_call_target="tpu_custom_call" | custom-call | flops 805306368 | bytes 8388608 | tf_op jit(solution)/shard_map/corners/pallas_call | solution.py:342
  115.0 0.3 broadcast_select_fusion.1
  115.3 0.2 pad_maximum_fusion.own
  115.6 1.1 collective-permute-start.27
  116.8 1.7 %collective-permute-start.25 = (f32[4,512,128]{2,1,0:T(8,128)S(1)}, f32[4,512,128]{2,1,0:T(8,128)S(1)}, u32[]{:S(2)}, u32[]{:S(2)}) collective-permute-start(f32[4,512,128]{2,1,0:T(8,128)S(1)} %collective-permute-done.16.refs_1_), channel_id=1, source_target_pairs={{0,12},{1,13},{2,14},{3,15},{4,8},{5,9},{6,10},{7,11},{8,4},{9,5},... | collective-permute-start | bytes 3145736 | tf_op jit(solution)/shard_map/ppermute | solution.py:638
  118.4 2.3 %collective-permute-start.28 = (f32[25,128,128]{2,1,0:T(8,128)S(1)}, f32[25,128,128]{2,1,0:T(8,128)S(1)}, u32[]{:S(2)}, u32[]{:S(2)}) collective-permute-start(f32[25,128,128]{2,1,0:T(8,128)S(1)} %get-tuple-element.115), channel_id=1, source_target_pairs={{0,64},{16,80},{32,96},{48,112},{64,0},{80,16},{96,32},{112,48},{1... | collective-permute-start | bytes 4915208 | tf_op jit(solution)/shard_map/ppermute | solution.py:596
  120.7 7.8 %right_factor.1 = (bf16[1024,1024]{1,0:T(8,128)(2,1)S(1)}, bf16[1024,1024]{1,0:T(8,128)(2,1)S(1)}, f32[512,1024]{1,0:T(8,128)S(1)}) custom-call(s32[64]{0:T(128)S(1)} %get-tuple-element.62.table, f32[512,1024]{1,0:T(8,128)S(1)} %pad_maximum_fusion.own, f32[512,1024]{1,0:T(8,128)S(1)} %collective-permute-done.27.swapped, ...), custom_call_target="tpu_custom_call" | custom-call | flops 6442450944 | bytes 14680064 | tf_op jit(solution)/shard_map/right_factor/pallas_call | solution.py:396
  128.5 3.4 %collective-permute-done.25.refs_3_ = f32[4,512,128]{2,1,0:T(8,128)S(1)} collective-permute-done((f32[4,512,128]{2,1,0:T(8,128)S(1)}, f32[4,512,128]{2,1,0:T(8,128)S(1)}, u32[]{:S(2)}, u32[]{:S(2)}) %collective-permute-start.25) | collective-permute-done | bytes 1048608 | tf_op jit(solution)/shard_map/ppermute | solution.py:638
  131.9 0.4 collective-permute-done.26.refs_7_
  132.4 20.7 %update.1 = f32[2,1024,1024]{2,1,0:T(8,128)} custom-call(s32[64]{0:T(128)S(1)} %get-tuple-element.62.table, f32[2,1024,1024]{2,1,0:T(8,128)} %extend.1.front, f32[4,512,128]{2,1,0:T(8,128)S(1)} %pad_maximum_fusion.1.refs_0_, f32[4,512,128]{2,1,0:T(8,128)S(1)} %collective-permute-done.16.refs_1_, f32[4,512,128]{2,1,0:T(8,128)S(1)} %collective-permute-done.21.refs_2_, ...), custom_call_target="tpu_custom_call" | custom-call | flops 12884901888 | bytes 33554432 | tf_op jit(solution)/shard_map/update/pallas_call | solution.py:515
  153.1 3.8 %collective-permute-done.28.got = f32[25,128,128]{2,1,0:T(8,128)S(1)} collective-permute-done((f32[25,128,128]{2,1,0:T(8,128)S(1)}, f32[25,128,128]{2,1,0:T(8,128)S(1)}, u32[]{:S(2)}, u32[]{:S(2)}) %collective-permute-start.28) | collective-permute-done | bytes 1638432 | tf_op jit(solution)/shard_map/ppermute | solution.py:596
  156.8 4.3 %finish.1 = f32[2048,1024]{1,0:T(8,128)} custom-call(s32[64]{0:T(128)S(1)} %get-tuple-element.62.table, s32[513]{0:T(1024)S(1)} %get-tuple-element.63.list_other, s32[513]{0:T(1024)S(1)} %get-tuple-element.70.list_mine, f32[2048,1024]{1,0:T(8,128)} %bitcast.17, f32[25,128,128]{2,1,0:T(8,128)S(1)} %collective-permute-done.28.got, ...), custom_call_target="tpu_custom_call", output_to_operand_aliasing={{}: (3, {})} | custom-call | bytes 8388608 | tf_op jit(solution)/shard_map/finish/pallas_call | solution.py:576
  (43 shorter events, 1.7 us)
Async XLA Ops:
  1.9 25.4 %collective-permute-start = (f32[10,128,128]{2,1,0:T(8,128)S(1)}, f32[10,128,128]{2,1,0:T(8,128)S(1)}, u32[]{:S(2)}, u32[]{:S(2)}) collective-permute-start(f32[10,128,128]{2,1,0:T(8,128)S(1)} %cut.1.first), channel_id=1, source_target_pairs={{0,64},{16,80},{32,96},{48,112},{64,0},{80,16},{96,32},{112,48},{1... | collective-permute-start | bytes 1966088 | tf_op jit(solution)/shard_map/ppermute | solution.py:596
  11.5 2.0 %collective-permute-start.1 = (f32[256,128]{1,0:T(8,128)S(1)}, f32[256,128]{1,0:T(8,128)S(1)}, u32[]{:S(2)}, u32[]{:S(2)}) collective-permute-start(f32[256,128]{1,0:T(8,128)S(1)} %get-tuple-element.68), channel_id=1, source_target_pairs={{0,16},{16,0},{32,48},{48,32},{64,80},{80,64},{96,112},{112,96},{1... | collective-permute-start | bytes 393224 | tf_op jit(solution)/shard_map/ppermute | solution.py:596
  13.5 12.2 %collective-permute-start.4 = (f32[256,128]{1,0:T(8,128)S(1)}, f32[256,128]{1,0:T(8,128)S(1)}, u32[]{:S(2)}, u32[]{:S(2)}) collective-permute-start(f32[256,128]{1,0:T(8,128)S(1)} %add.21), channel_id=1, source_target_pairs={{0,64},{16,80},{32,96},{48,112},{64,0},{80,16},{96,32},{112,48},{1... | collective-permute-start | bytes 393224 | tf_op jit(solution)/shard_map/ppermute | solution.py:596
  13.6 13.6 %collective-permute-start.3 = (f32[256,128]{1,0:T(8,128)S(1)}, f32[256,128]{1,0:T(8,128)S(1)}, u32[]{:S(2)}, u32[]{:S(2)}) collective-permute-start(f32[256,128]{1,0:T(8,128)S(1)} %add.21), channel_id=1, source_target_pairs={{0,96},{16,112},{32,64},{48,80},{64,32},{80,48},{96,0},{112,16},{1... | collective-permute-start | bytes 393224 | tf_op jit(solution)/shard_map/ppermute | solution.py:596
  16.7 10.5 %collective-permute-start.2 = (f32[256,128]{1,0:T(8,128)S(1)}, f32[256,128]{1,0:T(8,128)S(1)}, u32[]{:S(2)}, u32[]{:S(2)}) collective-permute-start(f32[256,128]{1,0:T(8,128)S(1)} %add.21), channel_id=1, source_target_pairs={{0,32},{16,48},{32,0},{48,16},{64,96},{80,112},{96,64},{112,80},{1... | collective-permute-start | bytes 393224 | tf_op jit(solution)/shard_map/ppermute | solution.py:596
  27.2 22.8 %collective-permute-start.7 = (f32[512,1024]{1,0:T(8,128)S(1)}, f32[512,1024]{1,0:T(8,128)S(1)}, u32[]{:S(2)}, u32[]{:S(2)}) collective-permute-start(f32[512,1024]{1,0:T(8,128)S(1)} %get-tuple-element.78), channel_id=1, source_target_pairs={{0,16},{16,0},{32,48},{48,32},{64,80},{80,64},{96,112},{112,96},{1... | collective-permute-start | bytes 6291464 | tf_op jit(solution)/shard_map/ppermute | solution.py:596
  28.6 24.8 %collective-permute-start.8 = (f32[15,128,128]{2,1,0:T(8,128)S(1)}, f32[15,128,128]{2,1,0:T(8,128)S(1)}, u32[]{:S(2)}, u32[]{:S(2)}) collective-permute-start(f32[15,128,128]{2,1,0:T(8,128)S(1)} %get-tuple-element.79), channel_id=1, source_target_pairs={{0,64},{16,80},{32,96},{48,112},{64,0},{80,16},{96,32},{112,48},{1... | collective-permute-start | bytes 2949128 | tf_op jit(solution)/shard_map/ppermute | solution.py:596
  31.6 18.4 %collective-permute-start.5 = (f32[1024,128]{1,0:T(8,128)S(1)}, f32[1024,128]{1,0:T(8,128)S(1)}, u32[]{:S(2)}, u32[]{:S(2)}) collective-permute-start(f32[1024,128]{1,0:T(8,128)S(1)} %get-tuple-element.75), channel_id=1, source_target_pairs={{0,12},{1,13},{2,14},{3,15},{4,8},{5,9},{6,10},{7,11},{16,28},{17,... | collective-permute-start | bytes 1572872 | tf_op jit(solution)/shard_map/ppermute | solution.py:600
  36.2 13.7 %collective-permute-start.6 = (f32[256,128]{1,0:T(8,128)S(1)}, f32[256,128]{1,0:T(8,128)S(1)}, u32[]{:S(2)}, u32[]{:S(2)}) collective-permute-start(f32[256,128]{1,0:T(8,128)S(1)} %add_add_fusion), channel_id=1, source_target_pairs={{0,12},{1,13},{2,14},{3,15},{4,8},{5,9},{6,10},{7,11},{16,28},{17,... | collective-permute-start | bytes 393224 | tf_op jit(solution)/shard_map/ppermute | solution.py:600
  53.4 6.9 %collective-permute-start.11 = (f32[1,512,128]{2,1,0:T(8,128)S(1)}, f32[1,512,128]{2,1,0:T(8,128)S(1)}, u32[]{:S(2)}, u32[]{:S(2)}) collective-permute-start(f32[1,512,128]{2,1,0:T(8,128)S(1)} %get-tuple-element.121), channel_id=1, source_target_pairs={{0,3},{1,2},{2,1},{3,0},{4,7},{5,6},{6,5},{7,4},{8,11},{9,10},{10,... | collective-permute-start | bytes 786440 | tf_op jit(solution)/shard_map/ppermute | solution.py:638
  56.2 9.3 %collective-permute-start.9 = (f32[1,512,128]{2,1,0:T(8,128)S(1)}, f32[1,512,128]{2,1,0:T(8,128)S(1)}, u32[]{:S(2)}, u32[]{:S(2)}) collective-permute-start(f32[1,512,128]{2,1,0:T(8,128)S(1)} %get-tuple-element.122), channel_id=1, source_target_pairs={{0,1},{1,0},{2,3},{3,2},{4,5},{5,4},{6,7},{7,6},{8,9},{9,8},{10,11... | collective-permute-start | bytes 786440 | tf_op jit(solution)/shard_map/ppermute | solution.py:638
  56.4 18.9 %collective-permute-start.15 = (f32[256,1024]{1,0:T(8,128)S(1)}, f32[256,1024]{1,0:T(8,128)S(1)}, u32[]{:S(2)}, u32[]{:S(2)}) collective-permute-start(f32[256,1024]{1,0:T(8,128)S(1)} %slice_select_fusion), channel_id=1, source_target_pairs={{0,32},{16,112},{32,0},{48,80},{64,96},{80,48},{96,64},{112,16},{1... | collective-permute-start | bytes 3145736 | tf_op jit(solution)/shard_map/ppermute | solution.py:625
  58.9 5.5 %collective-permute-start.13 = (f32[1,256,128]{2,1,0:T(8,128)S(1)}, f32[1,256,128]{2,1,0:T(8,128)S(1)}, u32[]{:S(2)}, u32[]{:S(2)}) collective-permute-start(f32[1,256,128]{2,1,0:T(8,128)S(1)} %select_bitcast_fusion), channel_id=1, source_target_pairs={{0,4},{1,5},{2,6},{3,7},{4,0},{5,1},{6,2},{7,3},{8,12},{9,13},{10,... | collective-permute-start | bytes 393224 | tf_op jit(solution)/shard_map/ppermute | solution.py:662
  60.3 11.4 %collective-permute-start.12 = (f32[2,512,128]{2,1,0:T(8,128)S(1)}, f32[2,512,128]{2,1,0:T(8,128)S(1)}, u32[]{:S(2)}, u32[]{:S(2)}) collective-permute-start(f32[2,512,128]{2,1,0:T(8,128)S(1)} %pad_maximum_fusion.6), channel_id=1, source_target_pairs={{0,1},{1,0},{2,3},{3,2},{4,5},{5,4},{6,7},{7,6},{8,9},{9,8},{10,11... | collective-permute-start | bytes 1572872 | tf_op jit(solution)/shard_map/ppermute | solution.py:638
  64.4 7.2 %collective-permute-start.14 = (f32[2,256,128]{2,1,0:T(8,128)S(1)}, f32[2,256,128]{2,1,0:T(8,128)S(1)}, u32[]{:S(2)}, u32[]{:S(2)}) collective-permute-start(f32[2,256,128]{2,1,0:T(8,128)S(1)} %pad_maximum_fusion.8), channel_id=1, source_target_pairs={{0,1},{1,0},{2,3},{3,2},{4,5},{5,4},{6,7},{7,6},{8,9},{9,8},{10,11... | collective-permute-start | bytes 786440 | tf_op jit(solution)/shard_map/ppermute | solution.py:662
  65.6 9.6 %collective-permute-start.10 = (f32[2,512,128]{2,1,0:T(8,128)S(1)}, f32[2,512,128]{2,1,0:T(8,128)S(1)}, u32[]{:S(2)}, u32[]{:S(2)}) collective-permute-start(f32[2,512,128]{2,1,0:T(8,128)S(1)} %pad_maximum_fusion.5), channel_id=1, source_target_pairs={{0,3},{1,2},{2,1},{3,0},{4,7},{5,6},{6,5},{7,4},{8,11},{9,10},{10,... | collective-permute-start | bytes 1572872 | tf_op jit(solution)/shard_map/ppermute | solution.py:638
  75.6 8.4 %collective-permute-start.19 = (f32[128,1024]{1,0:T(8,128)S(1)}, f32[128,1024]{1,0:T(8,128)S(1)}, u32[]{:S(2)}, u32[]{:S(2)}) collective-permute-start(f32[128,1024]{1,0:T(8,128)S(1)} %slice_select_fusion.1), channel_id=1, source_target_pairs={{0,96},{16,48},{32,64},{48,16},{64,32},{80,112},{96,0},{112,80},{1... | collective-permute-start | bytes 1572872 | tf_op jit(solution)/shard_map/ppermute | solution.py:625
  75.7 8.5 %collective-permute-start.18 = (f32[4,256,128]{2,1,0:T(8,128)S(1)}, f32[4,256,128]{2,1,0:T(8,128)S(1)}, u32[]{:S(2)}, u32[]{:S(2)}) collective-permute-start(f32[4,256,128]{2,1,0:T(8,128)S(1)} %pad_maximum_fusion.7), channel_id=1, source_target_pairs={{0,3},{1,2},{2,1},{3,0},{4,7},{5,6},{6,5},{7,4},{8,11},{9,10},{10,... | collective-permute-start | bytes 1572872 | tf_op jit(solution)/shard_map/ppermute | solution.py:662
  76.1 16.7 %collective-permute-start.16 = (f32[4,512,128]{2,1,0:T(8,128)S(1)}, f32[4,512,128]{2,1,0:T(8,128)S(1)}, u32[]{:S(2)}, u32[]{:S(2)}) collective-permute-start(f32[4,512,128]{2,1,0:T(8,128)S(1)} %pad_maximum_fusion.1.refs_0_), channel_id=1, source_target_pairs={{0,4},{1,5},{2,6},{3,7},{4,0},{5,1},{6,2},{7,3},{8,12},{9,13},{10,... | collective-permute-start | bytes 3145736 | tf_op jit(solution)/shard_map/ppermute | solution.py:638
  76.1 20.8 %collective-permute-start.17 = (f32[4,512,128]{2,1,0:T(8,128)S(1)}, f32[4,512,128]{2,1,0:T(8,128)S(1)}, u32[]{:S(2)}, u32[]{:S(2)}) collective-permute-start(f32[4,512,128]{2,1,0:T(8,128)S(1)} %pad_maximum_fusion.2.refs_4_), channel_id=1, source_target_pairs={{0,12},{1,13},{2,14},{3,15},{4,8},{5,9},{6,10},{7,11},{8,4},{9,5},... | collective-permute-start | bytes 3145736 | tf_op jit(solution)/shard_map/ppermute | solution.py:638
  84.2 8.4 %collective-permute-start.20 = (f32[128,1024]{1,0:T(8,128)S(1)}, f32[128,1024]{1,0:T(8,128)S(1)}, u32[]{:S(2)}, u32[]{:S(2)}) collective-permute-start(f32[128,1024]{1,0:T(8,128)S(1)} %select_add_fusion.1), channel_id=1, source_target_pairs={{0,96},{16,48},{32,64},{48,16},{64,32},{80,112},{96,0},{112,80},{1... | collective-permute-start | bytes 1572872 | tf_op jit(solution)/shard_map/ppermute | solution.py:628
  96.8 16.1 %collective-permute-start.24 = (f32[8,256,128]{2,1,0:T(8,128)S(1)}, f32[8,256,128]{2,1,0:T(8,128)S(1)}, u32[]{:S(2)}, u32[]{:S(2)}) collective-permute-start(f32[8,256,128]{2,1,0:T(8,128)S(1)} %pad_maximum_fusion.3.own), channel_id=1, source_target_pairs={{0,16},{16,0},{32,48},{48,32},{64,80},{80,64},{96,112},{112,96},{1... | collective-permute-start | bytes 3145736 | tf_op jit(solution)/shard_map/ppermute | solution.py:596
  99.0 16.0 %collective-permute-start.23 = (f32[256,1024]{1,0:T(8,128)S(1)}, f32[256,1024]{1,0:T(8,128)S(1)}, u32[]{:S(2)}, u32[]{:S(2)}) collective-permute-start(f32[256,1024]{1,0:T(8,128)S(1)} %pad_maximum_fusion.4), channel_id=1, source_target_pairs={{0,32},{16,112},{32,0},{48,80},{64,96},{80,48},{96,64},{112,16},{1... | collective-permute-start | bytes 3145736 | tf_op jit(solution)/shard_map/ppermute | solution.py:628
  100.1 15.4 %collective-permute-start.21 = (f32[4,512,128]{2,1,0:T(8,128)S(1)}, f32[4,512,128]{2,1,0:T(8,128)S(1)}, u32[]{:S(2)}, u32[]{:S(2)}) collective-permute-start(f32[4,512,128]{2,1,0:T(8,128)S(1)} %pad_maximum_fusion.1.refs_0_), channel_id=1, source_target_pairs={{0,12},{1,13},{2,14},{3,15},{4,8},{5,9},{6,10},{7,11},{8,4},{9,5},... | collective-permute-start | bytes 3145736 | tf_op jit(solution)/shard_map/ppermute | solution.py:638
  101.7 13.9 %collective-permute-start.22 = (f32[4,512,128]{2,1,0:T(8,128)S(1)}, f32[4,512,128]{2,1,0:T(8,128)S(1)}, u32[]{:S(2)}, u32[]{:S(2)}) collective-permute-start(f32[4,512,128]{2,1,0:T(8,128)S(1)} %pad_maximum_fusion.2.refs_4_), channel_id=1, source_target_pairs={{0,4},{1,5},{2,6},{3,7},{4,0},{5,1},{6,2},{7,3},{8,12},{9,13},{10,... | collective-permute-start | bytes 3145736 | tf_op jit(solution)/shard_map/ppermute | solution.py:638
  101.7 11.2 %copy-start = (f32[2,512,512]{2,1,0:T(8,128)S(1)}, f32[2,512,512]{2,1,0:T(8,128)}, u32[]{:S(2)}) copy-start(f32[2,512,512]{2,1,0:T(8,128)} %inverses.1) | copy-start | bytes 6291460
  115.6 5.1 %collective-permute-start.27 = (f32[512,1024]{1,0:T(8,128)S(1)}, f32[512,1024]{1,0:T(8,128)S(1)}, u32[]{:S(2)}, u32[]{:S(2)}) collective-permute-start(f32[512,1024]{1,0:T(8,128)S(1)} %pad_maximum_fusion.own), channel_id=1, source_target_pairs={{0,16},{16,0},{32,48},{48,32},{64,80},{80,64},{96,112},{112,96},{1... | collective-permute-start | bytes 6291464 | tf_op jit(solution)/shard_map/ppermute | solution.py:596
  116.8 15.2 %collective-permute-start.25 = (f32[4,512,128]{2,1,0:T(8,128)S(1)}, f32[4,512,128]{2,1,0:T(8,128)S(1)}, u32[]{:S(2)}, u32[]{:S(2)}) collective-permute-start(f32[4,512,128]{2,1,0:T(8,128)S(1)} %collective-permute-done.16.refs_1_), channel_id=1, source_target_pairs={{0,12},{1,13},{2,14},{3,15},{4,8},{5,9},{6,10},{7,11},{8,4},{9,5},... | collective-permute-start | bytes 3145736 | tf_op jit(solution)/shard_map/ppermute | solution.py:638
  118.4 13.9 %collective-permute-start.26 = (f32[4,512,128]{2,1,0:T(8,128)S(1)}, f32[4,512,128]{2,1,0:T(8,128)S(1)}, u32[]{:S(2)}, u32[]{:S(2)}) collective-permute-start(f32[4,512,128]{2,1,0:T(8,128)S(1)} %collective-permute-done.17.refs_5_), channel_id=1, source_target_pairs={{0,4},{1,5},{2,6},{3,7},{4,0},{5,1},{6,2},{7,3},{8,12},{9,13},{10,... | collective-permute-start | bytes 3145736 | tf_op jit(solution)/shard_map/ppermute | solution.py:638
  118.4 38.4 %collective-permute-start.28 = (f32[25,128,128]{2,1,0:T(8,128)S(1)}, f32[25,128,128]{2,1,0:T(8,128)S(1)}, u32[]{:S(2)}, u32[]{:S(2)}) collective-permute-start(f32[25,128,128]{2,1,0:T(8,128)S(1)} %get-tuple-element.115), channel_id=1, source_target_pairs={{0,64},{16,80},{32,96},{48,112},{64,0},{80,16},{96,32},{112,48},{1... | collective-permute-start | bytes 4915208 | tf_op jit(solution)/shard_map/ppermute | solution.py:596

commit v11 on v10

--- a/solution.py
+++ b/solution.py
@@ -399,7 +399,7 @@
         in_specs=[SMEM] + [VMEM] * 5,
         out_specs=[VMEM] * 3,
         compiler_params=params(24),
-        cost_estimate=cost(4 * 6 * PANEL * PANEL * 1024, 14 * MIB),
+        cost_estimate=cost(PANEL * PANEL * 1024, 4 * MIB),
         name="right_factor",
     )(table, own, swapped, *factors, cross)
 
@@ -527,7 +527,7 @@
             scratch_shapes=[pltpu.VMEM((2, PANEL, 1024), BF16)],
         ),
         compiler_params=params(24),
-        cost_estimate=cost(6 * 2048 * 1024 * 1024, 32 * MIB),
+        cost_estimate=cost(2048 * 1024 * 1024, 4 * MIB),
         name="update",
     )(table, in_hbm(front), *blocks[0], *blocks[1], *right, marks.reshape(2, 1024, BLK))
 

time: 162 us -> 161 us (level)
    ppermute x10, waiting for transfers between devices: 8.96 us -> 6.3 us  [swap(): return lax.ppermute(block, axis, [(i, partner(i)) for i in range(count)])]
    ppermute x10, waiting for transfers between devices: 11.7 us -> 14.2 us  [gather_step(): return lax.ppermute(block, ('row', 'col'), route)]
  transfers between devices with their start and end apart: 29 -> 29, of which waited for: 15 -> 15; matrix products, arithmetic and copies ran while one was open for 1% -> 1% of each run, Pallas kernels for 41% -> 40%
where the time goes in v11:
time: 161 us; the launch traced here: 160 us
  Pallas kernels  70.9 us (44%)
  waiting for transfers between devices  45.3 us (28%)
  starting transfers between devices  41.2 us (26%)
  other arithmetic  2.21 us (1%)
    pallas_call x1, Pallas kernels, update(): pl.pallas_call(update_kernel, out_shape=pltpu.HBM((2, 1024, 1024), F32),...  20.1 us
    pallas_call x2, Pallas kernels, pivot_terms(): pl.pallas_call(functools.partial(pivot_kernel, mine_half), out_shape=[jax...  18.1 us
    ppermute x10, starting transfers between devices, swap(): return lax.ppermute(block, axis, [(i, partner(i)) for i in range(count)])  17.8 us
    ppermute x10, waiting for transfers between devices, gather_step(): return lax.ppermute(block, ('row', 'col'), route)  14.2 us
    ppermute x10, starting transfers between devices, gather_step(): return lax.ppermute(block, ('row', 'col'), route)  11.2 us
    pallas_call x1, Pallas kernels, extend(): pl.pallas_call(extend_kernel, out_shape=pltpu.HBM((2, 1024, 1024), F32),...  10.9 us
    ppermute x2, waiting for transfers between devices, double(): came = lax.ppermute(part, 'row', rings[step])  8.22 us
    pallas_call x1, Pallas kernels, right_factor(): pl.pallas_call(factor_kernel, out_shape=[shape, shape, jax.ShapeDtypeStru...  7.86 us
  transfers between devices with their start and end apart: 29, of which 15 were waited for; matrix products, arithmetic and copies ran while one was open for 1% of the time, Pallas kernels for 40%

profile of v11, /device:TPU:1, one launch (start us, length us, event | category | flops | bytes accessed | tf_op | source)
XLA Modules:
  0.0 160.1 jit_solution(4525110978485240365)
XLA Ops:
  0.0 1.8 %cut.1.first = f32[10,128,128]{2,1,0:T(8,128)S(1)} custom-call(s32[2,80]{1,0:T(2,128)} %maps.7, f32[10,2,128,640]{3,2,1,0:T(8,128)} %bitcast.12), custom_call_target="tpu_custom_call" | custom-call | bytes 1048576 | tf_op jit(solution)/shard_map/cut/pallas_call | solution.py:67
  1.9 4.5 %collective-permute-start = (f32[10,128,128]{2,1,0:T(8,128)S(1)}, f32[10,128,128]{2,1,0:T(8,128)S(1)}, u32[]{:S(2)}, u32[]{:S(2)}) collective-permute-start(f32[10,128,128]{2,1,0:T(8,128)S(1)} %cut.1.first), channel_id=1, source_target_pairs={{0,64},{16,80},{32,96},{48,112},{64,0},{80,16},{96,32},{112,48},{1... | collective-permute-start | bytes 1966088 | tf_op jit(solution)/shard_map/ppermute | solution.py:596
  6.4 5.1 %prepare.1 = (f32[15,128,128]{2,1,0:T(8,128)S(1)}, f32[25,128,128]{2,1,0:T(8,128)S(1)}, f32[2048,128]{1,0:T(8,128)S(1)}, f32[256,128]{1,0:T(8,128)S(1)}, f32[256,128]{1,0:T(8,128)S(1)}, /*index=5*/s32[64]{0:T(128)S(1)}) custom-call(s32[2,80]{1,0:T(2,128)} %maps.7, s32[8,128]{1,0:T(8,128)} %bitcast.18, f32[2048,1024]{1,0:T(8,128)} %front.5, ...), custom_call_target="tpu_custom_call" | custom-call | bytes 9437184 | tf_op jit(solution)/shard_map/prepare/pallas_call | solution.py:172
  11.5 1.0 collective-permute-start.1
  12.5 1.0 collective-permute-done.1
  13.6 3.1 %collective-permute-start.3 = (f32[256,128]{1,0:T(8,128)S(1)}, f32[256,128]{1,0:T(8,128)S(1)}, u32[]{:S(2)}, u32[]{:S(2)}) collective-permute-start(f32[256,128]{1,0:T(8,128)S(1)} %add.21), channel_id=1, source_target_pairs={{0,96},{16,112},{32,64},{48,80},{64,32},{80,48},{96,0},{112,16},{1... | collective-permute-start | bytes 393224 | tf_op jit(solution)/shard_map/ppermute | solution.py:596
  16.7 9.1 %pivot_terms_other.1 = (f32[512,1024]{1,0:T(8,128)S(1)}, f32[2048,128]{1,0:T(8,128)S(1)}, s32[513]{0:T(1024)S(1)}) custom-call(s32[2,80]{1,0:T(2,128)} %maps.7, s32[1024]{0:T(1024)} %pivots.1, f32[2048,1024]{1,0:T(8,128)} %front.5, f32[2560,640]{1,0:T(8,128)} %children.3), custom_call_target="tpu_custom_call" | custom-call | bytes 25165824 | tf_op jit(solution)/shard_map/pivot_terms_other/pallas_call | solution.py:264
  25.8 1.4 collective-permute-done.3
  27.2 1.3 collective-permute-start.7
  28.6 2.2 %collective-permute-start.8 = (f32[15,128,128]{2,1,0:T(8,128)S(1)}, f32[15,128,128]{2,1,0:T(8,128)S(1)}, u32[]{:S(2)}, u32[]{:S(2)}) collective-permute-start(f32[15,128,128]{2,1,0:T(8,128)S(1)} %get-tuple-element.79), channel_id=1, source_target_pairs={{0,64},{16,80},{32,96},{48,112},{64,0},{80,16},{96,32},{112,48},{1... | collective-permute-start | bytes 2949128 | tf_op jit(solution)/shard_map/ppermute | solution.py:596
  30.8 0.8 whole_panel.1
  31.6 4.5 %collective-permute-start.5 = (f32[1024,128]{1,0:T(8,128)S(1)}, f32[1024,128]{1,0:T(8,128)S(1)}, u32[]{:S(2)}, u32[]{:S(2)}) collective-permute-start(f32[1024,128]{1,0:T(8,128)S(1)} %get-tuple-element.75), channel_id=1, source_target_pairs={{0,12},{1,13},{2,14},{3,15},{4,8},{5,9},{6,10},{7,11},{16,28},{17,... | collective-permute-start | bytes 1572872 | tf_op jit(solution)/shard_map/ppermute | solution.py:600
  36.1 1.3 collective-permute-start.6
  37.4 9.0 %pivot_terms_mine.1 = (f32[512,1024]{1,0:T(8,128)S(1)}, f32[2048,128]{1,0:T(8,128)S(1)}, s32[513]{0:T(1024)S(1)}) custom-call(s32[2,80]{1,0:T(2,128)} %maps.7, s32[1024]{0:T(1024)} %pivots.1, f32[2048,1024]{1,0:T(8,128)} %front.5, f32[2560,640]{1,0:T(8,128)} %children.3, f32[2048,128]{1,0:T(8,128)S(1)} %get-tuple-element.69.refs_0_), custom_call_target="tpu_custom_call" | custom-call | bytes 25165824 | tf_op jit(solution)/shard_map/pivot_terms_mine/pallas_call | solution.py:264
  46.4 3.4 %collective-permute-done.6 = f32[256,128]{1,0:T(8,128)S(1)} collective-permute-done((f32[256,128]{1,0:T(8,128)S(1)}, f32[256,128]{1,0:T(8,128)S(1)}, u32[]{:S(2)}, u32[]{:S(2)}) %collective-permute-start.6) | collective-permute-done | bytes 131104 | tf_op jit(solution)/shard_map/ppermute | solution.py:600
  49.9 0.4 add.25
  50.3 3.1 %collective-permute-done.8.refs_4_.refs_5_.refs_6_.refs_7_ = f32[15,128,128]{2,1,0:T(8,128)S(1)} collective-permute-done((f32[15,128,128]{2,1,0:T(8,128)S(1)}, f32[15,128,128]{2,1,0:T(8,128)S(1)}, u32[]{:S(2)}, u32[]{:S(2)}) %collective-permute-start.8) | collective-permute-done | bytes 983072 | tf_op jit(solution)/shard_map/ppermute | solution.py:596
  53.4 2.8 %collective-permute-start.11 = (f32[1,512,128]{2,1,0:T(8,128)S(1)}, f32[1,512,128]{2,1,0:T(8,128)S(1)}, u32[]{:S(2)}, u32[]{:S(2)}) collective-permute-start(f32[1,512,128]{2,1,0:T(8,128)S(1)} %get-tuple-element.121), channel_id=1, source_target_pairs={{0,3},{1,2},{2,1},{3,0},{4,7},{5,6},{6,5},{7,4},{8,11},{9,10},{10,... | collective-permute-start | bytes 786440 | tf_op jit(solution)/shard_map/ppermute | solution.py:638
  56.4 2.4 %collective-permute-start.15 = (f32[256,1024]{1,0:T(8,128)S(1)}, f32[256,1024]{1,0:T(8,128)S(1)}, u32[]{:S(2)}, u32[]{:S(2)}) collective-permute-start(f32[256,1024]{1,0:T(8,128)S(1)} %slice_select_fusion), channel_id=1, source_target_pairs={{0,32},{16,112},{32,0},{48,80},{64,96},{80,48},{96,64},{112,16},{1... | collective-permute-start | bytes 3145736 | tf_op jit(solution)/shard_map/ppermute | solution.py:625
  58.8 1.2 collective-permute-start.13
  60.3 1.3 collective-permute-start.12
  61.6 2.7 %collective-permute-done.13 = f32[1,256,128]{2,1,0:T(8,128)S(1)} collective-permute-done((f32[1,256,128]{2,1,0:T(8,128)S(1)}, f32[1,256,128]{2,1,0:T(8,128)S(1)}, u32[]{:S(2)}, u32[]{:S(2)}) %collective-permute-start.13) | collective-permute-done | bytes 131104 | tf_op jit(solution)/shard_map/ppermute | solution.py:662
  64.4 1.1 collective-permute-start.14
  65.6 2.1 %collective-permute-start.10 = (f32[2,512,128]{2,1,0:T(8,128)S(1)}, f32[2,512,128]{2,1,0:T(8,128)S(1)}, u32[]{:S(2)}, u32[]{:S(2)}) collective-permute-start(f32[2,512,128]{2,1,0:T(8,128)S(1)} %pad_maximum_fusion.5), channel_id=1, source_target_pairs={{0,3},{1,2},{2,1},{3,0},{4,7},{5,6},{6,5},{7,4},{8,11},{9,10},{10,... | collective-permute-start | bytes 1572872 | tf_op jit(solution)/shard_map/ppermute | solution.py:638
  67.7 4.0 %collective-permute-done.14 = f32[2,256,128]{2,1,0:T(8,128)S(1)} collective-permute-done((f32[2,256,128]{2,1,0:T(8,128)S(1)}, f32[2,256,128]{2,1,0:T(8,128)S(1)}, u32[]{:S(2)}, u32[]{:S(2)}) %collective-permute-start.14) | collective-permute-done | bytes 262176 | tf_op jit(solution)/shard_map/ppermute | solution.py:662
  71.8 3.4 %collective-permute-done.10 = f32[2,512,128]{2,1,0:T(8,128)S(1)} collective-permute-done((f32[2,512,128]{2,1,0:T(8,128)S(1)}, f32[2,512,128]{2,1,0:T(8,128)S(1)}, u32[]{:S(2)}, u32[]{:S(2)}) %collective-permute-start.10) | collective-permute-done | bytes 524320 | tf_op jit(solution)/shard_map/ppermute | solution.py:638
  75.3 0.3 select_add_fusion
  75.7 0.3 collective-permute-start.18
  76.0 1.6 %collective-permute-start.17 = (f32[4,512,128]{2,1,0:T(8,128)S(1)}, f32[4,512,128]{2,1,0:T(8,128)S(1)}, u32[]{:S(2)}, u32[]{:S(2)}) collective-permute-start(f32[4,512,128]{2,1,0:T(8,128)S(1)} %pad_maximum_fusion.2.refs_4_), channel_id=1, source_target_pairs={{0,12},{1,13},{2,14},{3,15},{4,8},{5,9},{6,10},{7,11},{8,4},{9,5},... | collective-permute-start | bytes 3145736 | tf_op jit(solution)/shard_map/ppermute | solution.py:638
  77.6 6.4 %collective-permute-done.19 = f32[128,1024]{1,0:T(8,128)S(1)} collective-permute-done((f32[128,1024]{1,0:T(8,128)S(1)}, f32[128,1024]{1,0:T(8,128)S(1)}, u32[]{:S(2)}, u32[]{:S(2)}) %collective-permute-start.19) | collective-permute-done | bytes 524320 | tf_op jit(solution)/shard_map/ppermute | solution.py:625
  84.3 8.2 %collective-permute-done.20 = f32[128,1024]{1,0:T(8,128)S(1)} collective-permute-done((f32[128,1024]{1,0:T(8,128)S(1)}, f32[128,1024]{1,0:T(8,128)S(1)}, u32[]{:S(2)}, u32[]{:S(2)}) %collective-permute-start.20) | collective-permute-done | bytes 524320 | tf_op jit(solution)/shard_map/ppermute | solution.py:628
  92.7 4.1 %collective-permute-done.17.refs_5_ = f32[4,512,128]{2,1,0:T(8,128)S(1)} collective-permute-done((f32[4,512,128]{2,1,0:T(8,128)S(1)}, f32[4,512,128]{2,1,0:T(8,128)S(1)}, u32[]{:S(2)}, u32[]{:S(2)}) %collective-permute-start.17) | collective-permute-done | bytes 1048608 | tf_op jit(solution)/shard_map/ppermute | solution.py:638
  96.8 2.2 %collective-permute-start.24 = (f32[8,256,128]{2,1,0:T(8,128)S(1)}, f32[8,256,128]{2,1,0:T(8,128)S(1)}, u32[]{:S(2)}, u32[]{:S(2)}) collective-permute-start(f32[8,256,128]{2,1,0:T(8,128)S(1)} %pad_maximum_fusion.3.own), channel_id=1, source_target_pairs={{0,16},{16,0},{32,48},{48,32},{64,80},{80,64},{96,112},{112,96},{1... | collective-permute-start | bytes 3145736 | tf_op jit(solution)/shard_map/ppermute | solution.py:596
  99.0 1.1 collective-permute-start.23
  100.1 1.6 %collective-permute-start.21 = (f32[4,512,128]{2,1,0:T(8,128)S(1)}, f32[4,512,128]{2,1,0:T(8,128)S(1)}, u32[]{:S(2)}, u32[]{:S(2)}) collective-permute-start(f32[4,512,128]{2,1,0:T(8,128)S(1)} %pad_maximum_fusion.1.refs_0_), channel_id=1, source_target_pairs={{0,12},{1,13},{2,14},{3,15},{4,8},{5,9},{6,10},{7,11},{8,4},{9,5},... | collective-permute-start | bytes 3145736 | tf_op jit(solution)/shard_map/ppermute | solution.py:638
  101.7 10.9 %extend.1.front = f32[2,1024,1024]{2,1,0:T(8,128)} custom-call(s32[64]{0:T(128)S(1)} %get-tuple-element.62.table, f32[2,1024,1024]{2,1,0:T(8,128)} %bitcast.16, f32[10,2,128,640]{3,2,1,0:T(8,128)} %bitcast.14, f32[10,2,128,640]{3,2,1,0:T(8,128)} %bitcast.15, f32[10,128,128]{2,1,0:T(8,128)S(1)} %collective-permute-done.got.refs_2_.refs_3_, ...), custom_call_target="tpu_custom_call" | custom-call | bytes 1048576 | tf_op jit(solution)/shard_map/extend/pallas_call | solution.py:452
  112.6 2.0 %corners.1 = (bf16[3,512,512]{2,1,0:T(8,128)(2,1)S(1)}, bf16[3,512,512]{2,1,0:T(8,128)(2,1)S(1)}, f32[512,512]{1,0:T(8,128)S(1)}) custom-call(s32[64]{0:T(128)S(1)} %get-tuple-element.62.table, f32[8,256,128]{2,1,0:T(8,128)S(1)} %pad_maximum_fusion.3.own, f32[8,256,128]{2,1,0:T(8,128)S(1)} %collective-permute-done.24.swapped, f32[2,512,512]{2,1,0:T(8,128)S(1)} %copy-done), custom_call_target="tpu_custom_call" | custom-call | flops 805306368 | bytes 8388608 | tf_op jit(solution)/shard_map/corners/pallas_call | solution.py:342
  114.6 0.3 broadcast_select_fusion.1
  115.2 0.5 collective-permute-done.22.refs_6_
  115.6 1.1 collective-permute-start.27
  116.7 2.3 %collective-permute-start.28 = (f32[25,128,128]{2,1,0:T(8,128)S(1)}, f32[25,128,128]{2,1,0:T(8,128)S(1)}, u32[]{:S(2)}, u32[]{:S(2)}) collective-permute-start(f32[25,128,128]{2,1,0:T(8,128)S(1)} %get-tuple-element.115), channel_id=1, source_target_pairs={{0,64},{16,80},{32,96},{48,112},{64,0},{80,16},{96,32},{112,48},{1... | collective-permute-start | bytes 4915208 | tf_op jit(solution)/shard_map/ppermute | solution.py:596
  119.0 1.7 %collective-permute-start.25 = (f32[4,512,128]{2,1,0:T(8,128)S(1)}, f32[4,512,128]{2,1,0:T(8,128)S(1)}, u32[]{:S(2)}, u32[]{:S(2)}) collective-permute-start(f32[4,512,128]{2,1,0:T(8,128)S(1)} %collective-permute-done.16.refs_1_), channel_id=1, source_target_pairs={{0,12},{1,13},{2,14},{3,15},{4,8},{5,9},{6,10},{7,11},{8,4},{9,5},... | collective-permute-start | bytes 3145736 | tf_op jit(solution)/shard_map/ppermute | solution.py:638
  120.7 7.9 %right_factor.1 = (bf16[1024,1024]{1,0:T(8,128)(2,1)S(1)}, bf16[1024,1024]{1,0:T(8,128)(2,1)S(1)}, f32[512,1024]{1,0:T(8,128)S(1)}) custom-call(s32[64]{0:T(128)S(1)} %get-tuple-element.62.table, f32[512,1024]{1,0:T(8,128)S(1)} %pad_maximum_fusion.own, f32[512,1024]{1,0:T(8,128)S(1)} %collective-permute-done.27.swapped, ...), custom_call_target="tpu_custom_call" | custom-call | flops 268435456 | bytes 4194304 | tf_op jit(solution)/shard_map/right_factor/pallas_call | solution.py:396
  128.6 5.6 %collective-permute-done.25.refs_3_ = f32[4,512,128]{2,1,0:T(8,128)S(1)} collective-permute-done((f32[4,512,128]{2,1,0:T(8,128)S(1)}, f32[4,512,128]{2,1,0:T(8,128)S(1)}, u32[]{:S(2)}, u32[]{:S(2)}) %collective-permute-start.25) | collective-permute-done | bytes 1048608 | tf_op jit(solution)/shard_map/ppermute | solution.py:638
  134.1 0.5 collective-permute-done.26.refs_7_
  134.7 20.1 %update.1 = f32[2,1024,1024]{2,1,0:T(8,128)} custom-call(s32[64]{0:T(128)S(1)} %get-tuple-element.62.table, f32[2,1024,1024]{2,1,0:T(8,128)} %extend.1.front, f32[4,512,128]{2,1,0:T(8,128)S(1)} %pad_maximum_fusion.1.refs_0_, f32[4,512,128]{2,1,0:T(8,128)S(1)} %collective-permute-done.16.refs_1_, f32[4,512,128]{2,1,0:T(8,128)S(1)} %collective-permute-done.21.refs_2_, ...), custom_call_target="tpu_custom_call" | custom-call | flops 2147483648 | bytes 4194304 | tf_op jit(solution)/shard_map/update/pallas_call | solution.py:515
  154.8 0.9 collective-permute-done.28.got
  155.6 4.3 %finish.1 = f32[2048,1024]{1,0:T(8,128)} custom-call(s32[64]{0:T(128)S(1)} %get-tuple-element.62.table, s32[513]{0:T(1024)S(1)} %get-tuple-element.63.list_other, s32[513]{0:T(1024)S(1)} %get-tuple-element.70.list_mine, f32[2048,1024]{1,0:T(8,128)} %bitcast.17, f32[25,128,128]{2,1,0:T(8,128)S(1)} %collective-permute-done.28.got, ...), custom_call_target="tpu_custom_call", output_to_operand_aliasing={{}: (3, {})} | custom-call | bytes 8388608 | tf_op jit(solution)/shard_map/finish/pallas_call | solution.py:576
  (43 shorter events, 1.9 us)
Async XLA Ops:
  1.9 25.4 %collective-permute-start = (f32[10,128,128]{2,1,0:T(8,128)S(1)}, f32[10,128,128]{2,1,0:T(8,128)S(1)}, u32[]{:S(2)}, u32[]{:S(2)}) collective-permute-start(f32[10,128,128]{2,1,0:T(8,128)S(1)} %cut.1.first), channel_id=1, source_target_pairs={{0,64},{16,80},{32,96},{48,112},{64,0},{80,16},{96,32},{112,48},{1... | collective-permute-start | bytes 1966088 | tf_op jit(solution)/shard_map/ppermute | solution.py:596
  11.5 2.0 %collective-permute-start.1 = (f32[256,128]{1,0:T(8,128)S(1)}, f32[256,128]{1,0:T(8,128)S(1)}, u32[]{:S(2)}, u32[]{:S(2)}) collective-permute-start(f32[256,128]{1,0:T(8,128)S(1)} %get-tuple-element.68), channel_id=1, source_target_pairs={{0,16},{16,0},{32,48},{48,32},{64,80},{80,64},{96,112},{112,96},{1... | collective-permute-start | bytes 393224 | tf_op jit(solution)/shard_map/ppermute | solution.py:596
  13.5 12.3 %collective-permute-start.4 = (f32[256,128]{1,0:T(8,128)S(1)}, f32[256,128]{1,0:T(8,128)S(1)}, u32[]{:S(2)}, u32[]{:S(2)}) collective-permute-start(f32[256,128]{1,0:T(8,128)S(1)} %add.21), channel_id=1, source_target_pairs={{0,64},{16,80},{32,96},{48,112},{64,0},{80,16},{96,32},{112,48},{1... | collective-permute-start | bytes 393224 | tf_op jit(solution)/shard_map/ppermute | solution.py:596
  13.6 13.6 %collective-permute-start.3 = (f32[256,128]{1,0:T(8,128)S(1)}, f32[256,128]{1,0:T(8,128)S(1)}, u32[]{:S(2)}, u32[]{:S(2)}) collective-permute-start(f32[256,128]{1,0:T(8,128)S(1)} %add.21), channel_id=1, source_target_pairs={{0,96},{16,112},{32,64},{48,80},{64,32},{80,48},{96,0},{112,16},{1... | collective-permute-start | bytes 393224 | tf_op jit(solution)/shard_map/ppermute | solution.py:596
  16.7 10.5 %collective-permute-start.2 = (f32[256,128]{1,0:T(8,128)S(1)}, f32[256,128]{1,0:T(8,128)S(1)}, u32[]{:S(2)}, u32[]{:S(2)}) collective-permute-start(f32[256,128]{1,0:T(8,128)S(1)} %add.21), channel_id=1, source_target_pairs={{0,32},{16,48},{32,0},{48,16},{64,96},{80,112},{96,64},{112,80},{1... | collective-permute-start | bytes 393224 | tf_op jit(solution)/shard_map/ppermute | solution.py:596
  27.2 22.6 %collective-permute-start.7 = (f32[512,1024]{1,0:T(8,128)S(1)}, f32[512,1024]{1,0:T(8,128)S(1)}, u32[]{:S(2)}, u32[]{:S(2)}) collective-permute-start(f32[512,1024]{1,0:T(8,128)S(1)} %get-tuple-element.78), channel_id=1, source_target_pairs={{0,16},{16,0},{32,48},{48,32},{64,80},{80,64},{96,112},{112,96},{1... | collective-permute-start | bytes 6291464 | tf_op jit(solution)/shard_map/ppermute | solution.py:596
  28.6 24.8 %collective-permute-start.8 = (f32[15,128,128]{2,1,0:T(8,128)S(1)}, f32[15,128,128]{2,1,0:T(8,128)S(1)}, u32[]{:S(2)}, u32[]{:S(2)}) collective-permute-start(f32[15,128,128]{2,1,0:T(8,128)S(1)} %get-tuple-element.79), channel_id=1, source_target_pairs={{0,64},{16,80},{32,96},{48,112},{64,0},{80,16},{96,32},{112,48},{1... | collective-permute-start | bytes 2949128 | tf_op jit(solution)/shard_map/ppermute | solution.py:596
  31.6 18.2 %collective-permute-start.5 = (f32[1024,128]{1,0:T(8,128)S(1)}, f32[1024,128]{1,0:T(8,128)S(1)}, u32[]{:S(2)}, u32[]{:S(2)}) collective-permute-start(f32[1024,128]{1,0:T(8,128)S(1)} %get-tuple-element.75), channel_id=1, source_target_pairs={{0,12},{1,13},{2,14},{3,15},{4,8},{5,9},{6,10},{7,11},{16,28},{17,... | collective-permute-start | bytes 1572872 | tf_op jit(solution)/shard_map/ppermute | solution.py:600
  36.1 13.7 %collective-permute-start.6 = (f32[256,128]{1,0:T(8,128)S(1)}, f32[256,128]{1,0:T(8,128)S(1)}, u32[]{:S(2)}, u32[]{:S(2)}) collective-permute-start(f32[256,128]{1,0:T(8,128)S(1)} %add_add_fusion), channel_id=1, source_target_pairs={{0,12},{1,13},{2,14},{3,15},{4,8},{5,9},{6,10},{7,11},{16,28},{17,... | collective-permute-start | bytes 393224 | tf_op jit(solution)/shard_map/ppermute | solution.py:600
  53.4 6.9 %collective-permute-start.11 = (f32[1,512,128]{2,1,0:T(8,128)S(1)}, f32[1,512,128]{2,1,0:T(8,128)S(1)}, u32[]{:S(2)}, u32[]{:S(2)}) collective-permute-start(f32[1,512,128]{2,1,0:T(8,128)S(1)} %get-tuple-element.121), channel_id=1, source_target_pairs={{0,3},{1,2},{2,1},{3,0},{4,7},{5,6},{6,5},{7,4},{8,11},{9,10},{10,... | collective-permute-start | bytes 786440 | tf_op jit(solution)/shard_map/ppermute | solution.py:638
  56.2 9.3 %collective-permute-start.9 = (f32[1,512,128]{2,1,0:T(8,128)S(1)}, f32[1,512,128]{2,1,0:T(8,128)S(1)}, u32[]{:S(2)}, u32[]{:S(2)}) collective-permute-start(f32[1,512,128]{2,1,0:T(8,128)S(1)} %get-tuple-element.122), channel_id=1, source_target_pairs={{0,1},{1,0},{2,3},{3,2},{4,5},{5,4},{6,7},{7,6},{8,9},{9,8},{10,11... | collective-permute-start | bytes 786440 | tf_op jit(solution)/shard_map/ppermute | solution.py:638
  56.4 18.9 %collective-permute-start.15 = (f32[256,1024]{1,0:T(8,128)S(1)}, f32[256,1024]{1,0:T(8,128)S(1)}, u32[]{:S(2)}, u32[]{:S(2)}) collective-permute-start(f32[256,1024]{1,0:T(8,128)S(1)} %slice_select_fusion), channel_id=1, source_target_pairs={{0,32},{16,112},{32,0},{48,80},{64,96},{80,48},{96,64},{112,16},{1... | collective-permute-start | bytes 3145736 | tf_op jit(solution)/shard_map/ppermute | solution.py:625
  58.8 5.5 %collective-permute-start.13 = (f32[1,256,128]{2,1,0:T(8,128)S(1)}, f32[1,256,128]{2,1,0:T(8,128)S(1)}, u32[]{:S(2)}, u32[]{:S(2)}) collective-permute-start(f32[1,256,128]{2,1,0:T(8,128)S(1)} %select_bitcast_fusion), channel_id=1, source_target_pairs={{0,4},{1,5},{2,6},{3,7},{4,0},{5,1},{6,2},{7,3},{8,12},{9,13},{10,... | collective-permute-start | bytes 393224 | tf_op jit(solution)/shard_map/ppermute | solution.py:662
  60.3 11.4 %collective-permute-start.12 = (f32[2,512,128]{2,1,0:T(8,128)S(1)}, f32[2,512,128]{2,1,0:T(8,128)S(1)}, u32[]{:S(2)}, u32[]{:S(2)}) collective-permute-start(f32[2,512,128]{2,1,0:T(8,128)S(1)} %pad_maximum_fusion.6), channel_id=1, source_target_pairs={{0,1},{1,0},{2,3},{3,2},{4,5},{5,4},{6,7},{7,6},{8,9},{9,8},{10,11... | collective-permute-start | bytes 1572872 | tf_op jit(solution)/shard_map/ppermute | solution.py:638
  64.4 7.3 %collective-permute-start.14 = (f32[2,256,128]{2,1,0:T(8,128)S(1)}, f32[2,256,128]{2,1,0:T(8,128)S(1)}, u32[]{:S(2)}, u32[]{:S(2)}) collective-permute-start(f32[2,256,128]{2,1,0:T(8,128)S(1)} %pad_maximum_fusion.8), channel_id=1, source_target_pairs={{0,1},{1,0},{2,3},{3,2},{4,5},{5,4},{6,7},{7,6},{8,9},{9,8},{10,11... | collective-permute-start | bytes 786440 | tf_op jit(solution)/shard_map/ppermute | solution.py:662
  65.6 9.6 %collective-permute-start.10 = (f32[2,512,128]{2,1,0:T(8,128)S(1)}, f32[2,512,128]{2,1,0:T(8,128)S(1)}, u32[]{:S(2)}, u32[]{:S(2)}) collective-permute-start(f32[2,512,128]{2,1,0:T(8,128)S(1)} %pad_maximum_fusion.5), channel_id=1, source_target_pairs={{0,3},{1,2},{2,1},{3,0},{4,7},{5,6},{6,5},{7,4},{8,11},{9,10},{10,... | collective-permute-start | bytes 1572872 | tf_op jit(solution)/shard_map/ppermute | solution.py:638
  75.6 8.4 %collective-permute-start.19 = (f32[128,1024]{1,0:T(8,128)S(1)}, f32[128,1024]{1,0:T(8,128)S(1)}, u32[]{:S(2)}, u32[]{:S(2)}) collective-permute-start(f32[128,1024]{1,0:T(8,128)S(1)} %slice_select_fusion.1), channel_id=1, source_target_pairs={{0,96},{16,48},{32,64},{48,16},{64,32},{80,112},{96,0},{112,80},{1... | collective-permute-start | bytes 1572872 | tf_op jit(solution)/shard_map/ppermute | solution.py:625
  75.7 8.5 %collective-permute-start.18 = (f32[4,256,128]{2,1,0:T(8,128)S(1)}, f32[4,256,128]{2,1,0:T(8,128)S(1)}, u32[]{:S(2)}, u32[]{:S(2)}) collective-permute-start(f32[4,256,128]{2,1,0:T(8,128)S(1)} %pad_maximum_fusion.7), channel_id=1, source_target_pairs={{0,3},{1,2},{2,1},{3,0},{4,7},{5,6},{6,5},{7,4},{8,11},{9,10},{10,... | collective-permute-start | bytes 1572872 | tf_op jit(solution)/shard_map/ppermute | solution.py:662
  76.0 16.7 %collective-permute-start.16 = (f32[4,512,128]{2,1,0:T(8,128)S(1)}, f32[4,512,128]{2,1,0:T(8,128)S(1)}, u32[]{:S(2)}, u32[]{:S(2)}) collective-permute-start(f32[4,512,128]{2,1,0:T(8,128)S(1)} %pad_maximum_fusion.1.refs_0_), channel_id=1, source_target_pairs={{0,4},{1,5},{2,6},{3,7},{4,0},{5,1},{6,2},{7,3},{8,12},{9,13},{10,... | collective-permute-start | bytes 3145736 | tf_op jit(solution)/shard_map/ppermute | solution.py:638
  76.0 20.8 %collective-permute-start.17 = (f32[4,512,128]{2,1,0:T(8,128)S(1)}, f32[4,512,128]{2,1,0:T(8,128)S(1)}, u32[]{:S(2)}, u32[]{:S(2)}) collective-permute-start(f32[4,512,128]{2,1,0:T(8,128)S(1)} %pad_maximum_fusion.2.refs_4_), channel_id=1, source_target_pairs={{0,12},{1,13},{2,14},{3,15},{4,8},{5,9},{6,10},{7,11},{8,4},{9,5},... | collective-permute-start | bytes 3145736 | tf_op jit(solution)/shard_map/ppermute | solution.py:638
  84.1 8.4 %collective-permute-start.20 = (f32[128,1024]{1,0:T(8,128)S(1)}, f32[128,1024]{1,0:T(8,128)S(1)}, u32[]{:S(2)}, u32[]{:S(2)}) collective-permute-start(f32[128,1024]{1,0:T(8,128)S(1)} %select_add_fusion.1), channel_id=1, source_target_pairs={{0,96},{16,48},{32,64},{48,16},{64,32},{80,112},{96,0},{112,80},{1... | collective-permute-start | bytes 1572872 | tf_op jit(solution)/shard_map/ppermute | solution.py:628
  96.8 15.8 %collective-permute-start.24 = (f32[8,256,128]{2,1,0:T(8,128)S(1)}, f32[8,256,128]{2,1,0:T(8,128)S(1)}, u32[]{:S(2)}, u32[]{:S(2)}) collective-permute-start(f32[8,256,128]{2,1,0:T(8,128)S(1)} %pad_maximum_fusion.3.own), channel_id=1, source_target_pairs={{0,16},{16,0},{32,48},{48,32},{64,80},{80,64},{96,112},{112,96},{1... | collective-permute-start | bytes 3145736 | tf_op jit(solution)/shard_map/ppermute | solution.py:596
  99.0 15.6 %collective-permute-start.23 = (f32[256,1024]{1,0:T(8,128)S(1)}, f32[256,1024]{1,0:T(8,128)S(1)}, u32[]{:S(2)}, u32[]{:S(2)}) collective-permute-start(f32[256,1024]{1,0:T(8,128)S(1)} %pad_maximum_fusion.4), channel_id=1, source_target_pairs={{0,32},{16,112},{32,0},{48,80},{64,96},{80,48},{96,64},{112,16},{1... | collective-permute-start | bytes 3145736 | tf_op jit(solution)/shard_map/ppermute | solution.py:628
  100.1 15.1 %collective-permute-start.21 = (f32[4,512,128]{2,1,0:T(8,128)S(1)}, f32[4,512,128]{2,1,0:T(8,128)S(1)}, u32[]{:S(2)}, u32[]{:S(2)}) collective-permute-start(f32[4,512,128]{2,1,0:T(8,128)S(1)} %pad_maximum_fusion.1.refs_0_), channel_id=1, source_target_pairs={{0,12},{1,13},{2,14},{3,15},{4,8},{5,9},{6,10},{7,11},{8,4},{9,5},... | collective-permute-start | bytes 3145736 | tf_op jit(solution)/shard_map/ppermute | solution.py:638
  101.7 13.9 %collective-permute-start.22 = (f32[4,512,128]{2,1,0:T(8,128)S(1)}, f32[4,512,128]{2,1,0:T(8,128)S(1)}, u32[]{:S(2)}, u32[]{:S(2)}) collective-permute-start(f32[4,512,128]{2,1,0:T(8,128)S(1)} %pad_maximum_fusion.2.refs_4_), channel_id=1, source_target_pairs={{0,4},{1,5},{2,6},{3,7},{4,0},{5,1},{6,2},{7,3},{8,12},{9,13},{10,... | collective-permute-start | bytes 3145736 | tf_op jit(solution)/shard_map/ppermute | solution.py:638
  101.7 10.9 %copy-start = (f32[2,512,512]{2,1,0:T(8,128)S(1)}, f32[2,512,512]{2,1,0:T(8,128)}, u32[]{:S(2)}) copy-start(f32[2,512,512]{2,1,0:T(8,128)} %inverses.1) | copy-start | bytes 6291460
  115.6 5.1 %collective-permute-start.27 = (f32[512,1024]{1,0:T(8,128)S(1)}, f32[512,1024]{1,0:T(8,128)S(1)}, u32[]{:S(2)}, u32[]{:S(2)}) collective-permute-start(f32[512,1024]{1,0:T(8,128)S(1)} %pad_maximum_fusion.own), channel_id=1, source_target_pairs={{0,16},{16,0},{32,48},{48,32},{64,80},{80,64},{96,112},{112,96},{1... | collective-permute-start | bytes 6291464 | tf_op jit(solution)/shard_map/ppermute | solution.py:596
  116.7 38.9 %collective-permute-start.28 = (f32[25,128,128]{2,1,0:T(8,128)S(1)}, f32[25,128,128]{2,1,0:T(8,128)S(1)}, u32[]{:S(2)}, u32[]{:S(2)}) collective-permute-start(f32[25,128,128]{2,1,0:T(8,128)S(1)} %get-tuple-element.115), channel_id=1, source_target_pairs={{0,64},{16,80},{32,96},{48,112},{64,0},{80,16},{96,32},{112,48},{1... | collective-permute-start | bytes 4915208 | tf_op jit(solution)/shard_map/ppermute | solution.py:596
  119.0 15.2 %collective-permute-start.25 = (f32[4,512,128]{2,1,0:T(8,128)S(1)}, f32[4,512,128]{2,1,0:T(8,128)S(1)}, u32[]{:S(2)}, u32[]{:S(2)}) collective-permute-start(f32[4,512,128]{2,1,0:T(8,128)S(1)} %collective-permute-done.16.refs_1_), channel_id=1, source_target_pairs={{0,12},{1,13},{2,14},{3,15},{4,8},{5,9},{6,10},{7,11},{8,4},{9,5},... | collective-permute-start | bytes 3145736 | tf_op jit(solution)/shard_map/ppermute | solution.py:638
  120.7 13.9 %collective-permute-start.26 = (f32[4,512,128]{2,1,0:T(8,128)S(1)}, f32[4,512,128]{2,1,0:T(8,128)S(1)}, u32[]{:S(2)}, u32[]{:S(2)}) collective-permute-start(f32[4,512,128]{2,1,0:T(8,128)S(1)} %collective-permute-done.17.refs_5_), channel_id=1, source_target_pairs={{0,4},{1,5},{2,6},{3,7},{4,0},{5,1},{6,2},{7,3},{8,12},{9,13},{10,... | collective-permute-start | bytes 3145736 | tf_op jit(solution)/shard_map/ppermute | solution.py:638

commit v12 on v11

--- a/solution.py
+++ b/solution.py
@@ -652,7 +652,8 @@
     got_a = by_row(rest_a, 4)
     own_rows, marks, list_mine = pivot_terms(child_maps, pivots, front, children, marks)
     total = own_rows + by_row(away_rows, 1)
-    mine, corner, total, got_a = together((mine, corner, total, got_a))
+    mine, corner = together((mine, corner))
+    total, got_a = together((total, got_a))
 
     def corner_step(block, step):
         masks = ((4, 1, 3), (1, 3, 4))

time: 161 us -> 162 us (level)
  waiting for transfers between devices: 45.3 us -> 50.1 us
  starting transfers between devices: 41.2 us -> 37.4 us
    ppermute x10, waiting for transfers between devices: 6.3 us -> 9.84 us  [swap(): return lax.ppermute(block, axis, [(i, partner(i)) for i in range(count)])]
    ppermute x10, starting transfers between devices: 11.2 us -> 8.02 us  [gather_step(): return lax.ppermute(block, ('row', 'col'), route)]
    ppermute x2, waiting for transfers between devices: 3.4 us -> 1.04 us  [fold(): came = lax.ppermute(block[1], 'col', [(c, c ^ 12) for c in range(8)])]
    ppermute x10, starting transfers between devices: 17.8 us -> 15.5 us  [swap(): return lax.ppermute(block, axis, [(i, partner(i)) for i in range(count)])]
  transfers between devices with their start and end apart: 29 -> 29, of which waited for: 15 -> 16; matrix products, arithmetic and copies ran while one was open for 1% -> 1% of each run, Pallas kernels for 40% -> 40%
where the time goes in v12:
time: 162 us
  Pallas kernels  71.5 us (44%)
  waiting for transfers between devices  50.1 us (31%)
  starting transfers between devices  37.4 us (23%)
  other arithmetic  2.2 us (1%)
    pallas_call x1, Pallas kernels, update(): pl.pallas_call(update_kernel, out_shape=pltpu.HBM((2, 1024, 1024), F32),...  20.1 us
    pallas_call x2, Pallas kernels, pivot_terms(): pl.pallas_call(functools.partial(pivot_kernel, mine_half), out_shape=[jax...  18.3 us
    ppermute x10, starting transfers between devices, swap(): return lax.ppermute(block, axis, [(i, partner(i)) for i in range(count)])  15.5 us
    ppermute x10, waiting for transfers between devices, gather_step(): return lax.ppermute(block, ('row', 'col'), route)  15 us
    pallas_call x1, Pallas kernels, extend(): pl.pallas_call(extend_kernel, out_shape=pltpu.HBM((2, 1024, 1024), F32),...  11 us
    ppermute x10, waiting for transfers between devices, swap(): return lax.ppermute(block, axis, [(i, partner(i)) for i in range(count)])  9.84 us
    ppermute x3, waiting for transfers between devices, corner_step(): lax.ppermute(block, ('row', 'col'), route)  8.34 us
    ppermute x2, waiting for transfers between devices, double(): came = lax.ppermute(part, 'row', rings[step])  8.16 us
  transfers between devices with their start and end apart: 29, of which 16 were waited for; matrix products, arithmetic and copies ran while one was open for 1% of the time, Pallas kernels for 40%

profile of v12, /device:TPU:1, one launch (start us, length us, event | category | flops | bytes accessed | tf_op | source)
XLA Modules:
  0.0 161.7 jit_solution(17843849004820845373)
XLA Ops:
  0.0 1.8 %cut.1.first = f32[10,128,128]{2,1,0:T(8,128)S(1)} custom-call(s32[2,80]{1,0:T(2,128)} %maps.7, f32[10,2,128,640]{3,2,1,0:T(8,128)} %bitcast.12), custom_call_target="tpu_custom_call" | custom-call | bytes 1048576 | tf_op jit(solution)/shard_map/cut/pallas_call | solution.py:67
  1.9 4.5 %collective-permute-start = (f32[10,128,128]{2,1,0:T(8,128)S(1)}, f32[10,128,128]{2,1,0:T(8,128)S(1)}, u32[]{:S(2)}, u32[]{:S(2)}) collective-permute-start(f32[10,128,128]{2,1,0:T(8,128)S(1)} %cut.1.first), channel_id=1, source_target_pairs={{0,64},{16,80},{32,96},{48,112},{64,0},{80,16},{96,32},{112,48},{1... | collective-permute-start | bytes 1966088 | tf_op jit(solution)/shard_map/ppermute | solution.py:596
  6.4 5.1 %prepare.1 = (f32[15,128,128]{2,1,0:T(8,128)S(1)}, f32[25,128,128]{2,1,0:T(8,128)S(1)}, f32[2048,128]{1,0:T(8,128)S(1)}, f32[256,128]{1,0:T(8,128)S(1)}, f32[256,128]{1,0:T(8,128)S(1)}, /*index=5*/s32[64]{0:T(128)S(1)}) custom-call(s32[2,80]{1,0:T(2,128)} %maps.7, s32[8,128]{1,0:T(8,128)} %bitcast.18, f32[2048,1024]{1,0:T(8,128)} %front.5, ...), custom_call_target="tpu_custom_call" | custom-call | bytes 9437184 | tf_op jit(solution)/shard_map/prepare/pallas_call | solution.py:172
  11.5 1.0 collective-permute-start.1
  12.5 1.0 collective-permute-done.1
  13.6 3.1 %collective-permute-start.3 = (f32[256,128]{1,0:T(8,128)S(1)}, f32[256,128]{1,0:T(8,128)S(1)}, u32[]{:S(2)}, u32[]{:S(2)}) collective-permute-start(f32[256,128]{1,0:T(8,128)S(1)} %add.21), channel_id=1, source_target_pairs={{0,96},{16,112},{32,64},{48,80},{64,32},{80,48},{96,0},{112,16},{1... | collective-permute-start | bytes 393224 | tf_op jit(solution)/shard_map/ppermute | solution.py:596
  16.7 8.9 %pivot_terms_other.1 = (f32[512,1024]{1,0:T(8,128)S(1)}, f32[2048,128]{1,0:T(8,128)S(1)}, s32[513]{0:T(1024)S(1)}) custom-call(s32[2,80]{1,0:T(2,128)} %maps.7, s32[1024]{0:T(1024)} %pivots.1, f32[2048,1024]{1,0:T(8,128)} %front.5, f32[2560,640]{1,0:T(8,128)} %children.3), custom_call_target="tpu_custom_call" | custom-call | bytes 25165824 | tf_op jit(solution)/shard_map/pivot_terms_other/pallas_call | solution.py:264
  25.7 1.5 collective-permute-done.3
  27.2 1.3 collective-permute-start.13
  28.6 0.8 whole_panel.1
  29.4 4.5 %collective-permute-start.5 = (f32[1024,128]{1,0:T(8,128)S(1)}, f32[1024,128]{1,0:T(8,128)S(1)}, u32[]{:S(2)}, u32[]{:S(2)}) collective-permute-start(f32[1024,128]{1,0:T(8,128)S(1)} %get-tuple-element.75), channel_id=1, source_target_pairs={{0,12},{1,13},{2,14},{3,15},{4,8},{5,9},{6,10},{7,11},{16,28},{17,... | collective-permute-start | bytes 1572872 | tf_op jit(solution)/shard_map/ppermute | solution.py:600
  33.9 2.4 %collective-permute-start.14 = (f32[15,128,128]{2,1,0:T(8,128)S(1)}, f32[15,128,128]{2,1,0:T(8,128)S(1)}, u32[]{:S(2)}, u32[]{:S(2)}) collective-permute-start(f32[15,128,128]{2,1,0:T(8,128)S(1)} %get-tuple-element.82), channel_id=1, source_target_pairs={{0,64},{16,80},{32,96},{48,112},{64,0},{80,16},{96,32},{112,48},{1... | collective-permute-start | bytes 2949128 | tf_op jit(solution)/shard_map/ppermute | solution.py:596
  36.3 1.3 collective-permute-start.6
  37.6 9.3 %pivot_terms_mine.1 = (f32[512,1024]{1,0:T(8,128)S(1)}, f32[2048,128]{1,0:T(8,128)S(1)}, s32[513]{0:T(1024)S(1)}) custom-call(s32[2,80]{1,0:T(2,128)} %maps.7, s32[1024]{0:T(1024)} %pivots.1, f32[2048,1024]{1,0:T(8,128)} %front.5, f32[2560,640]{1,0:T(8,128)} %children.3, f32[2048,128]{1,0:T(8,128)S(1)} %get-tuple-element.69.refs_0_), custom_call_target="tpu_custom_call" | custom-call | bytes 25165824 | tf_op jit(solution)/shard_map/pivot_terms_mine/pallas_call | solution.py:264
  46.9 1.0 collective-permute-done.6
  48.1 3.5 %collective-permute-start.9 = (f32[1,512,128]{2,1,0:T(8,128)S(1)}, f32[1,512,128]{2,1,0:T(8,128)S(1)}, u32[]{:S(2)}, u32[]{:S(2)}) collective-permute-start(f32[1,512,128]{2,1,0:T(8,128)S(1)} %get-tuple-element.121), channel_id=1, source_target_pairs={{0,3},{1,2},{2,1},{3,0},{4,7},{5,6},{6,5},{7,4},{8,11},{9,10},{10,... | collective-permute-start | bytes 786440 | tf_op jit(solution)/shard_map/ppermute | solution.py:638
  51.6 0.4 add.25
  52.0 6.5 %collective-permute-done.14.refs_4_.refs_5_.refs_6_.refs_7_ = f32[15,128,128]{2,1,0:T(8,128)S(1)} collective-permute-done((f32[15,128,128]{2,1,0:T(8,128)S(1)}, f32[15,128,128]{2,1,0:T(8,128)S(1)}, u32[]{:S(2)}, u32[]{:S(2)}) %collective-permute-start.14) | collective-permute-done | bytes 983072 | tf_op jit(solution)/shard_map/ppermute | solution.py:596
  58.5 0.1 slice_select_fusion
  58.6 2.6 %collective-permute-start.15 = (f32[256,1024]{1,0:T(8,128)S(1)}, f32[256,1024]{1,0:T(8,128)S(1)}, u32[]{:S(2)}, u32[]{:S(2)}) collective-permute-start(f32[256,1024]{1,0:T(8,128)S(1)} %slice_select_fusion), channel_id=1, source_target_pairs={{0,32},{16,112},{32,0},{48,80},{64,96},{80,48},{96,64},{112,16},{1... | collective-permute-start | bytes 3145736 | tf_op jit(solution)/shard_map/ppermute | solution.py:625
  61.3 1.0 collective-permute-start.11
  62.3 0.1 collective-permute-start.10
  62.4 4.0 %collective-permute-done.11 = f32[1,256,128]{2,1,0:T(8,128)S(1)} collective-permute-done((f32[1,256,128]{2,1,0:T(8,128)S(1)}, f32[1,256,128]{2,1,0:T(8,128)S(1)}, u32[]{:S(2)}, u32[]{:S(2)}) %collective-permute-start.11) | collective-permute-done | bytes 131104 | tf_op jit(solution)/shard_map/ppermute | solution.py:663
  66.5 2.5 %collective-permute-start.12 = (f32[2,256,128]{2,1,0:T(8,128)S(1)}, f32[2,256,128]{2,1,0:T(8,128)S(1)}, u32[]{:S(2)}, u32[]{:S(2)}) collective-permute-start(f32[2,256,128]{2,1,0:T(8,128)S(1)} %pad_maximum_fusion.8), channel_id=1, source_target_pairs={{0,1},{1,0},{2,3},{3,2},{4,5},{5,4},{6,7},{7,6},{8,9},{9,8},{10,11... | collective-permute-start | bytes 786440 | tf_op jit(solution)/shard_map/ppermute | solution.py:663
  69.1 4.3 %collective-permute-done.12 = f32[2,256,128]{2,1,0:T(8,128)S(1)} collective-permute-done((f32[2,256,128]{2,1,0:T(8,128)S(1)}, f32[2,256,128]{2,1,0:T(8,128)S(1)}, u32[]{:S(2)}, u32[]{:S(2)}) %collective-permute-start.12) | collective-permute-done | bytes 262176 | tf_op jit(solution)/shard_map/ppermute | solution.py:663
  73.4 5.1 %collective-permute-done.8 = f32[2,512,128]{2,1,0:T(8,128)S(1)} collective-permute-done((f32[2,512,128]{2,1,0:T(8,128)S(1)}, f32[2,512,128]{2,1,0:T(8,128)S(1)}, u32[]{:S(2)}, u32[]{:S(2)}) %collective-permute-start.8) | collective-permute-done | bytes 524320 | tf_op jit(solution)/shard_map/ppermute | solution.py:638
  78.7 0.3 select_add_fusion
  79.3 0.4 collective-permute-start.17
  79.7 7.7 %collective-permute-done.19 = f32[128,1024]{1,0:T(8,128)S(1)} collective-permute-done((f32[128,1024]{1,0:T(8,128)S(1)}, f32[128,1024]{1,0:T(8,128)S(1)}, u32[]{:S(2)}, u32[]{:S(2)}) %collective-permute-start.19) | collective-permute-done | bytes 524320 | tf_op jit(solution)/shard_map/ppermute | solution.py:625
  87.8 8.2 %collective-permute-done.20 = f32[128,1024]{1,0:T(8,128)S(1)} collective-permute-done((f32[128,1024]{1,0:T(8,128)S(1)}, f32[128,1024]{1,0:T(8,128)S(1)}, u32[]{:S(2)}, u32[]{:S(2)}) %collective-permute-start.20) | collective-permute-done | bytes 524320 | tf_op jit(solution)/shard_map/ppermute | solution.py:628
  96.0 0.1 pad_maximum_fusion.4
  96.2 4.0 %collective-permute-done.17.refs_5_ = f32[4,512,128]{2,1,0:T(8,128)S(1)} collective-permute-done((f32[4,512,128]{2,1,0:T(8,128)S(1)}, f32[4,512,128]{2,1,0:T(8,128)S(1)}, u32[]{:S(2)}, u32[]{:S(2)}) %collective-permute-start.17) | collective-permute-done | bytes 1048608 | tf_op jit(solution)/shard_map/ppermute | solution.py:638
  100.2 1.0 collective-permute-start.24
  101.1 1.8 %collective-permute-start.23 = (f32[256,1024]{1,0:T(8,128)S(1)}, f32[256,1024]{1,0:T(8,128)S(1)}, u32[]{:S(2)}, u32[]{:S(2)}) collective-permute-start(f32[256,1024]{1,0:T(8,128)S(1)} %pad_maximum_fusion.4), channel_id=1, source_target_pairs={{0,32},{16,112},{32,0},{48,80},{64,96},{80,48},{96,64},{112,16},{1... | collective-permute-start | bytes 3145736 | tf_op jit(solution)/shard_map/ppermute | solution.py:628
  102.9 1.9 %collective-permute-start.21 = (f32[4,512,128]{2,1,0:T(8,128)S(1)}, f32[4,512,128]{2,1,0:T(8,128)S(1)}, u32[]{:S(2)}, u32[]{:S(2)}) collective-permute-start(f32[4,512,128]{2,1,0:T(8,128)S(1)} %pad_maximum_fusion.1.refs_0_), channel_id=1, source_target_pairs={{0,12},{1,13},{2,14},{3,15},{4,8},{5,9},{6,10},{7,11},{8,4},{9,5},... | collective-permute-start | bytes 3145736 | tf_op jit(solution)/shard_map/ppermute | solution.py:638
  104.8 11.0 %extend.1.front = f32[2,1024,1024]{2,1,0:T(8,128)} custom-call(s32[64]{0:T(128)S(1)} %get-tuple-element.62.table, f32[2,1024,1024]{2,1,0:T(8,128)} %bitcast.16, f32[10,2,128,640]{3,2,1,0:T(8,128)} %bitcast.14, f32[10,2,128,640]{3,2,1,0:T(8,128)} %bitcast.15, f32[10,128,128]{2,1,0:T(8,128)S(1)} %collective-permute-done.got.refs_2_.refs_3_, ...), custom_call_target="tpu_custom_call" | custom-call | bytes 1048576 | tf_op jit(solution)/shard_map/extend/pallas_call | solution.py:452
  115.8 2.0 %corners.1 = (bf16[3,512,512]{2,1,0:T(8,128)(2,1)S(1)}, bf16[3,512,512]{2,1,0:T(8,128)(2,1)S(1)}, f32[512,512]{1,0:T(8,128)S(1)}) custom-call(s32[64]{0:T(128)S(1)} %get-tuple-element.62.table, f32[8,256,128]{2,1,0:T(8,128)S(1)} %pad_maximum_fusion.3.own, f32[8,256,128]{2,1,0:T(8,128)S(1)} %collective-permute-done.24.swapped, f32[2,512,512]{2,1,0:T(8,128)S(1)} %copy-done), custom_call_target="tpu_custom_call" | custom-call | flops 805306368 | bytes 8388608 | tf_op jit(solution)/shard_map/corners/pallas_call | solution.py:342
  117.8 0.3 broadcast_select_fusion.1
  118.1 0.2 pad_maximum_fusion.own
  118.5 2.0 %collective-permute-start.28 = (f32[25,128,128]{2,1,0:T(8,128)S(1)}, f32[25,128,128]{2,1,0:T(8,128)S(1)}, u32[]{:S(2)}, u32[]{:S(2)}) collective-permute-start(f32[25,128,128]{2,1,0:T(8,128)S(1)} %get-tuple-element.115), channel_id=1, source_target_pairs={{0,64},{16,80},{32,96},{48,112},{64,0},{80,16},{96,32},{112,48},{1... | collective-permute-start | bytes 4915208 | tf_op jit(solution)/shard_map/ppermute | solution.py:596
  120.5 1.9 %collective-permute-start.25 = (f32[4,512,128]{2,1,0:T(8,128)S(1)}, f32[4,512,128]{2,1,0:T(8,128)S(1)}, u32[]{:S(2)}, u32[]{:S(2)}) collective-permute-start(f32[4,512,128]{2,1,0:T(8,128)S(1)} %collective-permute-done.16.refs_1_), channel_id=1, source_target_pairs={{0,12},{1,13},{2,14},{3,15},{4,8},{5,9},{6,10},{7,11},{8,4},{9,5},... | collective-permute-start | bytes 3145736 | tf_op jit(solution)/shard_map/ppermute | solution.py:638
  122.4 0.3 collective-permute-done.27.swapped
  122.7 7.9 %right_factor.1 = (bf16[1024,1024]{1,0:T(8,128)(2,1)S(1)}, bf16[1024,1024]{1,0:T(8,128)(2,1)S(1)}, f32[512,1024]{1,0:T(8,128)S(1)}) custom-call(s32[64]{0:T(128)S(1)} %get-tuple-element.62.table, f32[512,1024]{1,0:T(8,128)S(1)} %pad_maximum_fusion.own, f32[512,1024]{1,0:T(8,128)S(1)} %collective-permute-done.27.swapped, ...), custom_call_target="tpu_custom_call" | custom-call | flops 268435456 | bytes 4194304 | tf_op jit(solution)/shard_map/right_factor/pallas_call | solution.py:396
  130.5 5.1 %collective-permute-done.25.refs_3_ = f32[4,512,128]{2,1,0:T(8,128)S(1)} collective-permute-done((f32[4,512,128]{2,1,0:T(8,128)S(1)}, f32[4,512,128]{2,1,0:T(8,128)S(1)}, u32[]{:S(2)}, u32[]{:S(2)}) %collective-permute-start.25) | collective-permute-done | bytes 1048608 | tf_op jit(solution)/shard_map/ppermute | solution.py:638
  135.6 0.7 collective-permute-done.26.refs_7_
  136.3 20.1 %update.1 = f32[2,1024,1024]{2,1,0:T(8,128)} custom-call(s32[64]{0:T(128)S(1)} %get-tuple-element.62.table, f32[2,1024,1024]{2,1,0:T(8,128)} %extend.1.front, f32[4,512,128]{2,1,0:T(8,128)S(1)} %pad_maximum_fusion.1.refs_0_, f32[4,512,128]{2,1,0:T(8,128)S(1)} %collective-permute-done.16.refs_1_, f32[4,512,128]{2,1,0:T(8,128)S(1)} %collective-permute-done.21.refs_2_, ...), custom_call_target="tpu_custom_call" | custom-call | flops 2147483648 | bytes 4194304 | tf_op jit(solution)/shard_map/update/pallas_call | solution.py:515
  156.5 0.6 collective-permute-done.28.got
  157.1 4.5 %finish.1 = f32[2048,1024]{1,0:T(8,128)} custom-call(s32[64]{0:T(128)S(1)} %get-tuple-element.62.table, s32[513]{0:T(1024)S(1)} %get-tuple-element.63.list_other, s32[513]{0:T(1024)S(1)} %get-tuple-element.70.list_mine, f32[2048,1024]{1,0:T(8,128)} %bitcast.17, f32[25,128,128]{2,1,0:T(8,128)S(1)} %collective-permute-done.28.got, ...), custom_call_target="tpu_custom_call", output_to_operand_aliasing={{}: (3, {})} | custom-call | bytes 8388608 | tf_op jit(solution)/shard_map/finish/pallas_call | solution.py:576
  (43 shorter events, 1.5 us)
Async XLA Ops:
  1.9 25.4 %collective-permute-start = (f32[10,128,128]{2,1,0:T(8,128)S(1)}, f32[10,128,128]{2,1,0:T(8,128)S(1)}, u32[]{:S(2)}, u32[]{:S(2)}) collective-permute-start(f32[10,128,128]{2,1,0:T(8,128)S(1)} %cut.1.first), channel_id=1, source_target_pairs={{0,64},{16,80},{32,96},{48,112},{64,0},{80,16},{96,32},{112,48},{1... | collective-permute-start | bytes 1966088 | tf_op jit(solution)/shard_map/ppermute | solution.py:596
  11.5 2.0 %collective-permute-start.1 = (f32[256,128]{1,0:T(8,128)S(1)}, f32[256,128]{1,0:T(8,128)S(1)}, u32[]{:S(2)}, u32[]{:S(2)}) collective-permute-start(f32[256,128]{1,0:T(8,128)S(1)} %get-tuple-element.68), channel_id=1, source_target_pairs={{0,16},{16,0},{32,48},{48,32},{64,80},{80,64},{96,112},{112,96},{1... | collective-permute-start | bytes 393224 | tf_op jit(solution)/shard_map/ppermute | solution.py:596
  13.5 12.2 %collective-permute-start.4 = (f32[256,128]{1,0:T(8,128)S(1)}, f32[256,128]{1,0:T(8,128)S(1)}, u32[]{:S(2)}, u32[]{:S(2)}) collective-permute-start(f32[256,128]{1,0:T(8,128)S(1)} %add.21), channel_id=1, source_target_pairs={{0,64},{16,80},{32,96},{48,112},{64,0},{80,16},{96,32},{112,48},{1... | collective-permute-start | bytes 393224 | tf_op jit(solution)/shard_map/ppermute | solution.py:596
  13.6 13.6 %collective-permute-start.3 = (f32[256,128]{1,0:T(8,128)S(1)}, f32[256,128]{1,0:T(8,128)S(1)}, u32[]{:S(2)}, u32[]{:S(2)}) collective-permute-start(f32[256,128]{1,0:T(8,128)S(1)} %add.21), channel_id=1, source_target_pairs={{0,96},{16,112},{32,64},{48,80},{64,32},{80,48},{96,0},{112,16},{1... | collective-permute-start | bytes 393224 | tf_op jit(solution)/shard_map/ppermute | solution.py:596
  16.7 10.5 %collective-permute-start.2 = (f32[256,128]{1,0:T(8,128)S(1)}, f32[256,128]{1,0:T(8,128)S(1)}, u32[]{:S(2)}, u32[]{:S(2)}) collective-permute-start(f32[256,128]{1,0:T(8,128)S(1)} %add.21), channel_id=1, source_target_pairs={{0,32},{16,48},{32,0},{48,16},{64,96},{80,112},{96,64},{112,80},{1... | collective-permute-start | bytes 393224 | tf_op jit(solution)/shard_map/ppermute | solution.py:596
  27.2 24.4 %collective-permute-start.13 = (f32[512,1024]{1,0:T(8,128)S(1)}, f32[512,1024]{1,0:T(8,128)S(1)}, u32[]{:S(2)}, u32[]{:S(2)}) collective-permute-start(f32[512,1024]{1,0:T(8,128)S(1)} %get-tuple-element.81), channel_id=1, source_target_pairs={{0,16},{16,0},{32,48},{48,32},{64,80},{80,64},{96,112},{112,96},{1... | collective-permute-start | bytes 6291464 | tf_op jit(solution)/shard_map/ppermute | solution.py:596
  29.4 18.6 %collective-permute-start.5 = (f32[1024,128]{1,0:T(8,128)S(1)}, f32[1024,128]{1,0:T(8,128)S(1)}, u32[]{:S(2)}, u32[]{:S(2)}) collective-permute-start(f32[1024,128]{1,0:T(8,128)S(1)} %get-tuple-element.75), channel_id=1, source_target_pairs={{0,12},{1,13},{2,14},{3,15},{4,8},{5,9},{6,10},{7,11},{16,28},{17,... | collective-permute-start | bytes 1572872 | tf_op jit(solution)/shard_map/ppermute | solution.py:600
  33.9 24.6 %collective-permute-start.14 = (f32[15,128,128]{2,1,0:T(8,128)S(1)}, f32[15,128,128]{2,1,0:T(8,128)S(1)}, u32[]{:S(2)}, u32[]{:S(2)}) collective-permute-start(f32[15,128,128]{2,1,0:T(8,128)S(1)} %get-tuple-element.82), channel_id=1, source_target_pairs={{0,64},{16,80},{32,96},{48,112},{64,0},{80,16},{96,32},{112,48},{1... | collective-permute-start | bytes 2949128 | tf_op jit(solution)/shard_map/ppermute | solution.py:596
  36.3 11.7 %collective-permute-start.6 = (f32[256,128]{1,0:T(8,128)S(1)}, f32[256,128]{1,0:T(8,128)S(1)}, u32[]{:S(2)}, u32[]{:S(2)}) collective-permute-start(f32[256,128]{1,0:T(8,128)S(1)} %add_add_fusion), channel_id=1, source_target_pairs={{0,12},{1,13},{2,14},{3,15},{4,8},{5,9},{6,10},{7,11},{16,28},{17,... | collective-permute-start | bytes 393224 | tf_op jit(solution)/shard_map/ppermute | solution.py:600
  48.1 14.2 %collective-permute-start.9 = (f32[1,512,128]{2,1,0:T(8,128)S(1)}, f32[1,512,128]{2,1,0:T(8,128)S(1)}, u32[]{:S(2)}, u32[]{:S(2)}) collective-permute-start(f32[1,512,128]{2,1,0:T(8,128)S(1)} %get-tuple-element.121), channel_id=1, source_target_pairs={{0,3},{1,2},{2,1},{3,0},{4,7},{5,6},{6,5},{7,4},{8,11},{9,10},{10,... | collective-permute-start | bytes 786440 | tf_op jit(solution)/shard_map/ppermute | solution.py:638
  51.6 17.3 %collective-permute-start.7 = (f32[1,512,128]{2,1,0:T(8,128)S(1)}, f32[1,512,128]{2,1,0:T(8,128)S(1)}, u32[]{:S(2)}, u32[]{:S(2)}) collective-permute-start(f32[1,512,128]{2,1,0:T(8,128)S(1)} %get-tuple-element.122), channel_id=1, source_target_pairs={{0,1},{1,0},{2,3},{3,2},{4,5},{5,4},{6,7},{7,6},{8,9},{9,8},{10,11... | collective-permute-start | bytes 786440 | tf_op jit(solution)/shard_map/ppermute | solution.py:638
  58.6 20.0 %collective-permute-start.15 = (f32[256,1024]{1,0:T(8,128)S(1)}, f32[256,1024]{1,0:T(8,128)S(1)}, u32[]{:S(2)}, u32[]{:S(2)}) collective-permute-start(f32[256,1024]{1,0:T(8,128)S(1)} %slice_select_fusion), channel_id=1, source_target_pairs={{0,32},{16,112},{32,0},{48,80},{64,96},{80,48},{96,64},{112,16},{1... | collective-permute-start | bytes 3145736 | tf_op jit(solution)/shard_map/ppermute | solution.py:625
  61.3 5.2 %collective-permute-start.11 = (f32[1,256,128]{2,1,0:T(8,128)S(1)}, f32[1,256,128]{2,1,0:T(8,128)S(1)}, u32[]{:S(2)}, u32[]{:S(2)}) collective-permute-start(f32[1,256,128]{2,1,0:T(8,128)S(1)} %select_bitcast_fusion), channel_id=1, source_target_pairs={{0,4},{1,5},{2,6},{3,7},{4,0},{5,1},{6,2},{7,3},{8,12},{9,13},{10,... | collective-permute-start | bytes 393224 | tf_op jit(solution)/shard_map/ppermute | solution.py:663
  62.3 11.0 %collective-permute-start.10 = (f32[2,512,128]{2,1,0:T(8,128)S(1)}, f32[2,512,128]{2,1,0:T(8,128)S(1)}, u32[]{:S(2)}, u32[]{:S(2)}) collective-permute-start(f32[2,512,128]{2,1,0:T(8,128)S(1)} %pad_maximum_fusion.6), channel_id=1, source_target_pairs={{0,1},{1,0},{2,3},{3,2},{4,5},{5,4},{6,7},{7,6},{8,9},{9,8},{10,11... | collective-permute-start | bytes 1572872 | tf_op jit(solution)/shard_map/ppermute | solution.py:638
  66.5 6.8 %collective-permute-start.12 = (f32[2,256,128]{2,1,0:T(8,128)S(1)}, f32[2,256,128]{2,1,0:T(8,128)S(1)}, u32[]{:S(2)}, u32[]{:S(2)}) collective-permute-start(f32[2,256,128]{2,1,0:T(8,128)S(1)} %pad_maximum_fusion.8), channel_id=1, source_target_pairs={{0,1},{1,0},{2,3},{3,2},{4,5},{5,4},{6,7},{7,6},{8,9},{9,8},{10,11... | collective-permute-start | bytes 786440 | tf_op jit(solution)/shard_map/ppermute | solution.py:663
  69.0 9.6 %collective-permute-start.8 = (f32[2,512,128]{2,1,0:T(8,128)S(1)}, f32[2,512,128]{2,1,0:T(8,128)S(1)}, u32[]{:S(2)}, u32[]{:S(2)}) collective-permute-start(f32[2,512,128]{2,1,0:T(8,128)S(1)} %pad_maximum_fusion.5), channel_id=1, source_target_pairs={{0,3},{1,2},{2,1},{3,0},{4,7},{5,6},{6,5},{7,4},{8,11},{9,10},{10,... | collective-permute-start | bytes 1572872 | tf_op jit(solution)/shard_map/ppermute | solution.py:638
  79.0 8.4 %collective-permute-start.19 = (f32[128,1024]{1,0:T(8,128)S(1)}, f32[128,1024]{1,0:T(8,128)S(1)}, u32[]{:S(2)}, u32[]{:S(2)}) collective-permute-start(f32[128,1024]{1,0:T(8,128)S(1)} %slice_select_fusion.1), channel_id=1, source_target_pairs={{0,96},{16,48},{32,64},{48,16},{64,32},{80,112},{96,0},{112,80},{1... | collective-permute-start | bytes 1572872 | tf_op jit(solution)/shard_map/ppermute | solution.py:625
  79.1 8.6 %collective-permute-start.18 = (f32[4,256,128]{2,1,0:T(8,128)S(1)}, f32[4,256,128]{2,1,0:T(8,128)S(1)}, u32[]{:S(2)}, u32[]{:S(2)}) collective-permute-start(f32[4,256,128]{2,1,0:T(8,128)S(1)} %pad_maximum_fusion.7), channel_id=1, source_target_pairs={{0,3},{1,2},{2,1},{3,0},{4,7},{5,6},{6,5},{7,4},{8,11},{9,10},{10,... | collective-permute-start | bytes 1572872 | tf_op jit(solution)/shard_map/ppermute | solution.py:663
  79.2 16.9 %collective-permute-start.16 = (f32[4,512,128]{2,1,0:T(8,128)S(1)}, f32[4,512,128]{2,1,0:T(8,128)S(1)}, u32[]{:S(2)}, u32[]{:S(2)}) collective-permute-start(f32[4,512,128]{2,1,0:T(8,128)S(1)} %pad_maximum_fusion.1.refs_0_), channel_id=1, source_target_pairs={{0,4},{1,5},{2,6},{3,7},{4,0},{5,1},{6,2},{7,3},{8,12},{9,13},{10,... | collective-permute-start | bytes 3145736 | tf_op jit(solution)/shard_map/ppermute | solution.py:638
  79.3 20.9 %collective-permute-start.17 = (f32[4,512,128]{2,1,0:T(8,128)S(1)}, f32[4,512,128]{2,1,0:T(8,128)S(1)}, u32[]{:S(2)}, u32[]{:S(2)}) collective-permute-start(f32[4,512,128]{2,1,0:T(8,128)S(1)} %pad_maximum_fusion.2.refs_4_), channel_id=1, source_target_pairs={{0,12},{1,13},{2,14},{3,15},{4,8},{5,9},{6,10},{7,11},{8,4},{9,5},... | collective-permute-start | bytes 3145736 | tf_op jit(solution)/shard_map/ppermute | solution.py:638
  87.5 8.4 %collective-permute-start.20 = (f32[128,1024]{1,0:T(8,128)S(1)}, f32[128,1024]{1,0:T(8,128)S(1)}, u32[]{:S(2)}, u32[]{:S(2)}) collective-permute-start(f32[128,1024]{1,0:T(8,128)S(1)} %select_add_fusion.1), channel_id=1, source_target_pairs={{0,96},{16,48},{32,64},{48,16},{64,32},{80,112},{96,0},{112,80},{1... | collective-permute-start | bytes 1572872 | tf_op jit(solution)/shard_map/ppermute | solution.py:628
  100.2 15.6 %collective-permute-start.24 = (f32[8,256,128]{2,1,0:T(8,128)S(1)}, f32[8,256,128]{2,1,0:T(8,128)S(1)}, u32[]{:S(2)}, u32[]{:S(2)}) collective-permute-start(f32[8,256,128]{2,1,0:T(8,128)S(1)} %pad_maximum_fusion.3.own), channel_id=1, source_target_pairs={{0,16},{16,0},{32,48},{48,32},{64,80},{80,64},{96,112},{112,96},{1... | collective-permute-start | bytes 3145736 | tf_op jit(solution)/shard_map/ppermute | solution.py:596
  101.1 16.7 %collective-permute-start.23 = (f32[256,1024]{1,0:T(8,128)S(1)}, f32[256,1024]{1,0:T(8,128)S(1)}, u32[]{:S(2)}, u32[]{:S(2)}) collective-permute-start(f32[256,1024]{1,0:T(8,128)S(1)} %pad_maximum_fusion.4), channel_id=1, source_target_pairs={{0,32},{16,112},{32,0},{48,80},{64,96},{80,48},{96,64},{112,16},{1... | collective-permute-start | bytes 3145736 | tf_op jit(solution)/shard_map/ppermute | solution.py:628
  102.9 15.5 %collective-permute-start.21 = (f32[4,512,128]{2,1,0:T(8,128)S(1)}, f32[4,512,128]{2,1,0:T(8,128)S(1)}, u32[]{:S(2)}, u32[]{:S(2)}) collective-permute-start(f32[4,512,128]{2,1,0:T(8,128)S(1)} %pad_maximum_fusion.1.refs_0_), channel_id=1, source_target_pairs={{0,12},{1,13},{2,14},{3,15},{4,8},{5,9},{6,10},{7,11},{8,4},{9,5},... | collective-permute-start | bytes 3145736 | tf_op jit(solution)/shard_map/ppermute | solution.py:638
  104.8 13.6 %collective-permute-start.22 = (f32[4,512,128]{2,1,0:T(8,128)S(1)}, f32[4,512,128]{2,1,0:T(8,128)S(1)}, u32[]{:S(2)}, u32[]{:S(2)}) collective-permute-start(f32[4,512,128]{2,1,0:T(8,128)S(1)} %pad_maximum_fusion.2.refs_4_), channel_id=1, source_target_pairs={{0,4},{1,5},{2,6},{3,7},{4,0},{5,1},{6,2},{7,3},{8,12},{9,13},{10,... | collective-permute-start | bytes 3145736 | tf_op jit(solution)/shard_map/ppermute | solution.py:638
  104.8 11.0 %copy-start = (f32[2,512,512]{2,1,0:T(8,128)S(1)}, f32[2,512,512]{2,1,0:T(8,128)}, u32[]{:S(2)}) copy-start(f32[2,512,512]{2,1,0:T(8,128)} %inverses.1) | copy-start | bytes 6291460
  118.5 4.2 %collective-permute-start.27 = (f32[512,1024]{1,0:T(8,128)S(1)}, f32[512,1024]{1,0:T(8,128)S(1)}, u32[]{:S(2)}, u32[]{:S(2)}) collective-permute-start(f32[512,1024]{1,0:T(8,128)S(1)} %pad_maximum_fusion.own), channel_id=1, source_target_pairs={{0,16},{16,0},{32,48},{48,32},{64,80},{80,64},{96,112},{112,96},{1... | collective-permute-start | bytes 6291464 | tf_op jit(solution)/shard_map/ppermute | solution.py:596
  118.5 38.5 %collective-permute-start.28 = (f32[25,128,128]{2,1,0:T(8,128)S(1)}, f32[25,128,128]{2,1,0:T(8,128)S(1)}, u32[]{:S(2)}, u32[]{:S(2)}) collective-permute-start(f32[25,128,128]{2,1,0:T(8,128)S(1)} %get-tuple-element.115), channel_id=1, source_target_pairs={{0,64},{16,80},{32,96},{48,112},{64,0},{80,16},{96,32},{112,48},{1... | collective-permute-start | bytes 4915208 | tf_op jit(solution)/shard_map/ppermute | solution.py:596
  120.5 15.2 %collective-permute-start.25 = (f32[4,512,128]{2,1,0:T(8,128)S(1)}, f32[4,512,128]{2,1,0:T(8,128)S(1)}, u32[]{:S(2)}, u32[]{:S(2)}) collective-permute-start(f32[4,512,128]{2,1,0:T(8,128)S(1)} %collective-permute-done.16.refs_1_), channel_id=1, source_target_pairs={{0,12},{1,13},{2,14},{3,15},{4,8},{5,9},{6,10},{7,11},{8,4},{9,5},... | collective-permute-start | bytes 3145736 | tf_op jit(solution)/shard_map/ppermute | solution.py:638
  122.4 13.9 %collective-permute-start.26 = (f32[4,512,128]{2,1,0:T(8,128)S(1)}, f32[4,512,128]{2,1,0:T(8,128)S(1)}, u32[]{:S(2)}, u32[]{:S(2)}) collective-permute-start(f32[4,512,128]{2,1,0:T(8,128)S(1)} %collective-permute-done.17.refs_5_), channel_id=1, source_target_pairs={{0,4},{1,5},{2,6},{3,7},{4,0},{5,1},{6,2},{7,3},{8,12},{9,13},{10,... | collective-permute-start | bytes 3145736 | tf_op jit(solution)/shard_map/ppermute | solution.py:638
